TPU v7x, 32 devices: a whole 2x2x4 slice. The times are simulated.
32 devices in a mesh: fsdp: 8 (over y, x, core), tensor: 4 (over z).
Axes of the slice: x: 2, y: 2, z: 4, core: 2. Of those that a mesh axis runs over, the one named last changes fastest.
Arguments:
- normed: bfloat16 [8192, 8192], P('fsdp', 'tensor')
- tile_values: bfloat16 [4, 128, 128, 128], P('tensor', 'fsdp'), may hold values from -0.09375 to 0.09375
- tile_rows: int32 [4, 128], P('tensor', 'fsdp'), may hold values from -1 to 15, as said below
- tile_columns: int32 [4, 128], P('tensor', 'fsdp'), may hold values from -1 to 7, as said below
- cotangent: bfloat16 [8192, 1024], P('fsdp', 'tensor')
Outputs:
- values: bfloat16 [8192, 1024], P('fsdp', 'tensor')
- grad_input: bfloat16 [8192, 8192], P('fsdp', 'tensor')
- tile_update: bfloat16 [4, 128, 128, 128], P('tensor', 'fsdp')
Inputs may be any that keep to these rules, and one draw needn't show every extreme that they name: tile_rows[q, s] is -1 exactly where tile_columns[q, s] is -1 (an empty slot). In every part q exactly 64 slots are filled, no (row block, column block) pair appears twice, and each column block holds exactly 8 of the 16 row blocks. The slots s with equal s // 16 belong to one owner; in every part some owner has all 16 of its slots filled. `tile_columns`: column block of the tile in each slot; -1 marks an empty slot, as in tile_rows.
All inputs are finite; a program needn't handle non-finite values.
Results may differ from a plain program's by a relative error of at most 0.001.
Values may be sent and summed in bfloat16 or wider, within the bound.
No kernel may reach another device: no remote copies, remote signals or barrier semaphores. Data moves between devices by JAX's collectives and lax.ppermute only.
A program may use at most 128 MiB of HBM per device.

v0:
```python
import jax
import jax.numpy as jnp
from jax import lax
from jax.sharding import PartitionSpec as P


def normalize(summed):
    inverse_rms = lax.rsqrt(jnp.mean(summed * summed, axis=(1, 2), keepdims=True) + 1e-06)
    return (summed * inverse_rms).astype(jnp.bfloat16)


def local(normed, tile_values, tile_rows, tile_columns, cotangent):
    feature_width = normed.shape[1]
    tile_size = tile_values.shape[-1]
    row_blocks = feature_width // tile_size
    gathered_values, gathered_rows, gathered_columns = (
        lax.all_gather(tile_values, "fsdp", axis=1, tiled=True),
        lax.all_gather(tile_rows, "fsdp", axis=1, tiled=True),
        lax.all_gather(tile_columns, "fsdp", axis=1, tiled=True),
    )
    gathered_values = gathered_values[0]
    gathered_rows = gathered_rows[0]
    gathered_columns = gathered_columns[0]
    full_cotangent = lax.all_gather(cotangent, "tensor", axis=1, tiled=True)
    column_blocks = full_cotangent.shape[1] // tile_size
    pair_total = row_blocks * column_blocks
    occupied = gathered_columns >= 0
    pair_index = jnp.where(occupied, gathered_rows * column_blocks + gathered_columns, 0)
    pair_hot = (
        (pair_index[:, None] == jnp.arange(pair_total, dtype=jnp.int32)[None, :])
        & occupied[:, None]
    ).astype(jnp.bfloat16)
    blocks = jnp.einsum(
        "sp,sij->pij", pair_hot, gathered_values, preferred_element_type=jnp.float32
    ).astype(jnp.bfloat16)
    weight = (
        blocks.reshape(row_blocks, column_blocks, tile_size, tile_size)
        .transpose(0, 2, 1, 3)
        .reshape(feature_width, column_blocks * tile_size)
    )
    partial_value = jnp.dot(normed, weight, preferred_element_type=jnp.float32)
    values = lax.psum_scatter(partial_value, "tensor", scatter_dimension=1, tiled=True).astype(
        jnp.bfloat16
    )
    grad_input = jnp.einsum(
        "tk,dk->td", full_cotangent, weight, preferred_element_type=jnp.float32
    ).astype(jnp.bfloat16)
    gradient = jnp.einsum("td,tk->dk", normed, full_cotangent, preferred_element_type=jnp.float32)
    grad_pairs = (
        gradient.reshape(row_blocks, tile_size, column_blocks, tile_size)
        .transpose(0, 2, 1, 3)
        .reshape(pair_total, tile_size, tile_size)
    )
    summed = lax.psum_scatter(
        jnp.where(occupied[:, None, None], jnp.take(grad_pairs, pair_index, axis=0), 0.0),
        "fsdp",
        scatter_dimension=0,
        tiled=True,
    )
    tile_update = normalize(summed)
    return (values, grad_input, tile_update[None])


def solution(mesh):
    in_specs = (
        P("fsdp", "tensor"),
        P("tensor", "fsdp", None, None),
        P("tensor", "fsdp"),
        P("tensor", "fsdp"),
        P("fsdp", "tensor"),
    )
    out_specs = (P("fsdp", "tensor"), P("fsdp", "tensor"), P("tensor", "fsdp", None, None))
    return jax.shard_map(local, mesh=mesh, in_specs=in_specs, out_specs=out_specs, check_vma=False)
```

profile of v0, /device:TPU:0, one launch (start us, length us, event | category | flops | bytes accessed | tf_op | source)
XLA Modules:
  0.0 260.3 jit_solution(3818393425666051459)
XLA Ops:
  7.2 0.0 all-gather.5.cloned.1.call-start
  7.2 0.7 all-gather.5.cloned.1.call-update
  7.9 0.0 all-gather.3.cloned.1.call-start
  7.9 2.2 copy.11
  10.1 0.0 all-gather.3.cloned.1.call-update
  10.1 0.0 reduce-scatter.5.cloned.1.call-start
  10.2 1.2 dynamic-slice
  12.1 0.8 bitcast_dynamic-update-slice_fusion
  12.9 0.7 bitcast_dynamic-update-slice_fusion.1
  13.6 9.5 %all-reduce.2 = (s32[128]{0:T(128)S(1)}, s32[128]{0:T(128)S(1)}) all-reduce(s32[128]{0:T(128)S(1)} %bitcast_dynamic-update-slice_fusion.1, s32[128]{0:T(128)S(1)} %bitcast_dynamic-update-slice_fusion), channel_id=1, replica_groups=mesh['fsdp'=8,'tensor'=4] {'fsdp'}, use_global_device_ids=true, to_apply=%add | all-reduce | flops 256 | bytes 2048
  23.1 35.4 %all-gather.5.cloned.1.call-done = bf16[1024,1024]{1,0:T(8,128)(2,1)} async-done(((bf16[1024,256]{1,0:T(8,128)(2,1)}), bf16[1024,1024]{1,0:T(8,128)(2,1)}) %all-gather.5.cloned.1.call-update) | async-done | bytes 2097168 | tf_op jit(solution)/shard_map/all_gather | solution.py:24
  58.5 7.1 %convolution_bitcast_fusion = f32[256,8,8,128]{3,1,2,0:T(8,128)S(1)} fusion(bf16[1024,2048]{1,0:T(8,128)(2,1)} %param.5, bf16[1024,1024]{1,0:T(8,128)(2,1)} %all-gather.5.cloned.1.call-done), kind=kOutput, calls=%fused_computation.12 | convolution fusion | flops 4294967296 | bytes 14680064 | tf_op jit(solution)/shard_map/td,tk->dk/dot_general | solution.py:48
  65.7 2.1 copy.17
  67.8 4.7 %copy.13 = f32[16,128,8,128]{3,1,2,0:T(8,128)} copy(f32[16,128,8,128]{3,2,1,0:T(8,128)S(1)} %bitcast.49) | data formatting | bytes 16777216 | tf_op jit(solution)/shard_map/reshape | solution.py:50
  72.5 7.7 %gather_fusion = f32[128,128,128]{2,1,0:T(8,128)} fusion(f32[128,128,128]{2,1,0:T(8,128)} %bitcast.48, s32[1024]{0:T(1024)S(1)} %pad_clamp_fusion), kind=kCustom, calls=%fused_computation | custom fusion | bytes 16777728 | tf_op jit(solution)/shard_map/jit(_take)/gather | solution.py:55
  80.1 7.0 %select_select_fusion = f32[128,128,128]{2,1,0:T(8,128)} fusion(f32[128,128,128]{2,1,0:T(8,128)} %gather_fusion, pred[128]{0:T(512)(128)(4,1)S(1)} %get-tuple-element.11, pred[128]{0:T(512)(128)(4,1)S(1)} %get-tuple-element.13), kind=kLoop, calls=%fused_computation.1 | loop fusion | flops 4194304 | bytes 16777472 | tf_op jit(solution)/shard_map/jit(_where)/select_n | solution.py:55
  87.1 0.0 reduce-scatter.5.cloned.1.call-update
  87.2 0.2 reduce-scatter.3.cloned.1.call-start
  87.4 9.3 %all-gather.3.cloned.1.call-done = bf16[1,128,128,128]{3,1,2,0:T(8,128)(2,1)} async-done(((bf16[1,16,128,128]{3,1,2,0:T(8,128)(2,1)}), bf16[1,128,128,128]{3,1,2,0:T(8,128)(2,1)}) %all-gather.3.cloned.1.call-update) | async-done | bytes 4194320 | tf_op jit(solution)/shard_map/all_gather | solution.py:17
  96.7 3.4 %convert_bitcast_fusion.1 = bf16[16,8,128,128]{3,1,0,2:T(8,128)(2,1)S(1)} fusion(bf16[1,128,128,128]{3,1,2,0:T(8,128)(2,1)} %all-gather.3.cloned.1.call-done, s32[128]{0:T(128)S(1)} %get-tuple-element.12, pred[128]{0:T(512)(128)(4,1)S(1)} %get-tuple-element.13), kind=kOutput, calls=%fused_computation.9 | convolution fusion | flops 539000832 | bytes 8389248 | tf_op jit(solution)/shard_map/sp,sij->pij/dot_general | solution.py:33
  100.1 0.0 copy-start.2
  100.1 1.1 copy.12
  101.2 0.0 copy-start
  101.2 2.0 copy-done
  103.2 0.0 copy-done.2
  103.2 6.1 %fusion.12 = f32[1024,1024]{0,1:T(8,128)} fusion(bf16[1024,2048]{1,0:T(8,128)(2,1)S(1)} %copy-done.2, bf16[256,8,8,128]{3,2,1,0:T(8,128)(2,1)S(1)} %bitcast.50), kind=kOutput, calls=%fused_computation.13 | convolution fusion | flops 4294967296 | bytes 12582912 | tf_op jit(solution)/shard_map/dot_general | solution.py:41
  109.3 0.0 copy-start.3
  109.3 0.0 reduce-scatter.3.cloned.1.call-update
  109.4 1.9 copy-done.3
  111.3 9.1 %convert_bitcast_fusion = bf16[1024,2048]{0,1:T(8,128)(2,1)} fusion(bf16[1024,1024]{1,0:T(8,128)(2,1)S(1)} %copy-done.3, bf16[256,8,8,128]{3,2,1,0:T(8,128)(2,1)} %bitcast.51), kind=kOutput, calls=%fused_computation.8 | convolution fusion | flops 4297064448 | bytes 10485760 | tf_op jit(solution)/shard_map/tk,dk->td/dot_general | solution.py:45
  120.4 6.6 %copy.15 = bf16[1024,2048]{1,0:T(8,128)(2,1)} copy(bf16[1024,2048]{0,1:T(8,128)(2,1)} %convert_bitcast_fusion) | data formatting | bytes 8388608
  127.0 44.5 %reduce-scatter.5.cloned.1.call-done = f32[16,128,128]{2,1,0:T(8,128)} async-done(((f32[128,128,128]{2,1,0:T(8,128)}), f32[16,128,128]{2,1,0:T(8,128)}) %reduce-scatter.5.cloned.1.call-update) | async-done | bytes 1048592 | tf_op jit(solution)/shard_map/reduce_scatter | solution.py:54
  171.5 0.0 copy-start.1
  171.5 1.5 multiply_reduce_fusion
  173.0 77.5 %reduce-scatter.3.cloned.1.call-done = f32[1024,256]{0,1:T(8,128)} async-done(((f32[1024,1024]{0,1:T(8,128)}), f32[1024,256]{0,1:T(8,128)}) %reduce-scatter.3.cloned.1.call-update) | async-done | bytes 1048592 | tf_op jit(solution)/shard_map/reduce_scatter | solution.py:42
  250.5 1.3 convert_element_type.17
  251.8 1.0 copy.14
  252.8 0.0 copy-done.1
  252.8 0.9 fusion.15
  (6 shorter events, 0.0 us)
Async XLA Ops:
  7.2 51.4 %all-gather.5.cloned.1.call-start = ((), (), s32[]{:S(2)}) async-start(), calls=%async_computation.4 | async-start | bytes 2621440 | tf_op jit(solution)/shard_map/all_gather | solution.py:24
  7.9 88.8 %all-gather.3.cloned.1.call-start = ((), (), s32[]{:S(2)}) async-start(), calls=%async_computation.2 | async-start | bytes 4718592 | tf_op jit(solution)/shard_map/all_gather | solution.py:17
  10.1 161.3 %reduce-scatter.5.cloned.1.call-start = ((), (), s32[]{:S(2)}) async-start(), calls=%async_computation.5 | async-start | bytes 9437184 | tf_op jit(solution)/shard_map/reduce_scatter | solution.py:54
  87.2 163.3 %reduce-scatter.3.cloned.1.call-start = ((), (), s32[]{:S(2)}) async-start(), calls=%async_computation.3 | async-start | bytes 5242880 | tf_op jit(solution)/shard_map/reduce_scatter | solution.py:42
  100.1 3.1 %copy-start.2 = (bf16[1024,2048]{1,0:T(8,128)(2,1)S(1)}, bf16[1024,2048]{1,0:T(8,128)(2,1)}, u32[]{:S(2)}) copy-start(bf16[1024,2048]{1,0:T(8,128)(2,1)} %param.5) | copy-start | bytes 12582916
  101.2 2.0 copy-start
  109.3 1.9 copy-start.3
  171.5 81.3 %copy-start.1 = (f32[16,128,128]{2,1,0:T(8,128)S(1)}, f32[16,128,128]{2,1,0:T(8,128)}, u32[]{:S(2)}) copy-start(f32[16,128,128]{2,1,0:T(8,128)} %reduce-scatter.5.cloned.1.call-done) | copy-start | bytes 3145732
Sparse Core Ops, SparseCore 0:
  9.6 48.9 all-gather.4
  61.0 35.6 all-gather.2
  100.1 71.2 reduce-scatter.4
  173.7 76.7 reduce-scatter.2
where the time goes:
time: 261 us; the launch traced here: 260 us
  waiting for transfers between devices  167 us (64%)
  local copies, waits for them, and re-layouts  32 us (12%)
  matrix products  25.8 us (10%)
  between operations  14.5 us (6%)
  other arithmetic  10.8 us (4%)
  blocking collectives  9.46 us (4%)
    reduce_scatter x1, waiting for transfers between devices, local(): lax.psum_scatter(partial_value, 'tensor', scatter_dimension=1, tiled=True)  77.5 us
    reduce_scatter x1, waiting for transfers between devices, local(): lax.psum_scatter(jnp.where(occupied[:, None, None], jnp.take(grad_pairs,...  44.5 us
    all_gather x1, waiting for transfers between devices, local(): full_cotangent = lax.all_gather(cotangent, 'tensor', axis=1, tiled=True)  35.4 us
    unnamed x17, local copies, waits for them, and re-layouts  18.5 us
    unnamed x1, blocking collectives  9.46 us
    all_gather x1, waiting for transfers between devices, local(): lax.all_gather(tile_values, 'fsdp', axis=1, tiled=True)  9.29 us
    dot_general x1, matrix products, local(): jnp.einsum('tk,dk->td', full_cotangent, weight, preferred_element_type=jn...  9.1 us
    gather x1, local copies, waits for them, and re-layouts, local(): jnp.take(grad_pairs, pair_index, axis=0)  7.69 us
  transfers between devices with their start and end apart: 4, of which 4 were waited for; matrix products, arithmetic and copies ran while one was open for 24% of the time, Pallas kernels for 0%

commit v1 on v0

v1 whole, which is shorter than its diff:
```python
import functools

import jax
import jax.numpy as jnp
from jax import lax
from jax.experimental import pallas as pl
from jax.experimental.pallas import tpu as pltpu
from jax.sharding import PartitionSpec as P

VMEM_BYTES = 48 * 1024 * 1024
GROUP = 128
PAD = 16


def encode(block):
    peak = jnp.max(jnp.abs(block), axis=0, keepdims=True)
    exponent = jnp.floor(jnp.log2(jnp.maximum(peak, 2.0**-100))) + 1.0
    exponent = jnp.clip(exponent, -100.0, 128.0)
    scaled = jnp.round(block * jnp.exp2(15.0 - exponent))
    codes = jnp.clip(scaled, -32767.0, 32767.0).astype(jnp.int32).astype(jnp.int16)
    return codes, exponent


def decode(codes, exponent):
    return codes.astype(jnp.int32).astype(jnp.float32) * jnp.exp2(exponent - 15.0)


def as_code(exponents):
    return exponents.astype(jnp.int32).astype(jnp.int16)


def exponent_rows(codes):
    return codes.astype(jnp.int32).astype(jnp.float32)


def params():
    return pltpu.CompilerParams(vmem_limit_bytes=VMEM_BYTES)


def whole(shape):
    zeros = (0,) * len(shape)
    return pl.BlockSpec(shape, lambda *_: zeros, pipeline_mode=pl.Buffered(1))


def aligned(index, size):
    return pl.ds(pl.multiple_of(index * size, size), size)


def write_message(message_ref, rows, blocks):
    place = lax.broadcasted_iota(jnp.int32, (PAD, message_ref.shape[1]), 0)
    exponents = jnp.zeros((PAD, message_ref.shape[1]), jnp.float32)
    for group in range(rows // GROUP):
        codes, exponent = encode(blocks(group))
        message_ref[group * GROUP : (group + 1) * GROUP, :] = codes
        exponents = jnp.where(place == group, exponent, exponents)
    message_ref[rows : rows + PAD, :] = as_code(exponents)


def read_message(message_ref, rows):
    exponents = exponent_rows(message_ref[rows : rows + PAD, :])

    def block(group):
        return decode(
            message_ref[group * GROUP : (group + 1) * GROUP, :], exponents[group : group + 1, :]
        )

    return block


def values_kernel(devices, column_blocks, codes_ref, place_ref, normed_ref, *refs):
    tile_refs = refs[:devices]
    partial_ref, first_ref, transposed_ref, weight = refs[devices:]
    step = pl.program_id(0)
    chunks, block, chunk_width = partial_ref.shape
    tile = tile_refs[0].shape[-1]

    @pl.when(step == 0)
    def _():
        weight[...] = jnp.zeros_like(weight)
        transposed_ref[...] = jnp.zeros_like(transposed_ref)
        for k in range(devices):

            @pl.loop(0, tile_refs[k].shape[0])
            def _(slot):
                code = codes_ref[k, slot]

                @pl.when(code >= 0)
                def _():
                    row = aligned(code // column_blocks, tile)
                    column = aligned(code % column_blocks, tile)
                    values = tile_refs[k][slot]
                    weight[row, column] = values
                    transposed_ref[column, row] = values.T

    left = normed_ref[...]
    for chunk in range(chunks):
        partial_ref[chunk] = jnp.dot(
            left,
            weight[:, chunk * chunk_width : (chunk + 1) * chunk_width],
            preferred_element_type=jnp.float32,
        )

    rows = first_ref.shape[0] - PAD
    far = chunks - 1 - place_ref[0]
    place = lax.broadcasted_iota(jnp.int32, (PAD, chunk_width), 0)
    old = exponent_rows(first_ref[rows : rows + PAD, :])
    exponents = jnp.where(step == 0, 0.0, old)
    for group in range(block // GROUP):
        codes, exponent = encode(partial_ref[far, group * GROUP : (group + 1) * GROUP, :])
        first_ref[aligned(step * (block // GROUP) + group, GROUP), :] = codes
        exponents = jnp.where(place == step * (block // GROUP) + group, exponent, exponents)
    first_ref[rows : rows + PAD, :] = as_code(exponents)


def partial_values(codes, place, normed, tiles, chunks, column_blocks):
    tokens, features = normed.shape
    tile = tiles[0].shape[-1]
    width = column_blocks * tile
    block = 256
    return pl.pallas_call(
        functools.partial(values_kernel, len(tiles), column_blocks),
        grid_spec=pltpu.PrefetchScalarGridSpec(
            num_scalar_prefetch=2,
            grid=(tokens // block,),
            in_specs=[pl.BlockSpec((block, features), lambda i, *_: (i, 0))]
            + [whole(t.shape) for t in tiles],
            out_specs=[
                pl.BlockSpec((chunks, block, width // chunks), lambda i, *_: (0, i, 0)),
                whole((tokens + PAD, width // chunks)),
                whole((width, features)),
            ],
            scratch_shapes=[pltpu.VMEM((features, width), jnp.bfloat16)],
        ),
        out_shape=[
            jax.ShapeDtypeStruct((chunks, tokens, width // chunks), jnp.float32),
            jax.ShapeDtypeStruct((tokens + PAD, width // chunks), jnp.int16),
            jax.ShapeDtypeStruct((width, features), jnp.bfloat16),
        ],
        compiler_params=params(),
        cost_estimate=pl.CostEstimate(
            flops=2 * tokens * features * width,
            bytes_accessed=20 * 1024 * 1024,
            transcendentals=0,
        ),
        name="partial_values",
    )(codes, place, normed, *tiles)


def hop_kernel(chunk_ref, partial_ref, arrived_ref, message_ref):
    rows = partial_ref.shape[1]
    arrived = read_message(arrived_ref, rows)

    def total(group):
        return partial_ref[0, group * GROUP : (group + 1) * GROUP, :] + arrived(group)

    write_message(message_ref, rows, total)


def hop(chunk, partial, arrived):
    _, tokens, width = partial.shape
    return pl.pallas_call(
        hop_kernel,
        grid_spec=pltpu.PrefetchScalarGridSpec(
            num_scalar_prefetch=1,
            grid=(1,),
            in_specs=[
                pl.BlockSpec((1, tokens, width), lambda i, c: (c[0], 0, 0)),
                whole(arrived.shape),
            ],
            out_specs=whole(arrived.shape),
        ),
        out_shape=jax.ShapeDtypeStruct(arrived.shape, jnp.int16),
        compiler_params=params(),
        cost_estimate=pl.CostEstimate(
            flops=8 * tokens * width, bytes_accessed=8 * tokens * width, transcendentals=0
        ),
        name="hop",
    )(chunk, partial, arrived)


def last_hop_kernel(chunk_ref, partial_ref, right_ref, left_ref, values_ref):
    rows = partial_ref.shape[1]
    right = read_message(right_ref, rows)
    left = read_message(left_ref, rows)
    for group in range(rows // GROUP):
        span = slice(group * GROUP, (group + 1) * GROUP)
        total = partial_ref[0, span, :] + right(group) + left(group)
        values_ref[span, :] = total.astype(values_ref.dtype)


def last_hop(chunk, partial, right, left):
    _, tokens, width = partial.shape
    return pl.pallas_call(
        last_hop_kernel,
        grid_spec=pltpu.PrefetchScalarGridSpec(
            num_scalar_prefetch=1,
            grid=(1,),
            in_specs=[
                pl.BlockSpec((1, tokens, width), lambda i, c: (c[0], 0, 0)),
                whole(right.shape),
                whole(left.shape),
            ],
            out_specs=whole((tokens, width)),
        ),
        out_shape=jax.ShapeDtypeStruct((tokens, width), jnp.bfloat16),
        compiler_params=params(),
        cost_estimate=pl.CostEstimate(
            flops=8 * tokens * width, bytes_accessed=10 * tokens * width, transcendentals=0
        ),
        name="last_hop",
    )(chunk, partial, right, left)


def gradient_kernel(
    chips, column_blocks, codes_ref, place_ref, normed_ref, own, r1, r2, r3, l1, l2, l3, *refs
):
    keep_refs = refs[:chips]
    send_refs = refs[chips : 2 * chips]
    cotangent_ref, turned, gradient = refs[2 * chips :]
    chunk_width = own.shape[1]
    chunks = cotangent_ref.shape[1] // chunk_width
    pieces = (own[...], l1[...] + r3[...], l2[...] + r2[...], r1[...] + l3[...])
    for r in range(chunks):
        span = aligned(lax.rem(place_ref[0] + r, chunks), chunk_width)
        cotangent_ref[:, span] = pieces[r]
        turned[span, :] = pieces[r].T
    step = 256
    for n in range(normed_ref.shape[1] // step):
        span = slice(n * step, (n + 1) * step)
        gradient[:, span] = jnp.dot(
            turned[...], normed_ref[:, span], preferred_element_type=jnp.float32
        )
    tile = 128
    capacity = codes_ref.shape[1]

    def term(k, slot):
        code = codes_ref[k, slot]
        safe = jnp.maximum(code, 0)
        block = gradient[aligned(safe % column_blocks, tile), aligned(safe // column_blocks, tile)]
        return jnp.where(code >= 0, block, 0.0)

    for chip in range(chips):
        for slot in range(capacity):
            keep_refs[chip][slot * tile : (slot + 1) * tile, :] = term(2 * chip, slot)
        write_message(
            send_refs[chip], capacity * tile, lambda slot: term(2 * chip + 1, slot)
        )


def gradient_terms(codes, place, normed, own, rights, lefts, column_blocks):
    tokens, features = normed.shape
    chips = codes.shape[0] // 2
    capacity = codes.shape[1]
    rows = capacity * GROUP
    width = column_blocks * GROUP
    inputs = (normed, own, *rights, *lefts)
    shapes = (
        [((rows, GROUP), jnp.float32)] * chips
        + [((rows + PAD, GROUP), jnp.int16)] * chips
        + [((tokens, width), jnp.bfloat16)]
    )
    outputs = pl.pallas_call(
        functools.partial(gradient_kernel, chips, column_blocks),
        grid_spec=pltpu.PrefetchScalarGridSpec(
            num_scalar_prefetch=2,
            grid=(1,),
            in_specs=[whole(a.shape) for a in inputs],
            out_specs=[whole(shape) for shape, _ in shapes],
            scratch_shapes=[
                pltpu.VMEM((width, tokens), jnp.bfloat16),
                pltpu.VMEM((width, features), jnp.float32),
            ],
        ),
        out_shape=[jax.ShapeDtypeStruct(shape, kind) for shape, kind in shapes],
        compiler_params=params(),
        cost_estimate=pl.CostEstimate(
            flops=2 * tokens * features * width,
            bytes_accessed=16 * 1024 * 1024,
            transcendentals=0,
        ),
        name="gradient_terms",
    )(codes, place, *inputs)
    return outputs[:chips], outputs[chips : 2 * chips], outputs[-1]


def combine_kernel(kept_ref, arrived_ref, out_ref):
    rows = kept_ref.shape[0]
    arrived = read_message(arrived_ref, rows)

    def total(group):
        return kept_ref[group * GROUP : (group + 1) * GROUP, :] + arrived(group)

    if out_ref.dtype == jnp.int16:
        write_message(out_ref, rows, total)
    else:
        for group in range(rows // GROUP):
            out_ref[group * GROUP : (group + 1) * GROUP, :] = total(group)


def combine(kept, arrived, kind):
    shape = arrived.shape if kind == jnp.int16 else kept.shape
    return pl.pallas_call(
        combine_kernel,
        grid=(1,),
        in_specs=[whole(kept.shape), whole(arrived.shape)],
        out_specs=whole(shape),
        out_shape=jax.ShapeDtypeStruct(shape, kind),
        compiler_params=params(),
        cost_estimate=pl.CostEstimate(
            flops=8 * kept.size, bytes_accessed=8 * kept.size, transcendentals=0
        ),
        name="combine",
    )(kept, arrived)


def update_kernel(count, *refs):
    kept_ref, out_ref = refs[0], refs[-1]
    tile = out_ref.shape[-1]
    arrived = [read_message(ref, kept_ref.shape[0]) for ref in refs[1 : 1 + count]]
    for slot in range(out_ref.shape[0]):
        total = kept_ref[slot * tile : (slot + 1) * tile, :]
        for block in arrived:
            total = total + block(slot)
        mean = jnp.sum(total * total) / (tile * tile)
        out_ref[slot] = (total * lax.rsqrt(mean + 1e-06)).T.astype(out_ref.dtype)


def normalized_update(kept, arrived, shape):
    return pl.pallas_call(
        functools.partial(update_kernel, len(arrived)),
        grid=(1,),
        in_specs=[whole(kept.shape)] + [whole(a.shape) for a in arrived],
        out_specs=whole(shape),
        out_shape=jax.ShapeDtypeStruct(shape, jnp.bfloat16),
        compiler_params=params(),
        cost_estimate=pl.CostEstimate(
            flops=16 * kept.size, bytes_accessed=12 * kept.size, transcendentals=0
        ),
        name="normalized_update",
    )(kept, *arrived)


def grad_input_kernel(cotangent_ref, transposed_ref, out_ref):
    step = 512
    for n in range(out_ref.shape[1] // step):
        span = slice(n * step, (n + 1) * step)
        out_ref[:, span] = jnp.dot(
            cotangent_ref[...], transposed_ref[:, span], preferred_element_type=jnp.float32
        ).astype(out_ref.dtype)


def grad_inputs(cotangent, transposed):
    tokens, width = cotangent.shape
    features = transposed.shape[1]
    block = 256
    return pl.pallas_call(
        grad_input_kernel,
        grid=(tokens // block,),
        in_specs=[
            pl.BlockSpec((block, width), lambda i: (i, 0)),
            whole(transposed.shape),
        ],
        out_specs=pl.BlockSpec((block, features), lambda i: (i, 0)),
        out_shape=jax.ShapeDtypeStruct((tokens, features), jnp.bfloat16),
        compiler_params=params(),
        cost_estimate=pl.CostEstimate(
            flops=2 * tokens * features * width,
            bytes_accessed=10 * 1024 * 1024,
            transcendentals=0,
        ),
        name="grad_inputs",
    )(cotangent, transposed)


def local(devices, parts, normed, tile_values, tile_rows, tile_columns, cotangent):
    tile = tile_values.shape[-1]
    tiles = tile_values[0]
    column_blocks = cotangent.shape[1] * parts // tile
    chips = devices // 2
    place = lax.axis_index("tensor").astype(jnp.int32).reshape(1)

    def swap(x, mask):
        return lax.ppermute(x, "fsdp", [(i, i ^ mask) for i in range(devices)])

    def right(x, *sources):
        return lax.ppermute(x, "tensor", [(i, i + 1) for i in sources])

    def left(x, *sources):
        return lax.ppermute(x, "tensor", [(i, i - 1) for i in sources])

    r1, l1 = right(cotangent, 0, 1, 2), left(cotangent, 3, 2, 1)
    same_core = [tiles] + [swap(tiles, 2 * chip) for chip in range(1, chips)]
    codes = jnp.where(tile_columns >= 0, tile_rows * column_blocks + tile_columns, -1)
    mask = 1
    while mask < devices:
        codes = jnp.concatenate([codes, swap(codes, mask)], axis=0)
        mask *= 2
    r2, l2 = right(r1, 1, 2), left(l1, 2, 1)
    r3, l3 = right(r2, 2), left(l2, 1)
    gathered = []
    for chip in range(chips):
        gathered += [same_core[chip], swap(same_core[chip], 1)]

    partial, first, transposed = partial_values(
        codes, place, normed, gathered, parts, column_blocks
    )
    keep, send, full_cotangent = gradient_terms(
        codes, place, normed, cotangent, (r1, r2, r3), (l1, l2, l3), column_blocks
    )

    arrived = lax.ppermute(first, "tensor", [(0, 1), (3, 2)])
    second = hop((place + 2) % parts, partial, arrived)
    from_left, from_right = right(second, 0, 1), left(second, 3, 2)
    from_left = right(hop((place + 1) % parts, partial, from_left), 0, 1, 2)
    from_right = left(hop((place + 3) % parts, partial, from_right), 3, 2, 1)
    values = last_hop(place, partial, from_left, from_right)

    other = [swap(message, 1) for message in send]
    terms = [
        swap(combine(keep[chip], other[chip], jnp.int16), 2 * chip)
        for chip in reversed(range(1, chips))
    ]
    own = combine(keep[0], other[0], jnp.float32)
    update = normalized_update(own, terms, tile_values.shape[1:])
    grad_input = grad_inputs(full_cotangent, transposed)
    return values, grad_input, update[None]


def solution(mesh):
    in_specs = (
        P("fsdp", "tensor"),
        P("tensor", "fsdp", None, None),
        P("tensor", "fsdp"),
        P("tensor", "fsdp"),
        P("fsdp", "tensor"),
    )
    out_specs = (P("fsdp", "tensor"), P("fsdp", "tensor"), P("tensor", "fsdp", None, None))
    return jax.shard_map(
        functools.partial(local, mesh.shape["fsdp"], mesh.shape["tensor"]),
        mesh=mesh,
        in_specs=in_specs,
        out_specs=out_specs,
        check_vma=False,
    )
```

time: 261 us -> 145 us (0.56)
  waiting for transfers between devices: 167 us -> 49.8 us
  Pallas kernels: 0 us -> 42.4 us
  starting transfers between devices: 0.34 us -> 42.3 us
  matrix products: 25.8 us -> 0 us
  local copies, waits for them, and re-layouts: 32 us -> 8.5 us
  between operations: 14.5 us -> 0.96 us
  other arithmetic: 10.8 us -> 0.7 us
  blocking collectives: 9.46 us -> 0 us
    reduce_scatter x2 -> x0, waiting for transfers between devices: 122 us -> none  [the longest x1 77.5 us: local(): lax.psum_scatter(partial_value, 'tensor', scatter_dimension=1, tiled=True)]
    ppermute x0 -> x28, waiting for transfers between devices: none -> 49.8 us  [the longest x17 32.8 us: swap(): return lax.ppermute(x, 'fsdp', [(i, i ^ mask) for i in range(devices)])]
    all_gather x2 -> x0, waiting for transfers between devices: 44.7 us -> none  [the longest x1 35.4 us: local(): full_cotangent = lax.all_gather(cotangent, 'tensor', axis=1, tiled=True)]
    pallas_call x0 -> x12, Pallas kernels: none -> 42.4 us  [the longest x1 17.1 us: partial_values(): pl.pallas_call(functools.partial(values_kernel, len(tiles), column_blocks...]
    ppermute x0 -> x28, starting transfers between devices: none -> 42.3 us  [the longest x5 16.8 us: right(): return lax.ppermute(x, 'tensor', [(i, i + 1) for i in sources])]
    dot_general x4 -> x0, matrix products: 25.8 us -> none  [the longest x1 9.1 us: local(): jnp.einsum('tk,dk->td', full_cotangent, weight, preferred_element_type=jn...]
    unnamed x17 -> x26, local copies, waits for them, and re-layouts: 18.5 us -> 8.5 us
    unnamed x1 -> x0, blocking collectives: 9.46 us -> none
  transfers between devices with their start and end apart: 4 -> 28, of which waited for: 4 -> 8; matrix products, arithmetic and copies ran while one was open for 24% -> 0% of each run, Pallas kernels for 0% -> 29%
where the time goes in v1:
time: 145 us
  waiting for transfers between devices  49.8 us (34%)
  Pallas kernels  42.4 us (29%)
  starting transfers between devices  42.3 us (29%)
  local copies, waits for them, and re-layouts  8.5 us (6%)
    ppermute x17, waiting for transfers between devices, swap(): return lax.ppermute(x, 'fsdp', [(i, i ^ mask) for i in range(devices)])  32.8 us
    pallas_call x1, Pallas kernels, partial_values(): pl.pallas_call(functools.partial(values_kernel, len(tiles), column_blocks...  17.1 us
    ppermute x5, starting transfers between devices, right(): return lax.ppermute(x, 'tensor', [(i, i + 1) for i in sources])  16.8 us
    ppermute x17, starting transfers between devices, swap(): return lax.ppermute(x, 'fsdp', [(i, i ^ mask) for i in range(devices)])  12.5 us
    pallas_call x1, Pallas kernels, gradient_terms(): pl.pallas_call(functools.partial(gradient_kernel, chips, column_blocks),...  11.8 us
    ppermute x5, waiting for transfers between devices, left(): return lax.ppermute(x, 'tensor', [(i, i - 1) for i in sources])  11.1 us
    unnamed x26, local copies, waits for them, and re-layouts  8.5 us
    pallas_call x1, Pallas kernels, grad_inputs(): pl.pallas_call(grad_input_kernel, grid=(tokens // block,), in_specs=[pl.B...  8.29 us
  transfers between devices with their start and end apart: 28, of which 8 were waited for; matrix products, arithmetic and copies ran while one was open for 0% of the time, Pallas kernels for 29%

profile of v1, /device:TPU:0, one launch (start us, length us, event | category | flops | bytes accessed | tf_op | source)
XLA Modules:
  0.0 144.7 jit_solution(5461656695009219291)
XLA Ops:
  0.6 5.0 %collective-permute-start.15 = (bf16[1024,256]{1,0:T(8,128)(2,1)}, bf16[1024,256]{1,0:T(8,128)(2,1)S(1)}, u32[]{:S(2)}, u32[]{:S(2)}) collective-permute-start(bf16[1024,256]{1,0:T(8,128)(2,1)} %own.1), channel_id=1, source_target_pairs={{0,1},{1,2},{2,3},{4,5},{5,6},{6,7},{8,9},{9,10},{10,11},{12,13},{... | collective-permute-start | bytes 1572872 | tf_op jit(solution)/shard_map/ppermute | solution.py:386
  5.6 1.6 %collective-permute-start.4 = (bf16[16,128,128]{2,1,0:T(8,128)(2,1)}, bf16[16,128,128]{2,1,0:T(8,128)(2,1)S(1)}, u32[]{:S(2)}, u32[]{:S(2)}) collective-permute-start(bf16[16,128,128]{2,1,0:T(8,128)(2,1)} %bitcast.3), channel_id=1, source_target_pairs={{0,8},{4,12},{8,0},{12,4},{16,24},{20,28},{24,16},{28,20},{1,9},{5... | collective-permute-start | bytes 1572872 | tf_op jit(solution)/shard_map/ppermute | solution.py:383
  7.2 1.5 %collective-permute-start.6 = (bf16[16,128,128]{2,1,0:T(8,128)(2,1)}, bf16[16,128,128]{2,1,0:T(8,128)(2,1)S(1)}, u32[]{:S(2)}, u32[]{:S(2)}) collective-permute-start(bf16[16,128,128]{2,1,0:T(8,128)(2,1)} %bitcast.4), channel_id=1, source_target_pairs={{0,16},{4,20},{8,24},{12,28},{16,0},{20,4},{24,8},{28,12},{1,17},{... | collective-permute-start | bytes 1572872 | tf_op jit(solution)/shard_map/ppermute | solution.py:383
  8.7 0.5 collective-permute-start.8
  9.2 0.7 compare_select_fusion
  9.8 1.1 collective-permute-done
  11.0 1.6 %collective-permute-start.1 = (s32[2,16]{1,0:T(2,128)S(1)}, s32[2,16]{1,0:T(2,128)S(1)}, u32[]{:S(2)}, u32[]{:S(2)}) collective-permute-start(s32[2,16]{1,0:T(2,128)S(1)} %pad_add_fusion.2), channel_id=1, source_target_pairs={{0,8},{4,12},{8,0},{12,4},{16,24},{20,28},{24,16},{28,20},{1,9},{5... | collective-permute-start | bytes 392 | tf_op jit(solution)/shard_map/ppermute | solution.py:383
  12.5 18.0 %collective-permute-done.1 = s32[2,16]{1,0:T(2,128)S(1)} collective-permute-done((s32[2,16]{1,0:T(2,128)S(1)}, s32[2,16]{1,0:T(2,128)S(1)}, u32[]{:S(2)}, u32[]{:S(2)}) %collective-permute-start.1) | collective-permute-done | bytes 160 | tf_op jit(solution)/shard_map/ppermute | solution.py:383
  30.6 1.6 %collective-permute-start.2 = (s32[4,16]{1,0:T(4,128)S(1)}, s32[4,16]{1,0:T(4,128)S(1)}, u32[]{:S(2)}, u32[]{:S(2)}) collective-permute-start(s32[4,16]{1,0:T(4,128)S(1)} %pad_add_fusion.1), channel_id=1, source_target_pairs={{0,16},{4,20},{8,24},{12,28},{16,0},{20,4},{24,8},{28,12},{1,17},{... | collective-permute-start | bytes 776 | tf_op jit(solution)/shard_map/ppermute | solution.py:383
  32.2 2.1 %collective-permute-done.2 = s32[4,16]{1,0:T(4,128)S(1)} collective-permute-done((s32[4,16]{1,0:T(4,128)S(1)}, s32[4,16]{1,0:T(4,128)S(1)}, u32[]{:S(2)}, u32[]{:S(2)}) %collective-permute-start.2) | collective-permute-done | bytes 288 | tf_op jit(solution)/shard_map/ppermute | solution.py:383
  34.2 1.3 collective-permute-start.18
  35.6 0.5 collective-permute-start.5
  36.2 0.4 collective-permute-start.9
  36.6 11.1 %collective-permute-done.18.l1 = bf16[1024,256]{1,0:T(8,128)(2,1)S(1)} collective-permute-done((bf16[1024,256]{1,0:T(8,128)(2,1)}, bf16[1024,256]{1,0:T(8,128)(2,1)S(1)}, u32[]{:S(2)}, u32[]{:S(2)}) %collective-permute-start.18) | collective-permute-done | bytes 524320 | tf_op jit(solution)/shard_map/ppermute | solution.py:389
  47.7 0.7 collective-permute-start.16
  48.4 1.3 collective-permute-start.19
  49.8 1.0 copy-done.6
  50.8 17.1 %partial_values.1 = (f32[4,1024,256]{2,1,0:T(8,128)}, s16[1040,256]{1,0:T(8,128)(2,1)S(1)}, bf16[1024,2048]{1,0:T(8,128)(2,1)}) custom-call(s32[8,16]{1,0:T(8,128)S(1)} %pad_add_fusion.codes_ref, s32[1]{0:T(128)} %bitcast.place_ref.chunk_ref, bf16[1024,2048]{1,0:T(8,128)(2,1)} %normed_ref.3, bf16[16,128,128]{2,1,0:T(8,128)(2,1)S(1)} %bitcast.7, ...), custom_call_target="tpu_custom_call" | custom-call | flops 4294967296 | bytes 20971520 | tf_op jit(solution)/shard_map/partial_values/pallas_call | solution.py:120
  67.9 6.9 %collective-permute-start.10 = (s16[1040,256]{1,0:T(8,128)(2,1)S(1)}, s16[1040,256]{1,0:T(8,128)(2,1)S(1)}, u32[]{:S(2)}, u32[]{:S(2)}) collective-permute-start(s16[1040,256]{1,0:T(8,128)(2,1)S(1)} %get-tuple-element.16), channel_id=1, source_target_pairs={{0,1},{3,2},{4,5},{7,6},{8,9},{11,10},{12,13},{15,14},{16,17},{19,... | collective-permute-start | bytes 1597448 | tf_op jit(solution)/shard_map/ppermute | solution.py:411
  74.8 0.7 collective-permute-start.17
  75.6 1.3 collective-permute-start.20
  76.9 5.8 %collective-permute-done.10.arrived_ref = s16[1040,256]{1,0:T(8,128)(2,1)S(1)} collective-permute-done((s16[1040,256]{1,0:T(8,128)(2,1)S(1)}, s16[1040,256]{1,0:T(8,128)(2,1)S(1)}, u32[]{:S(2)}, u32[]{:S(2)}) %collective-permute-start.10) | collective-permute-done | bytes 532512 | tf_op jit(solution)/shard_map/ppermute | solution.py:411
  82.7 2.2 %copy-done = f32[4,1024,256]{2,1,0:T(8,128)S(1)} copy-done((f32[4,1024,256]{2,1,0:T(8,128)S(1)}, f32[4,1024,256]{2,1,0:T(8,128)}, u32[]{:S(2)}) %copy-start) | copy-done | bytes 4194328
  84.9 0.3 hop.3
  85.2 0.8 collective-permute-start.13
  86.1 5.1 %collective-permute-start.11 = (s16[1040,256]{1,0:T(8,128)(2,1)S(1)}, s16[1040,256]{1,0:T(8,128)(2,1)S(1)}, u32[]{:S(2)}, u32[]{:S(2)}) collective-permute-start(s16[1040,256]{1,0:T(8,128)(2,1)S(1)} %hop.3), channel_id=1, source_target_pairs={{0,1},{1,2},{4,5},{5,6},{8,9},{9,10},{12,13},{13,14},{16,17},{17,1... | collective-permute-start | bytes 1597448 | tf_op jit(solution)/shard_map/ppermute | solution.py:386
  91.3 0.8 copy-done.8
  92.0 0.8 copy-done.10
  92.8 1.0 copy-done.9
  93.9 1.0 copy-done.11
  94.9 11.8 %gradient_terms.1 = (f32[2048,128]{1,0:T(8,128)}, f32[2048,128]{1,0:T(8,128)}, f32[2048,128]{1,0:T(8,128)}, f32[2048,128]{1,0:T(8,128)}, s16[2064,128]{1,0:T(8,1...) custom-call(s32[8,16]{1,0:T(8,128)S(1)} %pad_add_fusion.codes_ref, ...), custom_call_target="tpu_custom_call" | custom-call | flops 4294967296 | bytes 16777216 | tf_op jit(solution)/shard_map/gradient_terms/pallas_call | solution.py:262
  106.7 0.5 collective-permute-start.24
  107.2 0.5 collective-permute-start.21
  108.1 1.4 collective-permute-start.14
  109.5 0.3 hop.4
  109.9 5.4 %collective-permute-start.12 = (s16[1040,256]{1,0:T(8,128)(2,1)S(1)}, s16[1040,256]{1,0:T(8,128)(2,1)S(1)}, u32[]{:S(2)}, u32[]{:S(2)}) collective-permute-start(s16[1040,256]{1,0:T(8,128)(2,1)S(1)} %hop.4), channel_id=1, source_target_pairs={{0,1},{1,2},{2,3},{4,5},{5,6},{6,7},{8,9},{9,10},{10,11},{12,13},{... | collective-permute-start | bytes 1597448 | tf_op jit(solution)/shard_map/ppermute | solution.py:386
  115.2 0.4 combine.5
  115.6 2.3 %collective-permute-start.23 = (s16[2064,128]{1,0:T(8,128)(2,1)S(1)}, s16[2064,128]{1,0:T(8,128)(2,1)S(1)}, u32[]{:S(2)}, u32[]{:S(2)}) collective-permute-start(s16[2064,128]{1,0:T(8,128)(2,1)S(1)} %combine.5), channel_id=1, source_target_pairs={{0,24},{4,28},{8,16},{12,20},{16,8},{20,12},{24,0},{28,4},{1,25},{... | collective-permute-start | bytes 1585160 | tf_op jit(solution)/shard_map/ppermute | solution.py:383
  117.9 0.4 combine.6
  118.2 0.6 collective-permute-start.25
  118.9 0.4 combine.7
  119.2 0.8 collective-permute-start.27
  120.1 1.6 %copy-done.12 = bf16[1024,1024]{1,0:T(8,128)(2,1)S(1)} copy-done((bf16[1024,1024]{1,0:T(8,128)(2,1)S(1)}, bf16[1024,1024]{1,0:T(8,128)(2,1)}, u32[]{:S(2)}) %copy-start.12) | copy-done | bytes 2097176
  121.7 8.3 %grad_inputs.1 = bf16[1024,2048]{1,0:T(8,128)(2,1)} custom-call(bf16[1024,1024]{1,0:T(8,128)(2,1)S(1)} %copy-done.12, bf16[1024,2048]{1,0:T(8,128)(2,1)} %get-tuple-element.18.transposed_ref), custom_call_target="tpu_custom_call" | custom-call | flops 4294967296 | bytes 10485760 | tf_op jit(solution)/shard_map/grad_inputs/pallas_call | solution.py:356
  130.1 1.5 %collective-permute-done.23.refs_1_ = s16[2064,128]{1,0:T(8,128)(2,1)S(1)} collective-permute-done((s16[2064,128]{1,0:T(8,128)(2,1)S(1)}, s16[2064,128]{1,0:T(8,128)(2,1)S(1)}, u32[]{:S(2)}, u32[]{:S(2)}) %collective-permute-start.23) | collective-permute-done | bytes 528416 | tf_op jit(solution)/shard_map/ppermute | solution.py:383
  131.5 10.0 %collective-permute-done.25.refs_2_ = s16[2064,128]{1,0:T(8,128)(2,1)S(1)} collective-permute-done((s16[2064,128]{1,0:T(8,128)(2,1)S(1)}, s16[2064,128]{1,0:T(8,128)(2,1)S(1)}, u32[]{:S(2)}, u32[]{:S(2)}) %collective-permute-start.25) | collective-permute-done | bytes 528416 | tf_op jit(solution)/shard_map/ppermute | solution.py:383
  141.7 1.9 %normalized_update.1 = bf16[16,128,128]{2,1,0:T(8,128)(2,1)} custom-call(f32[2048,128]{1,0:T(8,128)S(1)} %combine.4.refs_0_, s16[2064,128]{1,0:T(8,128)(2,1)S(1)} %collective-permute-done.23.refs_1_, s16[2064,128]{1,0:T(8,128)(2,1)S(1)} %collective-permute-done.25.refs_2_, s16[2064,128]{1,0:T(8,128)(2,1)S(1)} %collective-permute-done.27.refs_3_), custom_call_target="tpu_custom_call" | custom-call | flops 4194304 | bytes 3145728 | tf_op jit(solution)/shard_map/normalized_update/pallas_call | solution.py:329
  143.6 1.1 last_hop.1
  (50 shorter events, 0.9 us)
Async XLA Ops:
  0.6 34.9 %collective-permute-start.15 = (bf16[1024,256]{1,0:T(8,128)(2,1)}, bf16[1024,256]{1,0:T(8,128)(2,1)S(1)}, u32[]{:S(2)}, u32[]{:S(2)}) collective-permute-start(bf16[1024,256]{1,0:T(8,128)(2,1)} %own.1), channel_id=1, source_target_pairs={{0,1},{1,2},{2,3},{4,5},{5,6},{6,7},{8,9},{9,10},{10,11},{12,13},{... | collective-permute-start | bytes 1572872 | tf_op jit(solution)/shard_map/ppermute | solution.py:386
  5.6 30.0 %collective-permute-start.4 = (bf16[16,128,128]{2,1,0:T(8,128)(2,1)}, bf16[16,128,128]{2,1,0:T(8,128)(2,1)S(1)}, u32[]{:S(2)}, u32[]{:S(2)}) collective-permute-start(bf16[16,128,128]{2,1,0:T(8,128)(2,1)} %bitcast.3), channel_id=1, source_target_pairs={{0,8},{4,12},{8,0},{12,4},{16,24},{20,28},{24,16},{28,20},{1,9},{5... | collective-permute-start | bytes 1572872 | tf_op jit(solution)/shard_map/ppermute | solution.py:383
  7.2 28.9 %collective-permute-start.6 = (bf16[16,128,128]{2,1,0:T(8,128)(2,1)}, bf16[16,128,128]{2,1,0:T(8,128)(2,1)S(1)}, u32[]{:S(2)}, u32[]{:S(2)}) collective-permute-start(bf16[16,128,128]{2,1,0:T(8,128)(2,1)} %bitcast.4), channel_id=1, source_target_pairs={{0,16},{4,20},{8,24},{12,28},{16,0},{20,4},{24,8},{28,12},{1,17},{... | collective-permute-start | bytes 1572872 | tf_op jit(solution)/shard_map/ppermute | solution.py:383
  8.7 27.5 %collective-permute-start.8 = (bf16[16,128,128]{2,1,0:T(8,128)(2,1)}, bf16[16,128,128]{2,1,0:T(8,128)(2,1)S(1)}, u32[]{:S(2)}, u32[]{:S(2)}) collective-permute-start(bf16[16,128,128]{2,1,0:T(8,128)(2,1)} %bitcast.5), channel_id=1, source_target_pairs={{0,24},{4,28},{8,16},{12,20},{16,8},{20,12},{24,0},{28,4},{1,25},{... | collective-permute-start | bytes 1572872 | tf_op jit(solution)/shard_map/ppermute | solution.py:383
  9.8 1.1 collective-permute-start
  11.0 19.6 %collective-permute-start.1 = (s32[2,16]{1,0:T(2,128)S(1)}, s32[2,16]{1,0:T(2,128)S(1)}, u32[]{:S(2)}, u32[]{:S(2)}) collective-permute-start(s32[2,16]{1,0:T(2,128)S(1)} %pad_add_fusion.2), channel_id=1, source_target_pairs={{0,8},{4,12},{8,0},{12,4},{16,24},{20,28},{24,16},{28,20},{1,9},{5... | collective-permute-start | bytes 392 | tf_op jit(solution)/shard_map/ppermute | solution.py:383
  30.6 3.7 %collective-permute-start.2 = (s32[4,16]{1,0:T(4,128)S(1)}, s32[4,16]{1,0:T(4,128)S(1)}, u32[]{:S(2)}, u32[]{:S(2)}) collective-permute-start(s32[4,16]{1,0:T(4,128)S(1)} %pad_add_fusion.1), channel_id=1, source_target_pairs={{0,16},{4,20},{8,24},{12,28},{16,0},{20,4},{24,8},{28,12},{1,17},{... | collective-permute-start | bytes 776 | tf_op jit(solution)/shard_map/ppermute | solution.py:383
  34.2 13.5 %collective-permute-start.18 = (bf16[1024,256]{1,0:T(8,128)(2,1)}, bf16[1024,256]{1,0:T(8,128)(2,1)S(1)}, u32[]{:S(2)}, u32[]{:S(2)}) collective-permute-start(bf16[1024,256]{1,0:T(8,128)(2,1)} %own.1), channel_id=1, source_target_pairs={{3,2},{2,1},{1,0},{7,6},{6,5},{5,4},{11,10},{10,9},{9,8},{15,14},{... | collective-permute-start | bytes 1572872 | tf_op jit(solution)/shard_map/ppermute | solution.py:389
  35.5 12.9 %collective-permute-start.3 = (bf16[16,128,128]{2,1,0:T(8,128)(2,1)}, bf16[16,128,128]{2,1,0:T(8,128)(2,1)S(1)}, u32[]{:S(2)}, u32[]{:S(2)}) collective-permute-start(bf16[16,128,128]{2,1,0:T(8,128)(2,1)} %bitcast.6), channel_id=1, source_target_pairs={{0,4},{4,0},{8,12},{12,8},{16,20},{20,16},{24,28},{28,24},{1,5},{5... | collective-permute-start | bytes 1572872 | tf_op jit(solution)/shard_map/ppermute | solution.py:383
  35.6 14.1 %collective-permute-start.5 = (bf16[16,128,128]{2,1,0:T(8,128)(2,1)S(1)}, bf16[16,128,128]{2,1,0:T(8,128)(2,1)}, u32[]{:S(2)}, u32[]{:S(2)}) collective-permute-start(bf16[16,128,128]{2,1,0:T(8,128)(2,1)S(1)} %collective-permute-done.4.refs_2_), channel_id=1, source_target_pairs={{0,4},{4,0},{8,12},{12,8},{16,20},{20,16},{24,28},{28,24},{1,5},{5... | collective-permute-start | bytes 1572872 | tf_op jit(solution)/shard_map/ppermute | solution.py:383
  36.1 13.7 %collective-permute-start.7 = (bf16[16,128,128]{2,1,0:T(8,128)(2,1)S(1)}, bf16[16,128,128]{2,1,0:T(8,128)(2,1)}, u32[]{:S(2)}, u32[]{:S(2)}) collective-permute-start(bf16[16,128,128]{2,1,0:T(8,128)(2,1)S(1)} %collective-permute-done.6.refs_4_), channel_id=1, source_target_pairs={{0,4},{4,0},{8,12},{12,8},{16,20},{20,16},{24,28},{28,24},{1,5},{5... | collective-permute-start | bytes 1572872 | tf_op jit(solution)/shard_map/ppermute | solution.py:383
  36.2 13.6 %collective-permute-start.9 = (bf16[16,128,128]{2,1,0:T(8,128)(2,1)S(1)}, bf16[16,128,128]{2,1,0:T(8,128)(2,1)}, u32[]{:S(2)}, u32[]{:S(2)}) collective-permute-start(bf16[16,128,128]{2,1,0:T(8,128)(2,1)S(1)} %collective-permute-done.8.refs_6_), channel_id=1, source_target_pairs={{0,4},{4,0},{8,12},{12,8},{16,20},{20,16},{24,28},{28,24},{1,5},{5... | collective-permute-start | bytes 1572872 | tf_op jit(solution)/shard_map/ppermute | solution.py:383
  47.7 27.1 %collective-permute-start.16 = (bf16[1024,256]{1,0:T(8,128)(2,1)S(1)}, bf16[1024,256]{1,0:T(8,128)(2,1)S(1)}, u32[]{:S(2)}, u32[]{:S(2)}) collective-permute-start(bf16[1024,256]{1,0:T(8,128)(2,1)S(1)} %collective-permute-done.15.r1), channel_id=1, source_target_pairs={{1,2},{2,3},{5,6},{6,7},{9,10},{10,11},{13,14},{14,15},{17,18},{18... | collective-permute-start | bytes 1572872 | tf_op jit(solution)/shard_map/ppermute | solution.py:386
  48.4 27.1 %collective-permute-start.19 = (bf16[1024,256]{1,0:T(8,128)(2,1)S(1)}, bf16[1024,256]{1,0:T(8,128)(2,1)S(1)}, u32[]{:S(2)}, u32[]{:S(2)}) collective-permute-start(bf16[1024,256]{1,0:T(8,128)(2,1)S(1)} %collective-permute-done.18.l1), channel_id=1, source_target_pairs={{2,1},{1,0},{6,5},{5,4},{10,9},{9,8},{14,13},{13,12},{18,17},{17,1... | collective-permute-start | bytes 1572872 | tf_op jit(solution)/shard_map/ppermute | solution.py:389
  49.8 1.0 copy-start.6
  50.8 42.0 %copy-start.7 = (bf16[1024,256]{1,0:T(8,128)(2,1)S(1)}, bf16[1024,256]{1,0:T(8,128)(2,1)}, u32[]{:S(2)}) copy-start(bf16[1024,256]{1,0:T(8,128)(2,1)} %own.1) | copy-start | bytes 1572868
  67.9 14.8 %collective-permute-start.10 = (s16[1040,256]{1,0:T(8,128)(2,1)S(1)}, s16[1040,256]{1,0:T(8,128)(2,1)S(1)}, u32[]{:S(2)}, u32[]{:S(2)}) collective-permute-start(s16[1040,256]{1,0:T(8,128)(2,1)S(1)} %get-tuple-element.16), channel_id=1, source_target_pairs={{0,1},{3,2},{4,5},{7,6},{8,9},{11,10},{12,13},{15,14},{16,17},{19,... | collective-permute-start | bytes 1597448 | tf_op jit(solution)/shard_map/ppermute | solution.py:411
  74.8 16.4 %collective-permute-start.17 = (bf16[1024,256]{1,0:T(8,128)(2,1)S(1)}, bf16[1024,256]{1,0:T(8,128)(2,1)S(1)}, u32[]{:S(2)}, u32[]{:S(2)}) collective-permute-start(bf16[1024,256]{1,0:T(8,128)(2,1)S(1)} %collective-permute-done.16.r2), channel_id=1, source_target_pairs={{2,3},{6,7},{10,11},{14,15},{18,19},{22,23},{26,27},{30,31}} | collective-permute-start | bytes 1572872 | tf_op jit(solution)/shard_map/ppermute | solution.py:386
  75.6 16.5 %collective-permute-start.20 = (bf16[1024,256]{1,0:T(8,128)(2,1)S(1)}, bf16[1024,256]{1,0:T(8,128)(2,1)S(1)}, u32[]{:S(2)}, u32[]{:S(2)}) collective-permute-start(bf16[1024,256]{1,0:T(8,128)(2,1)S(1)} %collective-permute-done.19.l2), channel_id=1, source_target_pairs={{1,0},{5,4},{9,8},{13,12},{17,16},{21,20},{25,24},{29,28}} | collective-permute-start | bytes 1572872 | tf_op jit(solution)/shard_map/ppermute | solution.py:389
  82.7 2.2 %copy-start = (f32[4,1024,256]{2,1,0:T(8,128)S(1)}, f32[4,1024,256]{2,1,0:T(8,128)}, u32[]{:S(2)}) copy-start(f32[4,1024,256]{2,1,0:T(8,128)} %get-tuple-element.15.partial_ref) | copy-start | bytes 12582916
  85.2 22.5 %copy-start.1 = (f32[4,1024,256]{2,1,0:T(8,128)S(1)}, f32[4,1024,256]{2,1,0:T(8,128)}, u32[]{:S(2)}) copy-start(f32[4,1024,256]{2,1,0:T(8,128)} %get-tuple-element.15.partial_ref) | copy-start | bytes 12582916
  85.2 22.0 %collective-permute-start.13 = (s16[1040,256]{1,0:T(8,128)(2,1)S(1)}, s16[1040,256]{1,0:T(8,128)(2,1)S(1)}, u32[]{:S(2)}, u32[]{:S(2)}) collective-permute-start(s16[1040,256]{1,0:T(8,128)(2,1)S(1)} %hop.3), channel_id=1, source_target_pairs={{3,2},{2,1},{7,6},{6,5},{11,10},{10,9},{15,14},{14,13},{19,18},{18... | collective-permute-start | bytes 1597448 | tf_op jit(solution)/shard_map/ppermute | solution.py:389
  86.1 22.0 %collective-permute-start.11 = (s16[1040,256]{1,0:T(8,128)(2,1)S(1)}, s16[1040,256]{1,0:T(8,128)(2,1)S(1)}, u32[]{:S(2)}, u32[]{:S(2)}) collective-permute-start(s16[1040,256]{1,0:T(8,128)(2,1)S(1)} %hop.3), channel_id=1, source_target_pairs={{0,1},{1,2},{4,5},{5,6},{8,9},{9,10},{12,13},{13,14},{16,17},{17,1... | collective-permute-start | bytes 1597448 | tf_op jit(solution)/shard_map/ppermute | solution.py:386
  91.2 0.8 copy-start.8
  92.0 0.8 copy-start.10
  92.8 1.0 copy-start.9
  93.9 1.0 copy-start.11
  106.7 3.2 %collective-permute-start.22 = (s16[2064,128]{1,0:T(8,128)(2,1)S(1)}, s16[2064,128]{1,0:T(8,128)(2,1)S(1)}, u32[]{:S(2)}, u32[]{:S(2)}) collective-permute-start(s16[2064,128]{1,0:T(8,128)(2,1)S(1)} %get-tuple-element.22), channel_id=1, source_target_pairs={{0,4},{4,0},{8,12},{12,8},{16,20},{20,16},{24,28},{28,24},{1,5},{5... | collective-permute-start | bytes 1585160 | tf_op jit(solution)/shard_map/ppermute | solution.py:383
  106.7 8.9 %collective-permute-start.24 = (s16[2064,128]{1,0:T(8,128)(2,1)S(1)}, s16[2064,128]{1,0:T(8,128)(2,1)S(1)}, u32[]{:S(2)}, u32[]{:S(2)}) collective-permute-start(s16[2064,128]{1,0:T(8,128)(2,1)S(1)} %get-tuple-element.24), channel_id=1, source_target_pairs={{0,4},{4,0},{8,12},{12,8},{16,20},{20,16},{24,28},{28,24},{1,5},{5... | collective-permute-start | bytes 1585160 | tf_op jit(solution)/shard_map/ppermute | solution.py:383
  107.2 11.0 %collective-permute-start.26 = (s16[2064,128]{1,0:T(8,128)(2,1)S(1)}, s16[2064,128]{1,0:T(8,128)(2,1)S(1)}, u32[]{:S(2)}, u32[]{:S(2)}) collective-permute-start(s16[2064,128]{1,0:T(8,128)(2,1)S(1)} %get-tuple-element.26), channel_id=1, source_target_pairs={{0,4},{4,0},{8,12},{12,8},{16,20},{20,16},{24,28},{28,24},{1,5},{5... | collective-permute-start | bytes 1585160 | tf_op jit(solution)/shard_map/ppermute | solution.py:383
  107.2 12.0 %collective-permute-start.21 = (s16[2064,128]{1,0:T(8,128)(2,1)S(1)}, s16[2064,128]{1,0:T(8,128)(2,1)S(1)}, u32[]{:S(2)}, u32[]{:S(2)}) collective-permute-start(s16[2064,128]{1,0:T(8,128)(2,1)S(1)} %get-tuple-element.20), channel_id=1, source_target_pairs={{0,4},{4,0},{8,12},{12,8},{16,20},{20,16},{24,28},{28,24},{1,5},{5... | collective-permute-start | bytes 1585160 | tf_op jit(solution)/shard_map/ppermute | solution.py:383
  107.7 7.5 %copy-start.5 = (f32[2048,128]{1,0:T(8,128)S(1)}, f32[2048,128]{1,0:T(8,128)}, u32[]{:S(2)}) copy-start(f32[2048,128]{1,0:T(8,128)} %get-tuple-element.21.kept_ref) | copy-start | bytes 3145732
  108.1 9.8 %copy-start.4 = (f32[2048,128]{1,0:T(8,128)S(1)}, f32[2048,128]{1,0:T(8,128)}, u32[]{:S(2)}) copy-start(f32[2048,128]{1,0:T(8,128)} %get-tuple-element.23.kept_ref) | copy-start | bytes 3145732
  108.1 10.8 %copy-start.3 = (f32[2048,128]{1,0:T(8,128)S(1)}, f32[2048,128]{1,0:T(8,128)}, u32[]{:S(2)}) copy-start(f32[2048,128]{1,0:T(8,128)} %get-tuple-element.25.kept_ref) | copy-start | bytes 3145732
  108.1 35.5 %collective-permute-start.14 = (s16[1040,256]{1,0:T(8,128)(2,1)S(1)}, s16[1040,256]{1,0:T(8,128)(2,1)S(1)}, u32[]{:S(2)}, u32[]{:S(2)}) collective-permute-start(s16[1040,256]{1,0:T(8,128)(2,1)S(1)} %hop.5), channel_id=1, source_target_pairs={{3,2},{2,1},{1,0},{7,6},{6,5},{5,4},{11,10},{10,9},{9,8},{15,14},{... | collective-permute-start | bytes 1597448 | tf_op jit(solution)/shard_map/ppermute | solution.py:389
  109.9 33.7 %collective-permute-start.12 = (s16[1040,256]{1,0:T(8,128)(2,1)S(1)}, s16[1040,256]{1,0:T(8,128)(2,1)S(1)}, u32[]{:S(2)}, u32[]{:S(2)}) collective-permute-start(s16[1040,256]{1,0:T(8,128)(2,1)S(1)} %hop.4), channel_id=1, source_target_pairs={{0,1},{1,2},{2,3},{4,5},{5,6},{6,7},{8,9},{9,10},{10,11},{12,13},{... | collective-permute-start | bytes 1597448 | tf_op jit(solution)/shard_map/ppermute | solution.py:386
  115.6 15.9 %collective-permute-start.23 = (s16[2064,128]{1,0:T(8,128)(2,1)S(1)}, s16[2064,128]{1,0:T(8,128)(2,1)S(1)}, u32[]{:S(2)}, u32[]{:S(2)}) collective-permute-start(s16[2064,128]{1,0:T(8,128)(2,1)S(1)} %combine.5), channel_id=1, source_target_pairs={{0,24},{4,28},{8,16},{12,20},{16,8},{20,12},{24,0},{28,4},{1,25},{... | collective-permute-start | bytes 1585160 | tf_op jit(solution)/shard_map/ppermute | solution.py:383
  118.2 23.3 %collective-permute-start.25 = (s16[2064,128]{1,0:T(8,128)(2,1)S(1)}, s16[2064,128]{1,0:T(8,128)(2,1)S(1)}, u32[]{:S(2)}, u32[]{:S(2)}) collective-permute-start(s16[2064,128]{1,0:T(8,128)(2,1)S(1)} %combine.6), channel_id=1, source_target_pairs={{0,16},{4,20},{8,24},{12,28},{16,0},{20,4},{24,8},{28,12},{1,17},{... | collective-permute-start | bytes 1585160 | tf_op jit(solution)/shard_map/ppermute | solution.py:383
  119.2 22.4 %collective-permute-start.27 = (s16[2064,128]{1,0:T(8,128)(2,1)S(1)}, s16[2064,128]{1,0:T(8,128)(2,1)S(1)}, u32[]{:S(2)}, u32[]{:S(2)}) collective-permute-start(s16[2064,128]{1,0:T(8,128)(2,1)S(1)} %combine.7), channel_id=1, source_target_pairs={{0,8},{4,12},{8,0},{12,4},{16,24},{20,28},{24,16},{28,20},{1,9},{5... | collective-permute-start | bytes 1585160 | tf_op jit(solution)/shard_map/ppermute | solution.py:383
  120.1 1.6 %copy-start.12 = (bf16[1024,1024]{1,0:T(8,128)(2,1)S(1)}, bf16[1024,1024]{1,0:T(8,128)(2,1)}, u32[]{:S(2)}) copy-start(bf16[1024,1024]{1,0:T(8,128)(2,1)} %get-tuple-element.17.cotangent_ref) | copy-start | bytes 6291460
  121.7 8.3 %copy-start.2 = (f32[2048,128]{1,0:T(8,128)S(1)}, f32[2048,128]{1,0:T(8,128)}, u32[]{:S(2)}) copy-start(f32[2048,128]{1,0:T(8,128)} %get-tuple-element.19.kept_ref) | copy-start | bytes 3145732

commit v2 on v1

v2 whole, which is shorter than its diff:
```python
import functools

import jax
import jax.numpy as jnp
from jax import lax
from jax.experimental import pallas as pl
from jax.experimental.pallas import tpu as pltpu
from jax.sharding import PartitionSpec as P

VMEM_BYTES = 48 * 1024 * 1024
GROUP = 128
PAD = 16


def encode(block):
    peak = jnp.max(jnp.abs(block), axis=0, keepdims=True)
    exponent = jnp.floor(jnp.log2(jnp.maximum(peak, 2.0**-100))) + 1.0
    exponent = jnp.clip(exponent, -100.0, 128.0)
    scaled = jnp.round(block * jnp.exp2(15.0 - exponent))
    codes = jnp.clip(scaled, -32767.0, 32767.0).astype(jnp.int32).astype(jnp.int16)
    return codes, exponent


def decode(codes, exponent):
    return codes.astype(jnp.int32).astype(jnp.float32) * jnp.exp2(exponent - 15.0)


def as_code(exponents):
    return exponents.astype(jnp.int32).astype(jnp.int16)


def exponent_rows(codes):
    return codes.astype(jnp.int32).astype(jnp.float32)


def params():
    return pltpu.CompilerParams(vmem_limit_bytes=VMEM_BYTES)


def whole(shape):
    zeros = (0,) * len(shape)
    return pl.BlockSpec(shape, lambda *_: zeros, pipeline_mode=pl.Buffered(1))


def aligned(index, size):
    return pl.ds(pl.multiple_of(index * size, size), size)


def write_message(message_ref, rows, blocks):
    place = lax.broadcasted_iota(jnp.int32, (PAD, message_ref.shape[1]), 0)
    exponents = jnp.zeros((PAD, message_ref.shape[1]), jnp.float32)
    for group in range(rows // GROUP):
        codes, exponent = encode(blocks(group))
        message_ref[group * GROUP : (group + 1) * GROUP, :] = codes
        exponents = jnp.where(place == group, exponent, exponents)
    message_ref[rows : rows + PAD, :] = as_code(exponents)


def read_message(message_ref, rows):
    exponents = exponent_rows(message_ref[rows : rows + PAD, :])

    def block(group):
        return decode(
            message_ref[group * GROUP : (group + 1) * GROUP, :], exponents[group : group + 1, :]
        )

    return block


def first_kernel(column_blocks, codes_ref, place_ref, normed_ref, *refs):
    message_refs = refs[:-2]
    weight_ref, first_ref = refs[-2:]
    tokens = normed_ref.shape[0]
    chunk_width = first_ref.shape[1]
    chunks = weight_ref.shape[1] // chunk_width
    tile = message_refs[0].shape[1]
    weight_ref[...] = jnp.zeros_like(weight_ref)
    for k in range(len(message_refs)):
        for slot in range(codes_ref.shape[1]):
            code = codes_ref[k, slot]

            @pl.when(code >= 0)
            def _():
                row = aligned(code // column_blocks, tile)
                column = aligned(code % column_blocks, tile)
                weight_ref[row, column] = message_refs[k][slot * tile : (slot + 1) * tile, :]

    far = weight_ref[:, aligned(chunks - 1 - place_ref[0], chunk_width)]
    partial = jnp.dot(normed_ref[...], far, preferred_element_type=jnp.float32)
    write_message(
        first_ref, tokens, lambda group: partial[group * GROUP : (group + 1) * GROUP, :]
    )


def first_values(codes, place, normed, messages, chunks, column_blocks):
    tokens, features = normed.shape
    tile = messages[0].shape[1]
    width = column_blocks * tile
    return pl.pallas_call(
        functools.partial(first_kernel, column_blocks),
        grid_spec=pltpu.PrefetchScalarGridSpec(
            num_scalar_prefetch=2,
            grid=(1,),
            in_specs=[whole(normed.shape)] + [whole(m.shape) for m in messages],
            out_specs=[whole((features, width)), whole((tokens + PAD, width // chunks))],
        ),
        out_shape=[
            jax.ShapeDtypeStruct((features, width), jnp.bfloat16),
            jax.ShapeDtypeStruct((tokens + PAD, width // chunks), jnp.int16),
        ],
        compiler_params=params(),
        cost_estimate=pl.CostEstimate(flops=1, bytes_accessed=1, transcendentals=0),
        name="first_values",
    )(codes, place, normed, *messages)


def partial_kernel(normed_ref, weight_ref, partial_ref):
    partial_ref[0] = jnp.dot(
        normed_ref[...], weight_ref[...], preferred_element_type=jnp.float32
    )


def partial_values(normed, weight, chunks):
    tokens, features = normed.shape
    width = weight.shape[1] // chunks
    return pl.pallas_call(
        partial_kernel,
        grid=(chunks,),
        in_specs=[whole(normed.shape), pl.BlockSpec((features, width), lambda h: (0, h))],
        out_specs=pl.BlockSpec((1, tokens, width), lambda h: (h, 0, 0)),
        out_shape=jax.ShapeDtypeStruct((chunks, tokens, width), jnp.float32),
        compiler_params=params(),
        cost_estimate=pl.CostEstimate(flops=1, bytes_accessed=1, transcendentals=0),
        name="partial_values",
    )(normed, weight)


def hop_kernel(place_ref, partial_ref, arrived_ref, message_ref):
    rows = partial_ref.shape[1]
    arrived = read_message(arrived_ref, rows)

    def total(group):
        return partial_ref[0, group * GROUP : (group + 1) * GROUP, :] + arrived(group)

    write_message(message_ref, rows, total)


def hop(place, ahead, partial, arrived):
    chunks, tokens, width = partial.shape
    return pl.pallas_call(
        hop_kernel,
        grid_spec=pltpu.PrefetchScalarGridSpec(
            num_scalar_prefetch=1,
            grid=(1,),
            in_specs=[
                pl.BlockSpec((1, tokens, width), lambda i, p: ((p[0] + ahead) % chunks, 0, 0)),
                whole(arrived.shape),
            ],
            out_specs=whole(arrived.shape),
        ),
        out_shape=jax.ShapeDtypeStruct(arrived.shape, jnp.int16),
        compiler_params=params(),
        cost_estimate=pl.CostEstimate(
            flops=8 * tokens * width, bytes_accessed=8 * tokens * width, transcendentals=0
        ),
        name="hop",
    )(place, partial, arrived)


def last_hop_kernel(place_ref, partial_ref, right_ref, left_ref, values_ref):
    rows = partial_ref.shape[1]
    right = read_message(right_ref, rows)
    left = read_message(left_ref, rows)
    for group in range(rows // GROUP):
        span = slice(group * GROUP, (group + 1) * GROUP)
        total = partial_ref[0, span, :] + right(group) + left(group)
        values_ref[span, :] = total.astype(values_ref.dtype)


def last_hop(place, partial, right, left):
    _, tokens, width = partial.shape
    return pl.pallas_call(
        last_hop_kernel,
        grid_spec=pltpu.PrefetchScalarGridSpec(
            num_scalar_prefetch=1,
            grid=(1,),
            in_specs=[
                pl.BlockSpec((1, tokens, width), lambda i, p: (p[0], 0, 0)),
                whole(right.shape),
                whole(left.shape),
            ],
            out_specs=whole((tokens, width)),
        ),
        out_shape=jax.ShapeDtypeStruct((tokens, width), jnp.bfloat16),
        compiler_params=params(),
        cost_estimate=pl.CostEstimate(
            flops=8 * tokens * width, bytes_accessed=10 * tokens * width, transcendentals=0
        ),
        name="last_hop",
    )(place, partial, right, left)


def chunk_order(place):
    return (
        place,
        jnp.where(place == 3, 2, place + 1),
        jnp.where(place == 0, 2, jnp.where(place == 1, 0, 1)),
        jnp.where(place < 2, 3, 0),
    )


def second_chunk(place, r1, l1):
    return jnp.where(place == 3, r1, l1)


def third_chunk(place, r1, r2, l2):
    return jnp.where((place == 1) | (place == 2), r1, r2 + l2)


def fourth_chunk(place, r2, l2, r3, l3):
    return jnp.where((place == 1) | (place == 2), r2 + l2, r3 + l3)


def product(turned, normed_ref, out_ref):
    step = 512
    for n in range(normed_ref.shape[1] // step):
        span = slice(n * step, (n + 1) * step)
        out_ref[:, span] = jnp.dot(turned, normed_ref[:, span], preferred_element_type=jnp.float32)


def chunk_kernel(pick, place_ref, normed_ref, *refs):
    tokens = normed_ref.shape[0]
    chunk = pick(place_ref[0], *[ref[:tokens, :] for ref in refs[:-1]])
    product(chunk.T, normed_ref, refs[-1])


def chunk_gradient(pick, place, normed, *chunks):
    tokens, features = normed.shape
    width = chunks[0].shape[1]
    return pl.pallas_call(
        functools.partial(chunk_kernel, pick),
        grid_spec=pltpu.PrefetchScalarGridSpec(
            num_scalar_prefetch=1,
            grid=(1,),
            in_specs=[whole(a.shape) for a in (normed, *chunks)],
            out_specs=whole((width, features)),
        ),
        out_shape=jax.ShapeDtypeStruct((width, features), jnp.float32),
        compiler_params=params(),
        cost_estimate=pl.CostEstimate(flops=1, bytes_accessed=1, transcendentals=0),
        name="chunk_gradient",
    )(place, normed, *chunks)


def slots_kernel(
    chips, column_blocks, codes_ref, place_ref, normed_ref, r2, l2, r3, l3, g1, g2, g3, *refs
):
    keep_refs = refs[:chips]
    send_refs = refs[chips : 2 * chips]
    gradient, sems = refs[2 * chips :]
    place = place_ref[0]
    copies = [
        pltpu.make_async_copy(g, gradient.at[i], sems.at[i]) for i, g in enumerate((g1, g2, g3))
    ]
    for copy in copies:
        copy.start()
    tokens = normed_ref.shape[0]
    chunk = fourth_chunk(place, *[ref[:tokens, :] for ref in (r2, l2, r3, l3)])
    product(chunk.T, normed_ref, gradient.at[3])
    for copy in copies:
        copy.wait()
    order = chunk_order(place)
    tile = GROUP
    capacity = codes_ref.shape[1]
    chunk_blocks = gradient.shape[1] // tile

    def term(k, slot):
        code = codes_ref[k, slot]
        safe = jnp.maximum(code, 0)
        row, column = safe // column_blocks, safe % column_blocks
        chunk = column // chunk_blocks
        stage = jnp.where(
            chunk == order[0],
            0,
            jnp.where(chunk == order[1], 1, jnp.where(chunk == order[2], 2, 3)),
        )
        block = gradient[stage, aligned(column % chunk_blocks, tile), aligned(row, tile)]
        return jnp.where(code >= 0, block, 0.0)

    for chip in reversed(range(chips)):
        write_message(send_refs[chip], capacity * tile, lambda slot: term(2 * chip + 1, slot))
        for slot in range(capacity):
            keep_refs[chip][slot * tile : (slot + 1) * tile, :] = term(2 * chip, slot)


def slot_terms(codes, place, normed, late, early, column_blocks):
    tokens, features = normed.shape
    chips = codes.shape[0] // 2
    rows = codes.shape[1] * GROUP
    width = early[0].shape[0]
    shapes = [((rows, GROUP), jnp.float32)] * chips + [((rows + PAD, GROUP), jnp.int16)] * chips
    outputs = pl.pallas_call(
        functools.partial(slots_kernel, chips, column_blocks),
        grid_spec=pltpu.PrefetchScalarGridSpec(
            num_scalar_prefetch=2,
            grid=(1,),
            in_specs=[whole(a.shape) for a in (normed, *late)]
            + [pl.BlockSpec(memory_space=pl.ANY)] * len(early),
            out_specs=[whole(shape) for shape, _ in shapes],
            scratch_shapes=[
                pltpu.VMEM((len(early) + 1, width, features), jnp.float32),
                pltpu.SemaphoreType.DMA((len(early),)),
            ],
        ),
        out_shape=[jax.ShapeDtypeStruct(shape, kind) for shape, kind in shapes],
        compiler_params=params(),
        cost_estimate=pl.CostEstimate(
            flops=2 * tokens * features * width,
            bytes_accessed=18 * 1024 * 1024,
            transcendentals=0,
        ),
        name="slot_terms",
    )(codes, place, normed, *late, *early)
    return outputs[:chips], outputs[chips:]


def combine_kernel(kept_ref, arrived_ref, out_ref):
    rows = kept_ref.shape[0]
    arrived = read_message(arrived_ref, rows)

    def total(group):
        return kept_ref[group * GROUP : (group + 1) * GROUP, :] + arrived(group)

    if out_ref.dtype == jnp.int16:
        write_message(out_ref, rows, total)
    else:
        for group in range(rows // GROUP):
            out_ref[group * GROUP : (group + 1) * GROUP, :] = total(group)


def combine(kept, arrived, kind):
    shape = arrived.shape if kind == jnp.int16 else kept.shape
    return pl.pallas_call(
        combine_kernel,
        grid=(1,),
        in_specs=[whole(kept.shape), whole(arrived.shape)],
        out_specs=whole(shape),
        out_shape=jax.ShapeDtypeStruct(shape, kind),
        compiler_params=params(),
        cost_estimate=pl.CostEstimate(
            flops=8 * kept.size, bytes_accessed=8 * kept.size, transcendentals=0
        ),
        name="combine",
    )(kept, arrived)


def update_kernel(count, *refs):
    kept_ref, out_ref = refs[0], refs[-1]
    tile = out_ref.shape[-1]
    arrived = [read_message(ref, kept_ref.shape[0]) for ref in refs[1 : 1 + count]]
    for slot in range(out_ref.shape[0]):
        total = kept_ref[slot * tile : (slot + 1) * tile, :]
        for block in arrived:
            total = total + block(slot)
        mean = jnp.sum(total * total) / (tile * tile)
        out_ref[slot] = (total * lax.rsqrt(mean + 1e-06)).T.astype(out_ref.dtype)


def normalized_update(kept, arrived, shape):
    return pl.pallas_call(
        functools.partial(update_kernel, len(arrived)),
        grid=(1,),
        in_specs=[whole(kept.shape)] + [whole(a.shape) for a in arrived],
        out_specs=whole(shape),
        out_shape=jax.ShapeDtypeStruct(shape, jnp.bfloat16),
        compiler_params=params(),
        cost_estimate=pl.CostEstimate(
            flops=16 * kept.size, bytes_accessed=12 * kept.size, transcendentals=0
        ),
        name="normalized_update",
    )(kept, *arrived)


def grad_input_kernel(place_ref, weight_ref, own, r1, r2, r3, l1, l2, l3, out_ref, cotangent):
    @pl.when(pl.program_id(0) == 0)
    def _():
        place = place_ref[0]
        order = chunk_order(place)
        width = own.shape[1]
        arrived = (r1, r2, r3, l1, l2, l3)
        v1, v2, v3, w1, w2, w3 = (ref[: own.shape[0], :] for ref in arrived)
        cotangent[:, aligned(order[0], width)] = own[...]
        cotangent[:, aligned(order[1], width)] = second_chunk(place, v1, w1)
        cotangent[:, aligned(order[2], width)] = third_chunk(place, v1, v2, w2)
        cotangent[:, aligned(order[3], width)] = fourth_chunk(place, v2, w2, v3, w3)

    out_ref[...] = lax.dot_general(
        cotangent[...],
        weight_ref[...],
        (((1,), (1,)), ((), ())),
        preferred_element_type=jnp.float32,
    ).astype(out_ref.dtype)


def grad_inputs(place, weight, *chunks):
    features, width = weight.shape
    tokens = chunks[0].shape[0]
    block = 256
    return pl.pallas_call(
        grad_input_kernel,
        grid_spec=pltpu.PrefetchScalarGridSpec(
            num_scalar_prefetch=1,
            grid=(features // block,),
            in_specs=[pl.BlockSpec((block, width), lambda i, p: (i, 0))]
            + [whole(chunk.shape) for chunk in chunks],
            out_specs=pl.BlockSpec((tokens, block), lambda i, p: (0, i)),
            scratch_shapes=[pltpu.VMEM((tokens, width), jnp.bfloat16)],
        ),
        out_shape=jax.ShapeDtypeStruct((tokens, features), jnp.bfloat16),
        compiler_params=params(),
        cost_estimate=pl.CostEstimate(
            flops=2 * tokens * features * width,
            bytes_accessed=12 * 1024 * 1024,
            transcendentals=0,
        ),
        name="grad_inputs",
    )(place, weight, *chunks)


def local(devices, parts, normed, tile_values, tile_rows, tile_columns, cotangent):
    capacity, tile = tile_values.shape[1], tile_values.shape[-1]
    column_blocks = cotangent.shape[1] * parts // tile
    chips = devices // 2
    rows = capacity * tile
    place = lax.axis_index("tensor").astype(jnp.int32).reshape(1)

    def swap(x, mask):
        return lax.ppermute(x, "fsdp", [(i, i ^ mask) for i in range(devices)])

    def right(x, *sources):
        return lax.ppermute(x, "tensor", [(i, i + 1) for i in sources])

    def left(x, *sources):
        return lax.ppermute(x, "tensor", [(i, i - 1) for i in sources])

    padded = jnp.pad(cotangent, ((0, PAD), (0, 0)))
    r1, l1 = right(padded, 0, 1, 2), left(padded, 3, 2, 1)
    positions = jnp.where(tile_columns >= 0, tile_rows * column_blocks + tile_columns + 1, 0)
    positions = jnp.pad(
        positions.astype(jnp.bfloat16), ((0, PAD - 1), (0, tile - capacity))
    )
    message = jnp.concatenate([tile_values.reshape(rows, tile), positions], axis=0)
    g1 = chunk_gradient(lambda place, own: own, place, normed, cotangent)
    direct = [1, 2] if chips == 4 else list(range(1, chips))
    same_core = [message] + [swap(message, 2 * chip) for chip in direct]
    beside = swap(message, 1)
    r1, l1, g1, beside, *same_core = lax.optimization_barrier((r1, l1, g1, beside, *same_core))

    r2, l2 = right(r1, 1, 2), left(l1, 2, 1)
    g2 = chunk_gradient(second_chunk, place, normed, r1, l1)
    if chips == 4:
        even = lax.axis_index("fsdp") % 2 == 0
        diagonal = lax.ppermute(
            jnp.where(even, same_core[2], same_core[1]),
            "fsdp",
            [(i, i ^ 2 if i % 2 == 0 else i ^ 4) for i in range(devices)],
        )
        across = [swap(m, 1) for m in same_core[1:]]
        diagonal, g2, *across = lax.optimization_barrier((diagonal, g2, *across))
        same_core.append(diagonal)
        across.append(swap(diagonal, 1))
    else:
        across = [swap(m, 1) for m in same_core[1:]]
    gathered = []
    for pair in zip(same_core, [beside] + across):
        gathered += pair
    r2, l2, *gathered = lax.optimization_barrier((r2, l2, *gathered))
    codes = jnp.stack([m[rows, :capacity] for m in gathered]).astype(jnp.int32) - 1

    r3, l3 = right(r2, 2), left(l2, 1)
    weight, first = first_values(codes, place, normed, gathered, parts, column_blocks)
    arrived = lax.ppermute(first, "tensor", [(0, 1), (3, 2)])
    partial = partial_values(normed, weight, parts)
    g3 = chunk_gradient(third_chunk, place, normed, r1, r2, l2)
    arrived, g3 = lax.optimization_barrier((arrived, g3))

    keep, send = slot_terms(
        codes, place, normed, (r2, l2, r3, l3), (g1, g2, g3), column_blocks
    )
    second = hop(place, 2, partial, arrived)
    from_left, from_right = right(second, 0, 1), left(second, 3, 2)
    other = [swap(m, 1) for m in send]
    terms = [
        swap(combine(keep[chip], other[chip], jnp.int16), 2 * chip)
        for chip in reversed(range(1, chips))
    ]
    own = combine(keep[0], other[0], jnp.float32)
    from_left = right(hop(place, 1, partial, from_left), 0, 1, 2)
    from_right = left(hop(place, 3, partial, from_right), 3, 2, 1)
    grad_input = grad_inputs(place, weight, cotangent, r1, r2, r3, l1, l2, l3)
    values = last_hop(place, partial, from_left, from_right)
    update = normalized_update(own, terms, tile_values.shape[1:])
    return values, grad_input, update[None]


def solution(mesh):
    in_specs = (
        P("fsdp", "tensor"),
        P("tensor", "fsdp", None, None),
        P("tensor", "fsdp"),
        P("tensor", "fsdp"),
        P("fsdp", "tensor"),
    )
    out_specs = (P("fsdp", "tensor"), P("fsdp", "tensor"), P("tensor", "fsdp", None, None))
    return jax.shard_map(
        functools.partial(local, mesh.shape["fsdp"], mesh.shape["tensor"]),
        mesh=mesh,
        in_specs=in_specs,
        out_specs=out_specs,
        check_vma=False,
    )
```

time: 145 us -> 134 us (0.924)
  waiting for transfers between devices: 49.8 us -> 31.1 us
  Pallas kernels: 42.4 us -> 51.7 us
  starting transfers between devices: 42.3 us -> 33.4 us
  local copies, waits for them, and re-layouts: 8.5 us -> 14 us
    ppermute x17 -> x13, waiting for transfers between devices: 32.8 us -> 18.6 us  [swap(): return lax.ppermute(x, 'fsdp', [(i, i ^ mask) for i in range(devices)])]
    pallas_call x3 -> x7, Pallas kernels: 37.1 us -> 45.6 us  [the longest x3 10.4 us: chunk_gradient(): pl.pallas_call(functools.partial(chunk_kernel, pick), grid_spec=pltpu.Pre...]
    ppermute x1, waiting for transfers between devices: 5.83 us -> 0.01 us  [local(): arrived = lax.ppermute(first, 'tensor', [(0, 1), (3, 2)])]
    ppermute x17 -> x13, starting transfers between devices: 12.5 us -> 8.28 us  [swap(): return lax.ppermute(x, 'fsdp', [(i, i ^ mask) for i in range(devices)])]
    ppermute x1, starting transfers between devices: 6.92 us -> 3.64 us  [local(): arrived = lax.ppermute(first, 'tensor', [(0, 1), (3, 2)])]
    unnamed x26 -> x38, local copies, waits for them, and re-layouts: 8.5 us -> 11.3 us
    ppermute x5, starting transfers between devices: 16.8 us -> 14.7 us  [right(): return lax.ppermute(x, 'tensor', [(i, i + 1) for i in sources])]
    pad x0 -> x1, local copies, waits for them, and re-layouts: none -> 1.95 us  [local(): padded = jnp.pad(cotangent, ((0, PAD), (0, 0)))]
  transfers between devices with their start and end apart: 28 -> 25, of which waited for: 8 -> 7; matrix products, arithmetic and copies ran while one was open for 0% -> 1% of each run, Pallas kernels for 29% -> 33%
where the time goes in v2:
time: 134 us; the launch traced here: 133 us
  Pallas kernels  51.7 us (39%)
  starting transfers between devices  33.4 us (25%)
  waiting for transfers between devices  31.1 us (23%)
  local copies, waits for them, and re-layouts  14 us (10%)
  other arithmetic  1.83 us (1%)
    ppermute x13, waiting for transfers between devices, swap(): return lax.ppermute(x, 'fsdp', [(i, i ^ mask) for i in range(devices)])  18.6 us
    ppermute x5, starting transfers between devices, right(): return lax.ppermute(x, 'tensor', [(i, i + 1) for i in sources])  14.7 us
    ppermute x5, waiting for transfers between devices, left(): return lax.ppermute(x, 'tensor', [(i, i - 1) for i in sources])  12.1 us
    unnamed x38, local copies, waits for them, and re-layouts  11.3 us
    pallas_call x3, Pallas kernels, chunk_gradient(): pl.pallas_call(functools.partial(chunk_kernel, pick), grid_spec=pltpu.Pre...  10.4 us
    pallas_call x1, Pallas kernels, slot_terms(): pl.pallas_call(functools.partial(slots_kernel, chips, column_blocks), gri...  10.1 us
    pallas_call x1, Pallas kernels, grad_inputs(): pl.pallas_call(grad_input_kernel, grid_spec=pltpu.PrefetchScalarGridSpec(...  9.87 us
    pallas_call x1, Pallas kernels, partial_values(): pl.pallas_call(partial_kernel, grid=(chunks,), in_specs=[whole(normed.sha...  8.35 us
  transfers between devices with their start and end apart: 25, of which 7 were waited for; matrix products, arithmetic and copies ran while one was open for 1% of the time, Pallas kernels for 33%

profile of v2, /device:TPU:0, one launch (start us, length us, event | category | flops | bytes accessed | tf_op | source)
XLA Modules:
  0.0 133.0 jit_solution(8564195709153940685)
XLA Ops:
  0.6 1.9 %pad.8 = bf16[1040,256]{1,0:T(8,128)(2,1)} pad(bf16[1024,256]{1,0:T(8,128)(2,1)} %own.1, bf16[]{:T(256)} %constant.24.clone.1), padding=0_16x0_0 | pad | bytes 1056770 | tf_op jit(solution)/shard_map/jit(_pad)/pad | solution.py:446
  2.6 4.9 %collective-permute-start = (bf16[1040,256]{1,0:T(8,128)(2,1)}, bf16[1040,256]{1,0:T(8,128)(2,1)S(1)}, u32[]{:S(2)}, u32[]{:S(2)}) collective-permute-start(bf16[1040,256]{1,0:T(8,128)(2,1)} %pad.8), channel_id=1, source_target_pairs={{0,1},{1,2},{2,3},{4,5},{5,6},{6,7},{8,9},{9,10},{10,11},{12,13},{... | collective-permute-start | bytes 1597448 | tf_op jit(solution)/shard_map/ppermute | solution.py:441
  7.5 1.3 collective-permute-start.1
  8.8 0.7 fusion.2
  9.5 1.1 fusion.1.refs_0_
  10.7 1.6 %collective-permute-start.3 = (bf16[2064,128]{1,0:T(8,128)(2,1)S(1)}, bf16[2064,128]{1,0:T(8,128)(2,1)S(1)}, u32[]{:S(2)}, u32[]{:S(2)}) collective-permute-start(bf16[2064,128]{1,0:T(8,128)(2,1)S(1)} %fusion.1.refs_0_), channel_id=1, source_target_pairs={{0,8},{4,12},{8,0},{12,4},{16,24},{20,28},{24,16},{28,20},{1,9},{5... | collective-permute-start | bytes 1585160 | tf_op jit(solution)/shard_map/ppermute | solution.py:438
  12.2 1.5 %collective-permute-start.4 = (bf16[2064,128]{1,0:T(8,128)(2,1)S(1)}, bf16[2064,128]{1,0:T(8,128)(2,1)S(1)}, u32[]{:S(2)}, u32[]{:S(2)}) collective-permute-start(bf16[2064,128]{1,0:T(8,128)(2,1)S(1)} %fusion.1.refs_0_), channel_id=1, source_target_pairs={{0,16},{4,20},{8,24},{12,28},{16,0},{20,4},{24,8},{28,12},{1,17},{... | collective-permute-start | bytes 1585160 | tf_op jit(solution)/shard_map/ppermute | solution.py:438
  13.8 3.5 %chunk_gradient.3.g1 = f32[256,2048]{1,0:T(8,128)S(1)} custom-call(s32[1]{0:T(128)} %bitcast.place_ref, bf16[1024,2048]{1,0:T(8,128)(2,1)} %normed_ref.11, bf16[1024,256]{1,0:T(8,128)(2,1)S(1)} %copy-done.3), custom_call_target="tpu_custom_call" | custom-call | flops 1 | bytes 1 | tf_op jit(solution)/shard_map/chunk_gradient/pallas_call | solution.py:240
  17.2 1.3 copy-done.1
  18.6 6.6 %collective-permute-done.3.refs_2_ = bf16[2064,128]{1,0:T(8,128)(2,1)S(1)} collective-permute-done((bf16[2064,128]{1,0:T(8,128)(2,1)S(1)}, bf16[2064,128]{1,0:T(8,128)(2,1)S(1)}, u32[]{:S(2)}, u32[]{:S(2)}) %collective-permute-start.3) | collective-permute-done | bytes 528416 | tf_op jit(solution)/shard_map/ppermute | solution.py:438
  25.1 1.2 collective-permute-done.4.refs_4_
  26.4 0.6 collective-permute-start.7
  27.5 0.7 collective-permute-start.5
  28.2 1.3 collective-permute-start.6
  29.5 1.0 copy-done.9
  30.6 3.5 %chunk_gradient.4.g2 = f32[256,2048]{1,0:T(8,128)S(1)} custom-call(s32[1]{0:T(128)} %bitcast.place_ref, bf16[1024,2048]{1,0:T(8,128)(2,1)} %normed_ref.11, bf16[1040,256]{1,0:T(8,128)(2,1)S(1)} %collective-permute-done.refs_0_.r1, bf16[1040,256]{1,0:T(8,128)(2,1)S(1)} %copy-done.9), custom_call_target="tpu_custom_call" | custom-call | flops 1 | bytes 1 | tf_op jit(solution)/shard_map/chunk_gradient/pallas_call | solution.py:240
  34.1 1.4 %copy-done.2 = f32[256,2048]{1,0:T(8,128)} copy-done((f32[256,2048]{1,0:T(8,128)}, f32[256,2048]{1,0:T(8,128)S(1)}, u32[]{:S(2)}) %copy-start.2) | copy-done | bytes 2097176
  35.7 12.1 %collective-permute-done.6.refs_2_.l2 = bf16[1040,256]{1,0:T(8,128)(2,1)S(1)} collective-permute-done((bf16[1040,256]{1,0:T(8,128)(2,1)}, bf16[1040,256]{1,0:T(8,128)(2,1)S(1)}, u32[]{:S(2)}, u32[]{:S(2)}) %collective-permute-start.6) | collective-permute-done | bytes 532512 | tf_op jit(solution)/shard_map/ppermute | solution.py:444
  47.9 0.7 slice.25
  48.5 0.8 copy-done.13
  49.4 0.8 copy-done.15
  50.2 0.8 copy-done.11
  51.0 0.8 copy-done.17
  51.9 1.0 copy-done.12
  52.9 1.0 copy-done.14
  54.0 1.0 copy-done.16
  55.0 1.0 copy-done.18
  56.1 6.9 %first_values.1 = (bf16[2048,1024]{1,0:T(8,128)(2,1)}, s16[1040,256]{1,0:T(8,128)(2,1)S(1)}) custom-call(s32[8,16]{1,0:T(8,128)S(1)} %convert_add_fusion.codes_ref, s32[1]{0:T(128)} %bitcast.place_ref, bf16[1024,2048]{1,0:T(8,128)(2,1)} %normed_ref.11, bf16[2064,128]{1,0:T(8,128)(2,1)S(1)} %fusion.1.refs_0_, ...), custom_call_target="tpu_custom_call" | custom-call | flops 1 | bytes 1 | tf_op jit(solution)/shard_map/first_values/pallas_call | solution.py:99
  63.0 3.6 %collective-permute-start.11 = (s16[1040,256]{1,0:T(8,128)(2,1)S(1)}, s16[1040,256]{1,0:T(8,128)(2,1)S(1)}, u32[]{:S(2)}, u32[]{:S(2)}) collective-permute-start(s16[1040,256]{1,0:T(8,128)(2,1)S(1)} %get-tuple-element.54), channel_id=1, source_target_pairs={{0,1},{3,2},{4,5},{7,6},{8,9},{11,10},{12,13},{15,14},{16,17},{19,... | collective-permute-start | bytes 1597448 | tf_op jit(solution)/shard_map/ppermute | solution.py:482
  66.6 0.7 collective-permute-start.16
  67.3 1.3 collective-permute-start.17
  68.6 3.5 %chunk_gradient.5.g3 = f32[256,2048]{1,0:T(8,128)S(1)} custom-call(s32[1]{0:T(128)} %bitcast.place_ref, bf16[1024,2048]{1,0:T(8,128)(2,1)} %normed_ref.11, bf16[1040,256]{1,0:T(8,128)(2,1)S(1)} %collective-permute-done.refs_0_.r1, bf16[1040,256]{1,0:T(8,128)(2,1)S(1)} %collective-permute-done.5.refs_1_.r2, ...), custom_call_target="tpu_custom_call" | custom-call | flops 1 | bytes 1 | tf_op jit(solution)/shard_map/chunk_gradient/pallas_call | solution.py:240
  72.1 8.3 %partial_values.1.partial_ref = f32[4,1024,256]{2,1,0:T(8,128)S(1)} custom-call(bf16[1024,2048]{1,0:T(8,128)(2,1)} %normed_ref.11, bf16[2048,1024]{1,0:T(8,128)(2,1)} %get-tuple-element.53.weight_ref), custom_call_target="tpu_custom_call" | custom-call | flops 1 | bytes 1 | tf_op jit(solution)/shard_map/partial_values/pallas_call | solution.py:126
  80.8 4.6 %collective-permute-start.12 = (s16[1040,256]{1,0:T(8,128)(2,1)S(1)}, s16[1040,256]{1,0:T(8,128)(2,1)S(1)}, u32[]{:S(2)}, u32[]{:S(2)}) collective-permute-start(s16[1040,256]{1,0:T(8,128)(2,1)S(1)} %hop.3), channel_id=1, source_target_pairs={{0,1},{1,2},{4,5},{5,6},{8,9},{9,10},{12,13},{13,14},{16,17},{17,1... | collective-permute-start | bytes 1597448 | tf_op jit(solution)/shard_map/ppermute | solution.py:441
  85.5 0.9 collective-permute-start.14
  86.4 10.1 %slot_terms.1 = (f32[2048,128]{1,0:T(8,128)S(1)}, f32[2048,128]{1,0:T(8,128)}, f32[2048,128]{1,0:T(8,128)}, f32[2048,128]{1,0:T(8,128)}, s16[2064,128]{1,0:T(8,1...) custom-call(s32[8,16]{1,0:T(8,128)S(1)} %convert_add_fusion.codes_ref, ...), custom_call_target="tpu_custom_call" | custom-call | flops 1073741824 | bytes 18874368 | tf_op jit(solution)/shard_map/slot_terms/pallas_call | solution.py:302
  96.5 0.5 collective-permute-start.21
  97.9 3.8 %collective-permute-start.13 = (s16[1040,256]{1,0:T(8,128)(2,1)S(1)}, s16[1040,256]{1,0:T(8,128)(2,1)S(1)}, u32[]{:S(2)}, u32[]{:S(2)}) collective-permute-start(s16[1040,256]{1,0:T(8,128)(2,1)S(1)} %hop.4), channel_id=1, source_target_pairs={{0,1},{1,2},{2,3},{4,5},{5,6},{6,7},{8,9},{9,10},{10,11},{12,13},{... | collective-permute-start | bytes 1597448 | tf_op jit(solution)/shard_map/ppermute | solution.py:441
  102.0 1.4 %collective-permute-start.15 = (s16[1040,256]{1,0:T(8,128)(2,1)S(1)}, s16[1040,256]{1,0:T(8,128)(2,1)S(1)}, u32[]{:S(2)}, u32[]{:S(2)}) collective-permute-start(s16[1040,256]{1,0:T(8,128)(2,1)S(1)} %hop.5), channel_id=1, source_target_pairs={{3,2},{2,1},{1,0},{7,6},{6,5},{5,4},{11,10},{10,9},{9,8},{15,14},{... | collective-permute-start | bytes 1597448 | tf_op jit(solution)/shard_map/ppermute | solution.py:444
  103.5 1.2 combine.5
  104.7 2.2 %collective-permute-start.20 = (s16[2064,128]{1,0:T(8,128)(2,1)}, s16[2064,128]{1,0:T(8,128)(2,1)S(1)}, u32[]{:S(2)}, u32[]{:S(2)}) collective-permute-start(s16[2064,128]{1,0:T(8,128)(2,1)} %combine.5), channel_id=1, source_target_pairs={{0,24},{4,28},{8,16},{12,20},{16,8},{20,12},{24,0},{28,4},{1,25},{... | collective-permute-start | bytes 1585160 | tf_op jit(solution)/shard_map/ppermute | solution.py:438
  107.2 0.6 collective-permute-start.22
  108.2 0.9 collective-permute-start.24
  109.0 9.9 %grad_inputs.1 = bf16[1024,2048]{1,0:T(8,128)(2,1)} custom-call(s32[1]{0:T(128)} %bitcast.place_ref, bf16[2048,1024]{1,0:T(8,128)(2,1)} %get-tuple-element.53.weight_ref, bf16[1024,256]{1,0:T(8,128)(2,1)S(1)} %copy-done.4, bf16[1040,256]{1,0:T(8,128)(2,1)S(1)} %collective-permute-done.refs_0_.r1, bf16[1040,256]{1,0:T(8,128)(2,1)S(1)} %collective-permute-done.5.refs_1_.r2, ...), custom_call_target="tpu_custom_call" | custom-call | flops 4294967296 | bytes 12582912 | tf_op jit(solution)/shard_map/grad_inputs/pallas_call | solution.py:409
  119.1 1.7 %collective-permute-done.20.refs_1_ = s16[2064,128]{1,0:T(8,128)(2,1)S(1)} collective-permute-done((s16[2064,128]{1,0:T(8,128)(2,1)}, s16[2064,128]{1,0:T(8,128)(2,1)S(1)}, u32[]{:S(2)}, u32[]{:S(2)}) %collective-permute-start.20) | collective-permute-done | bytes 528416 | tf_op jit(solution)/shard_map/ppermute | solution.py:438
  120.8 9.1 %collective-permute-done.22.refs_2_ = s16[2064,128]{1,0:T(8,128)(2,1)S(1)} collective-permute-done((s16[2064,128]{1,0:T(8,128)(2,1)S(1)}, s16[2064,128]{1,0:T(8,128)(2,1)S(1)}, u32[]{:S(2)}, u32[]{:S(2)}) %collective-permute-start.22) | collective-permute-done | bytes 528416 | tf_op jit(solution)/shard_map/ppermute | solution.py:438
  129.9 1.9 %normalized_update.1 = bf16[16,128,128]{2,1,0:T(8,128)(2,1)} custom-call(f32[2048,128]{1,0:T(8,128)S(1)} %combine.4.refs_0_, s16[2064,128]{1,0:T(8,128)(2,1)S(1)} %collective-permute-done.20.refs_1_, s16[2064,128]{1,0:T(8,128)(2,1)S(1)} %collective-permute-done.22.refs_2_, s16[2064,128]{1,0:T(8,128)(2,1)S(1)} %collective-permute-done.24.refs_3_), custom_call_target="tpu_custom_call" | custom-call | flops 4194304 | bytes 3145728 | tf_op jit(solution)/shard_map/normalized_update/pallas_call | solution.py:370
  131.9 1.1 last_hop.1
  (70 shorter events, 3.6 us)
Async XLA Ops:
  0.6 13.1 %copy-start.3 = (bf16[1024,256]{1,0:T(8,128)(2,1)S(1)}, bf16[1024,256]{1,0:T(8,128)(2,1)}, u32[]{:S(2)}) copy-start(bf16[1024,256]{1,0:T(8,128)(2,1)} %own.1) | copy-start | bytes 1572868
  2.6 23.7 %collective-permute-start = (bf16[1040,256]{1,0:T(8,128)(2,1)}, bf16[1040,256]{1,0:T(8,128)(2,1)S(1)}, u32[]{:S(2)}, u32[]{:S(2)}) collective-permute-start(bf16[1040,256]{1,0:T(8,128)(2,1)} %pad.8), channel_id=1, source_target_pairs={{0,1},{1,2},{2,3},{4,5},{5,6},{6,7},{8,9},{9,10},{10,11},{12,13},{... | collective-permute-start | bytes 1597448 | tf_op jit(solution)/shard_map/ppermute | solution.py:441
  7.5 18.8 %collective-permute-start.1 = (bf16[1040,256]{1,0:T(8,128)(2,1)}, bf16[1040,256]{1,0:T(8,128)(2,1)S(1)}, u32[]{:S(2)}, u32[]{:S(2)}) collective-permute-start(bf16[1040,256]{1,0:T(8,128)(2,1)} %pad.8), channel_id=1, source_target_pairs={{3,2},{2,1},{1,0},{7,6},{6,5},{5,4},{11,10},{10,9},{9,8},{15,14},{... | collective-permute-start | bytes 1597448 | tf_op jit(solution)/shard_map/ppermute | solution.py:444
  10.6 7.9 %collective-permute-start.2 = (bf16[2064,128]{1,0:T(8,128)(2,1)S(1)}, bf16[2064,128]{1,0:T(8,128)(2,1)}, u32[]{:S(2)}, u32[]{:S(2)}) collective-permute-start(bf16[2064,128]{1,0:T(8,128)(2,1)S(1)} %fusion.1.refs_0_), channel_id=1, source_target_pairs={{0,4},{4,0},{8,12},{12,8},{16,20},{20,16},{24,28},{28,24},{1,5},{5... | collective-permute-start | bytes 1585160 | tf_op jit(solution)/shard_map/ppermute | solution.py:438
  10.7 14.4 %collective-permute-start.3 = (bf16[2064,128]{1,0:T(8,128)(2,1)S(1)}, bf16[2064,128]{1,0:T(8,128)(2,1)S(1)}, u32[]{:S(2)}, u32[]{:S(2)}) collective-permute-start(bf16[2064,128]{1,0:T(8,128)(2,1)S(1)} %fusion.1.refs_0_), channel_id=1, source_target_pairs={{0,8},{4,12},{8,0},{12,4},{16,24},{20,28},{24,16},{28,20},{1,9},{5... | collective-permute-start | bytes 1585160 | tf_op jit(solution)/shard_map/ppermute | solution.py:438
  12.2 14.1 %collective-permute-start.4 = (bf16[2064,128]{1,0:T(8,128)(2,1)S(1)}, bf16[2064,128]{1,0:T(8,128)(2,1)S(1)}, u32[]{:S(2)}, u32[]{:S(2)}) collective-permute-start(bf16[2064,128]{1,0:T(8,128)(2,1)S(1)} %fusion.1.refs_0_), channel_id=1, source_target_pairs={{0,16},{4,20},{8,24},{12,28},{16,0},{20,4},{24,8},{28,12},{1,17},{... | collective-permute-start | bytes 1585160 | tf_op jit(solution)/shard_map/ppermute | solution.py:438
  17.2 1.3 copy-start.1
  26.3 0.8 copy-start.8
  26.4 9.3 %collective-permute-start.7 = (bf16[2064,128]{1,0:T(8,128)(2,1)S(1)}, bf16[2064,128]{1,0:T(8,128)(2,1)S(1)}, u32[]{:S(2)}, u32[]{:S(2)}) collective-permute-start(bf16[2064,128]{1,0:T(8,128)(2,1)S(1)} %broadcast_select_fusion), channel_id=1, source_target_pairs={{0,8},{4,20},{8,0},{12,28},{16,24},{20,4},{24,16},{28,12},{1,9},{5... | collective-permute-start | bytes 1585160 | tf_op jit(solution)/shard_map/ppermute | solution.py:463
  27.0 8.7 %collective-permute-start.8 = (bf16[2064,128]{1,0:T(8,128)(2,1)S(1)}, bf16[2064,128]{1,0:T(8,128)(2,1)S(1)}, u32[]{:S(2)}, u32[]{:S(2)}) collective-permute-start(bf16[2064,128]{1,0:T(8,128)(2,1)S(1)} %collective-permute-done.3.refs_2_), channel_id=1, source_target_pairs={{0,4},{4,0},{8,12},{12,8},{16,20},{20,16},{24,28},{28,24},{1,5},{5... | collective-permute-start | bytes 1585160 | tf_op jit(solution)/shard_map/ppermute | solution.py:438
  27.1 8.6 %collective-permute-start.9 = (bf16[2064,128]{1,0:T(8,128)(2,1)S(1)}, bf16[2064,128]{1,0:T(8,128)(2,1)S(1)}, u32[]{:S(2)}, u32[]{:S(2)}) collective-permute-start(bf16[2064,128]{1,0:T(8,128)(2,1)S(1)} %collective-permute-done.4.refs_4_), channel_id=1, source_target_pairs={{0,4},{4,0},{8,12},{12,8},{16,20},{20,16},{24,28},{28,24},{1,5},{5... | collective-permute-start | bytes 1585160 | tf_op jit(solution)/shard_map/ppermute | solution.py:438
  27.5 8.2 %collective-permute-start.5 = (bf16[1040,256]{1,0:T(8,128)(2,1)S(1)}, bf16[1040,256]{1,0:T(8,128)(2,1)S(1)}, u32[]{:S(2)}, u32[]{:S(2)}) collective-permute-start(bf16[1040,256]{1,0:T(8,128)(2,1)S(1)} %collective-permute-done.refs_0_.r1), channel_id=1, source_target_pairs={{1,2},{2,3},{5,6},{6,7},{9,10},{10,11},{13,14},{14,15},{17,18},{18... | collective-permute-start | bytes 1597448 | tf_op jit(solution)/shard_map/ppermute | solution.py:441
  28.2 19.6 %collective-permute-start.6 = (bf16[1040,256]{1,0:T(8,128)(2,1)}, bf16[1040,256]{1,0:T(8,128)(2,1)S(1)}, u32[]{:S(2)}, u32[]{:S(2)}) collective-permute-start(bf16[1040,256]{1,0:T(8,128)(2,1)} %copy-done.8), channel_id=1, source_target_pairs={{2,1},{1,0},{6,5},{5,4},{10,9},{9,8},{14,13},{13,12},{18,17},{17,1... | collective-permute-start | bytes 1597448 | tf_op jit(solution)/shard_map/ppermute | solution.py:444
  29.5 1.0 copy-start.9
  34.0 1.4 %copy-start.2 = (f32[256,2048]{1,0:T(8,128)}, f32[256,2048]{1,0:T(8,128)S(1)}, u32[]{:S(2)}) copy-start(f32[256,2048]{1,0:T(8,128)S(1)} %chunk_gradient.4.g2) | copy-start | bytes 6291460
  35.7 12.2 %collective-permute-start.10 = (bf16[2064,128]{1,0:T(8,128)(2,1)S(1)}, bf16[2064,128]{1,0:T(8,128)(2,1)S(1)}, u32[]{:S(2)}, u32[]{:S(2)}) collective-permute-start(bf16[2064,128]{1,0:T(8,128)(2,1)S(1)} %collective-permute-done.7.refs_6_), channel_id=1, source_target_pairs={{0,4},{4,0},{8,12},{12,8},{16,20},{20,16},{24,28},{28,24},{1,5},{5... | collective-permute-start | bytes 1585160 | tf_op jit(solution)/shard_map/ppermute | solution.py:438
  48.5 0.8 copy-start.13
  49.4 0.8 copy-start.15
  50.2 0.8 copy-start.11
  51.0 0.8 copy-start.17
  51.9 1.0 copy-start.12
  52.9 1.0 copy-start.14
  54.0 1.0 copy-start.16
  55.0 1.0 copy-start.18
  63.0 17.5 %collective-permute-start.11 = (s16[1040,256]{1,0:T(8,128)(2,1)S(1)}, s16[1040,256]{1,0:T(8,128)(2,1)S(1)}, u32[]{:S(2)}, u32[]{:S(2)}) collective-permute-start(s16[1040,256]{1,0:T(8,128)(2,1)S(1)} %get-tuple-element.54), channel_id=1, source_target_pairs={{0,1},{3,2},{4,5},{7,6},{8,9},{11,10},{12,13},{15,14},{16,17},{19,... | collective-permute-start | bytes 1597448 | tf_op jit(solution)/shard_map/ppermute | solution.py:482
  66.6 19.7 %collective-permute-start.16 = (bf16[1040,256]{1,0:T(8,128)(2,1)S(1)}, bf16[1040,256]{1,0:T(8,128)(2,1)S(1)}, u32[]{:S(2)}, u32[]{:S(2)}) collective-permute-start(bf16[1040,256]{1,0:T(8,128)(2,1)S(1)} %collective-permute-done.5.refs_1_.r2), channel_id=1, source_target_pairs={{2,3},{6,7},{10,11},{14,15},{18,19},{22,23},{26,27},{30,31}} | collective-permute-start | bytes 1597448 | tf_op jit(solution)/shard_map/ppermute | solution.py:441
  67.3 19.0 %collective-permute-start.17 = (bf16[1040,256]{1,0:T(8,128)(2,1)S(1)}, bf16[1040,256]{1,0:T(8,128)(2,1)S(1)}, u32[]{:S(2)}, u32[]{:S(2)}) collective-permute-start(bf16[1040,256]{1,0:T(8,128)(2,1)S(1)} %collective-permute-done.6.refs_2_.l2), channel_id=1, source_target_pairs={{1,0},{5,4},{9,8},{13,12},{17,16},{21,20},{25,24},{29,28}} | collective-permute-start | bytes 1597448 | tf_op jit(solution)/shard_map/ppermute | solution.py:444
  72.1 8.4 %copy-start = (f32[256,2048]{1,0:T(8,128)}, f32[256,2048]{1,0:T(8,128)S(1)}, u32[]{:S(2)}) copy-start(f32[256,2048]{1,0:T(8,128)S(1)} %chunk_gradient.5.g3) | copy-start | bytes 6291460
  80.8 16.3 %collective-permute-start.12 = (s16[1040,256]{1,0:T(8,128)(2,1)S(1)}, s16[1040,256]{1,0:T(8,128)(2,1)S(1)}, u32[]{:S(2)}, u32[]{:S(2)}) collective-permute-start(s16[1040,256]{1,0:T(8,128)(2,1)S(1)} %hop.3), channel_id=1, source_target_pairs={{0,1},{1,2},{4,5},{5,6},{8,9},{9,10},{12,13},{13,14},{16,17},{17,1... | collective-permute-start | bytes 1597448 | tf_op jit(solution)/shard_map/ppermute | solution.py:441
  85.5 12.4 %collective-permute-start.14 = (s16[1040,256]{1,0:T(8,128)(2,1)S(1)}, s16[1040,256]{1,0:T(8,128)(2,1)S(1)}, u32[]{:S(2)}, u32[]{:S(2)}) collective-permute-start(s16[1040,256]{1,0:T(8,128)(2,1)S(1)} %hop.3), channel_id=1, source_target_pairs={{3,2},{2,1},{7,6},{6,5},{11,10},{10,9},{15,14},{14,13},{19,18},{18... | collective-permute-start | bytes 1597448 | tf_op jit(solution)/shard_map/ppermute | solution.py:444
  96.4 5.6 %collective-permute-start.19 = (s16[2064,128]{1,0:T(8,128)(2,1)}, s16[2064,128]{1,0:T(8,128)(2,1)S(1)}, u32[]{:S(2)}, u32[]{:S(2)}) collective-permute-start(s16[2064,128]{1,0:T(8,128)(2,1)} %get-tuple-element.64), channel_id=1, source_target_pairs={{0,4},{4,0},{8,12},{12,8},{16,20},{20,16},{24,28},{28,24},{1,5},{5... | collective-permute-start | bytes 1585160 | tf_op jit(solution)/shard_map/ppermute | solution.py:438
  96.5 8.1 %collective-permute-start.21 = (s16[2064,128]{1,0:T(8,128)(2,1)}, s16[2064,128]{1,0:T(8,128)(2,1)S(1)}, u32[]{:S(2)}, u32[]{:S(2)}) collective-permute-start(s16[2064,128]{1,0:T(8,128)(2,1)} %get-tuple-element.66), channel_id=1, source_target_pairs={{0,4},{4,0},{8,12},{12,8},{16,20},{20,16},{24,28},{28,24},{1,5},{5... | collective-permute-start | bytes 1585160 | tf_op jit(solution)/shard_map/ppermute | solution.py:438
  97.0 10.2 %collective-permute-start.23 = (s16[2064,128]{1,0:T(8,128)(2,1)}, s16[2064,128]{1,0:T(8,128)(2,1)S(1)}, u32[]{:S(2)}, u32[]{:S(2)}) collective-permute-start(s16[2064,128]{1,0:T(8,128)(2,1)} %get-tuple-element.68), channel_id=1, source_target_pairs={{0,4},{4,0},{8,12},{12,8},{16,20},{20,16},{24,28},{28,24},{1,5},{5... | collective-permute-start | bytes 1585160 | tf_op jit(solution)/shard_map/ppermute | solution.py:438
  97.1 11.1 %collective-permute-start.18 = (s16[2064,128]{1,0:T(8,128)(2,1)}, s16[2064,128]{1,0:T(8,128)(2,1)S(1)}, u32[]{:S(2)}, u32[]{:S(2)}) collective-permute-start(s16[2064,128]{1,0:T(8,128)(2,1)} %get-tuple-element.62), channel_id=1, source_target_pairs={{0,4},{4,0},{8,12},{12,8},{16,20},{20,16},{24,28},{28,24},{1,5},{5... | collective-permute-start | bytes 1585160 | tf_op jit(solution)/shard_map/ppermute | solution.py:438
  97.9 5.6 %copy-start.7 = (f32[2048,128]{1,0:T(8,128)S(1)}, f32[2048,128]{1,0:T(8,128)}, u32[]{:S(2)}) copy-start(f32[2048,128]{1,0:T(8,128)} %get-tuple-element.63.kept_ref) | copy-start | bytes 3145732
  97.9 34.0 %collective-permute-start.13 = (s16[1040,256]{1,0:T(8,128)(2,1)S(1)}, s16[1040,256]{1,0:T(8,128)(2,1)S(1)}, u32[]{:S(2)}, u32[]{:S(2)}) collective-permute-start(s16[1040,256]{1,0:T(8,128)(2,1)S(1)} %hop.4), channel_id=1, source_target_pairs={{0,1},{1,2},{2,3},{4,5},{5,6},{6,7},{8,9},{9,10},{10,11},{12,13},{... | collective-permute-start | bytes 1597448 | tf_op jit(solution)/shard_map/ppermute | solution.py:441
  102.0 4.8 %copy-start.6 = (f32[2048,128]{1,0:T(8,128)S(1)}, f32[2048,128]{1,0:T(8,128)}, u32[]{:S(2)}) copy-start(f32[2048,128]{1,0:T(8,128)} %get-tuple-element.65.kept_ref) | copy-start | bytes 3145732
  102.0 29.8 %collective-permute-start.15 = (s16[1040,256]{1,0:T(8,128)(2,1)S(1)}, s16[1040,256]{1,0:T(8,128)(2,1)S(1)}, u32[]{:S(2)}, u32[]{:S(2)}) collective-permute-start(s16[1040,256]{1,0:T(8,128)(2,1)S(1)} %hop.5), channel_id=1, source_target_pairs={{3,2},{2,1},{1,0},{7,6},{6,5},{5,4},{11,10},{10,9},{9,8},{15,14},{... | collective-permute-start | bytes 1597448 | tf_op jit(solution)/shard_map/ppermute | solution.py:444
  103.5 4.3 %copy-start.5 = (f32[2048,128]{1,0:T(8,128)S(1)}, f32[2048,128]{1,0:T(8,128)}, u32[]{:S(2)}) copy-start(f32[2048,128]{1,0:T(8,128)} %get-tuple-element.67.kept_ref) | copy-start | bytes 3145732
  104.7 16.1 %collective-permute-start.20 = (s16[2064,128]{1,0:T(8,128)(2,1)}, s16[2064,128]{1,0:T(8,128)(2,1)S(1)}, u32[]{:S(2)}, u32[]{:S(2)}) collective-permute-start(s16[2064,128]{1,0:T(8,128)(2,1)} %combine.5), channel_id=1, source_target_pairs={{0,24},{4,28},{8,16},{12,20},{16,8},{20,12},{24,0},{28,4},{1,25},{... | collective-permute-start | bytes 1585160 | tf_op jit(solution)/shard_map/ppermute | solution.py:438
  106.8 2.2 %copy-start.4 = (bf16[1024,256]{1,0:T(8,128)(2,1)S(1)}, bf16[1024,256]{1,0:T(8,128)(2,1)}, u32[]{:S(2)}) copy-start(bf16[1024,256]{1,0:T(8,128)(2,1)} %own.1) | copy-start | bytes 1572868
  106.8 2.2 %copy-start.10 = (bf16[1040,256]{1,0:T(8,128)(2,1)S(1)}, bf16[1040,256]{1,0:T(8,128)(2,1)}, u32[]{:S(2)}) copy-start(bf16[1040,256]{1,0:T(8,128)(2,1)} %copy-done.8) | copy-start | bytes 1597444
  107.2 22.6 %collective-permute-start.22 = (s16[2064,128]{1,0:T(8,128)(2,1)S(1)}, s16[2064,128]{1,0:T(8,128)(2,1)S(1)}, u32[]{:S(2)}, u32[]{:S(2)}) collective-permute-start(s16[2064,128]{1,0:T(8,128)(2,1)S(1)} %combine.6), channel_id=1, source_target_pairs={{0,16},{4,20},{8,24},{12,28},{16,0},{20,4},{24,8},{28,12},{1,17},{... | collective-permute-start | bytes 1585160 | tf_op jit(solution)/shard_map/ppermute | solution.py:438
  108.2 21.7 %collective-permute-start.24 = (s16[2064,128]{1,0:T(8,128)(2,1)S(1)}, s16[2064,128]{1,0:T(8,128)(2,1)S(1)}, u32[]{:S(2)}, u32[]{:S(2)}) collective-permute-start(s16[2064,128]{1,0:T(8,128)(2,1)S(1)} %combine.7), channel_id=1, source_target_pairs={{0,8},{4,12},{8,0},{12,4},{16,24},{20,28},{24,16},{28,20},{1,9},{5... | collective-permute-start | bytes 1585160 | tf_op jit(solution)/shard_map/ppermute | solution.py:438

commit v3 on v2

--- a/solution.py
+++ b/solution.py
@@ -7,9 +7,10 @@
 from jax.experimental.pallas import tpu as pltpu
 from jax.sharding import PartitionSpec as P
 
-VMEM_BYTES = 48 * 1024 * 1024
+MIB = 1024 * 1024
 GROUP = 128
 PAD = 16
+EXTRA = 16
 
 
 def encode(block):
@@ -33,13 +34,13 @@
     return codes.astype(jnp.int32).astype(jnp.float32)
 
 
-def params():
-    return pltpu.CompilerParams(vmem_limit_bytes=VMEM_BYTES)
-
-
-def whole(shape):
-    zeros = (0,) * len(shape)
-    return pl.BlockSpec(shape, lambda *_: zeros, pipeline_mode=pl.Buffered(1))
+def params(mib):
+    return pltpu.CompilerParams(vmem_limit_bytes=mib * MIB)
+
+
+VMEM = pl.BlockSpec(memory_space=pltpu.VMEM)
+SMEM = pl.BlockSpec(memory_space=pltpu.SMEM)
+LITTLE = pl.CostEstimate(flops=1, bytes_accessed=1, transcendentals=0)
 
 
 def aligned(index, size):
@@ -67,135 +68,160 @@
     return block
 
 
-def first_kernel(column_blocks, codes_ref, place_ref, normed_ref, *refs):
-    message_refs = refs[:-2]
-    weight_ref, first_ref = refs[-2:]
+def pack_kernel(column_blocks, rows_ref, columns_ref, tiles_ref, chunk_ref, message_ref, padded_ref):
+    rows = tiles_ref.shape[0]
+    tokens = chunk_ref.shape[0]
+    message_ref[:rows, :] = tiles_ref[...]
+    lane = lax.broadcasted_iota(jnp.int32, (PAD, tiles_ref.shape[1]), 1)
+    positions = jnp.zeros(lane.shape, jnp.int32)
+    for slot in range(rows_ref.shape[1]):
+        row, column = rows_ref[0, slot], columns_ref[0, slot]
+        position = jnp.where(column >= 0, row * column_blocks + column + 1, 0)
+        positions = jnp.where(lane == slot, position, positions)
+    message_ref[rows:, :] = positions.astype(jnp.float32).astype(message_ref.dtype)
+    padded_ref[:tokens, :] = chunk_ref[...]
+    padded_ref[tokens:, :] = jnp.zeros((EXTRA, chunk_ref.shape[1]), padded_ref.dtype)
+
+
+def pack(rows, columns, tiles, chunk, column_blocks):
+    return pl.pallas_call(
+        functools.partial(pack_kernel, column_blocks),
+        in_specs=[SMEM, SMEM, VMEM, VMEM],
+        out_specs=[VMEM, VMEM],
+        out_shape=[
+            jax.ShapeDtypeStruct((tiles.shape[0] + PAD, tiles.shape[1]), tiles.dtype),
+            jax.ShapeDtypeStruct((chunk.shape[0] + EXTRA, chunk.shape[1]), chunk.dtype),
+        ],
+        compiler_params=params(8),
+        cost_estimate=LITTLE,
+        name="pack",
+    )(rows, columns, tiles, chunk)
+
+
+def first_kernel(column_blocks, place_ref, normed_ref, *refs):
+    message_refs = refs[:-6]
+    weight_ref, first_ref, codes_ref, partial, scalars, sem = refs[-6:]
     tokens = normed_ref.shape[0]
     chunk_width = first_ref.shape[1]
     chunks = weight_ref.shape[1] // chunk_width
     tile = message_refs[0].shape[1]
+    capacity = message_refs[0].shape[0] // tile
+    for k, message_ref in enumerate(message_refs):
+        positions = message_ref[capacity * tile : capacity * tile + PAD, :]
+        codes_ref[k : k + 1, :] = positions.astype(jnp.float32)[:1, :].astype(jnp.int32) - 1
+    copy = pltpu.make_async_copy(codes_ref, scalars, sem)
+    copy.start()
     weight_ref[...] = jnp.zeros_like(weight_ref)
-    for k in range(len(message_refs)):
-        for slot in range(codes_ref.shape[1]):
-            code = codes_ref[k, slot]
+    copy.wait()
+    for k, message_ref in enumerate(message_refs):
+        for slot in range(capacity):
+            code = scalars[k, slot]
 
             @pl.when(code >= 0)
             def _():
                 row = aligned(code // column_blocks, tile)
                 column = aligned(code % column_blocks, tile)
-                weight_ref[row, column] = message_refs[k][slot * tile : (slot + 1) * tile, :]
+                weight_ref[row, column] = message_ref[slot * tile : (slot + 1) * tile, :]
 
     far = weight_ref[:, aligned(chunks - 1 - place_ref[0], chunk_width)]
-    partial = jnp.dot(normed_ref[...], far, preferred_element_type=jnp.float32)
+    partial[...] = jnp.dot(normed_ref[...], far, preferred_element_type=jnp.float32)
     write_message(
         first_ref, tokens, lambda group: partial[group * GROUP : (group + 1) * GROUP, :]
     )
 
 
-def first_values(codes, place, normed, messages, chunks, column_blocks):
+def first_values(place, normed, messages, chunks, column_blocks):
     tokens, features = normed.shape
     tile = messages[0].shape[1]
     width = column_blocks * tile
     return pl.pallas_call(
         functools.partial(first_kernel, column_blocks),
-        grid_spec=pltpu.PrefetchScalarGridSpec(
-            num_scalar_prefetch=2,
-            grid=(1,),
-            in_specs=[whole(normed.shape)] + [whole(m.shape) for m in messages],
-            out_specs=[whole((features, width)), whole((tokens + PAD, width // chunks))],
-        ),
+        in_specs=[SMEM, VMEM] + [VMEM] * len(messages),
+        out_specs=[VMEM, VMEM, VMEM],
         out_shape=[
             jax.ShapeDtypeStruct((features, width), jnp.bfloat16),
             jax.ShapeDtypeStruct((tokens + PAD, width // chunks), jnp.int16),
+            jax.ShapeDtypeStruct((len(messages), tile), jnp.int32),
         ],
-        compiler_params=params(),
-        cost_estimate=pl.CostEstimate(flops=1, bytes_accessed=1, transcendentals=0),
+        scratch_shapes=[
+            pltpu.VMEM((tokens, width // chunks), jnp.float32),
+            pltpu.SMEM((len(messages), tile), jnp.int32),
+            pltpu.SemaphoreType.DMA,
+        ],
+        compiler_params=params(22),
+        cost_estimate=LITTLE,
         name="first_values",
-    )(codes, place, normed, *messages)
+    )(place, normed, *messages)
 
 
 def partial_kernel(normed_ref, weight_ref, partial_ref):
-    partial_ref[0] = jnp.dot(
-        normed_ref[...], weight_ref[...], preferred_element_type=jnp.float32
-    )
-
-
-def partial_values(normed, weight, chunks):
-    tokens, features = normed.shape
-    width = weight.shape[1] // chunks
+    step = 512
+    for n in range(partial_ref.shape[1] // step):
+        span = slice(n * step, (n + 1) * step)
+        partial_ref[:, span] = jnp.dot(
+            normed_ref[...], weight_ref[:, span], preferred_element_type=jnp.float32
+        )
+
+
+def partial_values(normed, weight):
     return pl.pallas_call(
         partial_kernel,
-        grid=(chunks,),
-        in_specs=[whole(normed.shape), pl.BlockSpec((features, width), lambda h: (0, h))],
-        out_specs=pl.BlockSpec((1, tokens, width), lambda h: (h, 0, 0)),
-        out_shape=jax.ShapeDtypeStruct((chunks, tokens, width), jnp.float32),
-        compiler_params=params(),
-        cost_estimate=pl.CostEstimate(flops=1, bytes_accessed=1, transcendentals=0),
+        in_specs=[VMEM, VMEM],
+        out_specs=VMEM,
+        out_shape=jax.ShapeDtypeStruct((normed.shape[0], weight.shape[1]), jnp.float32),
+        compiler_params=params(20),
+        cost_estimate=LITTLE,
         name="partial_values",
     )(normed, weight)
 
 
-def hop_kernel(place_ref, partial_ref, arrived_ref, message_ref):
-    rows = partial_ref.shape[1]
+def chunk_of(place_ref, ahead, partial_ref, width):
+    return aligned(lax.rem(place_ref[0] + ahead, partial_ref.shape[1] // width), width)
+
+
+def hop_kernel(ahead, place_ref, partial_ref, arrived_ref, message_ref):
+    rows, width = partial_ref.shape[0], message_ref.shape[1]
     arrived = read_message(arrived_ref, rows)
+    columns = chunk_of(place_ref, ahead, partial_ref, width)
 
     def total(group):
-        return partial_ref[0, group * GROUP : (group + 1) * GROUP, :] + arrived(group)
+        return partial_ref[group * GROUP : (group + 1) * GROUP, columns] + arrived(group)
 
     write_message(message_ref, rows, total)
 
 
 def hop(place, ahead, partial, arrived):
-    chunks, tokens, width = partial.shape
-    return pl.pallas_call(
-        hop_kernel,
-        grid_spec=pltpu.PrefetchScalarGridSpec(
-            num_scalar_prefetch=1,
-            grid=(1,),
-            in_specs=[
-                pl.BlockSpec((1, tokens, width), lambda i, p: ((p[0] + ahead) % chunks, 0, 0)),
-                whole(arrived.shape),
-            ],
-            out_specs=whole(arrived.shape),
-        ),
+    return pl.pallas_call(
+        functools.partial(hop_kernel, ahead),
+        in_specs=[SMEM, VMEM, VMEM],
+        out_specs=VMEM,
         out_shape=jax.ShapeDtypeStruct(arrived.shape, jnp.int16),
-        compiler_params=params(),
-        cost_estimate=pl.CostEstimate(
-            flops=8 * tokens * width, bytes_accessed=8 * tokens * width, transcendentals=0
-        ),
+        compiler_params=params(12),
+        cost_estimate=LITTLE,
         name="hop",
     )(place, partial, arrived)
 
 
 def last_hop_kernel(place_ref, partial_ref, right_ref, left_ref, values_ref):
-    rows = partial_ref.shape[1]
+    rows, width = values_ref.shape
     right = read_message(right_ref, rows)
     left = read_message(left_ref, rows)
+    columns = chunk_of(place_ref, 0, partial_ref, width)
     for group in range(rows // GROUP):
         span = slice(group * GROUP, (group + 1) * GROUP)
-        total = partial_ref[0, span, :] + right(group) + left(group)
+        total = partial_ref[span, columns] + right(group) + left(group)
         values_ref[span, :] = total.astype(values_ref.dtype)
 
 
 def last_hop(place, partial, right, left):
-    _, tokens, width = partial.shape
+    rows, width = right.shape[0] - PAD, right.shape[1]
     return pl.pallas_call(
         last_hop_kernel,
-        grid_spec=pltpu.PrefetchScalarGridSpec(
-            num_scalar_prefetch=1,
-            grid=(1,),
-            in_specs=[
-                pl.BlockSpec((1, tokens, width), lambda i, p: (p[0], 0, 0)),
-                whole(right.shape),
-                whole(left.shape),
-            ],
-            out_specs=whole((tokens, width)),
-        ),
-        out_shape=jax.ShapeDtypeStruct((tokens, width), jnp.bfloat16),
-        compiler_params=params(),
-        cost_estimate=pl.CostEstimate(
-            flops=8 * tokens * width, bytes_accessed=10 * tokens * width, transcendentals=0
-        ),
+        in_specs=[SMEM, VMEM, VMEM, VMEM],
+        out_specs=VMEM,
+        out_shape=jax.ShapeDtypeStruct((rows, width), jnp.bfloat16),
+        compiler_params=params(12),
+        cost_estimate=LITTLE,
         name="last_hop",
     )(place, partial, right, left)
 
@@ -222,7 +248,7 @@
 
 
 def product(turned, normed_ref, out_ref):
-    step = 512
+    step = 1024
     for n in range(normed_ref.shape[1] // step):
         span = slice(n * step, (n + 1) * step)
         out_ref[:, span] = jnp.dot(turned, normed_ref[:, span], preferred_element_type=jnp.float32)
@@ -235,19 +261,13 @@
 
 
 def chunk_gradient(pick, place, normed, *chunks):
-    tokens, features = normed.shape
-    width = chunks[0].shape[1]
     return pl.pallas_call(
         functools.partial(chunk_kernel, pick),
-        grid_spec=pltpu.PrefetchScalarGridSpec(
-            num_scalar_prefetch=1,
-            grid=(1,),
-            in_specs=[whole(a.shape) for a in (normed, *chunks)],
-            out_specs=whole((width, features)),
-        ),
-        out_shape=jax.ShapeDtypeStruct((width, features), jnp.float32),
-        compiler_params=params(),
-        cost_estimate=pl.CostEstimate(flops=1, bytes_accessed=1, transcendentals=0),
+        in_specs=[SMEM, VMEM] + [VMEM] * len(chunks),
+        out_specs=VMEM,
+        out_shape=jax.ShapeDtypeStruct((chunks[0].shape[1], normed.shape[1]), jnp.float32),
+        compiler_params=params(16),
+        cost_estimate=LITTLE,
         name="chunk_gradient",
     )(place, normed, *chunks)
 
@@ -271,7 +291,7 @@
         copy.wait()
     order = chunk_order(place)
     tile = GROUP
-    capacity = codes_ref.shape[1]
+    capacity = keep_refs[0].shape[0] // tile
     chunk_blocks = gradient.shape[1] // tile
 
     def term(k, slot):
@@ -293,32 +313,25 @@
             keep_refs[chip][slot * tile : (slot + 1) * tile, :] = term(2 * chip, slot)
 
 
-def slot_terms(codes, place, normed, late, early, column_blocks):
-    tokens, features = normed.shape
+def slot_terms(codes, place, normed, late, early, capacity, column_blocks):
+    features = normed.shape[1]
     chips = codes.shape[0] // 2
-    rows = codes.shape[1] * GROUP
+    rows = capacity * GROUP
     width = early[0].shape[0]
     shapes = [((rows, GROUP), jnp.float32)] * chips + [((rows + PAD, GROUP), jnp.int16)] * chips
     outputs = pl.pallas_call(
         functools.partial(slots_kernel, chips, column_blocks),
-        grid_spec=pltpu.PrefetchScalarGridSpec(
-            num_scalar_prefetch=2,
-            grid=(1,),
-            in_specs=[whole(a.shape) for a in (normed, *late)]
-            + [pl.BlockSpec(memory_space=pl.ANY)] * len(early),
-            out_specs=[whole(shape) for shape, _ in shapes],
-            scratch_shapes=[
-                pltpu.VMEM((len(early) + 1, width, features), jnp.float32),
-                pltpu.SemaphoreType.DMA((len(early),)),
-            ],
-        ),
+        in_specs=[SMEM, SMEM, VMEM]
+        + [VMEM] * len(late)
+        + [pl.BlockSpec(memory_space=pl.ANY)] * len(early),
+        out_specs=[VMEM] * len(shapes),
+        scratch_shapes=[
+            pltpu.VMEM((len(early) + 1, width, features), jnp.float32),
+            pltpu.SemaphoreType.DMA((len(early),)),
+        ],
         out_shape=[jax.ShapeDtypeStruct(shape, kind) for shape, kind in shapes],
-        compiler_params=params(),
-        cost_estimate=pl.CostEstimate(
-            flops=2 * tokens * features * width,
-            bytes_accessed=18 * 1024 * 1024,
-            transcendentals=0,
-        ),
+        compiler_params=params(30),
+        cost_estimate=LITTLE,
         name="slot_terms",
     )(codes, place, normed, *late, *early)
     return outputs[:chips], outputs[chips:]
@@ -342,14 +355,11 @@
     shape = arrived.shape if kind == jnp.int16 else kept.shape
     return pl.pallas_call(
         combine_kernel,
-        grid=(1,),
-        in_specs=[whole(kept.shape), whole(arrived.shape)],
-        out_specs=whole(shape),
+        in_specs=[VMEM, VMEM],
+        out_specs=VMEM,
         out_shape=jax.ShapeDtypeStruct(shape, kind),
-        compiler_params=params(),
-        cost_estimate=pl.CostEstimate(
-            flops=8 * kept.size, bytes_accessed=8 * kept.size, transcendentals=0
-        ),
+        compiler_params=params(8),
+        cost_estimate=LITTLE,
         name="combine",
     )(kept, arrived)
 
@@ -369,14 +379,11 @@
 def normalized_update(kept, arrived, shape):
     return pl.pallas_call(
         functools.partial(update_kernel, len(arrived)),
-        grid=(1,),
-        in_specs=[whole(kept.shape)] + [whole(a.shape) for a in arrived],
-        out_specs=whole(shape),
+        in_specs=[VMEM] * (1 + len(arrived)),
+        out_specs=VMEM,
         out_shape=jax.ShapeDtypeStruct(shape, jnp.bfloat16),
-        compiler_params=params(),
-        cost_estimate=pl.CostEstimate(
-            flops=16 * kept.size, bytes_accessed=12 * kept.size, transcendentals=0
-        ),
+        compiler_params=params(12),
+        cost_estimate=LITTLE,
         name="normalized_update",
     )(kept, *arrived)
 
@@ -405,22 +412,22 @@
 def grad_inputs(place, weight, *chunks):
     features, width = weight.shape
     tokens = chunks[0].shape[0]
-    block = 256
+    block = 512
     return pl.pallas_call(
         grad_input_kernel,
         grid_spec=pltpu.PrefetchScalarGridSpec(
             num_scalar_prefetch=1,
             grid=(features // block,),
             in_specs=[pl.BlockSpec((block, width), lambda i, p: (i, 0))]
-            + [whole(chunk.shape) for chunk in chunks],
+            + [VMEM] * len(chunks),
             out_specs=pl.BlockSpec((tokens, block), lambda i, p: (0, i)),
             scratch_shapes=[pltpu.VMEM((tokens, width), jnp.bfloat16)],
         ),
         out_shape=jax.ShapeDtypeStruct((tokens, features), jnp.bfloat16),
-        compiler_params=params(),
+        compiler_params=params(20),
         cost_estimate=pl.CostEstimate(
             flops=2 * tokens * features * width,
-            bytes_accessed=12 * 1024 * 1024,
+            bytes_accessed=12 * MIB,
             transcendentals=0,
         ),
         name="grad_inputs",
@@ -443,13 +450,10 @@
     def left(x, *sources):
         return lax.ppermute(x, "tensor", [(i, i - 1) for i in sources])
 
-    padded = jnp.pad(cotangent, ((0, PAD), (0, 0)))
+    message, padded = pack(
+        tile_rows, tile_columns, tile_values.reshape(rows, tile), cotangent, column_blocks
+    )
     r1, l1 = right(padded, 0, 1, 2), left(padded, 3, 2, 1)
-    positions = jnp.where(tile_columns >= 0, tile_rows * column_blocks + tile_columns + 1, 0)
-    positions = jnp.pad(
-        positions.astype(jnp.bfloat16), ((0, PAD - 1), (0, tile - capacity))
-    )
-    message = jnp.concatenate([tile_values.reshape(rows, tile), positions], axis=0)
     g1 = chunk_gradient(lambda place, own: own, place, normed, cotangent)
     direct = [1, 2] if chips == 4 else list(range(1, chips))
     same_core = [message] + [swap(message, 2 * chip) for chip in direct]
@@ -475,17 +479,16 @@
     for pair in zip(same_core, [beside] + across):
         gathered += pair
     r2, l2, *gathered = lax.optimization_barrier((r2, l2, *gathered))
-    codes = jnp.stack([m[rows, :capacity] for m in gathered]).astype(jnp.int32) - 1
 
     r3, l3 = right(r2, 2), left(l2, 1)
-    weight, first = first_values(codes, place, normed, gathered, parts, column_blocks)
+    weight, first, codes = first_values(place, normed, gathered, parts, column_blocks)
     arrived = lax.ppermute(first, "tensor", [(0, 1), (3, 2)])
-    partial = partial_values(normed, weight, parts)
+    partial = partial_values(normed, weight)
     g3 = chunk_gradient(third_chunk, place, normed, r1, r2, l2)
     arrived, g3 = lax.optimization_barrier((arrived, g3))
 
     keep, send = slot_terms(
-        codes, place, normed, (r2, l2, r3, l3), (g1, g2, g3), column_blocks
+        codes, place, normed, (r2, l2, r3, l3), (g1, g2, g3), capacity, column_blocks
     )
     second = hop(place, 2, partial, arrived)
     from_left, from_right = right(second, 0, 1), left(second, 3, 2)

time: 134 us -> 121 us (0.903)
  Pallas kernels: 51.7 us -> 34.2 us
  waiting for transfers between devices: 31.1 us -> 40.1 us
  local copies, waits for them, and re-layouts: 14 us -> 8.81 us
  starting transfers between devices: 33.4 us -> 35.2 us
    pallas_call x15 -> x16, Pallas kernels: 41.8 us -> 26.6 us  [the longest x1 5.27 us: first_values(): pl.pallas_call(functools.partial(first_kernel, column_blocks), in_specs=[...]
    ppermute x5, waiting for transfers between devices: 0.01 us -> 2.97 us  [right(): return lax.ppermute(x, 'tensor', [(i, i + 1) for i in sources])]
    unnamed x38 -> x18, local copies, waits for them, and re-layouts: 11.3 us -> 8.81 us
    ppermute x1, waiting for transfers between devices: 0.01 us -> 2.49 us  [local(): arrived = lax.ppermute(first, 'tensor', [(0, 1), (3, 2)])]
    ppermute x13, waiting for transfers between devices: 18.6 us -> 21.1 us  [swap(): return lax.ppermute(x, 'fsdp', [(i, i ^ mask) for i in range(devices)])]
    pallas_call x1, Pallas kernels: 9.87 us -> 7.66 us  [grad_inputs(): pl.pallas_call(grad_input_kernel, grid_spec=pltpu.PrefetchScalarGridSpec(...]
    ppermute x5, starting transfers between devices: 14.7 us -> 16.7 us  [right(): return lax.ppermute(x, 'tensor', [(i, i + 1) for i in sources])]
    pad x1 -> x0, local copies, waits for them, and re-layouts: 1.95 us -> none  [local(): padded = jnp.pad(cotangent, ((0, PAD), (0, 0)))]
  transfers between devices with their start and end apart: 25 -> 25, of which waited for: 7 -> 9; matrix products, arithmetic and copies ran while one was open for 1% -> 0% of each run, Pallas kernels for 33% -> 22%
where the time goes in v3:
time: 121 us; the launch traced here: 120 us
  waiting for transfers between devices  40.1 us (33%)
  starting transfers between devices  35.2 us (29%)
  Pallas kernels  34.2 us (28%)
  local copies, waits for them, and re-layouts  8.81 us (7%)
    ppermute x13, waiting for transfers between devices, swap(): return lax.ppermute(x, 'fsdp', [(i, i ^ mask) for i in range(devices)])  21.1 us
    ppermute x5, starting transfers between devices, right(): return lax.ppermute(x, 'tensor', [(i, i + 1) for i in sources])  16.7 us
    ppermute x5, waiting for transfers between devices, left(): return lax.ppermute(x, 'tensor', [(i, i - 1) for i in sources])  12 us
    unnamed x18, local copies, waits for them, and re-layouts  8.81 us
    ppermute x13, starting transfers between devices, swap(): return lax.ppermute(x, 'fsdp', [(i, i ^ mask) for i in range(devices)])  7.99 us
    pallas_call x1, Pallas kernels, grad_inputs(): pl.pallas_call(grad_input_kernel, grid_spec=pltpu.PrefetchScalarGridSpec(...  7.66 us
    ppermute x5, starting transfers between devices, left(): return lax.ppermute(x, 'tensor', [(i, i - 1) for i in sources])  6.18 us
    pallas_call x1, Pallas kernels, first_values(): pl.pallas_call(functools.partial(first_kernel, column_blocks), in_specs=[...  5.27 us
  transfers between devices with their start and end apart: 25, of which 9 were waited for; matrix products, arithmetic and copies ran while one was open for 0% of the time, Pallas kernels for 22%

profile of v3, /device:TPU:0, one launch (start us, length us, event | category | flops | bytes accessed | tf_op | source)
XLA Modules:
  0.0 120.3 jit_solution(14267666221230171758)
XLA Ops:
  0.6 1.0 copy-done.3
  1.7 1.0 copy-done.6
  2.7 0.7 copy-done.7
  3.4 0.7 copy-done.8
  4.0 1.6 %pack.1 = (bf16[2064,128]{1,0:T(8,128)(2,1)}, bf16[1040,256]{1,0:T(8,128)(2,1)}) custom-call(s32[1,16]{1,0:T(1,128)S(1)} %copy-done.7, s32[1,16]{1,0:T(1,128)S(1)} %copy-done.8, bf16[2048,128]{1,0:T(8,128)(2,1)S(1)} %bitcast.3, bf16[1024,256]{1,0:T(8,128)(2,1)S(1)} %copy-done.3), custom_call_target="tpu_custom_call" | custom-call | flops 1 | bytes 1 | tf_op jit(solution)/shard_map/pack/pallas_call | solution.py:87
  5.6 4.9 %collective-permute-start = (bf16[1040,256]{1,0:T(8,128)(2,1)}, bf16[1040,256]{1,0:T(8,128)(2,1)S(1)}, u32[]{:S(2)}, u32[]{:S(2)}) collective-permute-start(bf16[1040,256]{1,0:T(8,128)(2,1)} %get-tuple-element.39), channel_id=1, source_target_pairs={{0,1},{1,2},{2,3},{4,5},{5,6},{6,7},{8,9},{9,10},{10,11},{12,13},{... | collective-permute-start | bytes 1597448 | tf_op jit(solution)/shard_map/ppermute | solution.py:448
  10.6 1.3 %collective-permute-start.1 = (bf16[1040,256]{1,0:T(8,128)(2,1)}, bf16[1040,256]{1,0:T(8,128)(2,1)}, u32[]{:S(2)}, u32[]{:S(2)}) collective-permute-start(bf16[1040,256]{1,0:T(8,128)(2,1)} %get-tuple-element.39), channel_id=1, source_target_pairs={{3,2},{2,1},{1,0},{7,6},{6,5},{5,4},{11,10},{10,9},{9,8},{15,14},{... | collective-permute-start | bytes 1597448 | tf_op jit(solution)/shard_map/ppermute | solution.py:451
  11.9 1.6 %collective-permute-start.3 = (bf16[2064,128]{1,0:T(8,128)(2,1)}, bf16[2064,128]{1,0:T(8,128)(2,1)S(1)}, u32[]{:S(2)}, u32[]{:S(2)}) collective-permute-start(bf16[2064,128]{1,0:T(8,128)(2,1)} %get-tuple-element.50.refs_0_), channel_id=1, source_target_pairs={{0,8},{4,12},{8,0},{12,4},{16,24},{20,28},{24,16},{28,20},{1,9},{5... | collective-permute-start | bytes 1585160 | tf_op jit(solution)/shard_map/ppermute | solution.py:445
  13.5 1.5 %collective-permute-start.4 = (bf16[2064,128]{1,0:T(8,128)(2,1)}, bf16[2064,128]{1,0:T(8,128)(2,1)}, u32[]{:S(2)}, u32[]{:S(2)}) collective-permute-start(bf16[2064,128]{1,0:T(8,128)(2,1)} %get-tuple-element.50.refs_0_), channel_id=1, source_target_pairs={{0,16},{4,20},{8,24},{12,28},{16,0},{20,4},{24,8},{28,12},{1,17},{... | collective-permute-start | bytes 1585160 | tf_op jit(solution)/shard_map/ppermute | solution.py:445
  15.0 2.2 %copy-done = bf16[1024,2048]{1,0:T(8,128)(2,1)S(1)} copy-done((bf16[1024,2048]{1,0:T(8,128)(2,1)S(1)}, bf16[1024,2048]{1,0:T(8,128)(2,1)}, u32[]{:S(2)}) %copy-start) | copy-done | bytes 4194328
  17.2 1.0 copy-done.4
  18.3 1.3 %chunk_gradient.3.g1 = f32[256,2048]{1,0:T(8,128)S(1)} custom-call(s32[1]{0:T(128)} %bitcast.place_ref, bf16[1024,2048]{1,0:T(8,128)(2,1)S(1)} %copy-done, bf16[1024,256]{1,0:T(8,128)(2,1)S(1)} %copy-done.4), custom_call_target="tpu_custom_call" | custom-call | flops 1 | bytes 1 | tf_op jit(solution)/shard_map/chunk_gradient/pallas_call | solution.py:264
  19.6 7.0 %collective-permute-done.3.refs_2_ = bf16[2064,128]{1,0:T(8,128)(2,1)S(1)} collective-permute-done((bf16[2064,128]{1,0:T(8,128)(2,1)}, bf16[2064,128]{1,0:T(8,128)(2,1)S(1)}, u32[]{:S(2)}, u32[]{:S(2)}) %collective-permute-start.3) | collective-permute-done | bytes 528416 | tf_op jit(solution)/shard_map/ppermute | solution.py:445
  26.6 1.3 %collective-permute-done.4.refs_4_ = bf16[2064,128]{1,0:T(8,128)(2,1)} collective-permute-done((bf16[2064,128]{1,0:T(8,128)(2,1)}, bf16[2064,128]{1,0:T(8,128)(2,1)}, u32[]{:S(2)}, u32[]{:S(2)}) %collective-permute-start.4) | collective-permute-done | bytes 528416 | tf_op jit(solution)/shard_map/ppermute | solution.py:445
  27.9 1.1 broadcast_select_fusion
  29.0 0.6 collective-permute-start.7
  29.6 0.5 collective-permute-start.9
  30.1 0.7 collective-permute-start.5
  30.8 1.3 %collective-permute-start.6 = (bf16[1040,256]{1,0:T(8,128)(2,1)}, bf16[1040,256]{1,0:T(8,128)(2,1)S(1)}, u32[]{:S(2)}, u32[]{:S(2)}) collective-permute-start(bf16[1040,256]{1,0:T(8,128)(2,1)} %collective-permute-done.1.refs_1_.l1), channel_id=1, source_target_pairs={{2,1},{1,0},{6,5},{5,4},{10,9},{9,8},{14,13},{13,12},{18,17},{17,1... | collective-permute-start | bytes 1597448 | tf_op jit(solution)/shard_map/ppermute | solution.py:451
  32.1 2.2 %copy-done.1 = bf16[1024,2048]{1,0:T(8,128)(2,1)S(1)} copy-done((bf16[1024,2048]{1,0:T(8,128)(2,1)S(1)}, bf16[1024,2048]{1,0:T(8,128)(2,1)}, u32[]{:S(2)}) %copy-start.1) | copy-done | bytes 4194328
  34.3 2.5 %chunk_gradient.4.g2 = f32[256,2048]{1,0:T(8,128)S(1)} custom-call(s32[1]{0:T(128)} %bitcast.place_ref, bf16[1024,2048]{1,0:T(8,128)(2,1)S(1)} %copy-done.1, bf16[1040,256]{1,0:T(8,128)(2,1)S(1)} %collective-permute-done.refs_0_.r1, bf16[1040,256]{1,0:T(8,128)(2,1)} %collective-permute-done.1.refs_1_.l1), custom_call_target="tpu_custom_call" | custom-call | flops 1 | bytes 1 | tf_op jit(solution)/shard_map/chunk_gradient/pallas_call | solution.py:264
  36.8 1.5 %collective-permute-done.7.refs_6_ = bf16[2064,128]{1,0:T(8,128)(2,1)S(1)} collective-permute-done((bf16[2064,128]{1,0:T(8,128)(2,1)S(1)}, bf16[2064,128]{1,0:T(8,128)(2,1)S(1)}, u32[]{:S(2)}, u32[]{:S(2)}) %collective-permute-start.7) | collective-permute-done | bytes 528416 | tf_op jit(solution)/shard_map/ppermute | solution.py:467
  38.3 12.0 %collective-permute-done.6.refs_2_.l2 = bf16[1040,256]{1,0:T(8,128)(2,1)S(1)} collective-permute-done((bf16[1040,256]{1,0:T(8,128)(2,1)}, bf16[1040,256]{1,0:T(8,128)(2,1)S(1)}, u32[]{:S(2)}, u32[]{:S(2)}) %collective-permute-start.6) | collective-permute-done | bytes 532512 | tf_op jit(solution)/shard_map/ppermute | solution.py:451
  50.4 5.3 %first_values.1 = (bf16[2048,1024]{1,0:T(8,128)(2,1)S(1)}, s16[1040,256]{1,0:T(8,128)(2,1)S(1)}, s32[8,128]{1,0:T(8,128)S(1)}) custom-call(s32[1]{0:T(128)} %bitcast.place_ref, bf16[1024,2048]{1,0:T(8,128)(2,1)S(1)} %copy-done.2, bf16[2064,128]{1,0:T(8,128)(2,1)} %get-tuple-element.50.refs_0_, bf16[2064,128]{1,0:T(8,128)(2,1)} %collective-permute-done.2.refs_1_, ...), custom_call_target="tpu_custom_call" | custom-call | flops 1 | bytes 1 | tf_op jit(solution)/shard_map/first_values/pallas_call | solution.py:137
  55.6 3.7 %collective-permute-start.11 = (s16[1040,256]{1,0:T(8,128)(2,1)S(1)}, s16[1040,256]{1,0:T(8,128)(2,1)S(1)}, u32[]{:S(2)}, u32[]{:S(2)}) collective-permute-start(s16[1040,256]{1,0:T(8,128)(2,1)S(1)} %get-tuple-element.59), channel_id=1, source_target_pairs={{0,1},{3,2},{4,5},{7,6},{8,9},{11,10},{12,13},{15,14},{16,17},{19,... | collective-permute-start | bytes 1597448 | tf_op jit(solution)/shard_map/ppermute | solution.py:485
  59.3 0.7 collective-permute-start.16
  60.0 1.3 %collective-permute-start.17 = (bf16[1040,256]{1,0:T(8,128)(2,1)S(1)}, bf16[1040,256]{1,0:T(8,128)(2,1)S(1)}, u32[]{:S(2)}, u32[]{:S(2)}) collective-permute-start(bf16[1040,256]{1,0:T(8,128)(2,1)S(1)} %collective-permute-done.6.refs_2_.l2), channel_id=1, source_target_pairs={{1,0},{5,4},{9,8},{13,12},{17,16},{21,20},{25,24},{29,28}} | collective-permute-start | bytes 1597448 | tf_op jit(solution)/shard_map/ppermute | solution.py:451
  61.3 1.3 %chunk_gradient.5.g3 = f32[256,2048]{1,0:T(8,128)S(1)} custom-call(s32[1]{0:T(128)} %bitcast.place_ref, bf16[1024,2048]{1,0:T(8,128)(2,1)S(1)} %copy-done.2, bf16[1040,256]{1,0:T(8,128)(2,1)S(1)} %collective-permute-done.refs_0_.r1, bf16[1040,256]{1,0:T(8,128)(2,1)S(1)} %collective-permute-done.5.refs_1_.r2, ...), custom_call_target="tpu_custom_call" | custom-call | flops 1 | bytes 1 | tf_op jit(solution)/shard_map/chunk_gradient/pallas_call | solution.py:264
  62.7 4.5 %partial_values.1.partial_ref = f32[1024,1024]{1,0:T(8,128)S(1)} custom-call(bf16[1024,2048]{1,0:T(8,128)(2,1)S(1)} %copy-done.2, bf16[2048,1024]{1,0:T(8,128)(2,1)S(1)} %get-tuple-element.58.weight_ref), custom_call_target="tpu_custom_call" | custom-call | flops 1 | bytes 1 | tf_op jit(solution)/shard_map/partial_values/pallas_call | solution.py:167
  67.1 2.5 %collective-permute-done.11.arrived_ref = s16[1040,256]{1,0:T(8,128)(2,1)S(1)} collective-permute-done((s16[1040,256]{1,0:T(8,128)(2,1)S(1)}, s16[1040,256]{1,0:T(8,128)(2,1)S(1)}, u32[]{:S(2)}, u32[]{:S(2)}) %collective-permute-start.11) | collective-permute-done | bytes 532512 | tf_op jit(solution)/shard_map/ppermute | solution.py:485
  70.0 4.4 %collective-permute-start.12 = (s16[1040,256]{1,0:T(8,128)(2,1)S(1)}, s16[1040,256]{1,0:T(8,128)(2,1)S(1)}, u32[]{:S(2)}, u32[]{:S(2)}) collective-permute-start(s16[1040,256]{1,0:T(8,128)(2,1)S(1)} %hop.3), channel_id=1, source_target_pairs={{0,1},{1,2},{4,5},{5,6},{8,9},{9,10},{12,13},{13,14},{16,17},{17,1... | collective-permute-start | bytes 1597448 | tf_op jit(solution)/shard_map/ppermute | solution.py:448
  74.4 0.9 collective-permute-start.14
  75.3 4.9 %slot_terms.1 = (f32[2048,128]{1,0:T(8,128)S(1)}, f32[2048,128]{1,0:T(8,128)S(1)}, f32[2048,128]{1,0:T(8,128)S(1)}, f32[2048,128]{1,0:T(8,128)S(1)}, s16[2064,12...) custom-call(s32[8,128]{1,0:T(8,128)S(1)} %get-tuple-element.63.codes, ...), custom_call_target="tpu_custom_call" | custom-call | flops 1 | bytes 1 | tf_op jit(solution)/shard_map/slot_terms/pallas_call | solution.py:322
  80.2 0.5 collective-permute-start.21
  80.8 3.0 %collective-permute-done.12.arrived_ref = s16[1040,256]{1,0:T(8,128)(2,1)S(1)} collective-permute-done((s16[1040,256]{1,0:T(8,128)(2,1)S(1)}, s16[1040,256]{1,0:T(8,128)(2,1)S(1)}, u32[]{:S(2)}, u32[]{:S(2)}) %collective-permute-start.12) | collective-permute-done | bytes 532512 | tf_op jit(solution)/shard_map/ppermute | solution.py:448
  84.1 6.0 %collective-permute-start.13 = (s16[1040,256]{1,0:T(8,128)(2,1)S(1)}, s16[1040,256]{1,0:T(8,128)(2,1)S(1)}, u32[]{:S(2)}, u32[]{:S(2)}) collective-permute-start(s16[1040,256]{1,0:T(8,128)(2,1)S(1)} %hop.4), channel_id=1, source_target_pairs={{0,1},{1,2},{2,3},{4,5},{5,6},{6,7},{8,9},{9,10},{10,11},{12,13},{... | collective-permute-start | bytes 1597448 | tf_op jit(solution)/shard_map/ppermute | solution.py:448
  90.5 1.4 %collective-permute-start.15 = (s16[1040,256]{1,0:T(8,128)(2,1)S(1)}, s16[1040,256]{1,0:T(8,128)(2,1)S(1)}, u32[]{:S(2)}, u32[]{:S(2)}) collective-permute-start(s16[1040,256]{1,0:T(8,128)(2,1)S(1)} %hop.5), channel_id=1, source_target_pairs={{3,2},{2,1},{1,0},{7,6},{6,5},{5,4},{11,10},{10,9},{9,8},{15,14},{... | collective-permute-start | bytes 1597448 | tf_op jit(solution)/shard_map/ppermute | solution.py:451
  91.9 0.4 combine.5
  92.3 2.5 %collective-permute-start.20 = (s16[2064,128]{1,0:T(8,128)(2,1)S(1)}, s16[2064,128]{1,0:T(8,128)(2,1)S(1)}, u32[]{:S(2)}, u32[]{:S(2)}) collective-permute-start(s16[2064,128]{1,0:T(8,128)(2,1)S(1)} %combine.5), channel_id=1, source_target_pairs={{0,24},{4,28},{8,16},{12,20},{16,8},{20,12},{24,0},{28,4},{1,25},{... | collective-permute-start | bytes 1585160 | tf_op jit(solution)/shard_map/ppermute | solution.py:445
  94.8 0.4 combine.6
  95.2 0.6 collective-permute-start.22
  95.8 0.4 combine.7
  96.1 0.6 collective-permute-start.24
  96.7 7.7 %grad_inputs.1 = bf16[1024,2048]{1,0:T(8,128)(2,1)} custom-call(s32[1]{0:T(128)} %bitcast.place_ref, bf16[2048,1024]{1,0:T(8,128)(2,1)S(1)} %get-tuple-element.58.weight_ref, bf16[1024,256]{1,0:T(8,128)(2,1)S(1)} %copy-done.5, bf16[1040,256]{1,0:T(8,128)(2,1)S(1)} %collective-permute-done.refs_0_.r1, ...), custom_call_target="tpu_custom_call" | custom-call | flops 4294967296 | bytes 12582912 | tf_op jit(solution)/shard_map/grad_inputs/pallas_call | solution.py:416
  104.5 3.7 %collective-permute-done.20.refs_1_ = s16[2064,128]{1,0:T(8,128)(2,1)S(1)} collective-permute-done((s16[2064,128]{1,0:T(8,128)(2,1)S(1)}, s16[2064,128]{1,0:T(8,128)(2,1)S(1)}, u32[]{:S(2)}, u32[]{:S(2)}) %collective-permute-start.20) | collective-permute-done | bytes 528416 | tf_op jit(solution)/shard_map/ppermute | solution.py:445
  108.3 8.9 %collective-permute-done.22.refs_2_ = s16[2064,128]{1,0:T(8,128)(2,1)S(1)} collective-permute-done((s16[2064,128]{1,0:T(8,128)(2,1)S(1)}, s16[2064,128]{1,0:T(8,128)(2,1)S(1)}, u32[]{:S(2)}, u32[]{:S(2)}) %collective-permute-start.22) | collective-permute-done | bytes 528416 | tf_op jit(solution)/shard_map/ppermute | solution.py:445
  117.3 1.9 %normalized_update.1 = bf16[16,128,128]{2,1,0:T(8,128)(2,1)} custom-call(f32[2048,128]{1,0:T(8,128)S(1)} %combine.4.refs_0_, s16[2064,128]{1,0:T(8,128)(2,1)S(1)} %collective-permute-done.20.refs_1_, s16[2064,128]{1,0:T(8,128)(2,1)S(1)} %collective-permute-done.22.refs_2_, s16[2064,128]{1,0:T(8,128)(2,1)S(1)} %collective-permute-done.24.refs_3_), custom_call_target="tpu_custom_call" | custom-call | flops 1 | bytes 1 | tf_op jit(solution)/shard_map/normalized_update/pallas_call | solution.py:380
  119.2 1.1 last_hop.1
  (38 shorter events, 1.6 us)
Async XLA Ops:
  0.6 1.0 copy-start.3
  1.7 1.0 copy-start.6
  2.7 0.7 copy-start.7
  3.4 0.7 copy-start.8
  5.6 22.3 %collective-permute-start = (bf16[1040,256]{1,0:T(8,128)(2,1)}, bf16[1040,256]{1,0:T(8,128)(2,1)S(1)}, u32[]{:S(2)}, u32[]{:S(2)}) collective-permute-start(bf16[1040,256]{1,0:T(8,128)(2,1)} %get-tuple-element.39), channel_id=1, source_target_pairs={{0,1},{1,2},{2,3},{4,5},{5,6},{6,7},{8,9},{9,10},{10,11},{12,13},{... | collective-permute-start | bytes 1597448 | tf_op jit(solution)/shard_map/ppermute | solution.py:448
  10.6 17.3 %collective-permute-start.1 = (bf16[1040,256]{1,0:T(8,128)(2,1)}, bf16[1040,256]{1,0:T(8,128)(2,1)}, u32[]{:S(2)}, u32[]{:S(2)}) collective-permute-start(bf16[1040,256]{1,0:T(8,128)(2,1)} %get-tuple-element.39), channel_id=1, source_target_pairs={{3,2},{2,1},{1,0},{7,6},{6,5},{5,4},{11,10},{10,9},{9,8},{15,14},{... | collective-permute-start | bytes 1597448 | tf_op jit(solution)/shard_map/ppermute | solution.py:451
  11.9 7.7 %collective-permute-start.2 = (bf16[2064,128]{1,0:T(8,128)(2,1)}, bf16[2064,128]{1,0:T(8,128)(2,1)}, u32[]{:S(2)}, u32[]{:S(2)}) collective-permute-start(bf16[2064,128]{1,0:T(8,128)(2,1)} %get-tuple-element.50.refs_0_), channel_id=1, source_target_pairs={{0,4},{4,0},{8,12},{12,8},{16,20},{20,16},{24,28},{28,24},{1,5},{5... | collective-permute-start | bytes 1585160 | tf_op jit(solution)/shard_map/ppermute | solution.py:445
  11.9 14.6 %collective-permute-start.3 = (bf16[2064,128]{1,0:T(8,128)(2,1)}, bf16[2064,128]{1,0:T(8,128)(2,1)S(1)}, u32[]{:S(2)}, u32[]{:S(2)}) collective-permute-start(bf16[2064,128]{1,0:T(8,128)(2,1)} %get-tuple-element.50.refs_0_), channel_id=1, source_target_pairs={{0,8},{4,12},{8,0},{12,4},{16,24},{20,28},{24,16},{28,20},{1,9},{5... | collective-permute-start | bytes 1585160 | tf_op jit(solution)/shard_map/ppermute | solution.py:445
  13.5 14.4 %collective-permute-start.4 = (bf16[2064,128]{1,0:T(8,128)(2,1)}, bf16[2064,128]{1,0:T(8,128)(2,1)}, u32[]{:S(2)}, u32[]{:S(2)}) collective-permute-start(bf16[2064,128]{1,0:T(8,128)(2,1)} %get-tuple-element.50.refs_0_), channel_id=1, source_target_pairs={{0,16},{4,20},{8,24},{12,28},{16,0},{20,4},{24,8},{28,12},{1,17},{... | collective-permute-start | bytes 1585160 | tf_op jit(solution)/shard_map/ppermute | solution.py:445
  15.0 2.2 %copy-start = (bf16[1024,2048]{1,0:T(8,128)(2,1)S(1)}, bf16[1024,2048]{1,0:T(8,128)(2,1)}, u32[]{:S(2)}) copy-start(bf16[1024,2048]{1,0:T(8,128)(2,1)} %normed_ref.11) | copy-start | bytes 12582916
  17.2 1.0 copy-start.4
  29.0 9.3 %collective-permute-start.7 = (bf16[2064,128]{1,0:T(8,128)(2,1)S(1)}, bf16[2064,128]{1,0:T(8,128)(2,1)S(1)}, u32[]{:S(2)}, u32[]{:S(2)}) collective-permute-start(bf16[2064,128]{1,0:T(8,128)(2,1)S(1)} %broadcast_select_fusion), channel_id=1, source_target_pairs={{0,8},{4,20},{8,0},{12,28},{16,24},{20,4},{24,16},{28,12},{1,9},{5... | collective-permute-start | bytes 1585160 | tf_op jit(solution)/shard_map/ppermute | solution.py:467
  29.6 8.7 %collective-permute-start.8 = (bf16[2064,128]{1,0:T(8,128)(2,1)S(1)}, bf16[2064,128]{1,0:T(8,128)(2,1)S(1)}, u32[]{:S(2)}, u32[]{:S(2)}) collective-permute-start(bf16[2064,128]{1,0:T(8,128)(2,1)S(1)} %collective-permute-done.3.refs_2_), channel_id=1, source_target_pairs={{0,4},{4,0},{8,12},{12,8},{16,20},{20,16},{24,28},{28,24},{1,5},{5... | collective-permute-start | bytes 1585160 | tf_op jit(solution)/shard_map/ppermute | solution.py:445
  29.6 8.7 %collective-permute-start.9 = (bf16[2064,128]{1,0:T(8,128)(2,1)}, bf16[2064,128]{1,0:T(8,128)(2,1)S(1)}, u32[]{:S(2)}, u32[]{:S(2)}) collective-permute-start(bf16[2064,128]{1,0:T(8,128)(2,1)} %collective-permute-done.4.refs_4_), channel_id=1, source_target_pairs={{0,4},{4,0},{8,12},{12,8},{16,20},{20,16},{24,28},{28,24},{1,5},{5... | collective-permute-start | bytes 1585160 | tf_op jit(solution)/shard_map/ppermute | solution.py:445
  30.1 8.2 %collective-permute-start.5 = (bf16[1040,256]{1,0:T(8,128)(2,1)S(1)}, bf16[1040,256]{1,0:T(8,128)(2,1)S(1)}, u32[]{:S(2)}, u32[]{:S(2)}) collective-permute-start(bf16[1040,256]{1,0:T(8,128)(2,1)S(1)} %collective-permute-done.refs_0_.r1), channel_id=1, source_target_pairs={{1,2},{2,3},{5,6},{6,7},{9,10},{10,11},{13,14},{14,15},{17,18},{18... | collective-permute-start | bytes 1597448 | tf_op jit(solution)/shard_map/ppermute | solution.py:448
  30.8 19.5 %collective-permute-start.6 = (bf16[1040,256]{1,0:T(8,128)(2,1)}, bf16[1040,256]{1,0:T(8,128)(2,1)S(1)}, u32[]{:S(2)}, u32[]{:S(2)}) collective-permute-start(bf16[1040,256]{1,0:T(8,128)(2,1)} %collective-permute-done.1.refs_1_.l1), channel_id=1, source_target_pairs={{2,1},{1,0},{6,5},{5,4},{10,9},{9,8},{14,13},{13,12},{18,17},{17,1... | collective-permute-start | bytes 1597448 | tf_op jit(solution)/shard_map/ppermute | solution.py:451
  32.1 2.2 %copy-start.1 = (bf16[1024,2048]{1,0:T(8,128)(2,1)S(1)}, bf16[1024,2048]{1,0:T(8,128)(2,1)}, u32[]{:S(2)}) copy-start(bf16[1024,2048]{1,0:T(8,128)(2,1)} %normed_ref.11) | copy-start | bytes 12582916
  34.3 16.0 %copy-start.2 = (bf16[1024,2048]{1,0:T(8,128)(2,1)S(1)}, bf16[1024,2048]{1,0:T(8,128)(2,1)}, u32[]{:S(2)}) copy-start(bf16[1024,2048]{1,0:T(8,128)(2,1)} %normed_ref.11) | copy-start | bytes 12582916
  38.3 12.0 %collective-permute-start.10 = (bf16[2064,128]{1,0:T(8,128)(2,1)S(1)}, bf16[2064,128]{1,0:T(8,128)(2,1)S(1)}, u32[]{:S(2)}, u32[]{:S(2)}) collective-permute-start(bf16[2064,128]{1,0:T(8,128)(2,1)S(1)} %collective-permute-done.7.refs_6_), channel_id=1, source_target_pairs={{0,4},{4,0},{8,12},{12,8},{16,20},{20,16},{24,28},{28,24},{1,5},{5... | collective-permute-start | bytes 1585160 | tf_op jit(solution)/shard_map/ppermute | solution.py:445
  55.6 14.0 %collective-permute-start.11 = (s16[1040,256]{1,0:T(8,128)(2,1)S(1)}, s16[1040,256]{1,0:T(8,128)(2,1)S(1)}, u32[]{:S(2)}, u32[]{:S(2)}) collective-permute-start(s16[1040,256]{1,0:T(8,128)(2,1)S(1)} %get-tuple-element.59), channel_id=1, source_target_pairs={{0,1},{3,2},{4,5},{7,6},{8,9},{11,10},{12,13},{15,14},{16,17},{19,... | collective-permute-start | bytes 1597448 | tf_op jit(solution)/shard_map/ppermute | solution.py:485
  59.3 16.0 %collective-permute-start.16 = (bf16[1040,256]{1,0:T(8,128)(2,1)S(1)}, bf16[1040,256]{1,0:T(8,128)(2,1)S(1)}, u32[]{:S(2)}, u32[]{:S(2)}) collective-permute-start(bf16[1040,256]{1,0:T(8,128)(2,1)S(1)} %collective-permute-done.5.refs_1_.r2), channel_id=1, source_target_pairs={{2,3},{6,7},{10,11},{14,15},{18,19},{22,23},{26,27},{30,31}} | collective-permute-start | bytes 1597448 | tf_op jit(solution)/shard_map/ppermute | solution.py:448
  60.0 15.3 %collective-permute-start.17 = (bf16[1040,256]{1,0:T(8,128)(2,1)S(1)}, bf16[1040,256]{1,0:T(8,128)(2,1)S(1)}, u32[]{:S(2)}, u32[]{:S(2)}) collective-permute-start(bf16[1040,256]{1,0:T(8,128)(2,1)S(1)} %collective-permute-done.6.refs_2_.l2), channel_id=1, source_target_pairs={{1,0},{5,4},{9,8},{13,12},{17,16},{21,20},{25,24},{29,28}} | collective-permute-start | bytes 1597448 | tf_op jit(solution)/shard_map/ppermute | solution.py:451
  70.0 13.8 %collective-permute-start.12 = (s16[1040,256]{1,0:T(8,128)(2,1)S(1)}, s16[1040,256]{1,0:T(8,128)(2,1)S(1)}, u32[]{:S(2)}, u32[]{:S(2)}) collective-permute-start(s16[1040,256]{1,0:T(8,128)(2,1)S(1)} %hop.3), channel_id=1, source_target_pairs={{0,1},{1,2},{4,5},{5,6},{8,9},{9,10},{12,13},{13,14},{16,17},{17,1... | collective-permute-start | bytes 1597448 | tf_op jit(solution)/shard_map/ppermute | solution.py:448
  74.4 9.7 %collective-permute-start.14 = (s16[1040,256]{1,0:T(8,128)(2,1)S(1)}, s16[1040,256]{1,0:T(8,128)(2,1)S(1)}, u32[]{:S(2)}, u32[]{:S(2)}) collective-permute-start(s16[1040,256]{1,0:T(8,128)(2,1)S(1)} %hop.3), channel_id=1, source_target_pairs={{3,2},{2,1},{7,6},{6,5},{11,10},{10,9},{15,14},{14,13},{19,18},{18... | collective-permute-start | bytes 1597448 | tf_op jit(solution)/shard_map/ppermute | solution.py:451
  80.2 10.3 %collective-permute-start.19 = (s16[2064,128]{1,0:T(8,128)(2,1)S(1)}, s16[2064,128]{1,0:T(8,128)(2,1)S(1)}, u32[]{:S(2)}, u32[]{:S(2)}) collective-permute-start(s16[2064,128]{1,0:T(8,128)(2,1)S(1)} %get-tuple-element.70), channel_id=1, source_target_pairs={{0,4},{4,0},{8,12},{12,8},{16,20},{20,16},{24,28},{28,24},{1,5},{5... | collective-permute-start | bytes 1585160 | tf_op jit(solution)/shard_map/ppermute | solution.py:445
  80.2 12.1 %collective-permute-start.21 = (s16[2064,128]{1,0:T(8,128)(2,1)S(1)}, s16[2064,128]{1,0:T(8,128)(2,1)S(1)}, u32[]{:S(2)}, u32[]{:S(2)}) collective-permute-start(s16[2064,128]{1,0:T(8,128)(2,1)S(1)} %get-tuple-element.72), channel_id=1, source_target_pairs={{0,4},{4,0},{8,12},{12,8},{16,20},{20,16},{24,28},{28,24},{1,5},{5... | collective-permute-start | bytes 1585160 | tf_op jit(solution)/shard_map/ppermute | solution.py:445
  80.7 14.4 %collective-permute-start.23 = (s16[2064,128]{1,0:T(8,128)(2,1)S(1)}, s16[2064,128]{1,0:T(8,128)(2,1)S(1)}, u32[]{:S(2)}, u32[]{:S(2)}) collective-permute-start(s16[2064,128]{1,0:T(8,128)(2,1)S(1)} %get-tuple-element.74), channel_id=1, source_target_pairs={{0,4},{4,0},{8,12},{12,8},{16,20},{20,16},{24,28},{28,24},{1,5},{5... | collective-permute-start | bytes 1585160 | tf_op jit(solution)/shard_map/ppermute | solution.py:445
  83.8 12.3 %collective-permute-start.18 = (s16[2064,128]{1,0:T(8,128)(2,1)S(1)}, s16[2064,128]{1,0:T(8,128)(2,1)S(1)}, u32[]{:S(2)}, u32[]{:S(2)}) collective-permute-start(s16[2064,128]{1,0:T(8,128)(2,1)S(1)} %get-tuple-element.68), channel_id=1, source_target_pairs={{0,4},{4,0},{8,12},{12,8},{16,20},{20,16},{24,28},{28,24},{1,5},{5... | collective-permute-start | bytes 1585160 | tf_op jit(solution)/shard_map/ppermute | solution.py:445
  84.1 35.1 %collective-permute-start.13 = (s16[1040,256]{1,0:T(8,128)(2,1)S(1)}, s16[1040,256]{1,0:T(8,128)(2,1)S(1)}, u32[]{:S(2)}, u32[]{:S(2)}) collective-permute-start(s16[1040,256]{1,0:T(8,128)(2,1)S(1)} %hop.4), channel_id=1, source_target_pairs={{0,1},{1,2},{2,3},{4,5},{5,6},{6,7},{8,9},{9,10},{10,11},{12,13},{... | collective-permute-start | bytes 1597448 | tf_op jit(solution)/shard_map/ppermute | solution.py:448
  90.5 6.3 %copy-start.5 = (bf16[1024,256]{1,0:T(8,128)(2,1)S(1)}, bf16[1024,256]{1,0:T(8,128)(2,1)}, u32[]{:S(2)}) copy-start(bf16[1024,256]{1,0:T(8,128)(2,1)} %own.1) | copy-start | bytes 1572868
  90.5 28.7 %collective-permute-start.15 = (s16[1040,256]{1,0:T(8,128)(2,1)S(1)}, s16[1040,256]{1,0:T(8,128)(2,1)S(1)}, u32[]{:S(2)}, u32[]{:S(2)}) collective-permute-start(s16[1040,256]{1,0:T(8,128)(2,1)S(1)} %hop.5), channel_id=1, source_target_pairs={{3,2},{2,1},{1,0},{7,6},{6,5},{5,4},{11,10},{10,9},{9,8},{15,14},{... | collective-permute-start | bytes 1597448 | tf_op jit(solution)/shard_map/ppermute | solution.py:451
  92.3 16.0 %collective-permute-start.20 = (s16[2064,128]{1,0:T(8,128)(2,1)S(1)}, s16[2064,128]{1,0:T(8,128)(2,1)S(1)}, u32[]{:S(2)}, u32[]{:S(2)}) collective-permute-start(s16[2064,128]{1,0:T(8,128)(2,1)S(1)} %combine.5), channel_id=1, source_target_pairs={{0,24},{4,28},{8,16},{12,20},{16,8},{20,12},{24,0},{28,4},{1,25},{... | collective-permute-start | bytes 1585160 | tf_op jit(solution)/shard_map/ppermute | solution.py:445
  95.2 22.0 %collective-permute-start.22 = (s16[2064,128]{1,0:T(8,128)(2,1)S(1)}, s16[2064,128]{1,0:T(8,128)(2,1)S(1)}, u32[]{:S(2)}, u32[]{:S(2)}) collective-permute-start(s16[2064,128]{1,0:T(8,128)(2,1)S(1)} %combine.6), channel_id=1, source_target_pairs={{0,16},{4,20},{8,24},{12,28},{16,0},{20,4},{24,8},{28,12},{1,17},{... | collective-permute-start | bytes 1585160 | tf_op jit(solution)/shard_map/ppermute | solution.py:445
  96.1 21.1 %collective-permute-start.24 = (s16[2064,128]{1,0:T(8,128)(2,1)S(1)}, s16[2064,128]{1,0:T(8,128)(2,1)S(1)}, u32[]{:S(2)}, u32[]{:S(2)}) collective-permute-start(s16[2064,128]{1,0:T(8,128)(2,1)S(1)} %combine.7), channel_id=1, source_target_pairs={{0,8},{4,12},{8,0},{12,4},{16,24},{20,28},{24,16},{28,20},{1,9},{5... | collective-permute-start | bytes 1585160 | tf_op jit(solution)/shard_map/ppermute | solution.py:445

commit v4 on v3

--- a/solution.py
+++ b/solution.py
@@ -68,29 +68,45 @@
     return block
 
 
-def pack_kernel(column_blocks, rows_ref, columns_ref, tiles_ref, chunk_ref, message_ref, padded_ref):
+def pack_kernel(
+    column_blocks, rows_ref, columns_ref, tiles_ref, chunk_ref, message_ref, padded_ref, slots, sems
+):
     rows = tiles_ref.shape[0]
     tokens = chunk_ref.shape[0]
-    message_ref[:rows, :] = tiles_ref[...]
+    copies = [
+        pltpu.make_async_copy(rows_ref, slots.at[0], sems.at[0]),
+        pltpu.make_async_copy(columns_ref, slots.at[1], sems.at[1]),
+        pltpu.make_async_copy(chunk_ref, padded_ref.at[pl.ds(0, tokens)], sems.at[2]),
+        pltpu.make_async_copy(tiles_ref, message_ref.at[pl.ds(0, rows)], sems.at[3]),
+    ]
+    for copy in copies:
+        copy.start()
+    padded_ref[tokens:, :] = jnp.zeros((EXTRA, chunk_ref.shape[1]), padded_ref.dtype)
+    copies[0].wait()
+    copies[1].wait()
     lane = lax.broadcasted_iota(jnp.int32, (PAD, tiles_ref.shape[1]), 1)
     positions = jnp.zeros(lane.shape, jnp.int32)
     for slot in range(rows_ref.shape[1]):
-        row, column = rows_ref[0, slot], columns_ref[0, slot]
+        row, column = slots[0, 0, slot], slots[1, 0, slot]
         position = jnp.where(column >= 0, row * column_blocks + column + 1, 0)
         positions = jnp.where(lane == slot, position, positions)
     message_ref[rows:, :] = positions.astype(jnp.float32).astype(message_ref.dtype)
-    padded_ref[:tokens, :] = chunk_ref[...]
-    padded_ref[tokens:, :] = jnp.zeros((EXTRA, chunk_ref.shape[1]), padded_ref.dtype)
+    copies[2].wait()
+    copies[3].wait()
 
 
 def pack(rows, columns, tiles, chunk, column_blocks):
     return pl.pallas_call(
         functools.partial(pack_kernel, column_blocks),
-        in_specs=[SMEM, SMEM, VMEM, VMEM],
+        in_specs=[pl.BlockSpec(memory_space=pl.ANY)] * 4,
         out_specs=[VMEM, VMEM],
         out_shape=[
             jax.ShapeDtypeStruct((tiles.shape[0] + PAD, tiles.shape[1]), tiles.dtype),
             jax.ShapeDtypeStruct((chunk.shape[0] + EXTRA, chunk.shape[1]), chunk.dtype),
+        ],
+        scratch_shapes=[
+            pltpu.SMEM((2,) + rows.shape, jnp.int32),
+            pltpu.SemaphoreType.DMA((4,)),
         ],
         compiler_params=params(8),
         cost_estimate=LITTLE,
@@ -318,7 +334,7 @@
     chips = codes.shape[0] // 2
     rows = capacity * GROUP
     width = early[0].shape[0]
-    shapes = [((rows, GROUP), jnp.float32)] * chips + [((rows + PAD, GROUP), jnp.int16)] * chips
+    shapes = [((rows, GROUP), jnp.float32)] * chips + [((rows + 3 * PAD, GROUP), jnp.int16)] * chips
     outputs = pl.pallas_call(
         functools.partial(slots_kernel, chips, column_blocks),
         in_specs=[SMEM, SMEM, VMEM]
@@ -455,49 +471,36 @@
     )
     r1, l1 = right(padded, 0, 1, 2), left(padded, 3, 2, 1)
     g1 = chunk_gradient(lambda place, own: own, place, normed, cotangent)
-    direct = [1, 2] if chips == 4 else list(range(1, chips))
-    same_core = [message] + [swap(message, 2 * chip) for chip in direct]
+    same_core = [message] + [swap(message, 2 * chip) for chip in range(1, chips)]
     beside = swap(message, 1)
-    r1, l1, g1, beside, *same_core = lax.optimization_barrier((r1, l1, g1, beside, *same_core))
-
+    r1, l1, g1, beside = lax.optimization_barrier((r1, l1, g1, beside))
     r2, l2 = right(r1, 1, 2), left(l1, 2, 1)
     g2 = chunk_gradient(second_chunk, place, normed, r1, l1)
-    if chips == 4:
-        even = lax.axis_index("fsdp") % 2 == 0
-        diagonal = lax.ppermute(
-            jnp.where(even, same_core[2], same_core[1]),
-            "fsdp",
-            [(i, i ^ 2 if i % 2 == 0 else i ^ 4) for i in range(devices)],
-        )
-        across = [swap(m, 1) for m in same_core[1:]]
-        diagonal, g2, *across = lax.optimization_barrier((diagonal, g2, *across))
-        same_core.append(diagonal)
-        across.append(swap(diagonal, 1))
-    else:
-        across = [swap(m, 1) for m in same_core[1:]]
-    gathered = []
-    for pair in zip(same_core, [beside] + across):
-        gathered += pair
+    *same_core, g2 = lax.optimization_barrier((*same_core, g2))
+    gathered = [same_core[0], beside]
+    for m in same_core[1:]:
+        gathered += [m, swap(m, 1)]
     r2, l2, *gathered = lax.optimization_barrier((r2, l2, *gathered))
-
     r3, l3 = right(r2, 2), left(l2, 1)
+
     weight, first, codes = first_values(place, normed, gathered, parts, column_blocks)
     arrived = lax.ppermute(first, "tensor", [(0, 1), (3, 2)])
     partial = partial_values(normed, weight)
     g3 = chunk_gradient(third_chunk, place, normed, r1, r2, l2)
-    arrived, g3 = lax.optimization_barrier((arrived, g3))
-
+    g3, partial = lax.optimization_barrier((g3, partial))
     keep, send = slot_terms(
         codes, place, normed, (r2, l2, r3, l3), (g1, g2, g3), capacity, column_blocks
     )
+    arrived, keep, send = lax.optimization_barrier((arrived, keep, send))
+
     second = hop(place, 2, partial, arrived)
     from_left, from_right = right(second, 0, 1), left(second, 3, 2)
     other = [swap(m, 1) for m in send]
-    terms = [
-        swap(combine(keep[chip], other[chip], jnp.int16), 2 * chip)
-        for chip in reversed(range(1, chips))
-    ]
+    sums = [combine(keep[chip], other[chip], jnp.int16) for chip in range(1, chips)]
+    from_left, from_right, _ = lax.optimization_barrier((from_left, from_right, sums))
+    terms = [swap(m, 2 * chip) for chip, m in reversed(list(enumerate(sums, 1)))]
     own = combine(keep[0], other[0], jnp.float32)
+
     from_left = right(hop(place, 1, partial, from_left), 0, 1, 2)
     from_right = left(hop(place, 3, partial, from_right), 3, 2, 1)
     grad_input = grad_inputs(place, weight, cotangent, r1, r2, r3, l1, l2, l3)

time: 121 us -> 106 us (0.88)
  waiting for transfers between devices: 40.1 us -> 28.8 us
  Pallas kernels: 34.2 us -> 31.6 us
  local copies, waits for them, and re-layouts: 8.81 us -> 6.63 us
  starting transfers between devices: 35.2 us -> 36.9 us
    ppermute x13 -> x14, waiting for transfers between devices: 21.1 us -> 14.1 us  [swap(): return lax.ppermute(x, 'fsdp', [(i, i ^ mask) for i in range(devices)])]
    ppermute x5, waiting for transfers between devices: 12 us -> 5.13 us  [left(): return lax.ppermute(x, 'tensor', [(i, i - 1) for i in sources])]
    ppermute x5, waiting for transfers between devices: 2.97 us -> 9.13 us  [right(): return lax.ppermute(x, 'tensor', [(i, i + 1) for i in sources])]
    unnamed x18 -> x16, local copies, waits for them, and re-layouts: 8.81 us -> 6.63 us
    ppermute x1, waiting for transfers between devices: 2.49 us -> 0.45 us  [local(): arrived = lax.ppermute(first, 'tensor', [(0, 1), (3, 2)])]
    ppermute x1 -> x0, waiting for transfers between devices: 1.5 us -> none  [local(): lax.ppermute(jnp.where(even, same_core[2], same_core[1]), 'fsdp', [(i, i...]
    ppermute x13 -> x14, starting transfers between devices: 7.99 us -> 9.33 us  [swap(): return lax.ppermute(x, 'fsdp', [(i, i ^ mask) for i in range(devices)])]
  transfers between devices with their start and end apart: 25 -> 25, of which waited for: 9 -> 11; matrix products, arithmetic and copies ran while one was open for 0% -> 0% of each run, Pallas kernels for 22% -> 27%
where the time goes in v4:
time: 106 us; the launch traced here: 105 us
  starting transfers between devices  36.9 us (35%)
  Pallas kernels  31.6 us (30%)
  waiting for transfers between devices  28.8 us (27%)
  local copies, waits for them, and re-layouts  6.63 us (6%)
    ppermute x5, starting transfers between devices, right(): return lax.ppermute(x, 'tensor', [(i, i + 1) for i in sources])  16.9 us
    ppermute x14, waiting for transfers between devices, swap(): return lax.ppermute(x, 'fsdp', [(i, i ^ mask) for i in range(devices)])  14.1 us
    ppermute x14, starting transfers between devices, swap(): return lax.ppermute(x, 'fsdp', [(i, i ^ mask) for i in range(devices)])  9.33 us
    ppermute x5, waiting for transfers between devices, right(): return lax.ppermute(x, 'tensor', [(i, i + 1) for i in sources])  9.13 us
    pallas_call x1, Pallas kernels, grad_inputs(): pl.pallas_call(grad_input_kernel, grid_spec=pltpu.PrefetchScalarGridSpec(...  6.65 us
    unnamed x16, local copies, waits for them, and re-layouts  6.63 us
    ppermute x5, starting transfers between devices, left(): return lax.ppermute(x, 'tensor', [(i, i - 1) for i in sources])  5.84 us
    ppermute x5, waiting for transfers between devices, left(): return lax.ppermute(x, 'tensor', [(i, i - 1) for i in sources])  5.13 us
  transfers between devices with their start and end apart: 25, of which 11 were waited for; matrix products, arithmetic and copies ran while one was open for 0% of the time, Pallas kernels for 27%

profile of v4, /device:TPU:0, one launch (start us, length us, event | category | flops | bytes accessed | tf_op | source)
XLA Modules:
  0.0 104.8 jit_solution(1896097241290155181)
XLA Ops:
  0.6 1.0 copy-done.2
  1.7 1.0 copy-done.5
  2.7 0.7 copy-done.6
  3.4 0.7 copy-done.7
  4.0 1.4 %pack.1 = (bf16[2064,128]{1,0:T(8,128)(2,1)S(1)}, bf16[1040,256]{1,0:T(8,128)(2,1)}) custom-call(s32[1,16]{1,0:T(1,128)S(1)} %copy-done.6, s32[1,16]{1,0:T(1,128)S(1)} %copy-done.7, bf16[2048,128]{1,0:T(8,128)(2,1)S(1)} %bitcast.3, bf16[1024,256]{1,0:T(8,128)(2,1)S(1)} %copy-done.2), custom_call_target="tpu_custom_call" | custom-call | flops 1 | bytes 1 | tf_op jit(solution)/shard_map/pack/pallas_call | solution.py:99
  5.5 0.5 collective-permute-start.2
  6.0 1.3 %collective-permute-start.1 = (bf16[1040,256]{1,0:T(8,128)(2,1)}, bf16[1040,256]{1,0:T(8,128)(2,1)S(1)}, u32[]{:S(2)}, u32[]{:S(2)}) collective-permute-start(bf16[1040,256]{1,0:T(8,128)(2,1)} %get-tuple-element.48), channel_id=1, source_target_pairs={{3,2},{2,1},{1,0},{7,6},{6,5},{5,4},{11,10},{10,9},{9,8},{15,14},{... | collective-permute-start | bytes 1597448 | tf_op jit(solution)/shard_map/ppermute | solution.py:467
  7.3 5.2 %collective-permute-start = (bf16[1040,256]{1,0:T(8,128)(2,1)}, bf16[1040,256]{1,0:T(8,128)(2,1)S(1)}, u32[]{:S(2)}, u32[]{:S(2)}) collective-permute-start(bf16[1040,256]{1,0:T(8,128)(2,1)} %get-tuple-element.48), channel_id=1, source_target_pairs={{0,1},{1,2},{2,3},{4,5},{5,6},{6,7},{8,9},{9,10},{10,11},{12,13},{... | collective-permute-start | bytes 1597448 | tf_op jit(solution)/shard_map/ppermute | solution.py:464
  12.4 2.9 %collective-permute-start.7 = (bf16[2064,128]{1,0:T(8,128)(2,1)S(1)}, bf16[2064,128]{1,0:T(8,128)(2,1)S(1)}, u32[]{:S(2)}, u32[]{:S(2)}) collective-permute-start(bf16[2064,128]{1,0:T(8,128)(2,1)S(1)} %get-tuple-element.59.refs_0_), channel_id=1, source_target_pairs={{0,24},{4,28},{8,16},{12,20},{16,8},{20,12},{24,0},{28,4},{1,25},{... | collective-permute-start | bytes 1585160 | tf_op jit(solution)/shard_map/ppermute | solution.py:461
  15.4 0.5 collective-permute-start.6
  16.0 2.2 %copy-done = bf16[1024,2048]{1,0:T(8,128)(2,1)S(1)} copy-done((bf16[1024,2048]{1,0:T(8,128)(2,1)S(1)}, bf16[1024,2048]{1,0:T(8,128)(2,1)}, u32[]{:S(2)}) %copy-start) | copy-done | bytes 4194328
  18.2 1.0 copy-done.3
  19.3 1.3 %chunk_gradient.3.g1 = f32[256,2048]{1,0:T(8,128)S(1)} custom-call(s32[1]{0:T(128)} %bitcast.place_ref, bf16[1024,2048]{1,0:T(8,128)(2,1)S(1)} %copy-done, bf16[1024,256]{1,0:T(8,128)(2,1)S(1)} %copy-done.3), custom_call_target="tpu_custom_call" | custom-call | flops 1 | bytes 1 | tf_op jit(solution)/shard_map/chunk_gradient/pallas_call | solution.py:280
  20.6 2.9 %collective-permute-done.1.refs_1_.l1 = bf16[1040,256]{1,0:T(8,128)(2,1)S(1)} collective-permute-done((bf16[1040,256]{1,0:T(8,128)(2,1)}, bf16[1040,256]{1,0:T(8,128)(2,1)S(1)}, u32[]{:S(2)}, u32[]{:S(2)}) %collective-permute-start.1) | collective-permute-done | bytes 532512 | tf_op jit(solution)/shard_map/ppermute | solution.py:467
  23.4 1.3 %collective-permute-done.refs_0_.r1 = bf16[1040,256]{1,0:T(8,128)(2,1)S(1)} collective-permute-done((bf16[1040,256]{1,0:T(8,128)(2,1)}, bf16[1040,256]{1,0:T(8,128)(2,1)S(1)}, u32[]{:S(2)}, u32[]{:S(2)}) %collective-permute-start) | collective-permute-done | bytes 532512 | tf_op jit(solution)/shard_map/ppermute | solution.py:464
  24.7 1.3 %collective-permute-start.4 = (bf16[1040,256]{1,0:T(8,128)(2,1)S(1)}, bf16[1040,256]{1,0:T(8,128)(2,1)S(1)}, u32[]{:S(2)}, u32[]{:S(2)}) collective-permute-start(bf16[1040,256]{1,0:T(8,128)(2,1)S(1)} %collective-permute-done.1.refs_1_.l1), channel_id=1, source_target_pairs={{2,1},{1,0},{6,5},{5,4},{10,9},{9,8},{14,13},{13,12},{18,17},{17,1... | collective-permute-start | bytes 1597448 | tf_op jit(solution)/shard_map/ppermute | solution.py:467
  26.0 0.7 collective-permute-start.3
  26.7 1.3 %chunk_gradient.4.g2 = f32[256,2048]{1,0:T(8,128)S(1)} custom-call(s32[1]{0:T(128)} %bitcast.place_ref, bf16[1024,2048]{1,0:T(8,128)(2,1)S(1)} %copy-done.1, bf16[1040,256]{1,0:T(8,128)(2,1)S(1)} %collective-permute-done.refs_0_.r1, bf16[1040,256]{1,0:T(8,128)(2,1)S(1)} %collective-permute-done.1.refs_1_.l1), custom_call_target="tpu_custom_call" | custom-call | flops 1 | bytes 1 | tf_op jit(solution)/shard_map/chunk_gradient/pallas_call | solution.py:280
  28.3 10.5 %collective-permute-done.6.refs_4_ = bf16[2064,128]{1,0:T(8,128)(2,1)S(1)} collective-permute-done((bf16[2064,128]{1,0:T(8,128)(2,1)S(1)}, bf16[2064,128]{1,0:T(8,128)(2,1)S(1)}, u32[]{:S(2)}, u32[]{:S(2)}) %collective-permute-start.6) | collective-permute-done | bytes 528416 | tf_op jit(solution)/shard_map/ppermute | solution.py:461
  38.8 0.4 collective-permute-done.5.refs_2_
  39.2 0.5 collective-permute-start.9
  39.7 2.3 %collective-permute-done.8.refs_3_ = bf16[2064,128]{1,0:T(8,128)(2,1)S(1)} collective-permute-done((bf16[2064,128]{1,0:T(8,128)(2,1)}, bf16[2064,128]{1,0:T(8,128)(2,1)S(1)}, u32[]{:S(2)}, u32[]{:S(2)}) %collective-permute-start.8) | collective-permute-done | bytes 528416 | tf_op jit(solution)/shard_map/ppermute | solution.py:461
  42.0 0.6 collective-permute-done.10.refs_7_
  42.6 0.7 collective-permute-start.12
  43.3 1.3 %collective-permute-start.13 = (bf16[1040,256]{1,0:T(8,128)(2,1)S(1)}, bf16[1040,256]{1,0:T(8,128)(2,1)S(1)}, u32[]{:S(2)}, u32[]{:S(2)}) collective-permute-start(bf16[1040,256]{1,0:T(8,128)(2,1)S(1)} %collective-permute-done.4.refs_2_.l2), channel_id=1, source_target_pairs={{1,0},{5,4},{9,8},{13,12},{17,16},{21,20},{25,24},{29,28}} | collective-permute-start | bytes 1597448 | tf_op jit(solution)/shard_map/ppermute | solution.py:467
  44.6 5.0 %first_values.1 = (bf16[2048,1024]{1,0:T(8,128)(2,1)S(1)}, s16[1040,256]{1,0:T(8,128)(2,1)S(1)}, s32[8,128]{1,0:T(8,128)S(1)}) custom-call(s32[1]{0:T(128)} %bitcast.place_ref, bf16[1024,2048]{1,0:T(8,128)(2,1)S(1)} %copy-done.1, bf16[2064,128]{1,0:T(8,128)(2,1)S(1)} %get-tuple-element.59.refs_0_, bf16[2064,128]{1,0:T(8,128)(2,1)S(1)} %collective-permute-done.2.refs_1_, ...), custom_call_target="tpu_custom_call" | custom-call | flops 1 | bytes 1 | tf_op jit(solution)/shard_map/first_values/pallas_call | solution.py:153
  49.6 4.8 %collective-permute-start.11 = (s16[1040,256]{1,0:T(8,128)(2,1)S(1)}, s16[1040,256]{1,0:T(8,128)(2,1)S(1)}, u32[]{:S(2)}, u32[]{:S(2)}) collective-permute-start(s16[1040,256]{1,0:T(8,128)(2,1)S(1)} %get-tuple-element.69), channel_id=1, source_target_pairs={{0,1},{3,2},{4,5},{7,6},{8,9},{11,10},{12,13},{15,14},{16,17},{19,... | collective-permute-start | bytes 1597448 | tf_op jit(solution)/shard_map/ppermute | solution.py:487
  54.4 1.3 %chunk_gradient.5.g3 = f32[256,2048]{1,0:T(8,128)S(1)} custom-call(s32[1]{0:T(128)} %bitcast.place_ref, bf16[1024,2048]{1,0:T(8,128)(2,1)S(1)} %copy-done.1, bf16[1040,256]{1,0:T(8,128)(2,1)S(1)} %collective-permute-done.refs_0_.r1, bf16[1040,256]{1,0:T(8,128)(2,1)S(1)} %collective-permute-done.3.refs_1_.r2, ...), custom_call_target="tpu_custom_call" | custom-call | flops 1 | bytes 1 | tf_op jit(solution)/shard_map/chunk_gradient/pallas_call | solution.py:280
  55.7 4.5 %partial_values.1.partial_ref = f32[1024,1024]{1,0:T(8,128)S(1)} custom-call(bf16[1024,2048]{1,0:T(8,128)(2,1)S(1)} %copy-done.1, bf16[2048,1024]{1,0:T(8,128)(2,1)S(1)} %get-tuple-element.67.weight_ref), custom_call_target="tpu_custom_call" | custom-call | flops 1 | bytes 1 | tf_op jit(solution)/shard_map/partial_values/pallas_call | solution.py:183
  60.2 4.9 %slot_terms.1 = (f32[2048,128]{1,0:T(8,128)S(1)}, f32[2048,128]{1,0:T(8,128)S(1)}, f32[2048,128]{1,0:T(8,128)S(1)}, f32[2048,128]{1,0:T(8,128)S(1)}, s16[2096,12...) custom-call(s32[8,128]{1,0:T(8,128)S(1)} %get-tuple-element.70.codes, ...), custom_call_target="tpu_custom_call" | custom-call | flops 1 | bytes 1 | tf_op jit(solution)/shard_map/slot_terms/pallas_call | solution.py:338
  65.1 0.4 collective-permute-done.11.arrived_ref
  65.5 0.5 collective-permute-start.17
  66.1 0.5 collective-permute-start.21
  66.9 0.7 collective-permute-start.15
  67.6 5.0 %collective-permute-start.14 = (s16[1040,256]{1,0:T(8,128)(2,1)S(1)}, s16[1040,256]{1,0:T(8,128)(2,1)S(1)}, u32[]{:S(2)}, u32[]{:S(2)}) collective-permute-start(s16[1040,256]{1,0:T(8,128)(2,1)S(1)} %hop.3), channel_id=1, source_target_pairs={{0,1},{1,2},{4,5},{5,6},{8,9},{9,10},{12,13},{13,14},{16,17},{17,1... | collective-permute-start | bytes 1597448 | tf_op jit(solution)/shard_map/ppermute | solution.py:464
  72.7 0.4 combine.4
  73.0 1.6 %collective-permute-start.24 = (s16[2096,128]{1,0:T(8,128)(2,1)S(1)}, s16[2096,128]{1,0:T(8,128)(2,1)S(1)}, u32[]{:S(2)}, u32[]{:S(2)}) collective-permute-start(s16[2096,128]{1,0:T(8,128)(2,1)S(1)} %combine.4), channel_id=1, source_target_pairs={{0,8},{4,12},{8,0},{12,4},{16,24},{20,28},{24,16},{28,20},{1,9},{5... | collective-permute-start | bytes 1609736 | tf_op jit(solution)/shard_map/ppermute | solution.py:461
  74.6 0.4 combine.5
  75.0 0.6 collective-permute-start.23
  75.9 1.6 %collective-permute-start.22 = (s16[2096,128]{1,0:T(8,128)(2,1)S(1)}, s16[2096,128]{1,0:T(8,128)(2,1)S(1)}, u32[]{:S(2)}, u32[]{:S(2)}) collective-permute-start(s16[2096,128]{1,0:T(8,128)(2,1)S(1)} %combine.6), channel_id=1, source_target_pairs={{0,24},{4,28},{8,16},{12,20},{16,8},{20,12},{24,0},{28,4},{1,25},{... | collective-permute-start | bytes 1609736 | tf_op jit(solution)/shard_map/ppermute | solution.py:461
  77.5 6.6 %collective-permute-done.14.arrived_ref = s16[1040,256]{1,0:T(8,128)(2,1)S(1)} collective-permute-done((s16[1040,256]{1,0:T(8,128)(2,1)S(1)}, s16[1040,256]{1,0:T(8,128)(2,1)S(1)}, u32[]{:S(2)}, u32[]{:S(2)}) %collective-permute-start.14) | collective-permute-done | bytes 532512 | tf_op jit(solution)/shard_map/ppermute | solution.py:464
  84.8 1.3 %collective-permute-start.20 = (s16[1040,256]{1,0:T(8,128)(2,1)S(1)}, s16[1040,256]{1,0:T(8,128)(2,1)S(1)}, u32[]{:S(2)}, u32[]{:S(2)}) collective-permute-start(s16[1040,256]{1,0:T(8,128)(2,1)S(1)} %hop.5), channel_id=1, source_target_pairs={{3,2},{2,1},{1,0},{7,6},{6,5},{5,4},{11,10},{10,9},{9,8},{15,14},{... | collective-permute-start | bytes 1597448 | tf_op jit(solution)/shard_map/ppermute | solution.py:467
  86.1 5.4 %collective-permute-start.19 = (s16[1040,256]{1,0:T(8,128)(2,1)S(1)}, s16[1040,256]{1,0:T(8,128)(2,1)S(1)}, u32[]{:S(2)}, u32[]{:S(2)}) collective-permute-start(s16[1040,256]{1,0:T(8,128)(2,1)S(1)} %hop.4), channel_id=1, source_target_pairs={{0,1},{1,2},{2,3},{4,5},{5,6},{6,7},{8,9},{9,10},{10,11},{12,13},{... | collective-permute-start | bytes 1597448 | tf_op jit(solution)/shard_map/ppermute | solution.py:464
  91.5 6.7 %grad_inputs.1 = bf16[1024,2048]{1,0:T(8,128)(2,1)} custom-call(s32[1]{0:T(128)} %bitcast.place_ref, bf16[2048,1024]{1,0:T(8,128)(2,1)S(1)} %get-tuple-element.67.weight_ref, bf16[1024,256]{1,0:T(8,128)(2,1)S(1)} %copy-done.4, bf16[1040,256]{1,0:T(8,128)(2,1)S(1)} %collective-permute-done.refs_0_.r1, ...), custom_call_target="tpu_custom_call" | custom-call | flops 4294967296 | bytes 12582912 | tf_op jit(solution)/shard_map/grad_inputs/pallas_call | solution.py:432
  98.3 2.3 %collective-permute-done.20.left_ref = s16[1040,256]{1,0:T(8,128)(2,1)S(1)} collective-permute-done((s16[1040,256]{1,0:T(8,128)(2,1)S(1)}, s16[1040,256]{1,0:T(8,128)(2,1)S(1)}, u32[]{:S(2)}, u32[]{:S(2)}) %collective-permute-start.20) | collective-permute-done | bytes 532512 | tf_op jit(solution)/shard_map/ppermute | solution.py:467
  100.6 1.2 %collective-permute-done.19.right_ref = s16[1040,256]{1,0:T(8,128)(2,1)S(1)} collective-permute-done((s16[1040,256]{1,0:T(8,128)(2,1)S(1)}, s16[1040,256]{1,0:T(8,128)(2,1)S(1)}, u32[]{:S(2)}, u32[]{:S(2)}) %collective-permute-start.19) | collective-permute-done | bytes 532512 | tf_op jit(solution)/shard_map/ppermute | solution.py:464
  101.8 1.1 %last_hop.1 = bf16[1024,256]{1,0:T(8,128)(2,1)} custom-call(s32[1]{0:T(128)} %bitcast.place_ref, f32[1024,1024]{1,0:T(8,128)S(1)} %partial_values.1.partial_ref, s16[1040,256]{1,0:T(8,128)(2,1)S(1)} %collective-permute-done.19.right_ref, s16[1040,256]{1,0:T(8,128)(2,1)S(1)} %collective-permute-done.20.left_ref), custom_call_target="tpu_custom_call" | custom-call | flops 1 | bytes 1 | tf_op jit(solution)/shard_map/last_hop/pallas_call | solution.py:234
  102.9 1.9 %normalized_update.1 = bf16[16,128,128]{2,1,0:T(8,128)(2,1)} custom-call(f32[2048,128]{1,0:T(8,128)S(1)} %combine.7.refs_0_, s16[2096,128]{1,0:T(8,128)(2,1)S(1)} %collective-permute-done.22.refs_1_, s16[2096,128]{1,0:T(8,128)(2,1)S(1)} %collective-permute-done.23.refs_2_, s16[2096,128]{1,0:T(8,128)(2,1)S(1)} %collective-permute-done.24.refs_3_), custom_call_target="tpu_custom_call" | custom-call | flops 1 | bytes 1 | tf_op jit(solution)/shard_map/normalized_update/pallas_call | solution.py:396
  (35 shorter events, 2.0 us)
Async XLA Ops:
  0.6 1.0 copy-start.2
  1.7 1.0 copy-start.5
  2.7 0.7 copy-start.6
  3.4 0.7 copy-start.7
  5.5 10.4 %collective-permute-start.2 = (bf16[2064,128]{1,0:T(8,128)(2,1)S(1)}, bf16[2064,128]{1,0:T(8,128)(2,1)S(1)}, u32[]{:S(2)}, u32[]{:S(2)}) collective-permute-start(bf16[2064,128]{1,0:T(8,128)(2,1)S(1)} %get-tuple-element.59.refs_0_), channel_id=1, source_target_pairs={{0,4},{4,0},{8,12},{12,8},{16,20},{20,16},{24,28},{28,24},{1,5},{5... | collective-permute-start | bytes 1585160 | tf_op jit(solution)/shard_map/ppermute | solution.py:461
  6.0 17.4 %collective-permute-start.1 = (bf16[1040,256]{1,0:T(8,128)(2,1)}, bf16[1040,256]{1,0:T(8,128)(2,1)S(1)}, u32[]{:S(2)}, u32[]{:S(2)}) collective-permute-start(bf16[1040,256]{1,0:T(8,128)(2,1)} %get-tuple-element.48), channel_id=1, source_target_pairs={{3,2},{2,1},{1,0},{7,6},{6,5},{5,4},{11,10},{10,9},{9,8},{15,14},{... | collective-permute-start | bytes 1597448 | tf_op jit(solution)/shard_map/ppermute | solution.py:467
  7.3 17.4 %collective-permute-start = (bf16[1040,256]{1,0:T(8,128)(2,1)}, bf16[1040,256]{1,0:T(8,128)(2,1)S(1)}, u32[]{:S(2)}, u32[]{:S(2)}) collective-permute-start(bf16[1040,256]{1,0:T(8,128)(2,1)} %get-tuple-element.48), channel_id=1, source_target_pairs={{0,1},{1,2},{2,3},{4,5},{5,6},{6,7},{8,9},{9,10},{10,11},{12,13},{... | collective-permute-start | bytes 1597448 | tf_op jit(solution)/shard_map/ppermute | solution.py:464
  12.4 15.9 %collective-permute-start.7 = (bf16[2064,128]{1,0:T(8,128)(2,1)S(1)}, bf16[2064,128]{1,0:T(8,128)(2,1)S(1)}, u32[]{:S(2)}, u32[]{:S(2)}) collective-permute-start(bf16[2064,128]{1,0:T(8,128)(2,1)S(1)} %get-tuple-element.59.refs_0_), channel_id=1, source_target_pairs={{0,24},{4,28},{8,16},{12,20},{16,8},{20,12},{24,0},{28,4},{1,25},{... | collective-permute-start | bytes 1585160 | tf_op jit(solution)/shard_map/ppermute | solution.py:461
  15.4 23.5 %collective-permute-start.6 = (bf16[2064,128]{1,0:T(8,128)(2,1)S(1)}, bf16[2064,128]{1,0:T(8,128)(2,1)S(1)}, u32[]{:S(2)}, u32[]{:S(2)}) collective-permute-start(bf16[2064,128]{1,0:T(8,128)(2,1)S(1)} %get-tuple-element.59.refs_0_), channel_id=1, source_target_pairs={{0,16},{4,20},{8,24},{12,28},{16,0},{20,4},{24,8},{28,12},{1,17},{... | collective-permute-start | bytes 1585160 | tf_op jit(solution)/shard_map/ppermute | solution.py:461
  15.9 23.3 %collective-permute-start.5 = (bf16[2064,128]{1,0:T(8,128)(2,1)S(1)}, bf16[2064,128]{1,0:T(8,128)(2,1)}, u32[]{:S(2)}, u32[]{:S(2)}) collective-permute-start(bf16[2064,128]{1,0:T(8,128)(2,1)S(1)} %get-tuple-element.59.refs_0_), channel_id=1, source_target_pairs={{0,8},{4,12},{8,0},{12,4},{16,24},{20,28},{24,16},{28,20},{1,9},{5... | collective-permute-start | bytes 1585160 | tf_op jit(solution)/shard_map/ppermute | solution.py:461
  16.0 2.2 %copy-start = (bf16[1024,2048]{1,0:T(8,128)(2,1)S(1)}, bf16[1024,2048]{1,0:T(8,128)(2,1)}, u32[]{:S(2)}) copy-start(bf16[1024,2048]{1,0:T(8,128)(2,1)} %normed_ref.11) | copy-start | bytes 12582916
  18.2 1.0 copy-start.3
  19.3 7.4 %copy-start.1 = (bf16[1024,2048]{1,0:T(8,128)(2,1)S(1)}, bf16[1024,2048]{1,0:T(8,128)(2,1)}, u32[]{:S(2)}) copy-start(bf16[1024,2048]{1,0:T(8,128)(2,1)} %normed_ref.11) | copy-start | bytes 12582916
  24.7 17.9 %collective-permute-start.4 = (bf16[1040,256]{1,0:T(8,128)(2,1)S(1)}, bf16[1040,256]{1,0:T(8,128)(2,1)S(1)}, u32[]{:S(2)}, u32[]{:S(2)}) collective-permute-start(bf16[1040,256]{1,0:T(8,128)(2,1)S(1)} %collective-permute-done.1.refs_1_.l1), channel_id=1, source_target_pairs={{2,1},{1,0},{6,5},{5,4},{10,9},{9,8},{14,13},{13,12},{18,17},{17,1... | collective-permute-start | bytes 1597448 | tf_op jit(solution)/shard_map/ppermute | solution.py:467
  26.0 16.6 %collective-permute-start.3 = (bf16[1040,256]{1,0:T(8,128)(2,1)S(1)}, bf16[1040,256]{1,0:T(8,128)(2,1)S(1)}, u32[]{:S(2)}, u32[]{:S(2)}) collective-permute-start(bf16[1040,256]{1,0:T(8,128)(2,1)S(1)} %collective-permute-done.refs_0_.r1), channel_id=1, source_target_pairs={{1,2},{2,3},{5,6},{6,7},{9,10},{10,11},{13,14},{14,15},{17,18},{18... | collective-permute-start | bytes 1597448 | tf_op jit(solution)/shard_map/ppermute | solution.py:464
  39.2 2.8 %collective-permute-start.8 = (bf16[2064,128]{1,0:T(8,128)(2,1)}, bf16[2064,128]{1,0:T(8,128)(2,1)S(1)}, u32[]{:S(2)}, u32[]{:S(2)}) collective-permute-start(bf16[2064,128]{1,0:T(8,128)(2,1)} %collective-permute-done.5.refs_2_), channel_id=1, source_target_pairs={{0,4},{4,0},{8,12},{12,8},{16,20},{20,16},{24,28},{28,24},{1,5},{5... | collective-permute-start | bytes 1585160 | tf_op jit(solution)/shard_map/ppermute | solution.py:461
  39.2 2.8 %collective-permute-start.9 = (bf16[2064,128]{1,0:T(8,128)(2,1)S(1)}, bf16[2064,128]{1,0:T(8,128)(2,1)S(1)}, u32[]{:S(2)}, u32[]{:S(2)}) collective-permute-start(bf16[2064,128]{1,0:T(8,128)(2,1)S(1)} %collective-permute-done.6.refs_4_), channel_id=1, source_target_pairs={{0,4},{4,0},{8,12},{12,8},{16,20},{20,16},{24,28},{28,24},{1,5},{5... | collective-permute-start | bytes 1585160 | tf_op jit(solution)/shard_map/ppermute | solution.py:461
  39.7 2.9 %collective-permute-start.10 = (bf16[2064,128]{1,0:T(8,128)(2,1)S(1)}, bf16[2064,128]{1,0:T(8,128)(2,1)S(1)}, u32[]{:S(2)}, u32[]{:S(2)}) collective-permute-start(bf16[2064,128]{1,0:T(8,128)(2,1)S(1)} %collective-permute-done.7.refs_6_), channel_id=1, source_target_pairs={{0,4},{4,0},{8,12},{12,8},{16,20},{20,16},{24,28},{28,24},{1,5},{5... | collective-permute-start | bytes 1585160 | tf_op jit(solution)/shard_map/ppermute | solution.py:461
  42.6 17.6 %collective-permute-start.12 = (bf16[1040,256]{1,0:T(8,128)(2,1)S(1)}, bf16[1040,256]{1,0:T(8,128)(2,1)S(1)}, u32[]{:S(2)}, u32[]{:S(2)}) collective-permute-start(bf16[1040,256]{1,0:T(8,128)(2,1)S(1)} %collective-permute-done.3.refs_1_.r2), channel_id=1, source_target_pairs={{2,3},{6,7},{10,11},{14,15},{18,19},{22,23},{26,27},{30,31}} | collective-permute-start | bytes 1597448 | tf_op jit(solution)/shard_map/ppermute | solution.py:464
  43.3 16.9 %collective-permute-start.13 = (bf16[1040,256]{1,0:T(8,128)(2,1)S(1)}, bf16[1040,256]{1,0:T(8,128)(2,1)S(1)}, u32[]{:S(2)}, u32[]{:S(2)}) collective-permute-start(bf16[1040,256]{1,0:T(8,128)(2,1)S(1)} %collective-permute-done.4.refs_2_.l2), channel_id=1, source_target_pairs={{1,0},{5,4},{9,8},{13,12},{17,16},{21,20},{25,24},{29,28}} | collective-permute-start | bytes 1597448 | tf_op jit(solution)/shard_map/ppermute | solution.py:467
  49.6 16.0 %collective-permute-start.11 = (s16[1040,256]{1,0:T(8,128)(2,1)S(1)}, s16[1040,256]{1,0:T(8,128)(2,1)S(1)}, u32[]{:S(2)}, u32[]{:S(2)}) collective-permute-start(s16[1040,256]{1,0:T(8,128)(2,1)S(1)} %get-tuple-element.69), channel_id=1, source_target_pairs={{0,1},{3,2},{4,5},{7,6},{8,9},{11,10},{12,13},{15,14},{16,17},{19,... | collective-permute-start | bytes 1597448 | tf_op jit(solution)/shard_map/ppermute | solution.py:487
  65.5 2.1 %collective-permute-start.16 = (s16[2096,128]{1,0:T(8,128)(2,1)S(1)}, s16[2096,128]{1,0:T(8,128)(2,1)S(1)}, u32[]{:S(2)}, u32[]{:S(2)}) collective-permute-start(s16[2096,128]{1,0:T(8,128)(2,1)S(1)} %get-tuple-element.84), channel_id=1, source_target_pairs={{0,4},{4,0},{8,12},{12,8},{16,20},{20,16},{24,28},{28,24},{1,5},{5... | collective-permute-start | bytes 1609736 | tf_op jit(solution)/shard_map/ppermute | solution.py:461
  65.5 7.5 %collective-permute-start.17 = (s16[2096,128]{1,0:T(8,128)(2,1)S(1)}, s16[2096,128]{1,0:T(8,128)(2,1)S(1)}, u32[]{:S(2)}, u32[]{:S(2)}) collective-permute-start(s16[2096,128]{1,0:T(8,128)(2,1)S(1)} %get-tuple-element.86), channel_id=1, source_target_pairs={{0,4},{4,0},{8,12},{12,8},{16,20},{20,16},{24,28},{28,24},{1,5},{5... | collective-permute-start | bytes 1609736 | tf_op jit(solution)/shard_map/ppermute | solution.py:461
  66.1 8.9 %collective-permute-start.18 = (s16[2096,128]{1,0:T(8,128)(2,1)S(1)}, s16[2096,128]{1,0:T(8,128)(2,1)S(1)}, u32[]{:S(2)}, u32[]{:S(2)}) collective-permute-start(s16[2096,128]{1,0:T(8,128)(2,1)S(1)} %get-tuple-element.88), channel_id=1, source_target_pairs={{0,4},{4,0},{8,12},{12,8},{16,20},{20,16},{24,28},{28,24},{1,5},{5... | collective-permute-start | bytes 1609736 | tf_op jit(solution)/shard_map/ppermute | solution.py:461
  66.1 20.1 %collective-permute-start.21 = (s16[2096,128]{1,0:T(8,128)(2,1)S(1)}, s16[2096,128]{1,0:T(8,128)(2,1)S(1)}, u32[]{:S(2)}, u32[]{:S(2)}) collective-permute-start(s16[2096,128]{1,0:T(8,128)(2,1)S(1)} %get-tuple-element.92), channel_id=1, source_target_pairs={{0,4},{4,0},{8,12},{12,8},{16,20},{20,16},{24,28},{28,24},{1,5},{5... | collective-permute-start | bytes 1609736 | tf_op jit(solution)/shard_map/ppermute | solution.py:461
  66.9 9.0 %collective-permute-start.15 = (s16[1040,256]{1,0:T(8,128)(2,1)S(1)}, s16[1040,256]{1,0:T(8,128)(2,1)S(1)}, u32[]{:S(2)}, u32[]{:S(2)}) collective-permute-start(s16[1040,256]{1,0:T(8,128)(2,1)S(1)} %hop.3), channel_id=1, source_target_pairs={{3,2},{2,1},{7,6},{6,5},{11,10},{10,9},{15,14},{14,13},{19,18},{18... | collective-permute-start | bytes 1597448 | tf_op jit(solution)/shard_map/ppermute | solution.py:467
  67.6 16.5 %collective-permute-start.14 = (s16[1040,256]{1,0:T(8,128)(2,1)S(1)}, s16[1040,256]{1,0:T(8,128)(2,1)S(1)}, u32[]{:S(2)}, u32[]{:S(2)}) collective-permute-start(s16[1040,256]{1,0:T(8,128)(2,1)S(1)} %hop.3), channel_id=1, source_target_pairs={{0,1},{1,2},{4,5},{5,6},{8,9},{9,10},{12,13},{13,14},{16,17},{17,1... | collective-permute-start | bytes 1597448 | tf_op jit(solution)/shard_map/ppermute | solution.py:464
  73.0 29.9 %collective-permute-start.24 = (s16[2096,128]{1,0:T(8,128)(2,1)S(1)}, s16[2096,128]{1,0:T(8,128)(2,1)S(1)}, u32[]{:S(2)}, u32[]{:S(2)}) collective-permute-start(s16[2096,128]{1,0:T(8,128)(2,1)S(1)} %combine.4), channel_id=1, source_target_pairs={{0,8},{4,12},{8,0},{12,4},{16,24},{20,28},{24,16},{28,20},{1,9},{5... | collective-permute-start | bytes 1609736 | tf_op jit(solution)/shard_map/ppermute | solution.py:461
  75.0 27.9 %collective-permute-start.23 = (s16[2096,128]{1,0:T(8,128)(2,1)S(1)}, s16[2096,128]{1,0:T(8,128)(2,1)S(1)}, u32[]{:S(2)}, u32[]{:S(2)}) collective-permute-start(s16[2096,128]{1,0:T(8,128)(2,1)S(1)} %combine.5), channel_id=1, source_target_pairs={{0,16},{4,20},{8,24},{12,28},{16,0},{20,4},{24,8},{28,12},{1,17},{... | collective-permute-start | bytes 1609736 | tf_op jit(solution)/shard_map/ppermute | solution.py:461
  75.9 15.6 %copy-start.4 = (bf16[1024,256]{1,0:T(8,128)(2,1)S(1)}, bf16[1024,256]{1,0:T(8,128)(2,1)}, u32[]{:S(2)}) copy-start(bf16[1024,256]{1,0:T(8,128)(2,1)} %own.1) | copy-start | bytes 1572868
  75.9 27.0 %collective-permute-start.22 = (s16[2096,128]{1,0:T(8,128)(2,1)S(1)}, s16[2096,128]{1,0:T(8,128)(2,1)S(1)}, u32[]{:S(2)}, u32[]{:S(2)}) collective-permute-start(s16[2096,128]{1,0:T(8,128)(2,1)S(1)} %combine.6), channel_id=1, source_target_pairs={{0,24},{4,28},{8,16},{12,20},{16,8},{20,12},{24,0},{28,4},{1,25},{... | collective-permute-start | bytes 1609736 | tf_op jit(solution)/shard_map/ppermute | solution.py:461
  84.8 15.8 %collective-permute-start.20 = (s16[1040,256]{1,0:T(8,128)(2,1)S(1)}, s16[1040,256]{1,0:T(8,128)(2,1)S(1)}, u32[]{:S(2)}, u32[]{:S(2)}) collective-permute-start(s16[1040,256]{1,0:T(8,128)(2,1)S(1)} %hop.5), channel_id=1, source_target_pairs={{3,2},{2,1},{1,0},{7,6},{6,5},{5,4},{11,10},{10,9},{9,8},{15,14},{... | collective-permute-start | bytes 1597448 | tf_op jit(solution)/shard_map/ppermute | solution.py:467
  86.1 15.7 %collective-permute-start.19 = (s16[1040,256]{1,0:T(8,128)(2,1)S(1)}, s16[1040,256]{1,0:T(8,128)(2,1)S(1)}, u32[]{:S(2)}, u32[]{:S(2)}) collective-permute-start(s16[1040,256]{1,0:T(8,128)(2,1)S(1)} %hop.4), channel_id=1, source_target_pairs={{0,1},{1,2},{2,3},{4,5},{5,6},{6,7},{8,9},{9,10},{10,11},{12,13},{... | collective-permute-start | bytes 1597448 | tf_op jit(solution)/shard_map/ppermute | solution.py:464

commit v5 on v4

--- a/solution.py
+++ b/solution.py
@@ -98,7 +98,7 @@
 def pack(rows, columns, tiles, chunk, column_blocks):
     return pl.pallas_call(
         functools.partial(pack_kernel, column_blocks),
-        in_specs=[pl.BlockSpec(memory_space=pl.ANY)] * 4,
+        in_specs=[pl.BlockSpec(memory_space=pltpu.HBM)] * 4,
         out_specs=[VMEM, VMEM],
         out_shape=[
             jax.ShapeDtypeStruct((tiles.shape[0] + PAD, tiles.shape[1]), tiles.dtype),
@@ -108,7 +108,7 @@
             pltpu.SMEM((2,) + rows.shape, jnp.int32),
             pltpu.SemaphoreType.DMA((4,)),
         ],
-        compiler_params=params(8),
+        compiler_params=params(63),
         cost_estimate=LITTLE,
         name="pack",
     )(rows, columns, tiles, chunk)
@@ -170,35 +170,39 @@
     )(place, normed, *messages)
 
 
-def partial_kernel(normed_ref, weight_ref, partial_ref):
-    step = 512
+def partial_kernel(place_ref, normed_ref, weight_ref, partial_ref, second_ref):
+    rows, chunk_width = normed_ref.shape[0], second_ref.shape[1]
+    step = 2 * chunk_width
     for n in range(partial_ref.shape[1] // step):
         span = slice(n * step, (n + 1) * step)
         partial_ref[:, span] = jnp.dot(
             normed_ref[...], weight_ref[:, span], preferred_element_type=jnp.float32
         )
-
-
-def partial_values(normed, weight):
+    columns = aligned(place_ref[0] ^ 2, chunk_width)
+    write_message(
+        second_ref, rows, lambda group: partial_ref[group * GROUP : (group + 1) * GROUP, columns]
+    )
+
+
+def partial_values(place, normed, weight, message_shape):
     return pl.pallas_call(
         partial_kernel,
-        in_specs=[VMEM, VMEM],
-        out_specs=VMEM,
-        out_shape=jax.ShapeDtypeStruct((normed.shape[0], weight.shape[1]), jnp.float32),
+        in_specs=[SMEM, VMEM, VMEM],
+        out_specs=[VMEM, VMEM],
+        out_shape=[
+            jax.ShapeDtypeStruct((normed.shape[0], weight.shape[1]), jnp.float32),
+            jax.ShapeDtypeStruct(message_shape, jnp.int16),
+        ],
         compiler_params=params(20),
         cost_estimate=LITTLE,
         name="partial_values",
-    )(normed, weight)
-
-
-def chunk_of(place_ref, ahead, partial_ref, width):
-    return aligned(lax.rem(place_ref[0] + ahead, partial_ref.shape[1] // width), width)
-
-
-def hop_kernel(ahead, place_ref, partial_ref, arrived_ref, message_ref):
+    )(place, normed, weight)
+
+
+def hop_kernel(pick, place_ref, partial_ref, arrived_ref, message_ref):
     rows, width = partial_ref.shape[0], message_ref.shape[1]
     arrived = read_message(arrived_ref, rows)
-    columns = chunk_of(place_ref, ahead, partial_ref, width)
+    columns = aligned(pick(place_ref[0]), width)
 
     def total(group):
         return partial_ref[group * GROUP : (group + 1) * GROUP, columns] + arrived(group)
@@ -206,9 +210,9 @@
     write_message(message_ref, rows, total)
 
 
-def hop(place, ahead, partial, arrived):
-    return pl.pallas_call(
-        functools.partial(hop_kernel, ahead),
+def hop(pick, place, partial, arrived):
+    return pl.pallas_call(
+        functools.partial(hop_kernel, pick),
         in_specs=[SMEM, VMEM, VMEM],
         out_specs=VMEM,
         out_shape=jax.ShapeDtypeStruct(arrived.shape, jnp.int16),
@@ -222,7 +226,7 @@
     rows, width = values_ref.shape
     right = read_message(right_ref, rows)
     left = read_message(left_ref, rows)
-    columns = chunk_of(place_ref, 0, partial_ref, width)
+    columns = aligned(place_ref[0], width)
     for group in range(rows // GROUP):
         span = slice(group * GROUP, (group + 1) * GROUP)
         total = partial_ref[span, columns] + right(group) + left(group)
@@ -245,22 +249,10 @@
 def chunk_order(place):
     return (
         place,
-        jnp.where(place == 3, 2, place + 1),
-        jnp.where(place == 0, 2, jnp.where(place == 1, 0, 1)),
+        place ^ 1,
+        jnp.where(place < 2, 2, 1),
         jnp.where(place < 2, 3, 0),
     )
-
-
-def second_chunk(place, r1, l1):
-    return jnp.where(place == 3, r1, l1)
-
-
-def third_chunk(place, r1, r2, l2):
-    return jnp.where((place == 1) | (place == 2), r1, r2 + l2)
-
-
-def fourth_chunk(place, r2, l2, r3, l3):
-    return jnp.where((place == 1) | (place == 2), r2 + l2, r3 + l3)
 
 
 def product(turned, normed_ref, out_ref):
@@ -270,26 +262,28 @@
         out_ref[:, span] = jnp.dot(turned, normed_ref[:, span], preferred_element_type=jnp.float32)
 
 
-def chunk_kernel(pick, place_ref, normed_ref, *refs):
-    tokens = normed_ref.shape[0]
-    chunk = pick(place_ref[0], *[ref[:tokens, :] for ref in refs[:-1]])
-    product(chunk.T, normed_ref, refs[-1])
-
-
-def chunk_gradient(pick, place, normed, *chunks):
-    return pl.pallas_call(
-        functools.partial(chunk_kernel, pick),
-        in_specs=[SMEM, VMEM] + [VMEM] * len(chunks),
+def joined(tokens, refs):
+    return functools.reduce(jnp.add, [ref[:tokens, :] for ref in refs])
+
+
+def chunk_kernel(normed_ref, *refs):
+    product(joined(normed_ref.shape[0], refs[:-1]).T, normed_ref, refs[-1])
+
+
+def chunk_gradient(normed, *chunks):
+    return pl.pallas_call(
+        chunk_kernel,
+        in_specs=[VMEM] + [VMEM] * len(chunks),
         out_specs=VMEM,
         out_shape=jax.ShapeDtypeStruct((chunks[0].shape[1], normed.shape[1]), jnp.float32),
         compiler_params=params(16),
         cost_estimate=LITTLE,
         name="chunk_gradient",
-    )(place, normed, *chunks)
+    )(normed, *chunks)
 
 
 def slots_kernel(
-    chips, column_blocks, codes_ref, place_ref, normed_ref, r2, l2, r3, l3, g1, g2, g3, *refs
+    chips, column_blocks, codes_ref, place_ref, normed_ref, m2, d3, g1, g2, g3, *refs
 ):
     keep_refs = refs[:chips]
     send_refs = refs[chips : 2 * chips]
@@ -300,9 +294,7 @@
     ]
     for copy in copies:
         copy.start()
-    tokens = normed_ref.shape[0]
-    chunk = fourth_chunk(place, *[ref[:tokens, :] for ref in (r2, l2, r3, l3)])
-    product(chunk.T, normed_ref, gradient.at[3])
+    product(joined(normed_ref.shape[0], (m2, d3)).T, normed_ref, gradient.at[3])
     for copy in copies:
         copy.wait()
     order = chunk_order(place)
@@ -404,18 +396,12 @@
     )(kept, *arrived)
 
 
-def grad_input_kernel(place_ref, weight_ref, own, r1, r2, r3, l1, l2, l3, out_ref, cotangent):
+def grad_input_kernel(place_ref, weight_ref, own, a1, b1, e2, m2, d3, out_ref, cotangent):
     @pl.when(pl.program_id(0) == 0)
     def _():
-        place = place_ref[0]
-        order = chunk_order(place)
-        width = own.shape[1]
-        arrived = (r1, r2, r3, l1, l2, l3)
-        v1, v2, v3, w1, w2, w3 = (ref[: own.shape[0], :] for ref in arrived)
-        cotangent[:, aligned(order[0], width)] = own[...]
-        cotangent[:, aligned(order[1], width)] = second_chunk(place, v1, w1)
-        cotangent[:, aligned(order[2], width)] = third_chunk(place, v1, v2, w2)
-        cotangent[:, aligned(order[3], width)] = fourth_chunk(place, v2, w2, v3, w3)
+        tokens, width = own.shape
+        for chunk, refs in zip(chunk_order(place_ref[0]), ((own,), (a1,), (b1, e2), (m2, d3))):
+            cotangent[:, aligned(chunk, width)] = joined(tokens, refs)
 
     out_ref[...] = lax.dot_general(
         cotangent[...],
@@ -460,52 +446,56 @@
     def swap(x, mask):
         return lax.ppermute(x, "fsdp", [(i, i ^ mask) for i in range(devices)])
 
-    def right(x, *sources):
-        return lax.ppermute(x, "tensor", [(i, i + 1) for i in sources])
-
-    def left(x, *sources):
-        return lax.ppermute(x, "tensor", [(i, i - 1) for i in sources])
+    def pairs(x):
+        return lax.ppermute(x, "tensor", [(0, 1), (1, 0), (2, 3), (3, 2)])
+
+    def middle(x):
+        return lax.ppermute(x, "tensor", [(1, 2), (2, 1)])
+
+    def outward(x):
+        return lax.ppermute(x, "tensor", [(1, 0), (2, 3)])
+
+    def inward(x):
+        return lax.ppermute(x, "tensor", [(0, 1), (3, 2)])
 
     message, padded = pack(
         tile_rows, tile_columns, tile_values.reshape(rows, tile), cotangent, column_blocks
     )
-    r1, l1 = right(padded, 0, 1, 2), left(padded, 3, 2, 1)
-    g1 = chunk_gradient(lambda place, own: own, place, normed, cotangent)
+    a1, b1 = pairs(padded), middle(padded)
+    g1 = chunk_gradient(normed, cotangent)
     same_core = [message] + [swap(message, 2 * chip) for chip in range(1, chips)]
     beside = swap(message, 1)
-    r1, l1, g1, beside = lax.optimization_barrier((r1, l1, g1, beside))
-    r2, l2 = right(r1, 1, 2), left(l1, 2, 1)
-    g2 = chunk_gradient(second_chunk, place, normed, r1, l1)
+    a1, b1, g1, beside = lax.optimization_barrier((a1, b1, g1, beside))
+    m2, e2 = middle(a1), outward(b1)
+    g2 = chunk_gradient(normed, a1)
     *same_core, g2 = lax.optimization_barrier((*same_core, g2))
     gathered = [same_core[0], beside]
     for m in same_core[1:]:
         gathered += [m, swap(m, 1)]
-    r2, l2, *gathered = lax.optimization_barrier((r2, l2, *gathered))
-    r3, l3 = right(r2, 2), left(l2, 1)
+    d3 = outward(m2)
 
     weight, first, codes = first_values(place, normed, gathered, parts, column_blocks)
-    arrived = lax.ppermute(first, "tensor", [(0, 1), (3, 2)])
-    partial = partial_values(normed, weight)
-    g3 = chunk_gradient(third_chunk, place, normed, r1, r2, l2)
-    g3, partial = lax.optimization_barrier((g3, partial))
-    keep, send = slot_terms(
-        codes, place, normed, (r2, l2, r3, l3), (g1, g2, g3), capacity, column_blocks
-    )
+    arrived = inward(first)
+    partial, second = partial_values(place, normed, weight, first.shape)
+    g3 = chunk_gradient(normed, b1, e2)
+    g3, partial, second = lax.optimization_barrier((g3, partial, second))
+    keep, send = slot_terms(codes, place, normed, (m2, d3), (g1, g2, g3), capacity, column_blocks)
     arrived, keep, send = lax.optimization_barrier((arrived, keep, send))
 
-    second = hop(place, 2, partial, arrived)
-    from_left, from_right = right(second, 0, 1), left(second, 3, 2)
+    to_middle = inward(second)
+    crossing = middle(hop(lambda p: p ^ 2, place, partial, arrived))
     other = [swap(m, 1) for m in send]
     sums = [combine(keep[chip], other[chip], jnp.int16) for chip in range(1, chips)]
-    from_left, from_right, _ = lax.optimization_barrier((from_left, from_right, sums))
+    crossing, to_middle, _ = lax.optimization_barrier((crossing, to_middle, sums))
     terms = [swap(m, 2 * chip) for chip, m in reversed(list(enumerate(sums, 1)))]
     own = combine(keep[0], other[0], jnp.float32)
 
-    from_left = right(hop(place, 1, partial, from_left), 0, 1, 2)
-    from_right = left(hop(place, 3, partial, from_right), 3, 2, 1)
-    grad_input = grad_inputs(place, weight, cotangent, r1, r2, r3, l1, l2, l3)
-    values = last_hop(place, partial, from_left, from_right)
+    by_pair = pairs(hop(lambda p: p ^ 1, place, partial, crossing))
+    by_middle = middle(hop(lambda p: 3 - p, place, partial, to_middle))
+    grad_input = grad_inputs(place, weight, cotangent, a1, b1, e2, m2, d3)
     update = normalized_update(own, terms, tile_values.shape[1:])
+    by_pair, by_middle, update = lax.optimization_barrier((by_pair, by_middle, update))
+    values = last_hop(place, partial, by_pair, by_middle)
     return values, grad_input, update[None]
 
 

time: 106 us -> 105 us (level)
  starting transfers between devices: 36.9 us -> 31.3 us
  Pallas kernels: 31.6 us -> 35.9 us
  local copies, waits for them, and re-layouts: 6.63 us -> 9.66 us
  waiting for transfers between devices: 28.8 us -> 26.4 us
    ppermute x11 -> x10, starting transfers between devices: 27.6 us -> 21.9 us  [the longest x2 9.79 us: pairs(): return lax.ppermute(x, 'tensor', [(0, 1), (1, 0), (2, 3), (3, 2)])]
    unnamed x16 -> x22, local copies, waits for them, and re-layouts: 6.63 us -> 9.66 us
    ppermute x14, waiting for transfers between devices: 14.1 us -> 11.1 us  [swap(): return lax.ppermute(x, 'fsdp', [(i, i ^ mask) for i in range(devices)])]
    pallas_call x7, Pallas kernels: 9.42 us -> 10.6 us  [the longest x3 4.89 us: chunk_gradient(): pl.pallas_call(chunk_kernel, in_specs=[VMEM] + [VMEM] * len(chunks), out_...]
    ppermute x11 -> x10, waiting for transfers between devices: 14.7 us -> 15.2 us  [the longest x2 7.16 us: inward(): return lax.ppermute(x, 'tensor', [(0, 1), (3, 2)])]
  transfers between devices with their start and end apart: 25 -> 24, of which waited for: 11 -> 7; matrix products, arithmetic and copies ran while one was open for 0% -> 0% of each run, Pallas kernels for 27% -> 31%
where the time goes in v5:
time: 105 us; the launch traced here: 104 us
  Pallas kernels  35.9 us (34%)
  starting transfers between devices  31.3 us (30%)
  waiting for transfers between devices  26.4 us (25%)
  local copies, waits for them, and re-layouts  9.66 us (9%)
    ppermute x14, waiting for transfers between devices, swap(): return lax.ppermute(x, 'fsdp', [(i, i ^ mask) for i in range(devices)])  11.1 us
    ppermute x2, starting transfers between devices, pairs(): return lax.ppermute(x, 'tensor', [(0, 1), (1, 0), (2, 3), (3, 2)])  9.79 us
    unnamed x22, local copies, waits for them, and re-layouts  9.66 us
    ppermute x14, starting transfers between devices, swap(): return lax.ppermute(x, 'fsdp', [(i, i ^ mask) for i in range(devices)])  9.38 us
    pallas_call x1, Pallas kernels, grad_inputs(): pl.pallas_call(grad_input_kernel, grid_spec=pltpu.PrefetchScalarGridSpec(...  7.7 us
    ppermute x2, waiting for transfers between devices, inward(): return lax.ppermute(x, 'tensor', [(0, 1), (3, 2)])  7.16 us
    pallas_call x1, Pallas kernels, first_values(): pl.pallas_call(functools.partial(first_kernel, column_blocks), in_specs=[...  5.89 us
    ppermute x2, starting transfers between devices, inward(): return lax.ppermute(x, 'tensor', [(0, 1), (3, 2)])  5.78 us
  transfers between devices with their start and end apart: 24, of which 7 were waited for; matrix products, arithmetic and copies ran while one was open for 0% of the time, Pallas kernels for 31%

profile of v5, /device:TPU:0, one launch (start us, length us, event | category | flops | bytes accessed | tf_op | source)
XLA Modules:
  0.0 104.2 jit_solution(9427066127463959288)
XLA Ops:
  0.6 2.2 %pack.1 = (bf16[2064,128]{1,0:T(8,128)(2,1)}, bf16[1040,256]{1,0:T(8,128)(2,1)}) custom-call(s32[1,16]{1,0:T(1,128)} %rows_ref.1, s32[1,16]{1,0:T(1,128)} %columns_ref.1, bf16[2048,128]{1,0:T(8,128)(2,1)} %bitcast.4, bf16[1024,256]{1,0:T(8,128)(2,1)} %own.1), custom_call_target="tpu_custom_call" | custom-call | flops 1 | bytes 1 | tf_op jit(solution)/shard_map/pack/pallas_call | solution.py:99
  2.8 0.5 collective-permute-start.2
  3.4 0.7 collective-permute-start.1
  4.1 5.5 %collective-permute-start = (bf16[1040,256]{1,0:T(8,128)(2,1)}, bf16[1040,256]{1,0:T(8,128)(2,1)}, u32[]{:S(2)}, u32[]{:S(2)}) collective-permute-start(bf16[1040,256]{1,0:T(8,128)(2,1)} %get-tuple-element.44), channel_id=1, source_target_pairs={{0,1},{1,0},{2,3},{3,2},{4,5},{5,4},{6,7},{7,6},{8,9},{9,8},{10,11... | collective-permute-start | bytes 1597448 | tf_op jit(solution)/shard_map/ppermute | solution.py:450
  9.5 2.4 %collective-permute-start.6 = (bf16[2064,128]{1,0:T(8,128)(2,1)}, bf16[2064,128]{1,0:T(8,128)(2,1)}, u32[]{:S(2)}, u32[]{:S(2)}) collective-permute-start(bf16[2064,128]{1,0:T(8,128)(2,1)} %get-tuple-element.48.refs_0_), channel_id=1, source_target_pairs={{0,24},{4,28},{8,16},{12,20},{16,8},{20,12},{24,0},{28,4},{1,25},{... | collective-permute-start | bytes 1585160 | tf_op jit(solution)/shard_map/ppermute | solution.py:447
  12.0 0.5 collective-permute-start.5
  12.5 0.8 copy-done.9
  13.3 0.5 collective-permute-start.4
  13.8 2.2 %copy-done = bf16[1024,2048]{1,0:T(8,128)(2,1)S(1)} copy-done((bf16[1024,2048]{1,0:T(8,128)(2,1)S(1)}, bf16[1024,2048]{1,0:T(8,128)(2,1)}, u32[]{:S(2)}) %copy-start) | copy-done | bytes 4194328
  16.0 1.0 copy-done.6
  17.1 1.3 %chunk_gradient.3.g1 = f32[256,2048]{1,0:T(8,128)S(1)} custom-call(bf16[1024,2048]{1,0:T(8,128)(2,1)S(1)} %copy-done, bf16[1024,256]{1,0:T(8,128)(2,1)S(1)} %copy-done.6), custom_call_target="tpu_custom_call" | custom-call | flops 1 | bytes 1 | tf_op jit(solution)/shard_map/chunk_gradient/pallas_call | solution.py:274
  18.3 3.9 %collective-permute-done.refs_0_.a1 = bf16[1040,256]{1,0:T(8,128)(2,1)} collective-permute-done((bf16[1040,256]{1,0:T(8,128)(2,1)}, bf16[1040,256]{1,0:T(8,128)(2,1)}, u32[]{:S(2)}, u32[]{:S(2)}) %collective-permute-start) | collective-permute-done | bytes 532512 | tf_op jit(solution)/shard_map/ppermute | solution.py:450
  22.3 1.5 %collective-permute-start.11 = (bf16[1040,256]{1,0:T(8,128)(2,1)}, bf16[1040,256]{1,0:T(8,128)(2,1)}, u32[]{:S(2)}, u32[]{:S(2)}) collective-permute-start(bf16[1040,256]{1,0:T(8,128)(2,1)} %collective-permute-done.refs_0_.a1), channel_id=1, source_target_pairs={{1,2},{2,1},{5,6},{6,5},{9,10},{10,9},{13,14},{14,13},{17,18},{18,... | collective-permute-start | bytes 1597448 | tf_op jit(solution)/shard_map/ppermute | solution.py:453
  23.8 2.3 %chunk_gradient.5.g2 = f32[256,2048]{1,0:T(8,128)S(1)} custom-call(bf16[1024,2048]{1,0:T(8,128)(2,1)S(1)} %copy-done.1, bf16[1040,256]{1,0:T(8,128)(2,1)} %collective-permute-done.refs_0_.a1), custom_call_target="tpu_custom_call" | custom-call | flops 1 | bytes 1 | tf_op jit(solution)/shard_map/chunk_gradient/pallas_call | solution.py:274
  26.1 1.3 %copy-done.4 = f32[256,2048]{1,0:T(8,128)} copy-done((f32[256,2048]{1,0:T(8,128)}, f32[256,2048]{1,0:T(8,128)S(1)}, u32[]{:S(2)}) %copy-start.4) | copy-done | bytes 2097176
  27.4 8.5 %collective-permute-done.5.refs_4_ = bf16[2064,128]{1,0:T(8,128)(2,1)} collective-permute-done((bf16[2064,128]{1,0:T(8,128)(2,1)}, bf16[2064,128]{1,0:T(8,128)(2,1)}, u32[]{:S(2)}, u32[]{:S(2)}) %collective-permute-start.5) | collective-permute-done | bytes 528416 | tf_op jit(solution)/shard_map/ppermute | solution.py:447
  36.0 0.5 collective-permute-start.8
  36.5 1.3 %collective-permute-start.3 = (bf16[1040,256]{1,0:T(8,128)(2,1)S(1)}, bf16[1040,256]{1,0:T(8,128)(2,1)S(1)}, u32[]{:S(2)}, u32[]{:S(2)}) collective-permute-start(bf16[1040,256]{1,0:T(8,128)(2,1)S(1)} %collective-permute-done.1.refs_0_.b1), channel_id=1, source_target_pairs={{1,0},{2,3},{5,4},{6,7},{9,8},{10,11},{13,12},{14,15},{17,16},{18,... | collective-permute-start | bytes 1597448 | tf_op jit(solution)/shard_map/ppermute | solution.py:456
  37.8 1.3 %collective-permute-start.12 = (bf16[1040,256]{1,0:T(8,128)(2,1)}, bf16[1040,256]{1,0:T(8,128)(2,1)S(1)}, u32[]{:S(2)}, u32[]{:S(2)}) collective-permute-start(bf16[1040,256]{1,0:T(8,128)(2,1)} %collective-permute-done.11.m2), channel_id=1, source_target_pairs={{1,0},{2,3},{5,4},{6,7},{9,8},{10,11},{13,12},{14,15},{17,16},{18,... | collective-permute-start | bytes 1597448 | tf_op jit(solution)/shard_map/ppermute | solution.py:456
  39.1 0.6 collective-permute-done.9.refs_7_
  39.8 2.2 %copy-done.2 = bf16[1024,2048]{1,0:T(8,128)(2,1)S(1)} copy-done((bf16[1024,2048]{1,0:T(8,128)(2,1)S(1)}, bf16[1024,2048]{1,0:T(8,128)(2,1)}, u32[]{:S(2)}) %copy-start.2) | copy-done | bytes 4194328
  41.9 1.0 copy-done.8
  43.0 1.0 copy-done.10
  44.0 5.9 %first_values.1 = (bf16[2048,1024]{1,0:T(8,128)(2,1)S(1)}, s16[1040,256]{1,0:T(8,128)(2,1)S(1)}, s32[8,128]{1,0:T(8,128)S(1)}) custom-call(s32[1]{0:T(128)} %bitcast.place_ref, bf16[1024,2048]{1,0:T(8,128)(2,1)S(1)} %copy-done.2, bf16[2064,128]{1,0:T(8,128)(2,1)S(1)} %copy-done.8, bf16[2064,128]{1,0:T(8,128)(2,1)S(1)} %copy-done.10, ...), custom_call_target="tpu_custom_call" | custom-call | flops 1 | bytes 1 | tf_op jit(solution)/shard_map/first_values/pallas_call | solution.py:153
  49.9 4.2 %collective-permute-start.10 = (s16[1040,256]{1,0:T(8,128)(2,1)S(1)}, s16[1040,256]{1,0:T(8,128)(2,1)S(1)}, u32[]{:S(2)}, u32[]{:S(2)}) collective-permute-start(s16[1040,256]{1,0:T(8,128)(2,1)S(1)} %get-tuple-element.57), channel_id=1, source_target_pairs={{0,1},{3,2},{4,5},{7,6},{8,9},{11,10},{12,13},{15,14},{16,17},{19,... | collective-permute-start | bytes 1597448 | tf_op jit(solution)/shard_map/ppermute | solution.py:459
  54.2 4.7 %partial_values.1 = (f32[1024,1024]{1,0:T(8,128)S(1)}, s16[1040,256]{1,0:T(8,128)(2,1)S(1)}) custom-call(s32[1]{0:T(128)} %bitcast.place_ref, bf16[1024,2048]{1,0:T(8,128)(2,1)S(1)} %copy-done.3, bf16[2048,1024]{1,0:T(8,128)(2,1)S(1)} %get-tuple-element.53.weight_ref), custom_call_target="tpu_custom_call" | custom-call | flops 1 | bytes 1 | tf_op jit(solution)/shard_map/partial_values/pallas_call | solution.py:188
  58.9 1.3 %chunk_gradient.4.g3 = f32[256,2048]{1,0:T(8,128)S(1)} custom-call(bf16[1024,2048]{1,0:T(8,128)(2,1)S(1)} %copy-done.3, bf16[1040,256]{1,0:T(8,128)(2,1)S(1)} %collective-permute-done.1.refs_0_.b1, bf16[1040,256]{1,0:T(8,128)(2,1)S(1)} %collective-permute-done.3.refs_1_.e2), custom_call_target="tpu_custom_call" | custom-call | flops 1 | bytes 1 | tf_op jit(solution)/shard_map/chunk_gradient/pallas_call | solution.py:274
  60.2 4.1 %collective-permute-done.12.d3 = bf16[1040,256]{1,0:T(8,128)(2,1)S(1)} collective-permute-done((bf16[1040,256]{1,0:T(8,128)(2,1)}, bf16[1040,256]{1,0:T(8,128)(2,1)S(1)}, u32[]{:S(2)}, u32[]{:S(2)}) %collective-permute-start.12) | collective-permute-done | bytes 532512 | tf_op jit(solution)/shard_map/ppermute | solution.py:456
  64.3 5.3 %slot_terms.1 = (f32[2048,128]{1,0:T(8,128)S(1)}, f32[2048,128]{1,0:T(8,128)S(1)}, f32[2048,128]{1,0:T(8,128)S(1)}, f32[2048,128]{1,0:T(8,128)S(1)}, s16[2096,12...) custom-call(s32[8,128]{1,0:T(8,128)S(1)} %get-tuple-element.58.codes, ...), custom_call_target="tpu_custom_call" | custom-call | flops 1 | bytes 1 | tf_op jit(solution)/shard_map/slot_terms/pallas_call | solution.py:330
  69.7 0.5 collective-permute-start.16
  70.2 1.6 %collective-permute-start.14 = (s16[1040,256]{1,0:T(8,128)(2,1)S(1)}, s16[1040,256]{1,0:T(8,128)(2,1)S(1)}, u32[]{:S(2)}, u32[]{:S(2)}) collective-permute-start(s16[1040,256]{1,0:T(8,128)(2,1)S(1)} %get-tuple-element.71), channel_id=1, source_target_pairs={{0,1},{3,2},{4,5},{7,6},{8,9},{11,10},{12,13},{15,14},{16,17},{19,... | collective-permute-start | bytes 1597448 | tf_op jit(solution)/shard_map/ppermute | solution.py:459
  72.1 0.3 hop.3
  72.4 0.7 collective-permute-start.13
  73.1 0.4 combine.4
  73.5 1.5 %collective-permute-start.23 = (s16[2096,128]{1,0:T(8,128)(2,1)S(1)}, s16[2096,128]{1,0:T(8,128)(2,1)S(1)}, u32[]{:S(2)}, u32[]{:S(2)}) collective-permute-start(s16[2096,128]{1,0:T(8,128)(2,1)S(1)} %combine.4), channel_id=1, source_target_pairs={{0,8},{4,12},{8,0},{12,4},{16,24},{20,28},{24,16},{28,20},{1,9},{5... | collective-permute-start | bytes 1609736 | tf_op jit(solution)/shard_map/ppermute | solution.py:447
  75.1 0.4 combine.5
  75.4 0.8 collective-permute-start.22
  76.2 0.4 combine.6
  76.6 7.2 %collective-permute-done.14.arrived_ref = s16[1040,256]{1,0:T(8,128)(2,1)S(1)} collective-permute-done((s16[1040,256]{1,0:T(8,128)(2,1)S(1)}, s16[1040,256]{1,0:T(8,128)(2,1)S(1)}, u32[]{:S(2)}, u32[]{:S(2)}) %collective-permute-start.14) | collective-permute-done | bytes 532512 | tf_op jit(solution)/shard_map/ppermute | solution.py:459
  83.8 1.6 %collective-permute-start.21 = (s16[2096,128]{1,0:T(8,128)(2,1)S(1)}, s16[2096,128]{1,0:T(8,128)(2,1)S(1)}, u32[]{:S(2)}, u32[]{:S(2)}) collective-permute-start(s16[2096,128]{1,0:T(8,128)(2,1)S(1)} %combine.6), channel_id=1, source_target_pairs={{0,24},{4,28},{8,16},{12,20},{16,8},{20,12},{24,0},{28,4},{1,25},{... | collective-permute-start | bytes 1609736 | tf_op jit(solution)/shard_map/ppermute | solution.py:447
  85.4 0.3 hop.4
  85.7 0.3 hop.5
  86.1 0.9 collective-permute-start.19
  87.0 4.3 %collective-permute-start.18 = (s16[1040,256]{1,0:T(8,128)(2,1)S(1)}, s16[1040,256]{1,0:T(8,128)(2,1)S(1)}, u32[]{:S(2)}, u32[]{:S(2)}) collective-permute-start(s16[1040,256]{1,0:T(8,128)(2,1)S(1)} %hop.4), channel_id=1, source_target_pairs={{0,1},{1,0},{2,3},{3,2},{4,5},{5,4},{6,7},{7,6},{8,9},{9,8},{10,11... | collective-permute-start | bytes 1597448 | tf_op jit(solution)/shard_map/ppermute | solution.py:450
  91.4 7.7 %grad_inputs.1 = bf16[1024,2048]{1,0:T(8,128)(2,1)} custom-call(s32[1]{0:T(128)} %bitcast.place_ref, bf16[2048,1024]{1,0:T(8,128)(2,1)S(1)} %get-tuple-element.53.weight_ref, bf16[1024,256]{1,0:T(8,128)(2,1)S(1)} %copy-done.7, bf16[1040,256]{1,0:T(8,128)(2,1)} %collective-permute-done.refs_0_.a1, bf16[1040,256]{1,0:T(8,128)(2,1)S(1)} %collective-permute-done.1.refs_0_.b1, ...), custom_call_target="tpu_custom_call" | custom-call | flops 4294967296 | bytes 12582912 | tf_op jit(solution)/shard_map/grad_inputs/pallas_call | solution.py:418
  99.2 1.9 %collective-permute-done.22.refs_2_ = s16[2096,128]{1,0:T(8,128)(2,1)S(1)} collective-permute-done((s16[2096,128]{1,0:T(8,128)(2,1)S(1)}, s16[2096,128]{1,0:T(8,128)(2,1)S(1)}, u32[]{:S(2)}, u32[]{:S(2)}) %collective-permute-start.22) | collective-permute-done | bytes 536608 | tf_op jit(solution)/shard_map/ppermute | solution.py:447
  101.2 1.9 %normalized_update.1 = bf16[16,128,128]{2,1,0:T(8,128)(2,1)} custom-call(f32[2048,128]{1,0:T(8,128)S(1)} %combine.7.refs_0_, s16[2096,128]{1,0:T(8,128)(2,1)S(1)} %collective-permute-done.21.refs_1_, s16[2096,128]{1,0:T(8,128)(2,1)S(1)} %collective-permute-done.22.refs_2_, s16[2096,128]{1,0:T(8,128)(2,1)S(1)} %collective-permute-done.23.refs_3_), custom_call_target="tpu_custom_call" | custom-call | flops 1 | bytes 1 | tf_op jit(solution)/shard_map/normalized_update/pallas_call | solution.py:388
  103.1 1.1 %last_hop.1 = bf16[1024,256]{1,0:T(8,128)(2,1)} custom-call(s32[1]{0:T(128)} %bitcast.place_ref, f32[1024,1024]{1,0:T(8,128)S(1)} %get-tuple-element.56.partial_ref, s16[1040,256]{1,0:T(8,128)(2,1)S(1)} %collective-permute-done.18.right_ref, s16[1040,256]{1,0:T(8,128)(2,1)S(1)} %collective-permute-done.19.left_ref), custom_call_target="tpu_custom_call" | custom-call | flops 1 | bytes 1 | tf_op jit(solution)/shard_map/last_hop/pallas_call | solution.py:238
  (39 shorter events, 0.7 us)
Async XLA Ops:
  2.8 9.6 %collective-permute-start.2 = (bf16[2064,128]{1,0:T(8,128)(2,1)}, bf16[2064,128]{1,0:T(8,128)(2,1)S(1)}, u32[]{:S(2)}, u32[]{:S(2)}) collective-permute-start(bf16[2064,128]{1,0:T(8,128)(2,1)} %get-tuple-element.48.refs_0_), channel_id=1, source_target_pairs={{0,4},{4,0},{8,12},{12,8},{16,20},{20,16},{24,28},{28,24},{1,5},{5... | collective-permute-start | bytes 1585160 | tf_op jit(solution)/shard_map/ppermute | solution.py:447
  3.4 15.0 %collective-permute-start.1 = (bf16[1040,256]{1,0:T(8,128)(2,1)}, bf16[1040,256]{1,0:T(8,128)(2,1)S(1)}, u32[]{:S(2)}, u32[]{:S(2)}) collective-permute-start(bf16[1040,256]{1,0:T(8,128)(2,1)} %get-tuple-element.44), channel_id=1, source_target_pairs={{1,2},{2,1},{5,6},{6,5},{9,10},{10,9},{13,14},{14,13},{17,18},{18,... | collective-permute-start | bytes 1597448 | tf_op jit(solution)/shard_map/ppermute | solution.py:453
  4.1 18.2 %collective-permute-start = (bf16[1040,256]{1,0:T(8,128)(2,1)}, bf16[1040,256]{1,0:T(8,128)(2,1)}, u32[]{:S(2)}, u32[]{:S(2)}) collective-permute-start(bf16[1040,256]{1,0:T(8,128)(2,1)} %get-tuple-element.44), channel_id=1, source_target_pairs={{0,1},{1,0},{2,3},{3,2},{4,5},{5,4},{6,7},{7,6},{8,9},{9,8},{10,11... | collective-permute-start | bytes 1597448 | tf_op jit(solution)/shard_map/ppermute | solution.py:450
  9.5 17.9 %collective-permute-start.6 = (bf16[2064,128]{1,0:T(8,128)(2,1)}, bf16[2064,128]{1,0:T(8,128)(2,1)}, u32[]{:S(2)}, u32[]{:S(2)}) collective-permute-start(bf16[2064,128]{1,0:T(8,128)(2,1)} %get-tuple-element.48.refs_0_), channel_id=1, source_target_pairs={{0,24},{4,28},{8,16},{12,20},{16,8},{20,12},{24,0},{28,4},{1,25},{... | collective-permute-start | bytes 1585160 | tf_op jit(solution)/shard_map/ppermute | solution.py:447
  12.0 23.9 %collective-permute-start.5 = (bf16[2064,128]{1,0:T(8,128)(2,1)}, bf16[2064,128]{1,0:T(8,128)(2,1)}, u32[]{:S(2)}, u32[]{:S(2)}) collective-permute-start(bf16[2064,128]{1,0:T(8,128)(2,1)} %get-tuple-element.48.refs_0_), channel_id=1, source_target_pairs={{0,16},{4,20},{8,24},{12,28},{16,0},{20,4},{24,8},{28,12},{1,17},{... | collective-permute-start | bytes 1585160 | tf_op jit(solution)/shard_map/ppermute | solution.py:447
  12.5 0.8 copy-start.9
  13.3 22.7 %collective-permute-start.4 = (bf16[2064,128]{1,0:T(8,128)(2,1)}, bf16[2064,128]{1,0:T(8,128)(2,1)}, u32[]{:S(2)}, u32[]{:S(2)}) collective-permute-start(bf16[2064,128]{1,0:T(8,128)(2,1)} %get-tuple-element.48.refs_0_), channel_id=1, source_target_pairs={{0,8},{4,12},{8,0},{12,4},{16,24},{20,28},{24,16},{28,20},{1,9},{5... | collective-permute-start | bytes 1585160 | tf_op jit(solution)/shard_map/ppermute | solution.py:447
  13.8 2.2 %copy-start = (bf16[1024,2048]{1,0:T(8,128)(2,1)S(1)}, bf16[1024,2048]{1,0:T(8,128)(2,1)}, u32[]{:S(2)}) copy-start(bf16[1024,2048]{1,0:T(8,128)(2,1)} %normed_ref.11) | copy-start | bytes 12582916
  16.0 1.0 copy-start.6
  17.1 6.7 %copy-start.1 = (bf16[1024,2048]{1,0:T(8,128)(2,1)S(1)}, bf16[1024,2048]{1,0:T(8,128)(2,1)}, u32[]{:S(2)}) copy-start(bf16[1024,2048]{1,0:T(8,128)(2,1)} %normed_ref.11) | copy-start | bytes 12582916
  22.3 15.5 %collective-permute-start.11 = (bf16[1040,256]{1,0:T(8,128)(2,1)}, bf16[1040,256]{1,0:T(8,128)(2,1)}, u32[]{:S(2)}, u32[]{:S(2)}) collective-permute-start(bf16[1040,256]{1,0:T(8,128)(2,1)} %collective-permute-done.refs_0_.a1), channel_id=1, source_target_pairs={{1,2},{2,1},{5,6},{6,5},{9,10},{10,9},{13,14},{14,13},{17,18},{18,... | collective-permute-start | bytes 1597448 | tf_op jit(solution)/shard_map/ppermute | solution.py:453
  26.1 1.3 %copy-start.4 = (f32[256,2048]{1,0:T(8,128)}, f32[256,2048]{1,0:T(8,128)S(1)}, u32[]{:S(2)}) copy-start(f32[256,2048]{1,0:T(8,128)S(1)} %chunk_gradient.5.g2) | copy-start | bytes 6291460
  36.0 3.1 %collective-permute-start.7 = (bf16[2064,128]{1,0:T(8,128)(2,1)}, bf16[2064,128]{1,0:T(8,128)(2,1)}, u32[]{:S(2)}, u32[]{:S(2)}) collective-permute-start(bf16[2064,128]{1,0:T(8,128)(2,1)} %collective-permute-done.4.refs_2_), channel_id=1, source_target_pairs={{0,4},{4,0},{8,12},{12,8},{16,20},{20,16},{24,28},{28,24},{1,5},{5... | collective-permute-start | bytes 1585160 | tf_op jit(solution)/shard_map/ppermute | solution.py:447
  36.0 3.1 %collective-permute-start.8 = (bf16[2064,128]{1,0:T(8,128)(2,1)}, bf16[2064,128]{1,0:T(8,128)(2,1)}, u32[]{:S(2)}, u32[]{:S(2)}) collective-permute-start(bf16[2064,128]{1,0:T(8,128)(2,1)} %collective-permute-done.5.refs_4_), channel_id=1, source_target_pairs={{0,4},{4,0},{8,12},{12,8},{16,20},{20,16},{24,28},{28,24},{1,5},{5... | collective-permute-start | bytes 1585160 | tf_op jit(solution)/shard_map/ppermute | solution.py:447
  36.5 3.3 %collective-permute-start.9 = (bf16[2064,128]{1,0:T(8,128)(2,1)}, bf16[2064,128]{1,0:T(8,128)(2,1)}, u32[]{:S(2)}, u32[]{:S(2)}) collective-permute-start(bf16[2064,128]{1,0:T(8,128)(2,1)} %collective-permute-done.6.refs_6_), channel_id=1, source_target_pairs={{0,4},{4,0},{8,12},{12,8},{16,20},{20,16},{24,28},{28,24},{1,5},{5... | collective-permute-start | bytes 1585160 | tf_op jit(solution)/shard_map/ppermute | solution.py:447
  36.5 22.4 %collective-permute-start.3 = (bf16[1040,256]{1,0:T(8,128)(2,1)S(1)}, bf16[1040,256]{1,0:T(8,128)(2,1)S(1)}, u32[]{:S(2)}, u32[]{:S(2)}) collective-permute-start(bf16[1040,256]{1,0:T(8,128)(2,1)S(1)} %collective-permute-done.1.refs_0_.b1), channel_id=1, source_target_pairs={{1,0},{2,3},{5,4},{6,7},{9,8},{10,11},{13,12},{14,15},{17,16},{18,... | collective-permute-start | bytes 1597448 | tf_op jit(solution)/shard_map/ppermute | solution.py:456
  37.8 26.5 %collective-permute-start.12 = (bf16[1040,256]{1,0:T(8,128)(2,1)}, bf16[1040,256]{1,0:T(8,128)(2,1)S(1)}, u32[]{:S(2)}, u32[]{:S(2)}) collective-permute-start(bf16[1040,256]{1,0:T(8,128)(2,1)} %collective-permute-done.11.m2), channel_id=1, source_target_pairs={{1,0},{2,3},{5,4},{6,7},{9,8},{10,11},{13,12},{14,15},{17,16},{18,... | collective-permute-start | bytes 1597448 | tf_op jit(solution)/shard_map/ppermute | solution.py:456
  39.8 2.2 %copy-start.2 = (bf16[1024,2048]{1,0:T(8,128)(2,1)S(1)}, bf16[1024,2048]{1,0:T(8,128)(2,1)}, u32[]{:S(2)}) copy-start(bf16[1024,2048]{1,0:T(8,128)(2,1)} %normed_ref.11) | copy-start | bytes 12582916
  41.9 1.0 %copy-start.8 = (bf16[2064,128]{1,0:T(8,128)(2,1)S(1)}, bf16[2064,128]{1,0:T(8,128)(2,1)}, u32[]{:S(2)}) copy-start(bf16[2064,128]{1,0:T(8,128)(2,1)} %get-tuple-element.48.refs_0_) | copy-start | bytes 1585156
  43.0 1.0 %copy-start.10 = (bf16[2064,128]{1,0:T(8,128)(2,1)S(1)}, bf16[2064,128]{1,0:T(8,128)(2,1)}, u32[]{:S(2)}) copy-start(bf16[2064,128]{1,0:T(8,128)(2,1)} %copy-done.9) | copy-start | bytes 1585156
  44.0 10.1 %copy-start.3 = (bf16[1024,2048]{1,0:T(8,128)(2,1)S(1)}, bf16[1024,2048]{1,0:T(8,128)(2,1)}, u32[]{:S(2)}) copy-start(bf16[1024,2048]{1,0:T(8,128)(2,1)} %normed_ref.11) | copy-start | bytes 12582916
  49.9 19.7 %collective-permute-start.10 = (s16[1040,256]{1,0:T(8,128)(2,1)S(1)}, s16[1040,256]{1,0:T(8,128)(2,1)S(1)}, u32[]{:S(2)}, u32[]{:S(2)}) collective-permute-start(s16[1040,256]{1,0:T(8,128)(2,1)S(1)} %get-tuple-element.57), channel_id=1, source_target_pairs={{0,1},{3,2},{4,5},{7,6},{8,9},{11,10},{12,13},{15,14},{16,17},{19,... | collective-permute-start | bytes 1597448 | tf_op jit(solution)/shard_map/ppermute | solution.py:459
  58.9 5.4 %copy-start.5 = (f32[256,2048]{1,0:T(8,128)S(1)}, f32[256,2048]{1,0:T(8,128)}, u32[]{:S(2)}) copy-start(f32[256,2048]{1,0:T(8,128)} %copy-done.4) | copy-start | bytes 6291460
  69.6 2.8 %collective-permute-start.15 = (s16[2096,128]{1,0:T(8,128)(2,1)S(1)}, s16[2096,128]{1,0:T(8,128)(2,1)S(1)}, u32[]{:S(2)}, u32[]{:S(2)}) collective-permute-start(s16[2096,128]{1,0:T(8,128)(2,1)S(1)} %get-tuple-element.73), channel_id=1, source_target_pairs={{0,4},{4,0},{8,12},{12,8},{16,20},{20,16},{24,28},{28,24},{1,5},{5... | collective-permute-start | bytes 1609736 | tf_op jit(solution)/shard_map/ppermute | solution.py:447
  69.7 3.8 %collective-permute-start.16 = (s16[2096,128]{1,0:T(8,128)(2,1)S(1)}, s16[2096,128]{1,0:T(8,128)(2,1)S(1)}, u32[]{:S(2)}, u32[]{:S(2)}) collective-permute-start(s16[2096,128]{1,0:T(8,128)(2,1)S(1)} %get-tuple-element.75), channel_id=1, source_target_pairs={{0,4},{4,0},{8,12},{12,8},{16,20},{20,16},{24,28},{28,24},{1,5},{5... | collective-permute-start | bytes 1609736 | tf_op jit(solution)/shard_map/ppermute | solution.py:447
  70.2 5.2 %collective-permute-start.17 = (s16[2096,128]{1,0:T(8,128)(2,1)S(1)}, s16[2096,128]{1,0:T(8,128)(2,1)S(1)}, u32[]{:S(2)}, u32[]{:S(2)}) collective-permute-start(s16[2096,128]{1,0:T(8,128)(2,1)S(1)} %get-tuple-element.77), channel_id=1, source_target_pairs={{0,4},{4,0},{8,12},{12,8},{16,20},{20,16},{24,28},{28,24},{1,5},{5... | collective-permute-start | bytes 1609736 | tf_op jit(solution)/shard_map/ppermute | solution.py:447
  70.2 13.5 %collective-permute-start.14 = (s16[1040,256]{1,0:T(8,128)(2,1)S(1)}, s16[1040,256]{1,0:T(8,128)(2,1)S(1)}, u32[]{:S(2)}, u32[]{:S(2)}) collective-permute-start(s16[1040,256]{1,0:T(8,128)(2,1)S(1)} %get-tuple-element.71), channel_id=1, source_target_pairs={{0,1},{3,2},{4,5},{7,6},{8,9},{11,10},{12,13},{15,14},{16,17},{19,... | collective-permute-start | bytes 1597448 | tf_op jit(solution)/shard_map/ppermute | solution.py:459
  71.8 15.2 %collective-permute-start.20 = (s16[2096,128]{1,0:T(8,128)(2,1)S(1)}, s16[2096,128]{1,0:T(8,128)(2,1)S(1)}, u32[]{:S(2)}, u32[]{:S(2)}) collective-permute-start(s16[2096,128]{1,0:T(8,128)(2,1)S(1)} %get-tuple-element.81), channel_id=1, source_target_pairs={{0,4},{4,0},{8,12},{12,8},{16,20},{20,16},{24,28},{28,24},{1,5},{5... | collective-permute-start | bytes 1609736 | tf_op jit(solution)/shard_map/ppermute | solution.py:447
  72.4 13.0 %collective-permute-start.13 = (s16[1040,256]{1,0:T(8,128)(2,1)S(1)}, s16[1040,256]{1,0:T(8,128)(2,1)S(1)}, u32[]{:S(2)}, u32[]{:S(2)}) collective-permute-start(s16[1040,256]{1,0:T(8,128)(2,1)S(1)} %hop.3), channel_id=1, source_target_pairs={{1,2},{2,1},{5,6},{6,5},{9,10},{10,9},{13,14},{14,13},{17,18},{18,... | collective-permute-start | bytes 1597448 | tf_op jit(solution)/shard_map/ppermute | solution.py:453
  73.5 25.7 %collective-permute-start.23 = (s16[2096,128]{1,0:T(8,128)(2,1)S(1)}, s16[2096,128]{1,0:T(8,128)(2,1)S(1)}, u32[]{:S(2)}, u32[]{:S(2)}) collective-permute-start(s16[2096,128]{1,0:T(8,128)(2,1)S(1)} %combine.4), channel_id=1, source_target_pairs={{0,8},{4,12},{8,0},{12,4},{16,24},{20,28},{24,16},{28,20},{1,9},{5... | collective-permute-start | bytes 1609736 | tf_op jit(solution)/shard_map/ppermute | solution.py:447
  75.4 25.7 %collective-permute-start.22 = (s16[2096,128]{1,0:T(8,128)(2,1)S(1)}, s16[2096,128]{1,0:T(8,128)(2,1)S(1)}, u32[]{:S(2)}, u32[]{:S(2)}) collective-permute-start(s16[2096,128]{1,0:T(8,128)(2,1)S(1)} %combine.5), channel_id=1, source_target_pairs={{0,16},{4,20},{8,24},{12,28},{16,0},{20,4},{24,8},{28,12},{1,17},{... | collective-permute-start | bytes 1609736 | tf_op jit(solution)/shard_map/ppermute | solution.py:447
  76.6 14.8 %copy-start.7 = (bf16[1024,256]{1,0:T(8,128)(2,1)S(1)}, bf16[1024,256]{1,0:T(8,128)(2,1)}, u32[]{:S(2)}) copy-start(bf16[1024,256]{1,0:T(8,128)(2,1)} %own.1) | copy-start | bytes 1572868
  83.8 17.4 %collective-permute-start.21 = (s16[2096,128]{1,0:T(8,128)(2,1)S(1)}, s16[2096,128]{1,0:T(8,128)(2,1)S(1)}, u32[]{:S(2)}, u32[]{:S(2)}) collective-permute-start(s16[2096,128]{1,0:T(8,128)(2,1)S(1)} %combine.6), channel_id=1, source_target_pairs={{0,24},{4,28},{8,16},{12,20},{16,8},{20,12},{24,0},{28,4},{1,25},{... | collective-permute-start | bytes 1609736 | tf_op jit(solution)/shard_map/ppermute | solution.py:447
  86.1 17.0 %collective-permute-start.19 = (s16[1040,256]{1,0:T(8,128)(2,1)S(1)}, s16[1040,256]{1,0:T(8,128)(2,1)S(1)}, u32[]{:S(2)}, u32[]{:S(2)}) collective-permute-start(s16[1040,256]{1,0:T(8,128)(2,1)S(1)} %hop.5), channel_id=1, source_target_pairs={{1,2},{2,1},{5,6},{6,5},{9,10},{10,9},{13,14},{14,13},{17,18},{18,... | collective-permute-start | bytes 1597448 | tf_op jit(solution)/shard_map/ppermute | solution.py:453
  87.0 16.1 %collective-permute-start.18 = (s16[1040,256]{1,0:T(8,128)(2,1)S(1)}, s16[1040,256]{1,0:T(8,128)(2,1)S(1)}, u32[]{:S(2)}, u32[]{:S(2)}) collective-permute-start(s16[1040,256]{1,0:T(8,128)(2,1)S(1)} %hop.4), channel_id=1, source_target_pairs={{0,1},{1,0},{2,3},{3,2},{4,5},{5,4},{6,7},{7,6},{8,9},{9,8},{10,11... | collective-permute-start | bytes 1597448 | tf_op jit(solution)/shard_map/ppermute | solution.py:450

commit v6 on v5

--- a/solution.py
+++ b/solution.py
@@ -270,6 +270,30 @@
     product(joined(normed_ref.shape[0], refs[:-1]).T, normed_ref, refs[-1])
 
 
+def own_kernel(normed_ref, chunk_ref, held_ref, out_ref, sem):
+    copy = pltpu.make_async_copy(normed_ref, held_ref, sem)
+    copy.start()
+    turned = chunk_ref[...].T
+    copy.wait()
+    product(turned, held_ref, out_ref)
+
+
+def own_gradient(normed, chunk):
+    return pl.pallas_call(
+        own_kernel,
+        in_specs=[pl.BlockSpec(memory_space=pl.ANY), VMEM],
+        out_specs=[VMEM, VMEM],
+        out_shape=[
+            jax.ShapeDtypeStruct(normed.shape, normed.dtype),
+            jax.ShapeDtypeStruct((chunk.shape[1], normed.shape[1]), jnp.float32),
+        ],
+        scratch_shapes=[pltpu.SemaphoreType.DMA],
+        compiler_params=params(16),
+        cost_estimate=LITTLE,
+        name="own_gradient",
+    )(normed, chunk)
+
+
 def chunk_gradient(normed, *chunks):
     return pl.pallas_call(
         chunk_kernel,
@@ -462,7 +486,7 @@
         tile_rows, tile_columns, tile_values.reshape(rows, tile), cotangent, column_blocks
     )
     a1, b1 = pairs(padded), middle(padded)
-    g1 = chunk_gradient(normed, cotangent)
+    normed, g1 = own_gradient(normed, cotangent)
     same_core = [message] + [swap(message, 2 * chip) for chip in range(1, chips)]
     beside = swap(message, 1)
     a1, b1, g1, beside = lax.optimization_barrier((a1, b1, g1, beside))
@@ -472,6 +496,7 @@
     gathered = [same_core[0], beside]
     for m in same_core[1:]:
         gathered += [m, swap(m, 1)]
+    m2, e2, *gathered = lax.optimization_barrier((m2, e2, *gathered))
     d3 = outward(m2)
 
     weight, first, codes = first_values(place, normed, gathered, parts, column_blocks)
@@ -486,9 +511,9 @@
     crossing = middle(hop(lambda p: p ^ 2, place, partial, arrived))
     other = [swap(m, 1) for m in send]
     sums = [combine(keep[chip], other[chip], jnp.int16) for chip in range(1, chips)]
-    crossing, to_middle, _ = lax.optimization_barrier((crossing, to_middle, sums))
+    own = combine(keep[0], other[0], jnp.float32)
+    crossing, to_middle, own, _ = lax.optimization_barrier((crossing, to_middle, own, sums))
     terms = [swap(m, 2 * chip) for chip, m in reversed(list(enumerate(sums, 1)))]
-    own = combine(keep[0], other[0], jnp.float32)
 
     by_pair = pairs(hop(lambda p: p ^ 1, place, partial, crossing))
     by_middle = middle(hop(lambda p: 3 - p, place, partial, to_middle))

time: 105 us -> 105 us (level)
  waiting for transfers between devices: 26.4 us -> 19.3 us
  starting transfers between devices: 31.3 us -> 35.9 us
  local copies, waits for them, and re-layouts: 9.66 us -> 11.7 us
    ppermute x2, waiting for transfers between devices: 4.11 us -> 0.01 us  [outward(): return lax.ppermute(x, 'tensor', [(1, 0), (2, 3)])]
    ppermute x2, starting transfers between devices: 5.78 us -> 8.94 us  [inward(): return lax.ppermute(x, 'tensor', [(0, 1), (3, 2)])]
    unnamed x22, local copies, waits for them, and re-layouts: 9.66 us -> 11.7 us
    ppermute x2, waiting for transfers between devices: 3.95 us -> 2.17 us  [pairs(): return lax.ppermute(x, 'tensor', [(0, 1), (1, 0), (2, 3), (3, 2)])]
    ppermute x2, waiting for transfers between devices: 7.16 us -> 5.43 us  [inward(): return lax.ppermute(x, 'tensor', [(0, 1), (3, 2)])]
    pallas_call x0 -> x1, Pallas kernels: none -> 1.73 us  [own_gradient(): pl.pallas_call(own_kernel, in_specs=[pl.BlockSpec(memory_space=pl.ANY), V...]
    ppermute x2, starting transfers between devices: 9.79 us -> 11.3 us  [pairs(): return lax.ppermute(x, 'tensor', [(0, 1), (1, 0), (2, 3), (3, 2)])]
    pallas_call x3 -> x2, Pallas kernels: 4.89 us -> 3.62 us  [chunk_gradient(): pl.pallas_call(chunk_kernel, in_specs=[VMEM] + [VMEM] * len(chunks), out_...]
  transfers between devices with their start and end apart: 24 -> 24, of which waited for: 7 -> 8; matrix products, arithmetic and copies ran while one was open for 0% -> 0% of each run, Pallas kernels for 31% -> 32%
where the time goes in v6:
time: 105 us; the launch traced here: 104 us
  Pallas kernels  36.4 us (35%)
  starting transfers between devices  35.9 us (34%)
  waiting for transfers between devices  19.3 us (18%)
  local copies, waits for them, and re-layouts  11.7 us (11%)
    ppermute x14, waiting for transfers between devices, swap(): return lax.ppermute(x, 'fsdp', [(i, i ^ mask) for i in range(devices)])  11.7 us
    unnamed x22, local copies, waits for them, and re-layouts  11.7 us
    ppermute x2, starting transfers between devices, pairs(): return lax.ppermute(x, 'tensor', [(0, 1), (1, 0), (2, 3), (3, 2)])  11.3 us
    ppermute x14, starting transfers between devices, swap(): return lax.ppermute(x, 'fsdp', [(i, i ^ mask) for i in range(devices)])  9.28 us
    ppermute x2, starting transfers between devices, inward(): return lax.ppermute(x, 'tensor', [(0, 1), (3, 2)])  8.94 us
    pallas_call x1, Pallas kernels, grad_inputs(): pl.pallas_call(grad_input_kernel, grid_spec=pltpu.PrefetchScalarGridSpec(...  7.68 us
    pallas_call x1, Pallas kernels, first_values(): pl.pallas_call(functools.partial(first_kernel, column_blocks), in_specs=[...  5.9 us
    ppermute x2, waiting for transfers between devices, inward(): return lax.ppermute(x, 'tensor', [(0, 1), (3, 2)])  5.43 us
  transfers between devices with their start and end apart: 24, of which 8 were waited for; matrix products, arithmetic and copies ran while one was open for 0% of the time, Pallas kernels for 32%

profile of v6, /device:TPU:0, one launch (start us, length us, event | category | flops | bytes accessed | tf_op | source)
XLA Modules:
  0.0 104.1 jit_solution(17029371206372521909)
XLA Ops:
  0.6 2.2 %pack.1 = (bf16[2064,128]{1,0:T(8,128)(2,1)}, bf16[1040,256]{1,0:T(8,128)(2,1)}) custom-call(s32[1,16]{1,0:T(1,128)} %rows_ref.1, s32[1,16]{1,0:T(1,128)} %columns_ref.1, bf16[2048,128]{1,0:T(8,128)(2,1)} %bitcast.4, bf16[1024,256]{1,0:T(8,128)(2,1)} %own.1), custom_call_target="tpu_custom_call" | custom-call | flops 1 | bytes 1 | tf_op jit(solution)/shard_map/pack/pallas_call | solution.py:99
  2.8 0.5 collective-permute-start.2
  3.4 0.7 collective-permute-start.1
  4.1 5.5 %collective-permute-start = (bf16[1040,256]{1,0:T(8,128)(2,1)}, bf16[1040,256]{1,0:T(8,128)(2,1)}, u32[]{:S(2)}, u32[]{:S(2)}) collective-permute-start(bf16[1040,256]{1,0:T(8,128)(2,1)} %get-tuple-element.58), channel_id=1, source_target_pairs={{0,1},{1,0},{2,3},{3,2},{4,5},{5,4},{6,7},{7,6},{8,9},{9,8},{10,11... | collective-permute-start | bytes 1597448 | tf_op jit(solution)/shard_map/ppermute | solution.py:474
  9.5 2.4 %collective-permute-start.7 = (bf16[2064,128]{1,0:T(8,128)(2,1)}, bf16[2064,128]{1,0:T(8,128)(2,1)}, u32[]{:S(2)}, u32[]{:S(2)}) collective-permute-start(bf16[2064,128]{1,0:T(8,128)(2,1)} %get-tuple-element.69.refs_0_), channel_id=1, source_target_pairs={{0,24},{4,28},{8,16},{12,20},{16,8},{20,12},{24,0},{28,4},{1,25},{... | collective-permute-start | bytes 1585160 | tf_op jit(solution)/shard_map/ppermute | solution.py:471
  12.0 0.5 collective-permute-start.6
  12.5 0.8 copy-done.9
  13.3 0.5 collective-permute-start.5
  13.8 2.2 %copy-done.3 = bf16[1024,2048]{1,0:T(8,128)(2,1)S(1)} copy-done((bf16[1024,2048]{1,0:T(8,128)(2,1)S(1)}, bf16[1024,2048]{1,0:T(8,128)(2,1)}, u32[]{:S(2)}) %copy-start.3) | copy-done | bytes 4194328
  16.0 1.0 copy-done.4
  17.0 1.7 %own_gradient.1 = (bf16[1024,2048]{1,0:T(8,128)(2,1)S(1)}, f32[256,2048]{1,0:T(8,128)S(1)}) custom-call(bf16[1024,2048]{1,0:T(8,128)(2,1)S(1)} %copy-done.3, bf16[1024,256]{1,0:T(8,128)(2,1)S(1)} %copy-done.4), custom_call_target="tpu_custom_call" | custom-call | flops 1 | bytes 1 | tf_op jit(solution)/shard_map/own_gradient/pallas_call | solution.py:282
  18.8 1.4 %copy-done.6 = f32[256,2048]{1,0:T(8,128)} copy-done((f32[256,2048]{1,0:T(8,128)}, f32[256,2048]{1,0:T(8,128)S(1)}, u32[]{:S(2)}) %copy-start.6) | copy-done | bytes 2097176
  20.1 2.2 %collective-permute-done.refs_0_.a1 = bf16[1040,256]{1,0:T(8,128)(2,1)} collective-permute-done((bf16[1040,256]{1,0:T(8,128)(2,1)}, bf16[1040,256]{1,0:T(8,128)(2,1)}, u32[]{:S(2)}, u32[]{:S(2)}) %collective-permute-start) | collective-permute-done | bytes 532512 | tf_op jit(solution)/shard_map/ppermute | solution.py:474
  22.3 1.3 %collective-permute-start.4 = (bf16[1040,256]{1,0:T(8,128)(2,1)S(1)}, bf16[1040,256]{1,0:T(8,128)(2,1)S(1)}, u32[]{:S(2)}, u32[]{:S(2)}) collective-permute-start(bf16[1040,256]{1,0:T(8,128)(2,1)S(1)} %collective-permute-done.1.refs_0_.b1), channel_id=1, source_target_pairs={{1,0},{2,3},{5,4},{6,7},{9,8},{10,11},{13,12},{14,15},{17,16},{18,... | collective-permute-start | bytes 1597448 | tf_op jit(solution)/shard_map/ppermute | solution.py:480
  23.6 1.5 %collective-permute-start.3 = (bf16[1040,256]{1,0:T(8,128)(2,1)}, bf16[1040,256]{1,0:T(8,128)(2,1)}, u32[]{:S(2)}, u32[]{:S(2)}) collective-permute-start(bf16[1040,256]{1,0:T(8,128)(2,1)} %collective-permute-done.refs_0_.a1), channel_id=1, source_target_pairs={{1,2},{2,1},{5,6},{6,5},{9,10},{10,9},{13,14},{14,13},{17,18},{18,... | collective-permute-start | bytes 1597448 | tf_op jit(solution)/shard_map/ppermute | solution.py:477
  25.0 2.3 %chunk_gradient.2.g2 = f32[256,2048]{1,0:T(8,128)S(1)} custom-call(bf16[1024,2048]{1,0:T(8,128)(2,1)S(1)} %get-tuple-element.57.normed_ref, bf16[1040,256]{1,0:T(8,128)(2,1)} %collective-permute-done.refs_0_.a1), custom_call_target="tpu_custom_call" | custom-call | flops 1 | bytes 1 | tf_op jit(solution)/shard_map/chunk_gradient/pallas_call | solution.py:298
  27.4 2.0 %copy-done = bf16[1024,2048]{1,0:T(8,128)(2,1)} copy-done((bf16[1024,2048]{1,0:T(8,128)(2,1)}, bf16[1024,2048]{1,0:T(8,128)(2,1)S(1)}, u32[]{:S(2)}) %copy-start) | copy-done | bytes 4194328
  29.4 6.5 %collective-permute-done.6.refs_4_ = bf16[2064,128]{1,0:T(8,128)(2,1)} collective-permute-done((bf16[2064,128]{1,0:T(8,128)(2,1)}, bf16[2064,128]{1,0:T(8,128)(2,1)}, u32[]{:S(2)}, u32[]{:S(2)}) %collective-permute-start.6) | collective-permute-done | bytes 528416 | tf_op jit(solution)/shard_map/ppermute | solution.py:471
  36.0 0.5 collective-permute-start.9
  36.5 1.7 %collective-permute-done.8.refs_3_ = bf16[2064,128]{1,0:T(8,128)(2,1)} collective-permute-done((bf16[2064,128]{1,0:T(8,128)(2,1)}, bf16[2064,128]{1,0:T(8,128)(2,1)}, u32[]{:S(2)}, u32[]{:S(2)}) %collective-permute-start.8) | collective-permute-done | bytes 528416 | tf_op jit(solution)/shard_map/ppermute | solution.py:471
  38.2 0.8 collective-permute-done.9.refs_5_
  39.0 0.8 collective-permute-done.10.refs_7_
  39.8 1.3 %collective-permute-start.12 = (bf16[1040,256]{1,0:T(8,128)(2,1)}, bf16[1040,256]{1,0:T(8,128)(2,1)S(1)}, u32[]{:S(2)}, u32[]{:S(2)}) collective-permute-start(bf16[1040,256]{1,0:T(8,128)(2,1)} %collective-permute-done.3.m2), channel_id=1, source_target_pairs={{1,0},{2,3},{5,4},{6,7},{9,8},{10,11},{13,12},{14,15},{17,16},{18,... | collective-permute-start | bytes 1597448 | tf_op jit(solution)/shard_map/ppermute | solution.py:480
  41.1 2.2 %copy-done.1 = bf16[1024,2048]{1,0:T(8,128)(2,1)S(1)} copy-done((bf16[1024,2048]{1,0:T(8,128)(2,1)S(1)}, bf16[1024,2048]{1,0:T(8,128)(2,1)}, u32[]{:S(2)}) %copy-start.1) | copy-done | bytes 4194328
  43.2 1.0 copy-done.8
  44.3 1.0 copy-done.10
  45.3 5.9 %first_values.1 = (bf16[2048,1024]{1,0:T(8,128)(2,1)S(1)}, s16[1040,256]{1,0:T(8,128)(2,1)S(1)}, s32[8,128]{1,0:T(8,128)S(1)}) custom-call(s32[1]{0:T(128)} %bitcast.place_ref, bf16[1024,2048]{1,0:T(8,128)(2,1)S(1)} %copy-done.1, bf16[2064,128]{1,0:T(8,128)(2,1)S(1)} %copy-done.8, bf16[2064,128]{1,0:T(8,128)(2,1)S(1)} %copy-done.10, ...), custom_call_target="tpu_custom_call" | custom-call | flops 1 | bytes 1 | tf_op jit(solution)/shard_map/first_values/pallas_call | solution.py:153
  51.2 4.8 %collective-permute-start.11 = (s16[1040,256]{1,0:T(8,128)(2,1)S(1)}, s16[1040,256]{1,0:T(8,128)(2,1)S(1)}, u32[]{:S(2)}, u32[]{:S(2)}) collective-permute-start(s16[1040,256]{1,0:T(8,128)(2,1)S(1)} %get-tuple-element.81), channel_id=1, source_target_pairs={{0,1},{3,2},{4,5},{7,6},{8,9},{11,10},{12,13},{15,14},{16,17},{19,... | collective-permute-start | bytes 1597448 | tf_op jit(solution)/shard_map/ppermute | solution.py:483
  56.0 1.3 %chunk_gradient.3.g3 = f32[256,2048]{1,0:T(8,128)S(1)} custom-call(bf16[1024,2048]{1,0:T(8,128)(2,1)S(1)} %copy-done.2, bf16[1040,256]{1,0:T(8,128)(2,1)S(1)} %collective-permute-done.1.refs_0_.b1, bf16[1040,256]{1,0:T(8,128)(2,1)S(1)} %collective-permute-done.4.refs_1_.e2), custom_call_target="tpu_custom_call" | custom-call | flops 1 | bytes 1 | tf_op jit(solution)/shard_map/chunk_gradient/pallas_call | solution.py:298
  57.4 4.7 %partial_values.1 = (f32[1024,1024]{1,0:T(8,128)S(1)}, s16[1040,256]{1,0:T(8,128)(2,1)S(1)}) custom-call(s32[1]{0:T(128)} %bitcast.place_ref, bf16[1024,2048]{1,0:T(8,128)(2,1)S(1)} %copy-done.2, bf16[2048,1024]{1,0:T(8,128)(2,1)S(1)} %get-tuple-element.77.weight_ref), custom_call_target="tpu_custom_call" | custom-call | flops 1 | bytes 1 | tf_op jit(solution)/shard_map/partial_values/pallas_call | solution.py:188
  62.1 5.3 %slot_terms.1 = (f32[2048,128]{1,0:T(8,128)S(1)}, f32[2048,128]{1,0:T(8,128)S(1)}, f32[2048,128]{1,0:T(8,128)S(1)}, f32[2048,128]{1,0:T(8,128)S(1)}, s16[2096,12...) custom-call(s32[8,128]{1,0:T(8,128)S(1)} %get-tuple-element.82.codes, ...), custom_call_target="tpu_custom_call" | custom-call | flops 1 | bytes 1 | tf_op jit(solution)/shard_map/slot_terms/pallas_call | solution.py:354
  67.4 0.5 collective-permute-start.17
  68.0 0.4 collective-permute-start.15
  68.4 4.2 %collective-permute-start.14 = (s16[1040,256]{1,0:T(8,128)(2,1)S(1)}, s16[1040,256]{1,0:T(8,128)(2,1)S(1)}, u32[]{:S(2)}, u32[]{:S(2)}) collective-permute-start(s16[1040,256]{1,0:T(8,128)(2,1)S(1)} %get-tuple-element.96), channel_id=1, source_target_pairs={{0,1},{3,2},{4,5},{7,6},{8,9},{11,10},{12,13},{15,14},{16,17},{19,... | collective-permute-start | bytes 1597448 | tf_op jit(solution)/shard_map/ppermute | solution.py:483
  73.0 0.7 collective-permute-start.13
  73.7 0.4 combine.5
  74.1 1.6 %collective-permute-start.23 = (s16[2096,128]{1,0:T(8,128)(2,1)S(1)}, s16[2096,128]{1,0:T(8,128)(2,1)S(1)}, u32[]{:S(2)}, u32[]{:S(2)}) collective-permute-start(s16[2096,128]{1,0:T(8,128)(2,1)S(1)} %combine.5), channel_id=1, source_target_pairs={{0,8},{4,12},{8,0},{12,4},{16,24},{20,28},{24,16},{28,20},{1,9},{5... | collective-permute-start | bytes 1609736 | tf_op jit(solution)/shard_map/ppermute | solution.py:471
  75.6 0.4 combine.6
  76.0 0.8 collective-permute-start.22
  76.8 0.4 combine.7
  77.2 1.3 %collective-permute-start.21 = (s16[2096,128]{1,0:T(8,128)(2,1)S(1)}, s16[2096,128]{1,0:T(8,128)(2,1)S(1)}, u32[]{:S(2)}, u32[]{:S(2)}) collective-permute-start(s16[2096,128]{1,0:T(8,128)(2,1)S(1)} %combine.7), channel_id=1, source_target_pairs={{0,24},{4,28},{8,16},{12,20},{16,8},{20,12},{24,0},{28,4},{1,25},{... | collective-permute-start | bytes 1609736 | tf_op jit(solution)/shard_map/ppermute | solution.py:471
  78.7 5.4 %collective-permute-done.14.arrived_ref = s16[1040,256]{1,0:T(8,128)(2,1)S(1)} collective-permute-done((s16[1040,256]{1,0:T(8,128)(2,1)S(1)}, s16[1040,256]{1,0:T(8,128)(2,1)S(1)}, u32[]{:S(2)}, u32[]{:S(2)}) %collective-permute-start.14) | collective-permute-done | bytes 532512 | tf_op jit(solution)/shard_map/ppermute | solution.py:483
  84.4 0.9 collective-permute-start.20
  85.7 5.9 %collective-permute-start.19 = (s16[1040,256]{1,0:T(8,128)(2,1)S(1)}, s16[1040,256]{1,0:T(8,128)(2,1)S(1)}, u32[]{:S(2)}, u32[]{:S(2)}) collective-permute-start(s16[1040,256]{1,0:T(8,128)(2,1)S(1)} %hop.4), channel_id=1, source_target_pairs={{0,1},{1,0},{2,3},{3,2},{4,5},{5,4},{6,7},{7,6},{8,9},{9,8},{10,11... | collective-permute-start | bytes 1597448 | tf_op jit(solution)/shard_map/ppermute | solution.py:474
  91.6 7.7 %grad_inputs.1 = bf16[1024,2048]{1,0:T(8,128)(2,1)} custom-call(s32[1]{0:T(128)} %bitcast.place_ref, bf16[2048,1024]{1,0:T(8,128)(2,1)S(1)} %get-tuple-element.77.weight_ref, bf16[1024,256]{1,0:T(8,128)(2,1)S(1)} %copy-done.5, bf16[1040,256]{1,0:T(8,128)(2,1)} %collective-permute-done.refs_0_.a1, bf16[1040,256]{1,0:T(8,128)(2,1)S(1)} %collective-permute-done.1.refs_0_.b1, ...), custom_call_target="tpu_custom_call" | custom-call | flops 4294967296 | bytes 12582912 | tf_op jit(solution)/shard_map/grad_inputs/pallas_call | solution.py:442
  99.3 1.8 %collective-permute-done.22.refs_2_ = s16[2096,128]{1,0:T(8,128)(2,1)S(1)} collective-permute-done((s16[2096,128]{1,0:T(8,128)(2,1)S(1)}, s16[2096,128]{1,0:T(8,128)(2,1)S(1)}, u32[]{:S(2)}, u32[]{:S(2)}) %collective-permute-start.22) | collective-permute-done | bytes 536608 | tf_op jit(solution)/shard_map/ppermute | solution.py:471
  101.1 1.9 %normalized_update.1 = bf16[16,128,128]{2,1,0:T(8,128)(2,1)} custom-call(f32[2048,128]{1,0:T(8,128)S(1)} %combine.4.refs_0_, s16[2096,128]{1,0:T(8,128)(2,1)S(1)} %collective-permute-done.21.refs_1_, s16[2096,128]{1,0:T(8,128)(2,1)S(1)} %collective-permute-done.22.refs_2_, s16[2096,128]{1,0:T(8,128)(2,1)S(1)} %collective-permute-done.23.refs_3_), custom_call_target="tpu_custom_call" | custom-call | flops 1 | bytes 1 | tf_op jit(solution)/shard_map/normalized_update/pallas_call | solution.py:412
  103.0 1.1 %last_hop.1 = bf16[1024,256]{1,0:T(8,128)(2,1)} custom-call(s32[1]{0:T(128)} %bitcast.place_ref, f32[1024,1024]{1,0:T(8,128)S(1)} %get-tuple-element.80.partial_ref, s16[1040,256]{1,0:T(8,128)(2,1)S(1)} %collective-permute-done.19.right_ref, s16[1040,256]{1,0:T(8,128)(2,1)S(1)} %collective-permute-done.20.left_ref), custom_call_target="tpu_custom_call" | custom-call | flops 1 | bytes 1 | tf_op jit(solution)/shard_map/last_hop/pallas_call | solution.py:238
  (39 shorter events, 1.5 us)
Async XLA Ops:
  2.8 9.6 %collective-permute-start.2 = (bf16[2064,128]{1,0:T(8,128)(2,1)}, bf16[2064,128]{1,0:T(8,128)(2,1)S(1)}, u32[]{:S(2)}, u32[]{:S(2)}) collective-permute-start(bf16[2064,128]{1,0:T(8,128)(2,1)} %get-tuple-element.69.refs_0_), channel_id=1, source_target_pairs={{0,4},{4,0},{8,12},{12,8},{16,20},{20,16},{24,28},{28,24},{1,5},{5... | collective-permute-start | bytes 1585160 | tf_op jit(solution)/shard_map/ppermute | solution.py:471
  3.4 16.8 %collective-permute-start.1 = (bf16[1040,256]{1,0:T(8,128)(2,1)}, bf16[1040,256]{1,0:T(8,128)(2,1)S(1)}, u32[]{:S(2)}, u32[]{:S(2)}) collective-permute-start(bf16[1040,256]{1,0:T(8,128)(2,1)} %get-tuple-element.58), channel_id=1, source_target_pairs={{1,2},{2,1},{5,6},{6,5},{9,10},{10,9},{13,14},{14,13},{17,18},{18,... | collective-permute-start | bytes 1597448 | tf_op jit(solution)/shard_map/ppermute | solution.py:477
  4.1 18.2 %collective-permute-start = (bf16[1040,256]{1,0:T(8,128)(2,1)}, bf16[1040,256]{1,0:T(8,128)(2,1)}, u32[]{:S(2)}, u32[]{:S(2)}) collective-permute-start(bf16[1040,256]{1,0:T(8,128)(2,1)} %get-tuple-element.58), channel_id=1, source_target_pairs={{0,1},{1,0},{2,3},{3,2},{4,5},{5,4},{6,7},{7,6},{8,9},{9,8},{10,11... | collective-permute-start | bytes 1597448 | tf_op jit(solution)/shard_map/ppermute | solution.py:474
  9.5 19.9 %collective-permute-start.7 = (bf16[2064,128]{1,0:T(8,128)(2,1)}, bf16[2064,128]{1,0:T(8,128)(2,1)}, u32[]{:S(2)}, u32[]{:S(2)}) collective-permute-start(bf16[2064,128]{1,0:T(8,128)(2,1)} %get-tuple-element.69.refs_0_), channel_id=1, source_target_pairs={{0,24},{4,28},{8,16},{12,20},{16,8},{20,12},{24,0},{28,4},{1,25},{... | collective-permute-start | bytes 1585160 | tf_op jit(solution)/shard_map/ppermute | solution.py:471
  12.0 23.9 %collective-permute-start.6 = (bf16[2064,128]{1,0:T(8,128)(2,1)}, bf16[2064,128]{1,0:T(8,128)(2,1)}, u32[]{:S(2)}, u32[]{:S(2)}) collective-permute-start(bf16[2064,128]{1,0:T(8,128)(2,1)} %get-tuple-element.69.refs_0_), channel_id=1, source_target_pairs={{0,16},{4,20},{8,24},{12,28},{16,0},{20,4},{24,8},{28,12},{1,17},{... | collective-permute-start | bytes 1585160 | tf_op jit(solution)/shard_map/ppermute | solution.py:471
  12.5 0.8 copy-start.9
  13.3 22.7 %collective-permute-start.5 = (bf16[2064,128]{1,0:T(8,128)(2,1)}, bf16[2064,128]{1,0:T(8,128)(2,1)}, u32[]{:S(2)}, u32[]{:S(2)}) collective-permute-start(bf16[2064,128]{1,0:T(8,128)(2,1)} %get-tuple-element.69.refs_0_), channel_id=1, source_target_pairs={{0,8},{4,12},{8,0},{12,4},{16,24},{20,28},{24,16},{28,20},{1,9},{5... | collective-permute-start | bytes 1585160 | tf_op jit(solution)/shard_map/ppermute | solution.py:471
  13.8 2.2 %copy-start.3 = (bf16[1024,2048]{1,0:T(8,128)(2,1)S(1)}, bf16[1024,2048]{1,0:T(8,128)(2,1)}, u32[]{:S(2)}) copy-start(bf16[1024,2048]{1,0:T(8,128)(2,1)} %normed_ref.1) | copy-start | bytes 12582916
  16.0 1.0 %copy-start.4 = (bf16[1024,256]{1,0:T(8,128)(2,1)S(1)}, bf16[1024,256]{1,0:T(8,128)(2,1)}, u32[]{:S(2)}) copy-start(bf16[1024,256]{1,0:T(8,128)(2,1)} %own.1) | copy-start | bytes 1572868
  18.8 1.4 %copy-start.6 = (f32[256,2048]{1,0:T(8,128)}, f32[256,2048]{1,0:T(8,128)S(1)}, u32[]{:S(2)}) copy-start(f32[256,2048]{1,0:T(8,128)S(1)} %get-tuple-element.84.g1) | copy-start | bytes 6291460
  22.3 17.5 %collective-permute-start.4 = (bf16[1040,256]{1,0:T(8,128)(2,1)S(1)}, bf16[1040,256]{1,0:T(8,128)(2,1)S(1)}, u32[]{:S(2)}, u32[]{:S(2)}) collective-permute-start(bf16[1040,256]{1,0:T(8,128)(2,1)S(1)} %collective-permute-done.1.refs_0_.b1), channel_id=1, source_target_pairs={{1,0},{2,3},{5,4},{6,7},{9,8},{10,11},{13,12},{14,15},{17,16},{18,... | collective-permute-start | bytes 1597448 | tf_op jit(solution)/shard_map/ppermute | solution.py:480
  23.6 16.2 %collective-permute-start.3 = (bf16[1040,256]{1,0:T(8,128)(2,1)}, bf16[1040,256]{1,0:T(8,128)(2,1)}, u32[]{:S(2)}, u32[]{:S(2)}) collective-permute-start(bf16[1040,256]{1,0:T(8,128)(2,1)} %collective-permute-done.refs_0_.a1), channel_id=1, source_target_pairs={{1,2},{2,1},{5,6},{6,5},{9,10},{10,9},{13,14},{14,13},{17,18},{18,... | collective-permute-start | bytes 1597448 | tf_op jit(solution)/shard_map/ppermute | solution.py:477
  27.4 2.0 %copy-start = (bf16[1024,2048]{1,0:T(8,128)(2,1)}, bf16[1024,2048]{1,0:T(8,128)(2,1)S(1)}, u32[]{:S(2)}) copy-start(bf16[1024,2048]{1,0:T(8,128)(2,1)S(1)} %get-tuple-element.57.normed_ref) | copy-start | bytes 12582916
  36.0 2.3 %collective-permute-start.8 = (bf16[2064,128]{1,0:T(8,128)(2,1)}, bf16[2064,128]{1,0:T(8,128)(2,1)}, u32[]{:S(2)}, u32[]{:S(2)}) collective-permute-start(bf16[2064,128]{1,0:T(8,128)(2,1)} %collective-permute-done.5.refs_2_), channel_id=1, source_target_pairs={{0,4},{4,0},{8,12},{12,8},{16,20},{20,16},{24,28},{28,24},{1,5},{5... | collective-permute-start | bytes 1585160 | tf_op jit(solution)/shard_map/ppermute | solution.py:471
  36.0 3.0 %collective-permute-start.9 = (bf16[2064,128]{1,0:T(8,128)(2,1)}, bf16[2064,128]{1,0:T(8,128)(2,1)}, u32[]{:S(2)}, u32[]{:S(2)}) collective-permute-start(bf16[2064,128]{1,0:T(8,128)(2,1)} %collective-permute-done.6.refs_4_), channel_id=1, source_target_pairs={{0,4},{4,0},{8,12},{12,8},{16,20},{20,16},{24,28},{28,24},{1,5},{5... | collective-permute-start | bytes 1585160 | tf_op jit(solution)/shard_map/ppermute | solution.py:471
  36.5 3.3 %collective-permute-start.10 = (bf16[2064,128]{1,0:T(8,128)(2,1)}, bf16[2064,128]{1,0:T(8,128)(2,1)}, u32[]{:S(2)}, u32[]{:S(2)}) collective-permute-start(bf16[2064,128]{1,0:T(8,128)(2,1)} %collective-permute-done.7.refs_6_), channel_id=1, source_target_pairs={{0,4},{4,0},{8,12},{12,8},{16,20},{20,16},{24,28},{28,24},{1,5},{5... | collective-permute-start | bytes 1585160 | tf_op jit(solution)/shard_map/ppermute | solution.py:471
  39.8 22.3 %collective-permute-start.12 = (bf16[1040,256]{1,0:T(8,128)(2,1)}, bf16[1040,256]{1,0:T(8,128)(2,1)S(1)}, u32[]{:S(2)}, u32[]{:S(2)}) collective-permute-start(bf16[1040,256]{1,0:T(8,128)(2,1)} %collective-permute-done.3.m2), channel_id=1, source_target_pairs={{1,0},{2,3},{5,4},{6,7},{9,8},{10,11},{13,12},{14,15},{17,16},{18,... | collective-permute-start | bytes 1597448 | tf_op jit(solution)/shard_map/ppermute | solution.py:480
  41.1 2.2 %copy-start.1 = (bf16[1024,2048]{1,0:T(8,128)(2,1)S(1)}, bf16[1024,2048]{1,0:T(8,128)(2,1)}, u32[]{:S(2)}) copy-start(bf16[1024,2048]{1,0:T(8,128)(2,1)} %copy-done) | copy-start | bytes 12582916
  43.2 1.0 %copy-start.8 = (bf16[2064,128]{1,0:T(8,128)(2,1)S(1)}, bf16[2064,128]{1,0:T(8,128)(2,1)}, u32[]{:S(2)}) copy-start(bf16[2064,128]{1,0:T(8,128)(2,1)} %get-tuple-element.69.refs_0_) | copy-start | bytes 1585156
  44.3 1.0 %copy-start.10 = (bf16[2064,128]{1,0:T(8,128)(2,1)S(1)}, bf16[2064,128]{1,0:T(8,128)(2,1)}, u32[]{:S(2)}) copy-start(bf16[2064,128]{1,0:T(8,128)(2,1)} %copy-done.9) | copy-start | bytes 1585156
  45.3 10.7 %copy-start.2 = (bf16[1024,2048]{1,0:T(8,128)(2,1)S(1)}, bf16[1024,2048]{1,0:T(8,128)(2,1)}, u32[]{:S(2)}) copy-start(bf16[1024,2048]{1,0:T(8,128)(2,1)} %copy-done) | copy-start | bytes 12582916
  51.2 16.1 %collective-permute-start.11 = (s16[1040,256]{1,0:T(8,128)(2,1)S(1)}, s16[1040,256]{1,0:T(8,128)(2,1)S(1)}, u32[]{:S(2)}, u32[]{:S(2)}) collective-permute-start(s16[1040,256]{1,0:T(8,128)(2,1)S(1)} %get-tuple-element.81), channel_id=1, source_target_pairs={{0,1},{3,2},{4,5},{7,6},{8,9},{11,10},{12,13},{15,14},{16,17},{19,... | collective-permute-start | bytes 1597448 | tf_op jit(solution)/shard_map/ppermute | solution.py:483
  57.4 4.7 %copy-start.7 = (f32[256,2048]{1,0:T(8,128)S(1)}, f32[256,2048]{1,0:T(8,128)}, u32[]{:S(2)}) copy-start(f32[256,2048]{1,0:T(8,128)} %copy-done.6) | copy-start | bytes 6291460
  67.4 5.6 %collective-permute-start.16 = (s16[2096,128]{1,0:T(8,128)(2,1)S(1)}, s16[2096,128]{1,0:T(8,128)(2,1)S(1)}, u32[]{:S(2)}, u32[]{:S(2)}) collective-permute-start(s16[2096,128]{1,0:T(8,128)(2,1)S(1)} %get-tuple-element.100), channel_id=1, source_target_pairs={{0,4},{4,0},{8,12},{12,8},{16,20},{20,16},{24,28},{28,24},{1,5},{5... | collective-permute-start | bytes 1609736 | tf_op jit(solution)/shard_map/ppermute | solution.py:471
  67.4 6.6 %collective-permute-start.17 = (s16[2096,128]{1,0:T(8,128)(2,1)S(1)}, s16[2096,128]{1,0:T(8,128)(2,1)S(1)}, u32[]{:S(2)}, u32[]{:S(2)}) collective-permute-start(s16[2096,128]{1,0:T(8,128)(2,1)S(1)} %get-tuple-element.102), channel_id=1, source_target_pairs={{0,4},{4,0},{8,12},{12,8},{16,20},{20,16},{24,28},{28,24},{1,5},{5... | collective-permute-start | bytes 1609736 | tf_op jit(solution)/shard_map/ppermute | solution.py:471
  67.9 8.0 %collective-permute-start.18 = (s16[2096,128]{1,0:T(8,128)(2,1)S(1)}, s16[2096,128]{1,0:T(8,128)(2,1)S(1)}, u32[]{:S(2)}, u32[]{:S(2)}) collective-permute-start(s16[2096,128]{1,0:T(8,128)(2,1)S(1)} %get-tuple-element.104), channel_id=1, source_target_pairs={{0,4},{4,0},{8,12},{12,8},{16,20},{20,16},{24,28},{28,24},{1,5},{5... | collective-permute-start | bytes 1609736 | tf_op jit(solution)/shard_map/ppermute | solution.py:471
  68.0 9.1 %collective-permute-start.15 = (s16[2096,128]{1,0:T(8,128)(2,1)S(1)}, s16[2096,128]{1,0:T(8,128)(2,1)S(1)}, u32[]{:S(2)}, u32[]{:S(2)}) collective-permute-start(s16[2096,128]{1,0:T(8,128)(2,1)S(1)} %get-tuple-element.98), channel_id=1, source_target_pairs={{0,4},{4,0},{8,12},{12,8},{16,20},{20,16},{24,28},{28,24},{1,5},{5... | collective-permute-start | bytes 1609736 | tf_op jit(solution)/shard_map/ppermute | solution.py:471
  68.4 15.6 %collective-permute-start.14 = (s16[1040,256]{1,0:T(8,128)(2,1)S(1)}, s16[1040,256]{1,0:T(8,128)(2,1)S(1)}, u32[]{:S(2)}, u32[]{:S(2)}) collective-permute-start(s16[1040,256]{1,0:T(8,128)(2,1)S(1)} %get-tuple-element.96), channel_id=1, source_target_pairs={{0,1},{3,2},{4,5},{7,6},{8,9},{11,10},{12,13},{15,14},{16,17},{19,... | collective-permute-start | bytes 1597448 | tf_op jit(solution)/shard_map/ppermute | solution.py:483
  73.0 11.1 %collective-permute-start.13 = (s16[1040,256]{1,0:T(8,128)(2,1)S(1)}, s16[1040,256]{1,0:T(8,128)(2,1)S(1)}, u32[]{:S(2)}, u32[]{:S(2)}) collective-permute-start(s16[1040,256]{1,0:T(8,128)(2,1)S(1)} %hop.3), channel_id=1, source_target_pairs={{1,2},{2,1},{5,6},{6,5},{9,10},{10,9},{13,14},{14,13},{17,18},{18,... | collective-permute-start | bytes 1597448 | tf_op jit(solution)/shard_map/ppermute | solution.py:477
  74.1 25.2 %collective-permute-start.23 = (s16[2096,128]{1,0:T(8,128)(2,1)S(1)}, s16[2096,128]{1,0:T(8,128)(2,1)S(1)}, u32[]{:S(2)}, u32[]{:S(2)}) collective-permute-start(s16[2096,128]{1,0:T(8,128)(2,1)S(1)} %combine.5), channel_id=1, source_target_pairs={{0,8},{4,12},{8,0},{12,4},{16,24},{20,28},{24,16},{28,20},{1,9},{5... | collective-permute-start | bytes 1609736 | tf_op jit(solution)/shard_map/ppermute | solution.py:471
  76.0 25.1 %collective-permute-start.22 = (s16[2096,128]{1,0:T(8,128)(2,1)S(1)}, s16[2096,128]{1,0:T(8,128)(2,1)S(1)}, u32[]{:S(2)}, u32[]{:S(2)}) collective-permute-start(s16[2096,128]{1,0:T(8,128)(2,1)S(1)} %combine.6), channel_id=1, source_target_pairs={{0,16},{4,20},{8,24},{12,28},{16,0},{20,4},{24,8},{28,12},{1,17},{... | collective-permute-start | bytes 1609736 | tf_op jit(solution)/shard_map/ppermute | solution.py:471
  77.2 23.9 %collective-permute-start.21 = (s16[2096,128]{1,0:T(8,128)(2,1)S(1)}, s16[2096,128]{1,0:T(8,128)(2,1)S(1)}, u32[]{:S(2)}, u32[]{:S(2)}) collective-permute-start(s16[2096,128]{1,0:T(8,128)(2,1)S(1)} %combine.7), channel_id=1, source_target_pairs={{0,24},{4,28},{8,16},{12,20},{16,8},{20,12},{24,0},{28,4},{1,25},{... | collective-permute-start | bytes 1609736 | tf_op jit(solution)/shard_map/ppermute | solution.py:471
  78.6 12.9 %copy-start.5 = (bf16[1024,256]{1,0:T(8,128)(2,1)S(1)}, bf16[1024,256]{1,0:T(8,128)(2,1)}, u32[]{:S(2)}) copy-start(bf16[1024,256]{1,0:T(8,128)(2,1)} %own.1) | copy-start | bytes 1572868
  84.4 18.6 %collective-permute-start.20 = (s16[1040,256]{1,0:T(8,128)(2,1)S(1)}, s16[1040,256]{1,0:T(8,128)(2,1)S(1)}, u32[]{:S(2)}, u32[]{:S(2)}) collective-permute-start(s16[1040,256]{1,0:T(8,128)(2,1)S(1)} %hop.5), channel_id=1, source_target_pairs={{1,2},{2,1},{5,6},{6,5},{9,10},{10,9},{13,14},{14,13},{17,18},{18,... | collective-permute-start | bytes 1597448 | tf_op jit(solution)/shard_map/ppermute | solution.py:477
  85.7 17.3 %collective-permute-start.19 = (s16[1040,256]{1,0:T(8,128)(2,1)S(1)}, s16[1040,256]{1,0:T(8,128)(2,1)S(1)}, u32[]{:S(2)}, u32[]{:S(2)}) collective-permute-start(s16[1040,256]{1,0:T(8,128)(2,1)S(1)} %hop.4), channel_id=1, source_target_pairs={{0,1},{1,0},{2,3},{3,2},{4,5},{5,4},{6,7},{7,6},{8,9},{9,8},{10,11... | collective-permute-start | bytes 1597448 | tf_op jit(solution)/shard_map/ppermute | solution.py:474

commit v7 on v6

--- a/solution.py
+++ b/solution.py
@@ -10,7 +10,6 @@
 MIB = 1024 * 1024
 GROUP = 128
 PAD = 16
-EXTRA = 16
 
 
 def encode(block):
@@ -66,52 +65,6 @@
         )
 
     return block
-
-
-def pack_kernel(
-    column_blocks, rows_ref, columns_ref, tiles_ref, chunk_ref, message_ref, padded_ref, slots, sems
-):
-    rows = tiles_ref.shape[0]
-    tokens = chunk_ref.shape[0]
-    copies = [
-        pltpu.make_async_copy(rows_ref, slots.at[0], sems.at[0]),
-        pltpu.make_async_copy(columns_ref, slots.at[1], sems.at[1]),
-        pltpu.make_async_copy(chunk_ref, padded_ref.at[pl.ds(0, tokens)], sems.at[2]),
-        pltpu.make_async_copy(tiles_ref, message_ref.at[pl.ds(0, rows)], sems.at[3]),
-    ]
-    for copy in copies:
-        copy.start()
-    padded_ref[tokens:, :] = jnp.zeros((EXTRA, chunk_ref.shape[1]), padded_ref.dtype)
-    copies[0].wait()
-    copies[1].wait()
-    lane = lax.broadcasted_iota(jnp.int32, (PAD, tiles_ref.shape[1]), 1)
-    positions = jnp.zeros(lane.shape, jnp.int32)
-    for slot in range(rows_ref.shape[1]):
-        row, column = slots[0, 0, slot], slots[1, 0, slot]
-        position = jnp.where(column >= 0, row * column_blocks + column + 1, 0)
-        positions = jnp.where(lane == slot, position, positions)
-    message_ref[rows:, :] = positions.astype(jnp.float32).astype(message_ref.dtype)
-    copies[2].wait()
-    copies[3].wait()
-
-
-def pack(rows, columns, tiles, chunk, column_blocks):
-    return pl.pallas_call(
-        functools.partial(pack_kernel, column_blocks),
-        in_specs=[pl.BlockSpec(memory_space=pltpu.HBM)] * 4,
-        out_specs=[VMEM, VMEM],
-        out_shape=[
-            jax.ShapeDtypeStruct((tiles.shape[0] + PAD, tiles.shape[1]), tiles.dtype),
-            jax.ShapeDtypeStruct((chunk.shape[0] + EXTRA, chunk.shape[1]), chunk.dtype),
-        ],
-        scratch_shapes=[
-            pltpu.SMEM((2,) + rows.shape, jnp.int32),
-            pltpu.SemaphoreType.DMA((4,)),
-        ],
-        compiler_params=params(63),
-        cost_estimate=LITTLE,
-        name="pack",
-    )(rows, columns, tiles, chunk)
 
 
 def first_kernel(column_blocks, place_ref, normed_ref, *refs):
@@ -129,17 +82,17 @@
     copy.start()
     weight_ref[...] = jnp.zeros_like(weight_ref)
     copy.wait()
+    features = normed_ref.shape[1]
     for k, message_ref in enumerate(message_refs):
         for slot in range(capacity):
             code = scalars[k, slot]
-
-            @pl.when(code >= 0)
-            def _():
-                row = aligned(code // column_blocks, tile)
-                column = aligned(code % column_blocks, tile)
-                weight_ref[row, column] = message_ref[slot * tile : (slot + 1) * tile, :]
-
-    far = weight_ref[:, aligned(chunks - 1 - place_ref[0], chunk_width)]
+            filled = code >= 0
+            row = jnp.where(filled, code // column_blocks, features // tile)
+            column = jnp.where(filled, code % column_blocks, 0)
+            weight_ref[aligned(row, tile), aligned(column, tile)] = message_ref[
+                slot * tile : (slot + 1) * tile, :
+            ]
+    far = weight_ref[:features, aligned(chunks - 1 - place_ref[0], chunk_width)]
     partial[...] = jnp.dot(normed_ref[...], far, preferred_element_type=jnp.float32)
     write_message(
         first_ref, tokens, lambda group: partial[group * GROUP : (group + 1) * GROUP, :]
@@ -155,7 +108,7 @@
         in_specs=[SMEM, VMEM] + [VMEM] * len(messages),
         out_specs=[VMEM, VMEM, VMEM],
         out_shape=[
-            jax.ShapeDtypeStruct((features, width), jnp.bfloat16),
+            jax.ShapeDtypeStruct((features + tile, width), jnp.bfloat16),
             jax.ShapeDtypeStruct((tokens + PAD, width // chunks), jnp.int16),
             jax.ShapeDtypeStruct((len(messages), tile), jnp.int32),
         ],
@@ -176,7 +129,9 @@
     for n in range(partial_ref.shape[1] // step):
         span = slice(n * step, (n + 1) * step)
         partial_ref[:, span] = jnp.dot(
-            normed_ref[...], weight_ref[:, span], preferred_element_type=jnp.float32
+            normed_ref[...],
+            weight_ref[: normed_ref.shape[1], span],
+            preferred_element_type=jnp.float32,
         )
     columns = aligned(place_ref[0] ^ 2, chunk_width)
     write_message(
@@ -253,6 +208,24 @@
         jnp.where(place < 2, 2, 1),
         jnp.where(place < 2, 3, 0),
     )
+
+
+def widen_kernel(chunk_ref, wide_ref):
+    tokens = chunk_ref.shape[0]
+    wide_ref[:tokens, :] = chunk_ref[...]
+    wide_ref[tokens:, :] = jnp.zeros((PAD, chunk_ref.shape[1]), chunk_ref.dtype)
+
+
+def widen(chunk):
+    return pl.pallas_call(
+        widen_kernel,
+        in_specs=[VMEM],
+        out_specs=VMEM,
+        out_shape=jax.ShapeDtypeStruct((chunk.shape[0] + PAD, chunk.shape[1]), chunk.dtype),
+        compiler_params=params(4),
+        cost_estimate=LITTLE,
+        name="widen",
+    )(chunk)
 
 
 def product(turned, normed_ref, out_ref):
@@ -435,8 +408,8 @@
     ).astype(out_ref.dtype)
 
 
-def grad_inputs(place, weight, *chunks):
-    features, width = weight.shape
+def grad_inputs(place, features, weight, *chunks):
+    width = weight.shape[1]
     tokens = chunks[0].shape[0]
     block = 512
     return pl.pallas_call(
@@ -482,10 +455,11 @@
     def inward(x):
         return lax.ppermute(x, "tensor", [(0, 1), (3, 2)])
 
-    message, padded = pack(
-        tile_rows, tile_columns, tile_values.reshape(rows, tile), cotangent, column_blocks
-    )
-    a1, b1 = pairs(padded), middle(padded)
+    positions = jnp.where(tile_columns >= 0, tile_rows * column_blocks + tile_columns + 1, 0)
+    positions = jnp.pad(positions.astype(jnp.bfloat16), ((0, PAD - 1), (0, tile - capacity)))
+    message = jnp.concatenate([tile_values.reshape(rows, tile), positions], axis=0)
+    wide = widen(cotangent)
+    a1, b1 = pairs(wide), middle(wide)
     normed, g1 = own_gradient(normed, cotangent)
     same_core = [message] + [swap(message, 2 * chip) for chip in range(1, chips)]
     beside = swap(message, 1)
@@ -517,7 +491,7 @@
 
     by_pair = pairs(hop(lambda p: p ^ 1, place, partial, crossing))
     by_middle = middle(hop(lambda p: 3 - p, place, partial, to_middle))
-    grad_input = grad_inputs(place, weight, cotangent, a1, b1, e2, m2, d3)
+    grad_input = grad_inputs(place, normed.shape[1], weight, cotangent, a1, b1, e2, m2, d3)
     update = normalized_update(own, terms, tile_values.shape[1:])
     by_pair, by_middle, update = lax.optimization_barrier((by_pair, by_middle, update))
     values = last_hop(place, partial, by_pair, by_middle)

time: 105 us -> 104 us (level)
  local copies, waits for them, and re-layouts: 11.7 us -> 8.62 us
  waiting for transfers between devices: 19.3 us -> 21.8 us
  other arithmetic: 0 us -> 1.81 us
  starting transfers between devices: 35.9 us -> 34.7 us
    unnamed x22 -> x20, local copies, waits for them, and re-layouts: 11.7 us -> 8.62 us
    pallas_call x1, Pallas kernels: 2.21 us -> 0.04 us  [widen(): pl.pallas_call(widen_kernel, in_specs=[VMEM], out_specs=VMEM, out_shape=j...]
    ppermute x14, waiting for transfers between devices: 11.7 us -> 13.3 us  [swap(): return lax.ppermute(x, 'fsdp', [(i, i ^ mask) for i in range(devices)])]
    ppermute x2, starting transfers between devices: 8.94 us -> 7.72 us  [inward(): return lax.ppermute(x, 'tensor', [(0, 1), (3, 2)])]
    pallas_call x2, Pallas kernels: 3.62 us -> 4.82 us  [chunk_gradient(): pl.pallas_call(chunk_kernel, in_specs=[VMEM] + [VMEM] * len(chunks), out_...]
    concatenate x0 -> x1, other arithmetic: none -> 1.08 us  [local(): jnp.concatenate([tile_values.reshape(rows, tile), positions], axis=0)]
  transfers between devices with their start and end apart: 24 -> 24, of which waited for: 8 -> 8; matrix products, arithmetic and copies ran while one was open for 0% -> 0% of each run, Pallas kernels for 32% -> 33%
where the time goes in v7:
time: 104 us; the launch traced here: 103 us
  Pallas kernels  35.4 us (34%)
  starting transfers between devices  34.7 us (33%)
  waiting for transfers between devices  21.8 us (21%)
  local copies, waits for them, and re-layouts  8.62 us (8%)
  other arithmetic  1.81 us (2%)
    ppermute x14, waiting for transfers between devices, swap(): return lax.ppermute(x, 'fsdp', [(i, i ^ mask) for i in range(devices)])  13.3 us
    ppermute x2, starting transfers between devices, pairs(): return lax.ppermute(x, 'tensor', [(0, 1), (1, 0), (2, 3), (3, 2)])  10.5 us
    ppermute x14, starting transfers between devices, swap(): return lax.ppermute(x, 'fsdp', [(i, i ^ mask) for i in range(devices)])  9.28 us
    unnamed x20, local copies, waits for them, and re-layouts  8.62 us
    pallas_call x1, Pallas kernels, grad_inputs(): pl.pallas_call(grad_input_kernel, grid_spec=pltpu.PrefetchScalarGridSpec(...  8.04 us
    ppermute x2, starting transfers between devices, inward(): return lax.ppermute(x, 'tensor', [(0, 1), (3, 2)])  7.72 us
    pallas_call x1, Pallas kernels, first_values(): pl.pallas_call(functools.partial(first_kernel, column_blocks), in_specs=[...  5.54 us
    ppermute x2, waiting for transfers between devices, inward(): return lax.ppermute(x, 'tensor', [(0, 1), (3, 2)])  5.45 us
  transfers between devices with their start and end apart: 24, of which 8 were waited for; matrix products, arithmetic and copies ran while one was open for 0% of the time, Pallas kernels for 33%

profile of v7, /device:TPU:0, one launch (start us, length us, event | category | flops | bytes accessed | tf_op | source)
XLA Modules:
  0.0 103.2 jit_solution(12132523517758536757)
XLA Ops:
  0.6 0.7 fusion.2
  1.4 1.1 %fusion.1.refs_0_ = bf16[2064,128]{1,0:T(8,128)(2,1)S(1)} fusion(bf16[1,16]{1,0:T(2,128)(2,1)S(1)} %fusion.2, bf16[2048,128]{1,0:T(8,128)(2,1)} %bitcast.4), kind=kLoop, calls=%fused_computation.2 | loop fusion | flops 1585152 | bytes 1052704 | tf_op jit(solution)/shard_map/concatenate | solution.py:460
  2.5 0.5 collective-permute-start.2
  3.0 1.0 %copy-done.4 = bf16[1024,256]{1,0:T(8,128)(2,1)S(1)} copy-done((bf16[1024,256]{1,0:T(8,128)(2,1)S(1)}, bf16[1024,256]{1,0:T(8,128)(2,1)}, u32[]{:S(2)}) %copy-start.4) | copy-done | bytes 524312
  4.1 1.5 %collective-permute-start.1 = (bf16[1040,256]{1,0:T(8,128)(2,1)S(1)}, bf16[1040,256]{1,0:T(8,128)(2,1)}, u32[]{:S(2)}, u32[]{:S(2)}) collective-permute-start(bf16[1040,256]{1,0:T(8,128)(2,1)S(1)} %widen.1), channel_id=1, source_target_pairs={{1,2},{2,1},{5,6},{6,5},{9,10},{10,9},{13,14},{14,13},{17,18},{18,... | collective-permute-start | bytes 1597448 | tf_op jit(solution)/shard_map/ppermute | solution.py:450
  5.5 4.7 %collective-permute-start = (bf16[1040,256]{1,0:T(8,128)(2,1)S(1)}, bf16[1040,256]{1,0:T(8,128)(2,1)}, u32[]{:S(2)}, u32[]{:S(2)}) collective-permute-start(bf16[1040,256]{1,0:T(8,128)(2,1)S(1)} %widen.1), channel_id=1, source_target_pairs={{0,1},{1,0},{2,3},{3,2},{4,5},{5,4},{6,7},{7,6},{8,9},{9,8},{10,11... | collective-permute-start | bytes 1597448 | tf_op jit(solution)/shard_map/ppermute | solution.py:447
  10.2 2.4 %collective-permute-start.7 = (bf16[2064,128]{1,0:T(8,128)(2,1)S(1)}, bf16[2064,128]{1,0:T(8,128)(2,1)}, u32[]{:S(2)}, u32[]{:S(2)}) collective-permute-start(bf16[2064,128]{1,0:T(8,128)(2,1)S(1)} %fusion.1.refs_0_), channel_id=1, source_target_pairs={{0,24},{4,28},{8,16},{12,20},{16,8},{20,12},{24,0},{28,4},{1,25},{... | collective-permute-start | bytes 1585160 | tf_op jit(solution)/shard_map/ppermute | solution.py:444
  12.7 0.5 collective-permute-start.6
  13.2 0.8 copy-done.8
  14.0 0.5 collective-permute-start.5
  14.5 2.2 %copy-done.3 = bf16[1024,2048]{1,0:T(8,128)(2,1)S(1)} copy-done((bf16[1024,2048]{1,0:T(8,128)(2,1)S(1)}, bf16[1024,2048]{1,0:T(8,128)(2,1)}, u32[]{:S(2)}) %copy-start.3) | copy-done | bytes 4194328
  16.7 1.7 %own_gradient.1 = (bf16[1024,2048]{1,0:T(8,128)(2,1)S(1)}, f32[256,2048]{1,0:T(8,128)S(1)}) custom-call(bf16[1024,2048]{1,0:T(8,128)(2,1)S(1)} %copy-done.3, bf16[1024,256]{1,0:T(8,128)(2,1)S(1)} %copy-done.5), custom_call_target="tpu_custom_call" | custom-call | flops 1 | bytes 1 | tf_op jit(solution)/shard_map/own_gradient/pallas_call | solution.py:255
  18.4 1.3 %copy-done.6 = f32[256,2048]{1,0:T(8,128)} copy-done((f32[256,2048]{1,0:T(8,128)}, f32[256,2048]{1,0:T(8,128)S(1)}, u32[]{:S(2)}) %copy-start.6) | copy-done | bytes 2097176
  19.8 3.0 %collective-permute-done.refs_0_.a1 = bf16[1040,256]{1,0:T(8,128)(2,1)} collective-permute-done((bf16[1040,256]{1,0:T(8,128)(2,1)S(1)}, bf16[1040,256]{1,0:T(8,128)(2,1)}, u32[]{:S(2)}, u32[]{:S(2)}) %collective-permute-start) | collective-permute-done | bytes 532512 | tf_op jit(solution)/shard_map/ppermute | solution.py:447
  22.8 1.3 %collective-permute-start.4 = (bf16[1040,256]{1,0:T(8,128)(2,1)}, bf16[1040,256]{1,0:T(8,128)(2,1)}, u32[]{:S(2)}, u32[]{:S(2)}) collective-permute-start(bf16[1040,256]{1,0:T(8,128)(2,1)} %collective-permute-done.1.refs_0_.b1), channel_id=1, source_target_pairs={{1,0},{2,3},{5,4},{6,7},{9,8},{10,11},{13,12},{14,15},{17,16},{18,... | collective-permute-start | bytes 1597448 | tf_op jit(solution)/shard_map/ppermute | solution.py:453
  24.1 1.5 %collective-permute-start.3 = (bf16[1040,256]{1,0:T(8,128)(2,1)}, bf16[1040,256]{1,0:T(8,128)(2,1)}, u32[]{:S(2)}, u32[]{:S(2)}) collective-permute-start(bf16[1040,256]{1,0:T(8,128)(2,1)} %collective-permute-done.refs_0_.a1), channel_id=1, source_target_pairs={{1,2},{2,1},{5,6},{6,5},{9,10},{10,9},{13,14},{14,13},{17,18},{18,... | collective-permute-start | bytes 1597448 | tf_op jit(solution)/shard_map/ppermute | solution.py:450
  25.6 2.3 %chunk_gradient.2.g2 = f32[256,2048]{1,0:T(8,128)S(1)} custom-call(bf16[1024,2048]{1,0:T(8,128)(2,1)S(1)} %get-tuple-element.55.normed_ref, bf16[1040,256]{1,0:T(8,128)(2,1)} %collective-permute-done.refs_0_.a1), custom_call_target="tpu_custom_call" | custom-call | flops 1 | bytes 1 | tf_op jit(solution)/shard_map/chunk_gradient/pallas_call | solution.py:271
  27.9 8.5 %collective-permute-done.6.refs_4_ = bf16[2064,128]{1,0:T(8,128)(2,1)} collective-permute-done((bf16[2064,128]{1,0:T(8,128)(2,1)S(1)}, bf16[2064,128]{1,0:T(8,128)(2,1)}, u32[]{:S(2)}, u32[]{:S(2)}) %collective-permute-start.6) | collective-permute-done | bytes 528416 | tf_op jit(solution)/shard_map/ppermute | solution.py:444
  36.5 0.5 collective-permute-start.9
  37.0 1.7 %collective-permute-done.8.refs_3_ = bf16[2064,128]{1,0:T(8,128)(2,1)} collective-permute-done((bf16[2064,128]{1,0:T(8,128)(2,1)}, bf16[2064,128]{1,0:T(8,128)(2,1)}, u32[]{:S(2)}, u32[]{:S(2)}) %collective-permute-start.8) | collective-permute-done | bytes 528416 | tf_op jit(solution)/shard_map/ppermute | solution.py:444
  38.7 0.8 collective-permute-done.9.refs_5_
  39.5 0.8 collective-permute-done.10.refs_7_
  40.3 1.3 %collective-permute-start.12 = (bf16[1040,256]{1,0:T(8,128)(2,1)}, bf16[1040,256]{1,0:T(8,128)(2,1)S(1)}, u32[]{:S(2)}, u32[]{:S(2)}) collective-permute-start(bf16[1040,256]{1,0:T(8,128)(2,1)} %collective-permute-done.3.m2), channel_id=1, source_target_pairs={{1,0},{2,3},{5,4},{6,7},{9,8},{10,11},{13,12},{14,15},{17,16},{18,... | collective-permute-start | bytes 1597448 | tf_op jit(solution)/shard_map/ppermute | solution.py:453
  41.6 2.2 %copy-done.1 = bf16[1024,2048]{1,0:T(8,128)(2,1)S(1)} copy-done((bf16[1024,2048]{1,0:T(8,128)(2,1)S(1)}, bf16[1024,2048]{1,0:T(8,128)(2,1)}, u32[]{:S(2)}) %copy-start.1) | copy-done | bytes 4194328
  43.7 1.0 %copy-done.9 = bf16[2064,128]{1,0:T(8,128)(2,1)S(1)} copy-done((bf16[2064,128]{1,0:T(8,128)(2,1)S(1)}, bf16[2064,128]{1,0:T(8,128)(2,1)}, u32[]{:S(2)}) %copy-start.9) | copy-done | bytes 528408
  44.8 5.5 %first_values.1 = (bf16[2176,1024]{1,0:T(8,128)(2,1)S(1)}, s16[1040,256]{1,0:T(8,128)(2,1)S(1)}, s32[8,128]{1,0:T(8,128)S(1)}) custom-call(s32[1]{0:T(128)} %bitcast.place_ref, bf16[1024,2048]{1,0:T(8,128)(2,1)S(1)} %copy-done.1, bf16[2064,128]{1,0:T(8,128)(2,1)S(1)} %fusion.1.refs_0_, bf16[2064,128]{1,0:T(8,128)(2,1)S(1)} %copy-done.9, ...), custom_call_target="tpu_custom_call" | custom-call | flops 1 | bytes 1 | tf_op jit(solution)/shard_map/first_values/pallas_call | solution.py:106
  50.3 5.0 %collective-permute-start.11 = (s16[1040,256]{1,0:T(8,128)(2,1)S(1)}, s16[1040,256]{1,0:T(8,128)(2,1)S(1)}, u32[]{:S(2)}, u32[]{:S(2)}) collective-permute-start(s16[1040,256]{1,0:T(8,128)(2,1)S(1)} %get-tuple-element.77), channel_id=1, source_target_pairs={{0,1},{3,2},{4,5},{7,6},{8,9},{11,10},{12,13},{15,14},{16,17},{19,... | collective-permute-start | bytes 1597448 | tf_op jit(solution)/shard_map/ppermute | solution.py:456
  55.4 2.5 %chunk_gradient.3.g3 = f32[256,2048]{1,0:T(8,128)S(1)} custom-call(bf16[1024,2048]{1,0:T(8,128)(2,1)S(1)} %copy-done.2, bf16[1040,256]{1,0:T(8,128)(2,1)} %collective-permute-done.1.refs_0_.b1, bf16[1040,256]{1,0:T(8,128)(2,1)} %collective-permute-done.4.refs_1_.e2), custom_call_target="tpu_custom_call" | custom-call | flops 1 | bytes 1 | tf_op jit(solution)/shard_map/chunk_gradient/pallas_call | solution.py:271
  57.9 4.7 %partial_values.1 = (f32[1024,1024]{1,0:T(8,128)S(1)}, s16[1040,256]{1,0:T(8,128)(2,1)S(1)}) custom-call(s32[1]{0:T(128)} %bitcast.place_ref, bf16[1024,2048]{1,0:T(8,128)(2,1)S(1)} %copy-done.2, bf16[2176,1024]{1,0:T(8,128)(2,1)S(1)} %get-tuple-element.73.weight_ref), custom_call_target="tpu_custom_call" | custom-call | flops 1 | bytes 1 | tf_op jit(solution)/shard_map/partial_values/pallas_call | solution.py:143
  62.6 5.3 %slot_terms.1 = (f32[2048,128]{1,0:T(8,128)S(1)}, f32[2048,128]{1,0:T(8,128)S(1)}, f32[2048,128]{1,0:T(8,128)S(1)}, f32[2048,128]{1,0:T(8,128)S(1)}, s16[2096,12...) custom-call(s32[8,128]{1,0:T(8,128)S(1)} %get-tuple-element.78.codes, ...), custom_call_target="tpu_custom_call" | custom-call | flops 1 | bytes 1 | tf_op jit(solution)/shard_map/slot_terms/pallas_call | solution.py:327
  68.0 0.5 collective-permute-start.17
  68.6 0.4 collective-permute-start.15
  69.0 2.7 %collective-permute-start.14 = (s16[1040,256]{1,0:T(8,128)(2,1)S(1)}, s16[1040,256]{1,0:T(8,128)(2,1)S(1)}, u32[]{:S(2)}, u32[]{:S(2)}) collective-permute-start(s16[1040,256]{1,0:T(8,128)(2,1)S(1)} %get-tuple-element.92), channel_id=1, source_target_pairs={{0,1},{3,2},{4,5},{7,6},{8,9},{11,10},{12,13},{15,14},{16,17},{19,... | collective-permute-start | bytes 1597448 | tf_op jit(solution)/shard_map/ppermute | solution.py:456
  71.7 0.3 hop.3
  72.1 0.7 collective-permute-start.13
  72.8 0.4 combine.5
  73.1 1.6 %collective-permute-start.23 = (s16[2096,128]{1,0:T(8,128)(2,1)S(1)}, s16[2096,128]{1,0:T(8,128)(2,1)S(1)}, u32[]{:S(2)}, u32[]{:S(2)}) collective-permute-start(s16[2096,128]{1,0:T(8,128)(2,1)S(1)} %combine.5), channel_id=1, source_target_pairs={{0,8},{4,12},{8,0},{12,4},{16,24},{20,28},{24,16},{28,20},{1,9},{5... | collective-permute-start | bytes 1609736 | tf_op jit(solution)/shard_map/ppermute | solution.py:444
  74.7 0.4 combine.6
  75.1 0.8 collective-permute-start.22
  75.9 0.4 combine.7
  76.2 1.3 %collective-permute-start.21 = (s16[2096,128]{1,0:T(8,128)(2,1)S(1)}, s16[2096,128]{1,0:T(8,128)(2,1)S(1)}, u32[]{:S(2)}, u32[]{:S(2)}) collective-permute-start(s16[2096,128]{1,0:T(8,128)(2,1)S(1)} %combine.7), channel_id=1, source_target_pairs={{0,24},{4,28},{8,16},{12,20},{16,8},{20,12},{24,0},{28,4},{1,25},{... | collective-permute-start | bytes 1609736 | tf_op jit(solution)/shard_map/ppermute | solution.py:444
  77.7 5.4 %collective-permute-done.14.arrived_ref = s16[1040,256]{1,0:T(8,128)(2,1)S(1)} collective-permute-done((s16[1040,256]{1,0:T(8,128)(2,1)S(1)}, s16[1040,256]{1,0:T(8,128)(2,1)S(1)}, u32[]{:S(2)}, u32[]{:S(2)}) %collective-permute-start.14) | collective-permute-done | bytes 532512 | tf_op jit(solution)/shard_map/ppermute | solution.py:456
  83.5 0.9 collective-permute-start.20
  84.8 5.9 %collective-permute-start.19 = (s16[1040,256]{1,0:T(8,128)(2,1)S(1)}, s16[1040,256]{1,0:T(8,128)(2,1)S(1)}, u32[]{:S(2)}, u32[]{:S(2)}) collective-permute-start(s16[1040,256]{1,0:T(8,128)(2,1)S(1)} %hop.4), channel_id=1, source_target_pairs={{0,1},{1,0},{2,3},{3,2},{4,5},{5,4},{6,7},{7,6},{8,9},{9,8},{10,11... | collective-permute-start | bytes 1597448 | tf_op jit(solution)/shard_map/ppermute | solution.py:447
  90.7 8.0 %grad_inputs.1 = bf16[1024,2048]{1,0:T(8,128)(2,1)} custom-call(s32[1]{0:T(128)} %bitcast.place_ref, bf16[2176,1024]{1,0:T(8,128)(2,1)S(1)} %get-tuple-element.73.weight_ref, bf16[1024,256]{1,0:T(8,128)(2,1)S(1)} %copy-done.5, bf16[1040,256]{1,0:T(8,128)(2,1)} %collective-permute-done.refs_0_.a1, bf16[1040,256]{1,0:T(8,128)(2,1)} %collective-permute-done.1.refs_0_.b1, ...), custom_call_target="tpu_custom_call" | custom-call | flops 4294967296 | bytes 12582912 | tf_op jit(solution)/shard_map/grad_inputs/pallas_call | solution.py:415
  98.7 1.5 %collective-permute-done.22.refs_2_ = s16[2096,128]{1,0:T(8,128)(2,1)S(1)} collective-permute-done((s16[2096,128]{1,0:T(8,128)(2,1)S(1)}, s16[2096,128]{1,0:T(8,128)(2,1)S(1)}, u32[]{:S(2)}, u32[]{:S(2)}) %collective-permute-start.22) | collective-permute-done | bytes 536608 | tf_op jit(solution)/shard_map/ppermute | solution.py:444
  100.2 1.9 %normalized_update.1 = bf16[16,128,128]{2,1,0:T(8,128)(2,1)} custom-call(f32[2048,128]{1,0:T(8,128)S(1)} %combine.4.refs_0_, s16[2096,128]{1,0:T(8,128)(2,1)S(1)} %collective-permute-done.21.refs_1_, s16[2096,128]{1,0:T(8,128)(2,1)S(1)} %collective-permute-done.22.refs_2_, s16[2096,128]{1,0:T(8,128)(2,1)S(1)} %collective-permute-done.23.refs_3_), custom_call_target="tpu_custom_call" | custom-call | flops 1 | bytes 1 | tf_op jit(solution)/shard_map/normalized_update/pallas_call | solution.py:385
  102.1 1.1 %last_hop.1 = bf16[1024,256]{1,0:T(8,128)(2,1)} custom-call(s32[1]{0:T(128)} %bitcast.place_ref, f32[1024,1024]{1,0:T(8,128)S(1)} %get-tuple-element.76.partial_ref, s16[1040,256]{1,0:T(8,128)(2,1)S(1)} %collective-permute-done.19.right_ref, s16[1040,256]{1,0:T(8,128)(2,1)S(1)} %collective-permute-done.20.left_ref), custom_call_target="tpu_custom_call" | custom-call | flops 1 | bytes 1 | tf_op jit(solution)/shard_map/last_hop/pallas_call | solution.py:193
  (39 shorter events, 1.2 us)
Async XLA Ops:
  0.6 13.9 %copy-start.5 = (bf16[1024,256]{1,0:T(8,128)(2,1)S(1)}, bf16[1024,256]{1,0:T(8,128)(2,1)}, u32[]{:S(2)}) copy-start(bf16[1024,256]{1,0:T(8,128)(2,1)} %own.1) | copy-start | bytes 1572868
  2.5 10.7 %collective-permute-start.2 = (bf16[2064,128]{1,0:T(8,128)(2,1)S(1)}, bf16[2064,128]{1,0:T(8,128)(2,1)S(1)}, u32[]{:S(2)}, u32[]{:S(2)}) collective-permute-start(bf16[2064,128]{1,0:T(8,128)(2,1)S(1)} %fusion.1.refs_0_), channel_id=1, source_target_pairs={{0,4},{4,0},{8,12},{12,8},{16,20},{20,16},{24,28},{28,24},{1,5},{5... | collective-permute-start | bytes 1585160 | tf_op jit(solution)/shard_map/ppermute | solution.py:444
  3.0 1.0 %copy-start.4 = (bf16[1024,256]{1,0:T(8,128)(2,1)S(1)}, bf16[1024,256]{1,0:T(8,128)(2,1)}, u32[]{:S(2)}) copy-start(bf16[1024,256]{1,0:T(8,128)(2,1)} %own.1) | copy-start | bytes 1572868
  4.1 15.7 %collective-permute-start.1 = (bf16[1040,256]{1,0:T(8,128)(2,1)S(1)}, bf16[1040,256]{1,0:T(8,128)(2,1)}, u32[]{:S(2)}, u32[]{:S(2)}) collective-permute-start(bf16[1040,256]{1,0:T(8,128)(2,1)S(1)} %widen.1), channel_id=1, source_target_pairs={{1,2},{2,1},{5,6},{6,5},{9,10},{10,9},{13,14},{14,13},{17,18},{18,... | collective-permute-start | bytes 1597448 | tf_op jit(solution)/shard_map/ppermute | solution.py:450
  5.5 17.3 %collective-permute-start = (bf16[1040,256]{1,0:T(8,128)(2,1)S(1)}, bf16[1040,256]{1,0:T(8,128)(2,1)}, u32[]{:S(2)}, u32[]{:S(2)}) collective-permute-start(bf16[1040,256]{1,0:T(8,128)(2,1)S(1)} %widen.1), channel_id=1, source_target_pairs={{0,1},{1,0},{2,3},{3,2},{4,5},{5,4},{6,7},{7,6},{8,9},{9,8},{10,11... | collective-permute-start | bytes 1597448 | tf_op jit(solution)/shard_map/ppermute | solution.py:447
  10.2 17.7 %collective-permute-start.7 = (bf16[2064,128]{1,0:T(8,128)(2,1)S(1)}, bf16[2064,128]{1,0:T(8,128)(2,1)}, u32[]{:S(2)}, u32[]{:S(2)}) collective-permute-start(bf16[2064,128]{1,0:T(8,128)(2,1)S(1)} %fusion.1.refs_0_), channel_id=1, source_target_pairs={{0,24},{4,28},{8,16},{12,20},{16,8},{20,12},{24,0},{28,4},{1,25},{... | collective-permute-start | bytes 1585160 | tf_op jit(solution)/shard_map/ppermute | solution.py:444
  12.7 23.7 %collective-permute-start.6 = (bf16[2064,128]{1,0:T(8,128)(2,1)S(1)}, bf16[2064,128]{1,0:T(8,128)(2,1)}, u32[]{:S(2)}, u32[]{:S(2)}) collective-permute-start(bf16[2064,128]{1,0:T(8,128)(2,1)S(1)} %fusion.1.refs_0_), channel_id=1, source_target_pairs={{0,16},{4,20},{8,24},{12,28},{16,0},{20,4},{24,8},{28,12},{1,17},{... | collective-permute-start | bytes 1585160 | tf_op jit(solution)/shard_map/ppermute | solution.py:444
  13.2 0.8 copy-start.8
  14.0 22.5 %collective-permute-start.5 = (bf16[2064,128]{1,0:T(8,128)(2,1)S(1)}, bf16[2064,128]{1,0:T(8,128)(2,1)}, u32[]{:S(2)}, u32[]{:S(2)}) collective-permute-start(bf16[2064,128]{1,0:T(8,128)(2,1)S(1)} %fusion.1.refs_0_), channel_id=1, source_target_pairs={{0,8},{4,12},{8,0},{12,4},{16,24},{20,28},{24,16},{28,20},{1,9},{5... | collective-permute-start | bytes 1585160 | tf_op jit(solution)/shard_map/ppermute | solution.py:444
  14.5 2.2 %copy-start.3 = (bf16[1024,2048]{1,0:T(8,128)(2,1)S(1)}, bf16[1024,2048]{1,0:T(8,128)(2,1)}, u32[]{:S(2)}) copy-start(bf16[1024,2048]{1,0:T(8,128)(2,1)} %normed_ref.1) | copy-start | bytes 12582916
  18.4 1.4 %copy-start.6 = (f32[256,2048]{1,0:T(8,128)}, f32[256,2048]{1,0:T(8,128)S(1)}, u32[]{:S(2)}) copy-start(f32[256,2048]{1,0:T(8,128)S(1)} %get-tuple-element.80.g1) | copy-start | bytes 6291460
  19.8 8.1 %copy-start = (bf16[1024,2048]{1,0:T(8,128)(2,1)}, bf16[1024,2048]{1,0:T(8,128)(2,1)S(1)}, u32[]{:S(2)}) copy-start(bf16[1024,2048]{1,0:T(8,128)(2,1)S(1)} %get-tuple-element.55.normed_ref) | copy-start | bytes 12582916
  22.8 17.5 %collective-permute-start.4 = (bf16[1040,256]{1,0:T(8,128)(2,1)}, bf16[1040,256]{1,0:T(8,128)(2,1)}, u32[]{:S(2)}, u32[]{:S(2)}) collective-permute-start(bf16[1040,256]{1,0:T(8,128)(2,1)} %collective-permute-done.1.refs_0_.b1), channel_id=1, source_target_pairs={{1,0},{2,3},{5,4},{6,7},{9,8},{10,11},{13,12},{14,15},{17,16},{18,... | collective-permute-start | bytes 1597448 | tf_op jit(solution)/shard_map/ppermute | solution.py:453
  24.1 16.2 %collective-permute-start.3 = (bf16[1040,256]{1,0:T(8,128)(2,1)}, bf16[1040,256]{1,0:T(8,128)(2,1)}, u32[]{:S(2)}, u32[]{:S(2)}) collective-permute-start(bf16[1040,256]{1,0:T(8,128)(2,1)} %collective-permute-done.refs_0_.a1), channel_id=1, source_target_pairs={{1,2},{2,1},{5,6},{6,5},{9,10},{10,9},{13,14},{14,13},{17,18},{18,... | collective-permute-start | bytes 1597448 | tf_op jit(solution)/shard_map/ppermute | solution.py:450
  36.5 2.3 %collective-permute-start.8 = (bf16[2064,128]{1,0:T(8,128)(2,1)}, bf16[2064,128]{1,0:T(8,128)(2,1)}, u32[]{:S(2)}, u32[]{:S(2)}) collective-permute-start(bf16[2064,128]{1,0:T(8,128)(2,1)} %collective-permute-done.5.refs_2_), channel_id=1, source_target_pairs={{0,4},{4,0},{8,12},{12,8},{16,20},{20,16},{24,28},{28,24},{1,5},{5... | collective-permute-start | bytes 1585160 | tf_op jit(solution)/shard_map/ppermute | solution.py:444
  36.5 3.0 %collective-permute-start.9 = (bf16[2064,128]{1,0:T(8,128)(2,1)}, bf16[2064,128]{1,0:T(8,128)(2,1)}, u32[]{:S(2)}, u32[]{:S(2)}) collective-permute-start(bf16[2064,128]{1,0:T(8,128)(2,1)} %collective-permute-done.6.refs_4_), channel_id=1, source_target_pairs={{0,4},{4,0},{8,12},{12,8},{16,20},{20,16},{24,28},{28,24},{1,5},{5... | collective-permute-start | bytes 1585160 | tf_op jit(solution)/shard_map/ppermute | solution.py:444
  37.0 3.3 %collective-permute-start.10 = (bf16[2064,128]{1,0:T(8,128)(2,1)}, bf16[2064,128]{1,0:T(8,128)(2,1)}, u32[]{:S(2)}, u32[]{:S(2)}) collective-permute-start(bf16[2064,128]{1,0:T(8,128)(2,1)} %collective-permute-done.7.refs_6_), channel_id=1, source_target_pairs={{0,4},{4,0},{8,12},{12,8},{16,20},{20,16},{24,28},{28,24},{1,5},{5... | collective-permute-start | bytes 1585160 | tf_op jit(solution)/shard_map/ppermute | solution.py:444
  40.3 22.3 %collective-permute-start.12 = (bf16[1040,256]{1,0:T(8,128)(2,1)}, bf16[1040,256]{1,0:T(8,128)(2,1)S(1)}, u32[]{:S(2)}, u32[]{:S(2)}) collective-permute-start(bf16[1040,256]{1,0:T(8,128)(2,1)} %collective-permute-done.3.m2), channel_id=1, source_target_pairs={{1,0},{2,3},{5,4},{6,7},{9,8},{10,11},{13,12},{14,15},{17,16},{18,... | collective-permute-start | bytes 1597448 | tf_op jit(solution)/shard_map/ppermute | solution.py:453
  41.6 2.2 %copy-start.1 = (bf16[1024,2048]{1,0:T(8,128)(2,1)S(1)}, bf16[1024,2048]{1,0:T(8,128)(2,1)}, u32[]{:S(2)}) copy-start(bf16[1024,2048]{1,0:T(8,128)(2,1)} %copy-done) | copy-start | bytes 12582916
  43.7 1.0 %copy-start.9 = (bf16[2064,128]{1,0:T(8,128)(2,1)S(1)}, bf16[2064,128]{1,0:T(8,128)(2,1)}, u32[]{:S(2)}) copy-start(bf16[2064,128]{1,0:T(8,128)(2,1)} %copy-done.8) | copy-start | bytes 1585156
  44.8 10.6 %copy-start.2 = (bf16[1024,2048]{1,0:T(8,128)(2,1)S(1)}, bf16[1024,2048]{1,0:T(8,128)(2,1)}, u32[]{:S(2)}) copy-start(bf16[1024,2048]{1,0:T(8,128)(2,1)} %copy-done) | copy-start | bytes 12582916
  50.3 17.6 %collective-permute-start.11 = (s16[1040,256]{1,0:T(8,128)(2,1)S(1)}, s16[1040,256]{1,0:T(8,128)(2,1)S(1)}, u32[]{:S(2)}, u32[]{:S(2)}) collective-permute-start(s16[1040,256]{1,0:T(8,128)(2,1)S(1)} %get-tuple-element.77), channel_id=1, source_target_pairs={{0,1},{3,2},{4,5},{7,6},{8,9},{11,10},{12,13},{15,14},{16,17},{19,... | collective-permute-start | bytes 1597448 | tf_op jit(solution)/shard_map/ppermute | solution.py:456
  57.9 4.7 %copy-start.7 = (f32[256,2048]{1,0:T(8,128)S(1)}, f32[256,2048]{1,0:T(8,128)}, u32[]{:S(2)}) copy-start(f32[256,2048]{1,0:T(8,128)} %copy-done.6) | copy-start | bytes 6291460
  67.9 4.2 %collective-permute-start.16 = (s16[2096,128]{1,0:T(8,128)(2,1)S(1)}, s16[2096,128]{1,0:T(8,128)(2,1)S(1)}, u32[]{:S(2)}, u32[]{:S(2)}) collective-permute-start(s16[2096,128]{1,0:T(8,128)(2,1)S(1)} %get-tuple-element.96), channel_id=1, source_target_pairs={{0,4},{4,0},{8,12},{12,8},{16,20},{20,16},{24,28},{28,24},{1,5},{5... | collective-permute-start | bytes 1609736 | tf_op jit(solution)/shard_map/ppermute | solution.py:444
  68.0 5.2 %collective-permute-start.17 = (s16[2096,128]{1,0:T(8,128)(2,1)S(1)}, s16[2096,128]{1,0:T(8,128)(2,1)S(1)}, u32[]{:S(2)}, u32[]{:S(2)}) collective-permute-start(s16[2096,128]{1,0:T(8,128)(2,1)S(1)} %get-tuple-element.98), channel_id=1, source_target_pairs={{0,4},{4,0},{8,12},{12,8},{16,20},{20,16},{24,28},{28,24},{1,5},{5... | collective-permute-start | bytes 1609736 | tf_op jit(solution)/shard_map/ppermute | solution.py:444
  68.5 6.6 %collective-permute-start.18 = (s16[2096,128]{1,0:T(8,128)(2,1)S(1)}, s16[2096,128]{1,0:T(8,128)(2,1)S(1)}, u32[]{:S(2)}, u32[]{:S(2)}) collective-permute-start(s16[2096,128]{1,0:T(8,128)(2,1)S(1)} %get-tuple-element.100), channel_id=1, source_target_pairs={{0,4},{4,0},{8,12},{12,8},{16,20},{20,16},{24,28},{28,24},{1,5},{5... | collective-permute-start | bytes 1609736 | tf_op jit(solution)/shard_map/ppermute | solution.py:444
  68.6 7.7 %collective-permute-start.15 = (s16[2096,128]{1,0:T(8,128)(2,1)S(1)}, s16[2096,128]{1,0:T(8,128)(2,1)S(1)}, u32[]{:S(2)}, u32[]{:S(2)}) collective-permute-start(s16[2096,128]{1,0:T(8,128)(2,1)S(1)} %get-tuple-element.94), channel_id=1, source_target_pairs={{0,4},{4,0},{8,12},{12,8},{16,20},{20,16},{24,28},{28,24},{1,5},{5... | collective-permute-start | bytes 1609736 | tf_op jit(solution)/shard_map/ppermute | solution.py:444
  69.0 14.2 %collective-permute-start.14 = (s16[1040,256]{1,0:T(8,128)(2,1)S(1)}, s16[1040,256]{1,0:T(8,128)(2,1)S(1)}, u32[]{:S(2)}, u32[]{:S(2)}) collective-permute-start(s16[1040,256]{1,0:T(8,128)(2,1)S(1)} %get-tuple-element.92), channel_id=1, source_target_pairs={{0,1},{3,2},{4,5},{7,6},{8,9},{11,10},{12,13},{15,14},{16,17},{19,... | collective-permute-start | bytes 1597448 | tf_op jit(solution)/shard_map/ppermute | solution.py:456
  72.1 11.1 %collective-permute-start.13 = (s16[1040,256]{1,0:T(8,128)(2,1)S(1)}, s16[1040,256]{1,0:T(8,128)(2,1)S(1)}, u32[]{:S(2)}, u32[]{:S(2)}) collective-permute-start(s16[1040,256]{1,0:T(8,128)(2,1)S(1)} %hop.3), channel_id=1, source_target_pairs={{1,2},{2,1},{5,6},{6,5},{9,10},{10,9},{13,14},{14,13},{17,18},{18,... | collective-permute-start | bytes 1597448 | tf_op jit(solution)/shard_map/ppermute | solution.py:450
  73.1 25.6 %collective-permute-start.23 = (s16[2096,128]{1,0:T(8,128)(2,1)S(1)}, s16[2096,128]{1,0:T(8,128)(2,1)S(1)}, u32[]{:S(2)}, u32[]{:S(2)}) collective-permute-start(s16[2096,128]{1,0:T(8,128)(2,1)S(1)} %combine.5), channel_id=1, source_target_pairs={{0,8},{4,12},{8,0},{12,4},{16,24},{20,28},{24,16},{28,20},{1,9},{5... | collective-permute-start | bytes 1609736 | tf_op jit(solution)/shard_map/ppermute | solution.py:444
  75.1 25.1 %collective-permute-start.22 = (s16[2096,128]{1,0:T(8,128)(2,1)S(1)}, s16[2096,128]{1,0:T(8,128)(2,1)S(1)}, u32[]{:S(2)}, u32[]{:S(2)}) collective-permute-start(s16[2096,128]{1,0:T(8,128)(2,1)S(1)} %combine.6), channel_id=1, source_target_pairs={{0,16},{4,20},{8,24},{12,28},{16,0},{20,4},{24,8},{28,12},{1,17},{... | collective-permute-start | bytes 1609736 | tf_op jit(solution)/shard_map/ppermute | solution.py:444
  76.2 23.9 %collective-permute-start.21 = (s16[2096,128]{1,0:T(8,128)(2,1)S(1)}, s16[2096,128]{1,0:T(8,128)(2,1)S(1)}, u32[]{:S(2)}, u32[]{:S(2)}) collective-permute-start(s16[2096,128]{1,0:T(8,128)(2,1)S(1)} %combine.7), channel_id=1, source_target_pairs={{0,24},{4,28},{8,16},{12,20},{16,8},{20,12},{24,0},{28,4},{1,25},{... | collective-permute-start | bytes 1609736 | tf_op jit(solution)/shard_map/ppermute | solution.py:444
  83.5 18.6 %collective-permute-start.20 = (s16[1040,256]{1,0:T(8,128)(2,1)S(1)}, s16[1040,256]{1,0:T(8,128)(2,1)S(1)}, u32[]{:S(2)}, u32[]{:S(2)}) collective-permute-start(s16[1040,256]{1,0:T(8,128)(2,1)S(1)} %hop.5), channel_id=1, source_target_pairs={{1,2},{2,1},{5,6},{6,5},{9,10},{10,9},{13,14},{14,13},{17,18},{18,... | collective-permute-start | bytes 1597448 | tf_op jit(solution)/shard_map/ppermute | solution.py:450
  84.8 17.3 %collective-permute-start.19 = (s16[1040,256]{1,0:T(8,128)(2,1)S(1)}, s16[1040,256]{1,0:T(8,128)(2,1)S(1)}, u32[]{:S(2)}, u32[]{:S(2)}) collective-permute-start(s16[1040,256]{1,0:T(8,128)(2,1)S(1)} %hop.4), channel_id=1, source_target_pairs={{0,1},{1,0},{2,3},{3,2},{4,5},{5,4},{6,7},{7,6},{8,9},{9,8},{10,11... | collective-permute-start | bytes 1597448 | tf_op jit(solution)/shard_map/ppermute | solution.py:447

commit v8 on v7

--- a/solution.py
+++ b/solution.py
@@ -117,7 +117,7 @@
             pltpu.SMEM((len(messages), tile), jnp.int32),
             pltpu.SemaphoreType.DMA,
         ],
-        compiler_params=params(22),
+        compiler_params=params(17),
         cost_estimate=LITTLE,
         name="first_values",
     )(place, normed, *messages)
@@ -148,7 +148,7 @@
             jax.ShapeDtypeStruct((normed.shape[0], weight.shape[1]), jnp.float32),
             jax.ShapeDtypeStruct(message_shape, jnp.int16),
         ],
-        compiler_params=params(20),
+        compiler_params=params(16),
         cost_estimate=LITTLE,
         name="partial_values",
     )(place, normed, weight)
@@ -171,7 +171,7 @@
         in_specs=[SMEM, VMEM, VMEM],
         out_specs=VMEM,
         out_shape=jax.ShapeDtypeStruct(arrived.shape, jnp.int16),
-        compiler_params=params(12),
+        compiler_params=params(8),
         cost_estimate=LITTLE,
         name="hop",
     )(place, partial, arrived)
@@ -195,7 +195,7 @@
         in_specs=[SMEM, VMEM, VMEM, VMEM],
         out_specs=VMEM,
         out_shape=jax.ShapeDtypeStruct((rows, width), jnp.bfloat16),
-        compiler_params=params(12),
+        compiler_params=params(8),
         cost_estimate=LITTLE,
         name="last_hop",
     )(place, partial, right, left)
@@ -208,24 +208,6 @@
         jnp.where(place < 2, 2, 1),
         jnp.where(place < 2, 3, 0),
     )
-
-
-def widen_kernel(chunk_ref, wide_ref):
-    tokens = chunk_ref.shape[0]
-    wide_ref[:tokens, :] = chunk_ref[...]
-    wide_ref[tokens:, :] = jnp.zeros((PAD, chunk_ref.shape[1]), chunk_ref.dtype)
-
-
-def widen(chunk):
-    return pl.pallas_call(
-        widen_kernel,
-        in_specs=[VMEM],
-        out_specs=VMEM,
-        out_shape=jax.ShapeDtypeStruct((chunk.shape[0] + PAD, chunk.shape[1]), chunk.dtype),
-        compiler_params=params(4),
-        cost_estimate=LITTLE,
-        name="widen",
-    )(chunk)
 
 
 def product(turned, normed_ref, out_ref):
@@ -261,7 +243,7 @@
             jax.ShapeDtypeStruct((chunk.shape[1], normed.shape[1]), jnp.float32),
         ],
         scratch_shapes=[pltpu.SemaphoreType.DMA],
-        compiler_params=params(16),
+        compiler_params=params(10),
         cost_estimate=LITTLE,
         name="own_gradient",
     )(normed, chunk)
@@ -273,7 +255,7 @@
         in_specs=[VMEM] + [VMEM] * len(chunks),
         out_specs=VMEM,
         out_shape=jax.ShapeDtypeStruct((chunks[0].shape[1], normed.shape[1]), jnp.float32),
-        compiler_params=params(16),
+        compiler_params=params(10),
         cost_estimate=LITTLE,
         name="chunk_gradient",
     )(normed, *chunks)
@@ -335,7 +317,7 @@
             pltpu.SemaphoreType.DMA((len(early),)),
         ],
         out_shape=[jax.ShapeDtypeStruct(shape, kind) for shape, kind in shapes],
-        compiler_params=params(30),
+        compiler_params=params(22),
         cost_estimate=LITTLE,
         name="slot_terms",
     )(codes, place, normed, *late, *early)
@@ -363,7 +345,7 @@
         in_specs=[VMEM, VMEM],
         out_specs=VMEM,
         out_shape=jax.ShapeDtypeStruct(shape, kind),
-        compiler_params=params(8),
+        compiler_params=params(5),
         cost_estimate=LITTLE,
         name="combine",
     )(kept, arrived)
@@ -387,7 +369,7 @@
         in_specs=[VMEM] * (1 + len(arrived)),
         out_specs=VMEM,
         out_shape=jax.ShapeDtypeStruct(shape, jnp.bfloat16),
-        compiler_params=params(12),
+        compiler_params=params(6),
         cost_estimate=LITTLE,
         name="normalized_update",
     )(kept, *arrived)
@@ -423,7 +405,7 @@
             scratch_shapes=[pltpu.VMEM((tokens, width), jnp.bfloat16)],
         ),
         out_shape=jax.ShapeDtypeStruct((tokens, features), jnp.bfloat16),
-        compiler_params=params(20),
+        compiler_params=params(14),
         cost_estimate=pl.CostEstimate(
             flops=2 * tokens * features * width,
             bytes_accessed=12 * MIB,
@@ -458,31 +440,29 @@
     positions = jnp.where(tile_columns >= 0, tile_rows * column_blocks + tile_columns + 1, 0)
     positions = jnp.pad(positions.astype(jnp.bfloat16), ((0, PAD - 1), (0, tile - capacity)))
     message = jnp.concatenate([tile_values.reshape(rows, tile), positions], axis=0)
-    wide = widen(cotangent)
-    a1, b1 = pairs(wide), middle(wide)
+    same_core = [message] + [swap(message, 2 * chip) for chip in range(1, chips)]
+    a1, b1 = pairs(cotangent), middle(cotangent)
     normed, g1 = own_gradient(normed, cotangent)
-    same_core = [message] + [swap(message, 2 * chip) for chip in range(1, chips)]
-    beside = swap(message, 1)
-    a1, b1, g1, beside = lax.optimization_barrier((a1, b1, g1, beside))
+    a1, b1, g1, *same_core = lax.optimization_barrier((a1, b1, g1, *same_core))
     m2, e2 = middle(a1), outward(b1)
-    g2 = chunk_gradient(normed, a1)
-    *same_core, g2 = lax.optimization_barrier((*same_core, g2))
-    gathered = [same_core[0], beside]
-    for m in same_core[1:]:
+    gathered = []
+    for m in same_core:
         gathered += [m, swap(m, 1)]
-    m2, e2, *gathered = lax.optimization_barrier((m2, e2, *gathered))
-    d3 = outward(m2)
 
     weight, first, codes = first_values(place, normed, gathered, parts, column_blocks)
     arrived = inward(first)
+    m2, e2, codes = lax.optimization_barrier((m2, e2, codes))
+    d3 = outward(m2)
+    g2 = chunk_gradient(normed, a1)
+    g3 = chunk_gradient(normed, b1, e2)
     partial, second = partial_values(place, normed, weight, first.shape)
-    g3 = chunk_gradient(normed, b1, e2)
-    g3, partial, second = lax.optimization_barrier((g3, partial, second))
+    arrived, d3, g2, g3, partial = lax.optimization_barrier((arrived, d3, g2, g3, partial))
+    third = hop(lambda p: p ^ 2, place, partial, arrived)
+    third, second, codes = lax.optimization_barrier((third, second, codes))
     keep, send = slot_terms(codes, place, normed, (m2, d3), (g1, g2, g3), capacity, column_blocks)
-    arrived, keep, send = lax.optimization_barrier((arrived, keep, send))
 
     to_middle = inward(second)
-    crossing = middle(hop(lambda p: p ^ 2, place, partial, arrived))
+    crossing = middle(third)
     other = [swap(m, 1) for m in send]
     sums = [combine(keep[chip], other[chip], jnp.int16) for chip in range(1, chips)]
     own = combine(keep[0], other[0], jnp.float32)

time: 104 us -> 109 us (1.048)
  waiting for transfers between devices: 21.8 us -> 26.2 us
    ppermute x2, waiting for transfers between devices: 0.01 us -> 4.77 us  [outward(): return lax.ppermute(x, 'tensor', [(1, 0), (2, 3)])]
    ppermute x2, starting transfers between devices: 10.5 us -> 6.03 us  [pairs(): return lax.ppermute(x, 'tensor', [(0, 1), (1, 0), (2, 3), (3, 2)])]
    ppermute x2, starting transfers between devices: 7.72 us -> 11 us  [inward(): return lax.ppermute(x, 'tensor', [(0, 1), (3, 2)])]
    ppermute x14, waiting for transfers between devices: 13.3 us -> 12.1 us  [swap(): return lax.ppermute(x, 'fsdp', [(i, i ^ mask) for i in range(devices)])]
    ppermute x14, starting transfers between devices: 9.28 us -> 10.4 us  [swap(): return lax.ppermute(x, 'fsdp', [(i, i ^ mask) for i in range(devices)])]
    unnamed x20 -> x16, local copies, waits for them, and re-layouts: 8.62 us -> 9.27 us
  transfers between devices with their start and end apart: 24 -> 24, of which waited for: 8 -> 9; matrix products, arithmetic and copies ran while one was open for 0% -> 0% of each run, Pallas kernels for 33% -> 26%
where the time goes in v8:
time: 109 us; the launch traced here: 108 us
  Pallas kernels  35.2 us (32%)
  starting transfers between devices  34.8 us (32%)
  waiting for transfers between devices  26.2 us (24%)
  local copies, waits for them, and re-layouts  9.27 us (9%)
  other arithmetic  1.76 us (2%)
    ppermute x14, waiting for transfers between devices, swap(): return lax.ppermute(x, 'fsdp', [(i, i ^ mask) for i in range(devices)])  12.1 us
    ppermute x2, starting transfers between devices, inward(): return lax.ppermute(x, 'tensor', [(0, 1), (3, 2)])  11 us
    ppermute x14, starting transfers between devices, swap(): return lax.ppermute(x, 'fsdp', [(i, i ^ mask) for i in range(devices)])  10.4 us
    unnamed x16, local copies, waits for them, and re-layouts  9.27 us
    pallas_call x1, Pallas kernels, grad_inputs(): pl.pallas_call(grad_input_kernel, grid_spec=pltpu.PrefetchScalarGridSpec(...  8.03 us
    ppermute x2, waiting for transfers between devices, inward(): return lax.ppermute(x, 'tensor', [(0, 1), (3, 2)])  6.3 us
    ppermute x2, starting transfers between devices, pairs(): return lax.ppermute(x, 'tensor', [(0, 1), (1, 0), (2, 3), (3, 2)])  6.03 us
    pallas_call x1, Pallas kernels, slot_terms(): pl.pallas_call(functools.partial(slots_kernel, chips, column_blocks), in_...  5.27 us
  transfers between devices with their start and end apart: 24, of which 9 were waited for; matrix products, arithmetic and copies ran while one was open for 0% of the time, Pallas kernels for 26%

profile of v8, /device:TPU:0, one launch (start us, length us, event | category | flops | bytes accessed | tf_op | source)
XLA Modules:
  0.0 108.1 jit_solution(7107649197158454501)
XLA Ops:
  0.6 0.7 fusion.2
  1.3 1.1 fusion.1.refs_0_
  2.4 4.0 %collective-permute-start.4 = (bf16[2064,128]{1,0:T(8,128)(2,1)S(1)}, bf16[2064,128]{1,0:T(8,128)(2,1)S(1)}, u32[]{:S(2)}, u32[]{:S(2)}) collective-permute-start(bf16[2064,128]{1,0:T(8,128)(2,1)S(1)} %fusion.1.refs_0_), channel_id=1, source_target_pairs={{0,24},{4,28},{8,16},{12,20},{16,8},{20,12},{24,0},{28,4},{1,25},{... | collective-permute-start | bytes 1585160 | tf_op jit(solution)/shard_map/ppermute | solution.py:426
  6.3 0.5 collective-permute-start.3
  7.0 2.0 %collective-permute-start = (bf16[1024,256]{1,0:T(8,128)(2,1)}, bf16[1024,256]{1,0:T(8,128)(2,1)}, u32[]{:S(2)}, u32[]{:S(2)}) collective-permute-start(bf16[1024,256]{1,0:T(8,128)(2,1)} %own.1), channel_id=1, source_target_pairs={{0,1},{1,0},{2,3},{3,2},{4,5},{5,4},{6,7},{7,6},{8,9},{9,8},{10,11... | collective-permute-start | bytes 1572872 | tf_op jit(solution)/shard_map/ppermute | solution.py:429
  9.0 1.5 %collective-permute-start.1 = (bf16[1024,256]{1,0:T(8,128)(2,1)}, bf16[1024,256]{1,0:T(8,128)(2,1)}, u32[]{:S(2)}, u32[]{:S(2)}) collective-permute-start(bf16[1024,256]{1,0:T(8,128)(2,1)} %own.1), channel_id=1, source_target_pairs={{1,2},{2,1},{5,6},{6,5},{9,10},{10,9},{13,14},{14,13},{17,18},{18,... | collective-permute-start | bytes 1572872 | tf_op jit(solution)/shard_map/ppermute | solution.py:432
  10.4 2.2 %copy-done.3 = bf16[1024,2048]{1,0:T(8,128)(2,1)S(1)} copy-done((bf16[1024,2048]{1,0:T(8,128)(2,1)S(1)}, bf16[1024,2048]{1,0:T(8,128)(2,1)}, u32[]{:S(2)}) %copy-start.3) | copy-done | bytes 4194328
  12.6 1.0 copy-done.6
  13.7 1.7 %own_gradient.1 = (bf16[1024,2048]{1,0:T(8,128)(2,1)S(1)}, f32[256,2048]{1,0:T(8,128)S(1)}) custom-call(bf16[1024,2048]{1,0:T(8,128)(2,1)S(1)} %copy-done.3, bf16[1024,256]{1,0:T(8,128)(2,1)S(1)} %copy-done.6), custom_call_target="tpu_custom_call" | custom-call | flops 1 | bytes 1 | tf_op jit(solution)/shard_map/own_gradient/pallas_call | solution.py:237
  15.4 2.0 %copy-done = bf16[1024,2048]{1,0:T(8,128)(2,1)} copy-done((bf16[1024,2048]{1,0:T(8,128)(2,1)}, bf16[1024,2048]{1,0:T(8,128)(2,1)S(1)}, u32[]{:S(2)}) %copy-start) | copy-done | bytes 4194328
  17.4 3.0 %collective-permute-done.refs_0_.a1 = bf16[1024,256]{1,0:T(8,128)(2,1)} collective-permute-done((bf16[1024,256]{1,0:T(8,128)(2,1)}, bf16[1024,256]{1,0:T(8,128)(2,1)}, u32[]{:S(2)}, u32[]{:S(2)}) %collective-permute-start) | collective-permute-done | bytes 524320 | tf_op jit(solution)/shard_map/ppermute | solution.py:429
  20.4 9.4 %collective-permute-done.3.refs_4_ = bf16[2064,128]{1,0:T(8,128)(2,1)} collective-permute-done((bf16[2064,128]{1,0:T(8,128)(2,1)S(1)}, bf16[2064,128]{1,0:T(8,128)(2,1)}, u32[]{:S(2)}, u32[]{:S(2)}) %collective-permute-start.3) | collective-permute-done | bytes 528416 | tf_op jit(solution)/shard_map/ppermute | solution.py:426
  30.1 0.5 collective-permute-start.6
  30.6 0.5 collective-permute-start.8
  31.1 1.5 %collective-permute-start.10 = (bf16[1024,256]{1,0:T(8,128)(2,1)}, bf16[1024,256]{1,0:T(8,128)(2,1)}, u32[]{:S(2)}, u32[]{:S(2)}) collective-permute-start(bf16[1024,256]{1,0:T(8,128)(2,1)} %collective-permute-done.refs_0_.a1), channel_id=1, source_target_pairs={{1,2},{2,1},{5,6},{6,5},{9,10},{10,9},{13,14},{14,13},{17,18},{18,... | collective-permute-start | bytes 1572872 | tf_op jit(solution)/shard_map/ppermute | solution.py:432
  32.7 0.8 copy-done.4
  33.5 1.3 %collective-permute-start.11 = (bf16[1024,256]{1,0:T(8,128)(2,1)}, bf16[1024,256]{1,0:T(8,128)(2,1)}, u32[]{:S(2)}, u32[]{:S(2)}) collective-permute-start(bf16[1024,256]{1,0:T(8,128)(2,1)} %collective-permute-done.1.refs_0_.b1), channel_id=1, source_target_pairs={{1,0},{2,3},{5,4},{6,7},{9,8},{10,11},{13,12},{14,15},{17,16},{18,... | collective-permute-start | bytes 1572872 | tf_op jit(solution)/shard_map/ppermute | solution.py:435
  34.9 2.2 %copy-done.1 = bf16[1024,2048]{1,0:T(8,128)(2,1)S(1)} copy-done((bf16[1024,2048]{1,0:T(8,128)(2,1)S(1)}, bf16[1024,2048]{1,0:T(8,128)(2,1)}, u32[]{:S(2)}) %copy-start.1) | copy-done | bytes 4194328
  37.0 1.0 copy-done.5
  38.1 5.2 %first_values.1 = (bf16[2176,1024]{1,0:T(8,128)(2,1)S(1)}, s16[1040,256]{1,0:T(8,128)(2,1)S(1)}, s32[8,128]{1,0:T(8,128)S(1)}) custom-call(s32[1]{0:T(128)} %bitcast.place_ref, bf16[1024,2048]{1,0:T(8,128)(2,1)S(1)} %copy-done.1, bf16[2064,128]{1,0:T(8,128)(2,1)S(1)} %fusion.1.refs_0_, bf16[2064,128]{1,0:T(8,128)(2,1)S(1)} %copy-done.5, ...), custom_call_target="tpu_custom_call" | custom-call | flops 1 | bytes 1 | tf_op jit(solution)/shard_map/first_values/pallas_call | solution.py:106
  43.3 6.2 %collective-permute-start.9 = (s16[1040,256]{1,0:T(8,128)(2,1)S(1)}, s16[1040,256]{1,0:T(8,128)(2,1)S(1)}, u32[]{:S(2)}, u32[]{:S(2)}) collective-permute-start(s16[1040,256]{1,0:T(8,128)(2,1)S(1)} %get-tuple-element.48), channel_id=1, source_target_pairs={{0,1},{3,2},{4,5},{7,6},{8,9},{11,10},{12,13},{15,14},{16,17},{19,... | collective-permute-start | bytes 1597448 | tf_op jit(solution)/shard_map/ppermute | solution.py:438
  49.5 0.8 collective-permute-done.11.refs_1_.e2
  50.4 1.5 %collective-permute-start.12 = (bf16[1024,256]{1,0:T(8,128)(2,1)}, bf16[1024,256]{1,0:T(8,128)(2,1)S(1)}, u32[]{:S(2)}, u32[]{:S(2)}) collective-permute-start(bf16[1024,256]{1,0:T(8,128)(2,1)} %collective-permute-done.10.m2), channel_id=1, source_target_pairs={{1,0},{2,3},{5,4},{6,7},{9,8},{10,11},{13,12},{14,15},{17,16},{18,... | collective-permute-start | bytes 1572872 | tf_op jit(solution)/shard_map/ppermute | solution.py:435
  51.8 2.3 %chunk_gradient.2.g2 = f32[256,2048]{1,0:T(8,128)S(1)} custom-call(bf16[1024,2048]{1,0:T(8,128)(2,1)S(1)} %copy-done.1, bf16[1024,256]{1,0:T(8,128)(2,1)} %collective-permute-done.refs_0_.a1), custom_call_target="tpu_custom_call" | custom-call | flops 1 | bytes 1 | tf_op jit(solution)/shard_map/chunk_gradient/pallas_call | solution.py:253
  54.2 2.6 %chunk_gradient.3.g3 = f32[256,2048]{1,0:T(8,128)S(1)} custom-call(bf16[1024,2048]{1,0:T(8,128)(2,1)S(1)} %copy-done.1, bf16[1024,256]{1,0:T(8,128)(2,1)} %collective-permute-done.1.refs_0_.b1, bf16[1024,256]{1,0:T(8,128)(2,1)} %collective-permute-done.11.refs_1_.e2), custom_call_target="tpu_custom_call" | custom-call | flops 1 | bytes 1 | tf_op jit(solution)/shard_map/chunk_gradient/pallas_call | solution.py:253
  56.8 4.7 %partial_values.1 = (f32[1024,1024]{1,0:T(8,128)S(1)}, s16[1040,256]{1,0:T(8,128)(2,1)S(1)}) custom-call(s32[1]{0:T(128)} %bitcast.place_ref, bf16[1024,2048]{1,0:T(8,128)(2,1)S(1)} %copy-done.2, bf16[2176,1024]{1,0:T(8,128)(2,1)S(1)} %get-tuple-element.54.weight_ref), custom_call_target="tpu_custom_call" | custom-call | flops 1 | bytes 1 | tf_op jit(solution)/shard_map/partial_values/pallas_call | solution.py:143
  61.5 3.9 %collective-permute-done.12.d3 = bf16[1024,256]{1,0:T(8,128)(2,1)S(1)} collective-permute-done((bf16[1024,256]{1,0:T(8,128)(2,1)}, bf16[1024,256]{1,0:T(8,128)(2,1)S(1)}, u32[]{:S(2)}, u32[]{:S(2)}) %collective-permute-start.12) | collective-permute-done | bytes 524320 | tf_op jit(solution)/shard_map/ppermute | solution.py:435
  65.4 0.3 hop.3
  65.8 5.3 %slot_terms.1 = (f32[2048,128]{1,0:T(8,128)S(1)}, f32[2048,128]{1,0:T(8,128)S(1)}, f32[2048,128]{1,0:T(8,128)S(1)}, f32[2048,128]{1,0:T(8,128)S(1)}, s16[2096,12...) custom-call(s32[8,128]{1,0:T(8,128)S(1)} %get-tuple-element.62.codes, ...), custom_call_target="tpu_custom_call" | custom-call | flops 1 | bytes 1 | tf_op jit(solution)/shard_map/slot_terms/pallas_call | solution.py:309
  71.1 0.5 collective-permute-start.17
  71.7 0.4 collective-permute-start.15
  72.1 0.7 collective-permute-start.13
  73.1 4.8 %collective-permute-start.14 = (s16[1040,256]{1,0:T(8,128)(2,1)S(1)}, s16[1040,256]{1,0:T(8,128)(2,1)S(1)}, u32[]{:S(2)}, u32[]{:S(2)}) collective-permute-start(s16[1040,256]{1,0:T(8,128)(2,1)S(1)} %get-tuple-element.61), channel_id=1, source_target_pairs={{0,1},{3,2},{4,5},{7,6},{8,9},{11,10},{12,13},{15,14},{16,17},{19,... | collective-permute-start | bytes 1597448 | tf_op jit(solution)/shard_map/ppermute | solution.py:438
  77.8 0.4 combine.5
  78.2 1.6 %collective-permute-start.23 = (s16[2096,128]{1,0:T(8,128)(2,1)S(1)}, s16[2096,128]{1,0:T(8,128)(2,1)S(1)}, u32[]{:S(2)}, u32[]{:S(2)}) collective-permute-start(s16[2096,128]{1,0:T(8,128)(2,1)S(1)} %combine.5), channel_id=1, source_target_pairs={{0,8},{4,12},{8,0},{12,4},{16,24},{20,28},{24,16},{28,20},{1,9},{5... | collective-permute-start | bytes 1609736 | tf_op jit(solution)/shard_map/ppermute | solution.py:426
  79.8 0.4 combine.6
  80.1 0.8 collective-permute-start.22
  80.9 0.4 combine.7
  81.3 1.3 %collective-permute-start.21 = (s16[2096,128]{1,0:T(8,128)(2,1)S(1)}, s16[2096,128]{1,0:T(8,128)(2,1)S(1)}, u32[]{:S(2)}, u32[]{:S(2)}) collective-permute-start(s16[2096,128]{1,0:T(8,128)(2,1)S(1)} %combine.7), channel_id=1, source_target_pairs={{0,24},{4,28},{8,16},{12,20},{16,8},{20,12},{24,0},{28,4},{1,25},{... | collective-permute-start | bytes 1609736 | tf_op jit(solution)/shard_map/ppermute | solution.py:426
  82.8 6.3 %collective-permute-done.14.arrived_ref = s16[1040,256]{1,0:T(8,128)(2,1)S(1)} collective-permute-done((s16[1040,256]{1,0:T(8,128)(2,1)S(1)}, s16[1040,256]{1,0:T(8,128)(2,1)S(1)}, u32[]{:S(2)}, u32[]{:S(2)}) %collective-permute-start.14) | collective-permute-done | bytes 532512 | tf_op jit(solution)/shard_map/ppermute | solution.py:438
  89.1 0.3 hop.5
  89.5 1.0 collective-permute-start.20
  90.5 0.3 hop.4
  90.9 4.1 %collective-permute-start.19 = (s16[1040,256]{1,0:T(8,128)(2,1)S(1)}, s16[1040,256]{1,0:T(8,128)(2,1)S(1)}, u32[]{:S(2)}, u32[]{:S(2)}) collective-permute-start(s16[1040,256]{1,0:T(8,128)(2,1)S(1)} %hop.4), channel_id=1, source_target_pairs={{0,1},{1,0},{2,3},{3,2},{4,5},{5,4},{6,7},{7,6},{8,9},{9,8},{10,11... | collective-permute-start | bytes 1597448 | tf_op jit(solution)/shard_map/ppermute | solution.py:429
  94.9 8.0 %grad_inputs.1 = bf16[1024,2048]{1,0:T(8,128)(2,1)} custom-call(s32[1]{0:T(128)} %bitcast.place_ref, bf16[2176,1024]{1,0:T(8,128)(2,1)S(1)} %get-tuple-element.54.weight_ref, bf16[1024,256]{1,0:T(8,128)(2,1)S(1)} %copy-done.7, bf16[1024,256]{1,0:T(8,128)(2,1)} %collective-permute-done.refs_0_.a1, bf16[1024,256]{1,0:T(8,128)(2,1)} %collective-permute-done.1.refs_0_.b1, ...), custom_call_target="tpu_custom_call" | custom-call | flops 4294967296 | bytes 12582912 | tf_op jit(solution)/shard_map/grad_inputs/pallas_call | solution.py:397
  103.0 2.1 %collective-permute-done.22.refs_2_ = s16[2096,128]{1,0:T(8,128)(2,1)S(1)} collective-permute-done((s16[2096,128]{1,0:T(8,128)(2,1)S(1)}, s16[2096,128]{1,0:T(8,128)(2,1)S(1)}, u32[]{:S(2)}, u32[]{:S(2)}) %collective-permute-start.22) | collective-permute-done | bytes 536608 | tf_op jit(solution)/shard_map/ppermute | solution.py:426
  105.0 1.9 %normalized_update.1 = bf16[16,128,128]{2,1,0:T(8,128)(2,1)} custom-call(f32[2048,128]{1,0:T(8,128)S(1)} %combine.4.refs_0_, s16[2096,128]{1,0:T(8,128)(2,1)S(1)} %collective-permute-done.21.refs_1_, s16[2096,128]{1,0:T(8,128)(2,1)S(1)} %collective-permute-done.22.refs_2_, s16[2096,128]{1,0:T(8,128)(2,1)S(1)} %collective-permute-done.23.refs_3_), custom_call_target="tpu_custom_call" | custom-call | flops 1 | bytes 1 | tf_op jit(solution)/shard_map/normalized_update/pallas_call | solution.py:367
  107.0 1.1 %last_hop.1 = bf16[1024,256]{1,0:T(8,128)(2,1)} custom-call(s32[1]{0:T(128)} %bitcast.place_ref, f32[1024,1024]{1,0:T(8,128)S(1)} %get-tuple-element.56.partial_ref, s16[1040,256]{1,0:T(8,128)(2,1)S(1)} %collective-permute-done.19.right_ref, s16[1040,256]{1,0:T(8,128)(2,1)S(1)} %collective-permute-done.20.left_ref), custom_call_target="tpu_custom_call" | custom-call | flops 1 | bytes 1 | tf_op jit(solution)/shard_map/last_hop/pallas_call | solution.py:193
  (34 shorter events, 1.2 us)
Async XLA Ops:
  2.4 18.0 %collective-permute-start.4 = (bf16[2064,128]{1,0:T(8,128)(2,1)S(1)}, bf16[2064,128]{1,0:T(8,128)(2,1)S(1)}, u32[]{:S(2)}, u32[]{:S(2)}) collective-permute-start(bf16[2064,128]{1,0:T(8,128)(2,1)S(1)} %fusion.1.refs_0_), channel_id=1, source_target_pairs={{0,24},{4,28},{8,16},{12,20},{16,8},{20,12},{24,0},{28,4},{1,25},{... | collective-permute-start | bytes 1585160 | tf_op jit(solution)/shard_map/ppermute | solution.py:426
  6.3 23.4 %collective-permute-start.3 = (bf16[2064,128]{1,0:T(8,128)(2,1)S(1)}, bf16[2064,128]{1,0:T(8,128)(2,1)}, u32[]{:S(2)}, u32[]{:S(2)}) collective-permute-start(bf16[2064,128]{1,0:T(8,128)(2,1)S(1)} %fusion.1.refs_0_), channel_id=1, source_target_pairs={{0,16},{4,20},{8,24},{12,28},{16,0},{20,4},{24,8},{28,12},{1,17},{... | collective-permute-start | bytes 1585160 | tf_op jit(solution)/shard_map/ppermute | solution.py:426
  6.9 23.2 %collective-permute-start.2 = (bf16[2064,128]{1,0:T(8,128)(2,1)S(1)}, bf16[2064,128]{1,0:T(8,128)(2,1)}, u32[]{:S(2)}, u32[]{:S(2)}) collective-permute-start(bf16[2064,128]{1,0:T(8,128)(2,1)S(1)} %fusion.1.refs_0_), channel_id=1, source_target_pairs={{0,8},{4,12},{8,0},{12,4},{16,24},{20,28},{24,16},{28,20},{1,9},{5... | collective-permute-start | bytes 1585160 | tf_op jit(solution)/shard_map/ppermute | solution.py:426
  7.0 13.4 %collective-permute-start = (bf16[1024,256]{1,0:T(8,128)(2,1)}, bf16[1024,256]{1,0:T(8,128)(2,1)}, u32[]{:S(2)}, u32[]{:S(2)}) collective-permute-start(bf16[1024,256]{1,0:T(8,128)(2,1)} %own.1), channel_id=1, source_target_pairs={{0,1},{1,0},{2,3},{3,2},{4,5},{5,4},{6,7},{7,6},{8,9},{9,8},{10,11... | collective-permute-start | bytes 1572872 | tf_op jit(solution)/shard_map/ppermute | solution.py:429
  9.0 11.4 %collective-permute-start.1 = (bf16[1024,256]{1,0:T(8,128)(2,1)}, bf16[1024,256]{1,0:T(8,128)(2,1)}, u32[]{:S(2)}, u32[]{:S(2)}) collective-permute-start(bf16[1024,256]{1,0:T(8,128)(2,1)} %own.1), channel_id=1, source_target_pairs={{1,2},{2,1},{5,6},{6,5},{9,10},{10,9},{13,14},{14,13},{17,18},{18,... | collective-permute-start | bytes 1572872 | tf_op jit(solution)/shard_map/ppermute | solution.py:432
  10.4 2.2 %copy-start.3 = (bf16[1024,2048]{1,0:T(8,128)(2,1)S(1)}, bf16[1024,2048]{1,0:T(8,128)(2,1)}, u32[]{:S(2)}) copy-start(bf16[1024,2048]{1,0:T(8,128)(2,1)} %normed_ref.1) | copy-start | bytes 12582916
  12.6 1.0 copy-start.6
  15.4 2.0 %copy-start = (bf16[1024,2048]{1,0:T(8,128)(2,1)}, bf16[1024,2048]{1,0:T(8,128)(2,1)S(1)}, u32[]{:S(2)}) copy-start(bf16[1024,2048]{1,0:T(8,128)(2,1)S(1)} %get-tuple-element.42.normed_ref) | copy-start | bytes 12582916
  30.1 2.6 %collective-permute-start.5 = (bf16[2064,128]{1,0:T(8,128)(2,1)S(1)}, bf16[2064,128]{1,0:T(8,128)(2,1)S(1)}, u32[]{:S(2)}, u32[]{:S(2)}) collective-permute-start(bf16[2064,128]{1,0:T(8,128)(2,1)S(1)} %fusion.1.refs_0_), channel_id=1, source_target_pairs={{0,4},{4,0},{8,12},{12,8},{16,20},{20,16},{24,28},{28,24},{1,5},{5... | collective-permute-start | bytes 1585160 | tf_op jit(solution)/shard_map/ppermute | solution.py:426
  30.1 4.7 %collective-permute-start.6 = (bf16[2064,128]{1,0:T(8,128)(2,1)}, bf16[2064,128]{1,0:T(8,128)(2,1)}, u32[]{:S(2)}, u32[]{:S(2)}) collective-permute-start(bf16[2064,128]{1,0:T(8,128)(2,1)} %collective-permute-done.2.refs_2_), channel_id=1, source_target_pairs={{0,4},{4,0},{8,12},{12,8},{16,20},{20,16},{24,28},{28,24},{1,5},{5... | collective-permute-start | bytes 1585160 | tf_op jit(solution)/shard_map/ppermute | solution.py:426
  30.6 4.2 %collective-permute-start.7 = (bf16[2064,128]{1,0:T(8,128)(2,1)}, bf16[2064,128]{1,0:T(8,128)(2,1)}, u32[]{:S(2)}, u32[]{:S(2)}) collective-permute-start(bf16[2064,128]{1,0:T(8,128)(2,1)} %collective-permute-done.3.refs_4_), channel_id=1, source_target_pairs={{0,4},{4,0},{8,12},{12,8},{16,20},{20,16},{24,28},{28,24},{1,5},{5... | collective-permute-start | bytes 1585160 | tf_op jit(solution)/shard_map/ppermute | solution.py:426
  30.6 4.2 %collective-permute-start.8 = (bf16[2064,128]{1,0:T(8,128)(2,1)S(1)}, bf16[2064,128]{1,0:T(8,128)(2,1)}, u32[]{:S(2)}, u32[]{:S(2)}) collective-permute-start(bf16[2064,128]{1,0:T(8,128)(2,1)S(1)} %collective-permute-done.4.refs_6_), channel_id=1, source_target_pairs={{0,4},{4,0},{8,12},{12,8},{16,20},{20,16},{24,28},{28,24},{1,5},{5... | collective-permute-start | bytes 1585160 | tf_op jit(solution)/shard_map/ppermute | solution.py:426
  31.1 18.4 %collective-permute-start.10 = (bf16[1024,256]{1,0:T(8,128)(2,1)}, bf16[1024,256]{1,0:T(8,128)(2,1)}, u32[]{:S(2)}, u32[]{:S(2)}) collective-permute-start(bf16[1024,256]{1,0:T(8,128)(2,1)} %collective-permute-done.refs_0_.a1), channel_id=1, source_target_pairs={{1,2},{2,1},{5,6},{6,5},{9,10},{10,9},{13,14},{14,13},{17,18},{18,... | collective-permute-start | bytes 1572872 | tf_op jit(solution)/shard_map/ppermute | solution.py:432
  32.7 0.8 copy-start.4
  33.5 16.8 %collective-permute-start.11 = (bf16[1024,256]{1,0:T(8,128)(2,1)}, bf16[1024,256]{1,0:T(8,128)(2,1)}, u32[]{:S(2)}, u32[]{:S(2)}) collective-permute-start(bf16[1024,256]{1,0:T(8,128)(2,1)} %collective-permute-done.1.refs_0_.b1), channel_id=1, source_target_pairs={{1,0},{2,3},{5,4},{6,7},{9,8},{10,11},{13,12},{14,15},{17,16},{18,... | collective-permute-start | bytes 1572872 | tf_op jit(solution)/shard_map/ppermute | solution.py:435
  34.8 2.2 %copy-start.1 = (bf16[1024,2048]{1,0:T(8,128)(2,1)S(1)}, bf16[1024,2048]{1,0:T(8,128)(2,1)}, u32[]{:S(2)}) copy-start(bf16[1024,2048]{1,0:T(8,128)(2,1)} %copy-done) | copy-start | bytes 12582916
  37.0 1.0 copy-start.5
  43.3 22.1 %collective-permute-start.9 = (s16[1040,256]{1,0:T(8,128)(2,1)S(1)}, s16[1040,256]{1,0:T(8,128)(2,1)S(1)}, u32[]{:S(2)}, u32[]{:S(2)}) collective-permute-start(s16[1040,256]{1,0:T(8,128)(2,1)S(1)} %get-tuple-element.48), channel_id=1, source_target_pairs={{0,1},{3,2},{4,5},{7,6},{8,9},{11,10},{12,13},{15,14},{16,17},{19,... | collective-permute-start | bytes 1597448 | tf_op jit(solution)/shard_map/ppermute | solution.py:438
  50.4 15.1 %collective-permute-start.12 = (bf16[1024,256]{1,0:T(8,128)(2,1)}, bf16[1024,256]{1,0:T(8,128)(2,1)S(1)}, u32[]{:S(2)}, u32[]{:S(2)}) collective-permute-start(bf16[1024,256]{1,0:T(8,128)(2,1)} %collective-permute-done.10.m2), channel_id=1, source_target_pairs={{1,0},{2,3},{5,4},{6,7},{9,8},{10,11},{13,12},{14,15},{17,16},{18,... | collective-permute-start | bytes 1572872 | tf_op jit(solution)/shard_map/ppermute | solution.py:435
  54.2 2.7 %copy-start.2 = (bf16[1024,2048]{1,0:T(8,128)(2,1)S(1)}, bf16[1024,2048]{1,0:T(8,128)(2,1)}, u32[]{:S(2)}) copy-start(bf16[1024,2048]{1,0:T(8,128)(2,1)} %copy-done) | copy-start | bytes 12582916
  71.1 2.0 %collective-permute-start.16 = (s16[2096,128]{1,0:T(8,128)(2,1)S(1)}, s16[2096,128]{1,0:T(8,128)(2,1)S(1)}, u32[]{:S(2)}, u32[]{:S(2)}) collective-permute-start(s16[2096,128]{1,0:T(8,128)(2,1)S(1)} %get-tuple-element.70), channel_id=1, source_target_pairs={{0,4},{4,0},{8,12},{12,8},{16,20},{20,16},{24,28},{28,24},{1,5},{5... | collective-permute-start | bytes 1609736 | tf_op jit(solution)/shard_map/ppermute | solution.py:426
  71.1 7.1 %collective-permute-start.17 = (s16[2096,128]{1,0:T(8,128)(2,1)S(1)}, s16[2096,128]{1,0:T(8,128)(2,1)S(1)}, u32[]{:S(2)}, u32[]{:S(2)}) collective-permute-start(s16[2096,128]{1,0:T(8,128)(2,1)S(1)} %get-tuple-element.72), channel_id=1, source_target_pairs={{0,4},{4,0},{8,12},{12,8},{16,20},{20,16},{24,28},{28,24},{1,5},{5... | collective-permute-start | bytes 1609736 | tf_op jit(solution)/shard_map/ppermute | solution.py:426
  71.6 8.5 %collective-permute-start.18 = (s16[2096,128]{1,0:T(8,128)(2,1)S(1)}, s16[2096,128]{1,0:T(8,128)(2,1)S(1)}, u32[]{:S(2)}, u32[]{:S(2)}) collective-permute-start(s16[2096,128]{1,0:T(8,128)(2,1)S(1)} %get-tuple-element.74), channel_id=1, source_target_pairs={{0,4},{4,0},{8,12},{12,8},{16,20},{20,16},{24,28},{28,24},{1,5},{5... | collective-permute-start | bytes 1609736 | tf_op jit(solution)/shard_map/ppermute | solution.py:426
  71.7 9.6 %collective-permute-start.15 = (s16[2096,128]{1,0:T(8,128)(2,1)S(1)}, s16[2096,128]{1,0:T(8,128)(2,1)S(1)}, u32[]{:S(2)}, u32[]{:S(2)}) collective-permute-start(s16[2096,128]{1,0:T(8,128)(2,1)S(1)} %get-tuple-element.68), channel_id=1, source_target_pairs={{0,4},{4,0},{8,12},{12,8},{16,20},{20,16},{24,28},{28,24},{1,5},{5... | collective-permute-start | bytes 1609736 | tf_op jit(solution)/shard_map/ppermute | solution.py:426
  72.1 10.7 %collective-permute-start.13 = (s16[1040,256]{1,0:T(8,128)(2,1)S(1)}, s16[1040,256]{1,0:T(8,128)(2,1)S(1)}, u32[]{:S(2)}, u32[]{:S(2)}) collective-permute-start(s16[1040,256]{1,0:T(8,128)(2,1)S(1)} %hop.3), channel_id=1, source_target_pairs={{1,2},{2,1},{5,6},{6,5},{9,10},{10,9},{13,14},{14,13},{17,18},{18,... | collective-permute-start | bytes 1597448 | tf_op jit(solution)/shard_map/ppermute | solution.py:432
  73.1 16.1 %collective-permute-start.14 = (s16[1040,256]{1,0:T(8,128)(2,1)S(1)}, s16[1040,256]{1,0:T(8,128)(2,1)S(1)}, u32[]{:S(2)}, u32[]{:S(2)}) collective-permute-start(s16[1040,256]{1,0:T(8,128)(2,1)S(1)} %get-tuple-element.61), channel_id=1, source_target_pairs={{0,1},{3,2},{4,5},{7,6},{8,9},{11,10},{12,13},{15,14},{16,17},{19,... | collective-permute-start | bytes 1597448 | tf_op jit(solution)/shard_map/ppermute | solution.py:438
  78.2 24.7 %collective-permute-start.23 = (s16[2096,128]{1,0:T(8,128)(2,1)S(1)}, s16[2096,128]{1,0:T(8,128)(2,1)S(1)}, u32[]{:S(2)}, u32[]{:S(2)}) collective-permute-start(s16[2096,128]{1,0:T(8,128)(2,1)S(1)} %combine.5), channel_id=1, source_target_pairs={{0,8},{4,12},{8,0},{12,4},{16,24},{20,28},{24,16},{28,20},{1,9},{5... | collective-permute-start | bytes 1609736 | tf_op jit(solution)/shard_map/ppermute | solution.py:426
  80.1 24.9 %collective-permute-start.22 = (s16[2096,128]{1,0:T(8,128)(2,1)S(1)}, s16[2096,128]{1,0:T(8,128)(2,1)S(1)}, u32[]{:S(2)}, u32[]{:S(2)}) collective-permute-start(s16[2096,128]{1,0:T(8,128)(2,1)S(1)} %combine.6), channel_id=1, source_target_pairs={{0,16},{4,20},{8,24},{12,28},{16,0},{20,4},{24,8},{28,12},{1,17},{... | collective-permute-start | bytes 1609736 | tf_op jit(solution)/shard_map/ppermute | solution.py:426
  81.3 23.7 %collective-permute-start.21 = (s16[2096,128]{1,0:T(8,128)(2,1)S(1)}, s16[2096,128]{1,0:T(8,128)(2,1)S(1)}, u32[]{:S(2)}, u32[]{:S(2)}) collective-permute-start(s16[2096,128]{1,0:T(8,128)(2,1)S(1)} %combine.7), channel_id=1, source_target_pairs={{0,24},{4,28},{8,16},{12,20},{16,8},{20,12},{24,0},{28,4},{1,25},{... | collective-permute-start | bytes 1609736 | tf_op jit(solution)/shard_map/ppermute | solution.py:426
  89.5 5.5 %copy-start.7 = (bf16[1024,256]{1,0:T(8,128)(2,1)S(1)}, bf16[1024,256]{1,0:T(8,128)(2,1)}, u32[]{:S(2)}) copy-start(bf16[1024,256]{1,0:T(8,128)(2,1)} %own.1) | copy-start | bytes 1572868
  89.5 17.5 %collective-permute-start.20 = (s16[1040,256]{1,0:T(8,128)(2,1)S(1)}, s16[1040,256]{1,0:T(8,128)(2,1)S(1)}, u32[]{:S(2)}, u32[]{:S(2)}) collective-permute-start(s16[1040,256]{1,0:T(8,128)(2,1)S(1)} %hop.5), channel_id=1, source_target_pairs={{1,2},{2,1},{5,6},{6,5},{9,10},{10,9},{13,14},{14,13},{17,18},{18,... | collective-permute-start | bytes 1597448 | tf_op jit(solution)/shard_map/ppermute | solution.py:432
  90.9 16.1 %collective-permute-start.19 = (s16[1040,256]{1,0:T(8,128)(2,1)S(1)}, s16[1040,256]{1,0:T(8,128)(2,1)S(1)}, u32[]{:S(2)}, u32[]{:S(2)}) collective-permute-start(s16[1040,256]{1,0:T(8,128)(2,1)S(1)} %hop.4), channel_id=1, source_target_pairs={{0,1},{1,0},{2,3},{3,2},{4,5},{5,4},{6,7},{7,6},{8,9},{9,8},{10,11... | collective-permute-start | bytes 1597448 | tf_op jit(solution)/shard_map/ppermute | solution.py:429

commit v9 on v8

--- a/solution.py
+++ b/solution.py
@@ -10,6 +10,7 @@
 MIB = 1024 * 1024
 GROUP = 128
 PAD = 16
+WIDE = 48
 
 
 def encode(block):
@@ -67,12 +68,9 @@
     return block
 
 
-def first_kernel(column_blocks, place_ref, normed_ref, *refs):
-    message_refs = refs[:-6]
-    weight_ref, first_ref, codes_ref, partial, scalars, sem = refs[-6:]
-    tokens = normed_ref.shape[0]
-    chunk_width = first_ref.shape[1]
-    chunks = weight_ref.shape[1] // chunk_width
+def assembly_kernel(column_blocks, features, *refs):
+    message_refs = refs[:-4]
+    weight_ref, codes_ref, scalars, sem = refs[-4:]
     tile = message_refs[0].shape[1]
     capacity = message_refs[0].shape[0] // tile
     for k, message_ref in enumerate(message_refs):
@@ -82,7 +80,6 @@
     copy.start()
     weight_ref[...] = jnp.zeros_like(weight_ref)
     copy.wait()
-    features = normed_ref.shape[1]
     for k, message_ref in enumerate(message_refs):
         for slot in range(capacity):
             code = scalars[k, slot]
@@ -92,6 +89,33 @@
             weight_ref[aligned(row, tile), aligned(column, tile)] = message_ref[
                 slot * tile : (slot + 1) * tile, :
             ]
+
+
+def assembled(messages, features, column_blocks):
+    tile = messages[0].shape[1]
+    count = len(messages)
+    return pl.pallas_call(
+        functools.partial(assembly_kernel, column_blocks, features),
+        in_specs=[VMEM] * count,
+        out_specs=[VMEM, VMEM],
+        out_shape=[
+            jax.ShapeDtypeStruct((features + tile, column_blocks * tile), jnp.bfloat16),
+            jax.ShapeDtypeStruct((count, tile), jnp.int32),
+        ],
+        scratch_shapes=[
+            pltpu.SMEM((count, tile), jnp.int32),
+            pltpu.SemaphoreType.DMA,
+        ],
+        compiler_params=params(12),
+        cost_estimate=LITTLE,
+        name="assembled",
+    )(*messages)
+
+
+def first_kernel(place_ref, normed_ref, weight_ref, first_ref, partial):
+    tokens, features = normed_ref.shape
+    chunk_width = first_ref.shape[1]
+    chunks = weight_ref.shape[1] // chunk_width
     far = weight_ref[:features, aligned(chunks - 1 - place_ref[0], chunk_width)]
     partial[...] = jnp.dot(normed_ref[...], far, preferred_element_type=jnp.float32)
     write_message(
@@ -99,28 +123,19 @@
     )
 
 
-def first_values(place, normed, messages, chunks, column_blocks):
-    tokens, features = normed.shape
-    tile = messages[0].shape[1]
-    width = column_blocks * tile
-    return pl.pallas_call(
-        functools.partial(first_kernel, column_blocks),
-        in_specs=[SMEM, VMEM] + [VMEM] * len(messages),
-        out_specs=[VMEM, VMEM, VMEM],
-        out_shape=[
-            jax.ShapeDtypeStruct((features + tile, width), jnp.bfloat16),
-            jax.ShapeDtypeStruct((tokens + PAD, width // chunks), jnp.int16),
-            jax.ShapeDtypeStruct((len(messages), tile), jnp.int32),
-        ],
-        scratch_shapes=[
-            pltpu.VMEM((tokens, width // chunks), jnp.float32),
-            pltpu.SMEM((len(messages), tile), jnp.int32),
-            pltpu.SemaphoreType.DMA,
-        ],
-        compiler_params=params(17),
+def first_values(place, normed, weight, chunks):
+    tokens = normed.shape[0]
+    width = weight.shape[1] // chunks
+    return pl.pallas_call(
+        first_kernel,
+        in_specs=[SMEM, VMEM, VMEM],
+        out_specs=VMEM,
+        out_shape=jax.ShapeDtypeStruct((tokens + PAD, width), jnp.int16),
+        scratch_shapes=[pltpu.VMEM((tokens, width), jnp.float32)],
+        compiler_params=params(14),
         cost_estimate=LITTLE,
         name="first_values",
-    )(place, normed, *messages)
+    )(place, normed, weight)
 
 
 def partial_kernel(place_ref, normed_ref, weight_ref, partial_ref, second_ref):
@@ -208,6 +223,26 @@
         jnp.where(place < 2, 2, 1),
         jnp.where(place < 2, 3, 0),
     )
+
+
+def widen_kernel(a_ref, b_ref, wide_a_ref, wide_b_ref):
+    tokens = a_ref.shape[0]
+    for ref, wide_ref in ((a_ref, wide_a_ref), (b_ref, wide_b_ref)):
+        wide_ref[:tokens, :] = ref[...]
+        wide_ref[tokens:, :] = jnp.zeros((WIDE, ref.shape[1]), ref.dtype)
+
+
+def widen(a, b):
+    shape = (a.shape[0] + WIDE, a.shape[1])
+    return pl.pallas_call(
+        widen_kernel,
+        in_specs=[VMEM, VMEM],
+        out_specs=[VMEM, VMEM],
+        out_shape=[jax.ShapeDtypeStruct(shape, a.dtype)] * 2,
+        compiler_params=params(5),
+        cost_estimate=LITTLE,
+        name="widen",
+    )(a, b)
 
 
 def product(turned, normed_ref, out_ref):
@@ -440,20 +475,35 @@
     positions = jnp.where(tile_columns >= 0, tile_rows * column_blocks + tile_columns + 1, 0)
     positions = jnp.pad(positions.astype(jnp.bfloat16), ((0, PAD - 1), (0, tile - capacity)))
     message = jnp.concatenate([tile_values.reshape(rows, tile), positions], axis=0)
-    same_core = [message] + [swap(message, 2 * chip) for chip in range(1, chips)]
+    direct = [1, 2] if chips == 4 else list(range(1, chips))
+    same_core = [message] + [swap(message, 2 * chip) for chip in direct]
+    beside = swap(message, 1)
     a1, b1 = pairs(cotangent), middle(cotangent)
     normed, g1 = own_gradient(normed, cotangent)
-    a1, b1, g1, *same_core = lax.optimization_barrier((a1, b1, g1, *same_core))
-    m2, e2 = middle(a1), outward(b1)
+    a1, b1, g1, beside, *same_core = lax.optimization_barrier((a1, b1, g1, beside, *same_core))
+    wide_a, wide_b = widen(a1, b1)
+    m2, e2 = middle(wide_a), outward(wide_b)
+    g2 = chunk_gradient(normed, a1)
+    across = [beside] + [swap(m, 1) for m in same_core[1:]]
+    if chips == 4:
+        even = lax.axis_index("fsdp") % 2 == 0
+        diagonal = lax.ppermute(
+            jnp.where(even, same_core[2], same_core[1]),
+            "fsdp",
+            [(i, i ^ 2 if i % 2 == 0 else i ^ 4) for i in range(devices)],
+        )
+        diagonal, g2 = lax.optimization_barrier((diagonal, g2))
+        same_core.append(diagonal)
+        across.append(swap(diagonal, 1))
     gathered = []
-    for m in same_core:
-        gathered += [m, swap(m, 1)]
-
-    weight, first, codes = first_values(place, normed, gathered, parts, column_blocks)
+    for pair in zip(same_core, across):
+        gathered += pair
+
+    weight, codes = assembled(gathered, normed.shape[1], column_blocks)
+    first = first_values(place, normed, weight, parts)
     arrived = inward(first)
-    m2, e2, codes = lax.optimization_barrier((m2, e2, codes))
+    m2, e2, codes, _ = lax.optimization_barrier((m2, e2, codes, first))
     d3 = outward(m2)
-    g2 = chunk_gradient(normed, a1)
     g3 = chunk_gradient(normed, b1, e2)
     partial, second = partial_values(place, normed, weight, first.shape)
     arrived, d3, g2, g3, partial = lax.optimization_barrier((arrived, d3, g2, g3, partial))

time: 109 us -> 108 us (level)
  waiting for transfers between devices: 26.2 us -> 23 us
  local copies, waits for them, and re-layouts: 9.27 us -> 12.1 us
    ppermute x14 -> x13, waiting for transfers between devices: 12.1 us -> 3.34 us  [swap(): return lax.ppermute(x, 'fsdp', [(i, i ^ mask) for i in range(devices)])]
    ppermute x2, waiting for transfers between devices: 6.3 us -> 10.6 us  [inward(): return lax.ppermute(x, 'tensor', [(0, 1), (3, 2)])]
    unnamed x16 -> x30, local copies, waits for them, and re-layouts: 9.27 us -> 12.1 us
    pallas_call x2, Pallas kernels: 4.94 us -> 3.61 us  [chunk_gradient(): pl.pallas_call(chunk_kernel, in_specs=[VMEM] + [VMEM] * len(chunks), out_...]
    ppermute x2, waiting for transfers between devices: 3 us -> 4.21 us  [pairs(): return lax.ppermute(x, 'tensor', [(0, 1), (1, 0), (2, 3), (3, 2)])]
    pallas_call x1 -> x3, Pallas kernels: 5.23 us -> 6.29 us  [the longest x1 3.88 us: assembled(): pl.pallas_call(functools.partial(assembly_kernel, column_blocks, features...]
    ppermute x14 -> x13, starting transfers between devices: 10.4 us -> 10 us  [swap(): return lax.ppermute(x, 'fsdp', [(i, i ^ mask) for i in range(devices)])]
  transfers between devices with their start and end apart: 24 -> 24, of which waited for: 9 -> 8; matrix products, arithmetic and copies ran while one was open for 0% -> 0% of each run, Pallas kernels for 26% -> 26%
where the time goes in v9:
time: 108 us; the launch traced here: 107 us
  starting transfers between devices  34.9 us (32%)
  Pallas kernels  34.6 us (32%)
  waiting for transfers between devices  23 us (21%)
  local copies, waits for them, and re-layouts  12.1 us (11%)
  other arithmetic  1.83 us (2%)
    unnamed x30, local copies, waits for them, and re-layouts  12.1 us
    ppermute x2, starting transfers between devices, inward(): return lax.ppermute(x, 'tensor', [(0, 1), (3, 2)])  10.7 us
    ppermute x2, waiting for transfers between devices, inward(): return lax.ppermute(x, 'tensor', [(0, 1), (3, 2)])  10.6 us
    ppermute x13, starting transfers between devices, swap(): return lax.ppermute(x, 'fsdp', [(i, i ^ mask) for i in range(devices)])  10 us
    pallas_call x1, Pallas kernels, grad_inputs(): pl.pallas_call(grad_input_kernel, grid_spec=pltpu.PrefetchScalarGridSpec(...  7.72 us
    ppermute x2, starting transfers between devices, pairs(): return lax.ppermute(x, 'tensor', [(0, 1), (1, 0), (2, 3), (3, 2)])  7.06 us
    pallas_call x1, Pallas kernels, slot_terms(): pl.pallas_call(functools.partial(slots_kernel, chips, column_blocks), in_...  5.27 us
    ppermute x2, waiting for transfers between devices, outward(): return lax.ppermute(x, 'tensor', [(1, 0), (2, 3)])  4.77 us
  transfers between devices with their start and end apart: 24, of which 8 were waited for; matrix products, arithmetic and copies ran while one was open for 0% of the time, Pallas kernels for 26%

profile of v9, /device:TPU:0, one launch (start us, length us, event | category | flops | bytes accessed | tf_op | source)
XLA Modules:
  0.0 107.4 jit_solution(4393608441841950944)
XLA Ops:
  0.6 0.7 fusion.2
  1.3 1.1 %fusion.1.refs_0_ = bf16[2064,128]{1,0:T(8,128)(2,1)S(1)} fusion(bf16[1,16]{1,0:T(2,128)(2,1)S(1)} %fusion.2, bf16[2048,128]{1,0:T(8,128)(2,1)} %bitcast.4), kind=kLoop, calls=%fused_computation.2 | loop fusion | flops 1585152 | bytes 1052704 | tf_op jit(solution)/shard_map/concatenate | solution.py:477
  2.4 3.0 %collective-permute-start.4 = (bf16[2064,128]{1,0:T(8,128)(2,1)S(1)}, bf16[2064,128]{1,0:T(8,128)(2,1)S(1)}, u32[]{:S(2)}, u32[]{:S(2)}) collective-permute-start(bf16[2064,128]{1,0:T(8,128)(2,1)S(1)} %fusion.1.refs_0_), channel_id=1, source_target_pairs={{0,16},{4,20},{8,24},{12,28},{16,0},{20,4},{24,8},{28,12},{1,17},{... | collective-permute-start | bytes 1585160 | tf_op jit(solution)/shard_map/ppermute | solution.py:461
  5.4 1.5 %collective-permute-start.3 = (bf16[2064,128]{1,0:T(8,128)(2,1)S(1)}, bf16[2064,128]{1,0:T(8,128)(2,1)S(1)}, u32[]{:S(2)}, u32[]{:S(2)}) collective-permute-start(bf16[2064,128]{1,0:T(8,128)(2,1)S(1)} %fusion.1.refs_0_), channel_id=1, source_target_pairs={{0,8},{4,12},{8,0},{12,4},{16,24},{20,28},{24,16},{28,20},{1,9},{5... | collective-permute-start | bytes 1585160 | tf_op jit(solution)/shard_map/ppermute | solution.py:461
  6.9 1.6 %collective-permute-start = (bf16[1024,256]{1,0:T(8,128)(2,1)}, bf16[1024,256]{1,0:T(8,128)(2,1)S(1)}, u32[]{:S(2)}, u32[]{:S(2)}) collective-permute-start(bf16[1024,256]{1,0:T(8,128)(2,1)} %own.1), channel_id=1, source_target_pairs={{0,1},{1,0},{2,3},{3,2},{4,5},{5,4},{6,7},{7,6},{8,9},{9,8},{10,11... | collective-permute-start | bytes 1572872 | tf_op jit(solution)/shard_map/ppermute | solution.py:464
  8.5 0.7 collective-permute-start.1
  9.2 2.2 %copy-done.3 = bf16[1024,2048]{1,0:T(8,128)(2,1)S(1)} copy-done((bf16[1024,2048]{1,0:T(8,128)(2,1)S(1)}, bf16[1024,2048]{1,0:T(8,128)(2,1)}, u32[]{:S(2)}) %copy-start.3) | copy-done | bytes 4194328
  11.4 1.0 copy-done.13
  12.4 1.7 %own_gradient.1 = (bf16[1024,2048]{1,0:T(8,128)(2,1)S(1)}, f32[256,2048]{1,0:T(8,128)S(1)}) custom-call(bf16[1024,2048]{1,0:T(8,128)(2,1)S(1)} %copy-done.3, bf16[1024,256]{1,0:T(8,128)(2,1)S(1)} %copy-done.13), custom_call_target="tpu_custom_call" | custom-call | flops 1 | bytes 1 | tf_op jit(solution)/shard_map/own_gradient/pallas_call | solution.py:272
  14.2 2.0 %copy-done = bf16[1024,2048]{1,0:T(8,128)(2,1)} copy-done((bf16[1024,2048]{1,0:T(8,128)(2,1)}, bf16[1024,2048]{1,0:T(8,128)(2,1)S(1)}, u32[]{:S(2)}) %copy-start) | copy-done | bytes 4194328
  16.2 1.4 %copy-done.8 = f32[256,2048]{1,0:T(8,128)} copy-done((f32[256,2048]{1,0:T(8,128)}, f32[256,2048]{1,0:T(8,128)S(1)}, u32[]{:S(2)}) %copy-start.8) | copy-done | bytes 2097176
  17.6 3.9 %collective-permute-done.refs_0_.a_ref.a1 = bf16[1024,256]{1,0:T(8,128)(2,1)S(1)} collective-permute-done((bf16[1024,256]{1,0:T(8,128)(2,1)}, bf16[1024,256]{1,0:T(8,128)(2,1)S(1)}, u32[]{:S(2)}, u32[]{:S(2)}) %collective-permute-start) | collective-permute-done | bytes 524320 | tf_op jit(solution)/shard_map/ppermute | solution.py:464
  21.6 0.6 collective-permute-start.7
  22.2 1.1 widen.1
  23.3 1.5 %collective-permute-start.10 = (bf16[1072,256]{1,0:T(8,128)(2,1)}, bf16[1072,256]{1,0:T(8,128)(2,1)}, u32[]{:S(2)}, u32[]{:S(2)}) collective-permute-start(bf16[1072,256]{1,0:T(8,128)(2,1)} %get-tuple-element.55), channel_id=1, source_target_pairs={{1,2},{2,1},{5,6},{6,5},{9,10},{10,9},{13,14},{14,13},{17,18},{18,... | collective-permute-start | bytes 1646600 | tf_op jit(solution)/shard_map/ppermute | solution.py:467
  24.7 1.3 %collective-permute-start.11 = (bf16[1072,256]{1,0:T(8,128)(2,1)}, bf16[1072,256]{1,0:T(8,128)(2,1)}, u32[]{:S(2)}, u32[]{:S(2)}) collective-permute-start(bf16[1072,256]{1,0:T(8,128)(2,1)} %get-tuple-element.56), channel_id=1, source_target_pairs={{1,0},{2,3},{5,4},{6,7},{9,8},{10,11},{13,12},{14,15},{17,16},{18,... | collective-permute-start | bytes 1646600 | tf_op jit(solution)/shard_map/ppermute | solution.py:470
  26.1 0.5 collective-permute-start.6
  26.6 2.2 %copy-done.1 = bf16[1024,2048]{1,0:T(8,128)(2,1)S(1)} copy-done((bf16[1024,2048]{1,0:T(8,128)(2,1)S(1)}, bf16[1024,2048]{1,0:T(8,128)(2,1)}, u32[]{:S(2)}) %copy-start.1) | copy-done | bytes 4194328
  28.8 1.0 copy-done.11
  29.8 1.3 %chunk_gradient.2.g2 = f32[256,2048]{1,0:T(8,128)S(1)} custom-call(bf16[1024,2048]{1,0:T(8,128)(2,1)S(1)} %copy-done.1, bf16[1024,256]{1,0:T(8,128)(2,1)S(1)} %copy-done.11), custom_call_target="tpu_custom_call" | custom-call | flops 1 | bytes 1 | tf_op jit(solution)/shard_map/chunk_gradient/pallas_call | solution.py:288
  31.3 2.2 %collective-permute-done.8.refs_7_ = bf16[2064,128]{1,0:T(8,128)(2,1)} collective-permute-done((bf16[2064,128]{1,0:T(8,128)(2,1)}, bf16[2064,128]{1,0:T(8,128)(2,1)}, u32[]{:S(2)}, u32[]{:S(2)}) %collective-permute-start.8) | collective-permute-done | bytes 528416 | tf_op jit(solution)/shard_map/ppermute | solution.py:461
  33.4 1.0 copy-done.5
  34.5 3.9 %assembled.1 = (bf16[2176,1024]{1,0:T(8,128)(2,1)S(1)}, s32[8,128]{1,0:T(8,128)S(1)}) custom-call(bf16[2064,128]{1,0:T(8,128)(2,1)S(1)} %copy-done.5, bf16[2064,128]{1,0:T(8,128)(2,1)} %collective-permute-done.2.refs_1_, bf16[2064,128]{1,0:T(8,128)(2,1)S(1)} %collective-permute-done.3.refs_2_, bf16[2064,128]{1,0:T(8,128)(2,1)} %collective-permute-done.5.refs_3_, ...), custom_call_target="tpu_custom_call" | custom-call | flops 1 | bytes 1 | tf_op jit(solution)/shard_map/assembled/pallas_call | solution.py:97
  38.4 1.3 %first_values.1 = s16[1040,256]{1,0:T(8,128)(2,1)S(1)} custom-call(s32[1]{0:T(128)} %bitcast.place_ref, bf16[1024,2048]{1,0:T(8,128)(2,1)S(1)} %copy-done.2, bf16[2176,1024]{1,0:T(8,128)(2,1)S(1)} %get-tuple-element.53.weight_ref), custom_call_target="tpu_custom_call" | custom-call | flops 1 | bytes 1 | tf_op jit(solution)/shard_map/first_values/pallas_call | solution.py:129
  39.7 4.8 %collective-permute-done.11.refs_1_.e2 = bf16[1072,256]{1,0:T(8,128)(2,1)} collective-permute-done((bf16[1072,256]{1,0:T(8,128)(2,1)}, bf16[1072,256]{1,0:T(8,128)(2,1)}, u32[]{:S(2)}, u32[]{:S(2)}) %collective-permute-start.11) | collective-permute-done | bytes 548896 | tf_op jit(solution)/shard_map/ppermute | solution.py:470
  44.5 1.4 %collective-permute-start.12 = (bf16[1072,256]{1,0:T(8,128)(2,1)}, bf16[1072,256]{1,0:T(8,128)(2,1)S(1)}, u32[]{:S(2)}, u32[]{:S(2)}) collective-permute-start(bf16[1072,256]{1,0:T(8,128)(2,1)} %collective-permute-done.10.m2), channel_id=1, source_target_pairs={{1,0},{2,3},{5,4},{6,7},{9,8},{10,11},{13,12},{14,15},{17,16},{18,... | collective-permute-start | bytes 1646600 | tf_op jit(solution)/shard_map/ppermute | solution.py:470
  45.9 4.9 %collective-permute-start.9 = (s16[1040,256]{1,0:T(8,128)(2,1)S(1)}, s16[1040,256]{1,0:T(8,128)(2,1)S(1)}, u32[]{:S(2)}, u32[]{:S(2)}) collective-permute-start(s16[1040,256]{1,0:T(8,128)(2,1)S(1)} %first_values.1), channel_id=1, source_target_pairs={{0,1},{3,2},{4,5},{7,6},{8,9},{11,10},{12,13},{15,14},{16,17},{19,... | collective-permute-start | bytes 1597448 | tf_op jit(solution)/shard_map/ppermute | solution.py:473
  50.9 4.7 %partial_values.1 = (f32[1024,1024]{1,0:T(8,128)S(1)}, s16[1040,256]{1,0:T(8,128)(2,1)S(1)}) custom-call(s32[1]{0:T(128)} %bitcast.place_ref, bf16[1024,2048]{1,0:T(8,128)(2,1)S(1)} %copy-done.2, bf16[2176,1024]{1,0:T(8,128)(2,1)S(1)} %get-tuple-element.53.weight_ref), custom_call_target="tpu_custom_call" | custom-call | flops 1 | bytes 1 | tf_op jit(solution)/shard_map/partial_values/pallas_call | solution.py:158
  55.6 2.3 %chunk_gradient.3.g3 = f32[256,2048]{1,0:T(8,128)S(1)} custom-call(bf16[1024,2048]{1,0:T(8,128)(2,1)S(1)} %copy-done.2, bf16[1024,256]{1,0:T(8,128)(2,1)S(1)} %copy-done.7, bf16[1072,256]{1,0:T(8,128)(2,1)} %collective-permute-done.11.refs_1_.e2), custom_call_target="tpu_custom_call" | custom-call | flops 1 | bytes 1 | tf_op jit(solution)/shard_map/chunk_gradient/pallas_call | solution.py:288
  58.0 4.3 %collective-permute-done.9.arrived_ref = s16[1040,256]{1,0:T(8,128)(2,1)S(1)} collective-permute-done((s16[1040,256]{1,0:T(8,128)(2,1)S(1)}, s16[1040,256]{1,0:T(8,128)(2,1)S(1)}, u32[]{:S(2)}, u32[]{:S(2)}) %collective-permute-start.9) | collective-permute-done | bytes 532512 | tf_op jit(solution)/shard_map/ppermute | solution.py:473
  62.7 1.2 %copy-done.9 = f32[256,2048]{1,0:T(8,128)S(1)} copy-done((f32[256,2048]{1,0:T(8,128)S(1)}, f32[256,2048]{1,0:T(8,128)}, u32[]{:S(2)}) %copy-start.9) | copy-done | bytes 2097176
  63.9 5.3 %slot_terms.1 = (f32[2048,128]{1,0:T(8,128)S(1)}, f32[2048,128]{1,0:T(8,128)S(1)}, f32[2048,128]{1,0:T(8,128)S(1)}, f32[2048,128]{1,0:T(8,128)S(1)}, s16[2096,12...) custom-call(s32[8,128]{1,0:T(8,128)S(1)} %get-tuple-element.68.codes, ...), custom_call_target="tpu_custom_call" | custom-call | flops 1 | bytes 1 | tf_op jit(solution)/shard_map/slot_terms/pallas_call | solution.py:344
  69.2 0.5 collective-permute-start.17
  69.8 0.4 collective-permute-start.15
  70.3 0.7 collective-permute-start.13
  71.2 5.7 %collective-permute-start.14 = (s16[1040,256]{1,0:T(8,128)(2,1)S(1)}, s16[1040,256]{1,0:T(8,128)(2,1)S(1)}, u32[]{:S(2)}, u32[]{:S(2)}) collective-permute-start(s16[1040,256]{1,0:T(8,128)(2,1)S(1)} %get-tuple-element.67), channel_id=1, source_target_pairs={{0,1},{3,2},{4,5},{7,6},{8,9},{11,10},{12,13},{15,14},{16,17},{19,... | collective-permute-start | bytes 1597448 | tf_op jit(solution)/shard_map/ppermute | solution.py:473
  76.9 0.4 combine.5
  77.3 1.6 %collective-permute-start.23 = (s16[2096,128]{1,0:T(8,128)(2,1)S(1)}, s16[2096,128]{1,0:T(8,128)(2,1)S(1)}, u32[]{:S(2)}, u32[]{:S(2)}) collective-permute-start(s16[2096,128]{1,0:T(8,128)(2,1)S(1)} %combine.5), channel_id=1, source_target_pairs={{0,8},{4,12},{8,0},{12,4},{16,24},{20,28},{24,16},{28,20},{1,9},{5... | collective-permute-start | bytes 1609736 | tf_op jit(solution)/shard_map/ppermute | solution.py:461
  78.8 0.4 combine.6
  79.2 0.6 collective-permute-start.22
  80.2 1.6 %collective-permute-start.21 = (s16[2096,128]{1,0:T(8,128)(2,1)S(1)}, s16[2096,128]{1,0:T(8,128)(2,1)S(1)}, u32[]{:S(2)}, u32[]{:S(2)}) collective-permute-start(s16[2096,128]{1,0:T(8,128)(2,1)S(1)} %combine.7), channel_id=1, source_target_pairs={{0,24},{4,28},{8,16},{12,20},{16,8},{20,12},{24,0},{28,4},{1,25},{... | collective-permute-start | bytes 1609736 | tf_op jit(solution)/shard_map/ppermute | solution.py:461
  81.9 6.3 %collective-permute-done.14.arrived_ref = s16[1040,256]{1,0:T(8,128)(2,1)S(1)} collective-permute-done((s16[1040,256]{1,0:T(8,128)(2,1)S(1)}, s16[1040,256]{1,0:T(8,128)(2,1)S(1)}, u32[]{:S(2)}, u32[]{:S(2)}) %collective-permute-start.14) | collective-permute-done | bytes 532512 | tf_op jit(solution)/shard_map/ppermute | solution.py:473
  88.5 1.0 collective-permute-start.20
  89.9 5.5 %collective-permute-start.19 = (s16[1040,256]{1,0:T(8,128)(2,1)S(1)}, s16[1040,256]{1,0:T(8,128)(2,1)S(1)}, u32[]{:S(2)}, u32[]{:S(2)}) collective-permute-start(s16[1040,256]{1,0:T(8,128)(2,1)S(1)} %hop.4), channel_id=1, source_target_pairs={{0,1},{1,0},{2,3},{3,2},{4,5},{5,4},{6,7},{7,6},{8,9},{9,8},{10,11... | collective-permute-start | bytes 1597448 | tf_op jit(solution)/shard_map/ppermute | solution.py:464
  95.4 7.7 %grad_inputs.1 = bf16[1024,2048]{1,0:T(8,128)(2,1)} custom-call(s32[1]{0:T(128)} %bitcast.place_ref, bf16[2176,1024]{1,0:T(8,128)(2,1)S(1)} %get-tuple-element.53.weight_ref, bf16[1024,256]{1,0:T(8,128)(2,1)S(1)} %copy-done.14, bf16[1024,256]{1,0:T(8,128)(2,1)S(1)} %copy-done.12, bf16[1024,256]{1,0:T(8,128)(2,1)S(1)} %copy-done.7, ...), custom_call_target="tpu_custom_call" | custom-call | flops 4294967296 | bytes 12582912 | tf_op jit(solution)/shard_map/grad_inputs/pallas_call | solution.py:432
  103.2 0.9 collective-permute-done.22.refs_2_
  104.1 1.9 %normalized_update.1 = bf16[16,128,128]{2,1,0:T(8,128)(2,1)} custom-call(f32[2048,128]{1,0:T(8,128)S(1)} %combine.4.refs_0_, s16[2096,128]{1,0:T(8,128)(2,1)S(1)} %collective-permute-done.21.refs_1_, s16[2096,128]{1,0:T(8,128)(2,1)S(1)} %collective-permute-done.22.refs_2_, s16[2096,128]{1,0:T(8,128)(2,1)S(1)} %collective-permute-done.23.refs_3_), custom_call_target="tpu_custom_call" | custom-call | flops 1 | bytes 1 | tf_op jit(solution)/shard_map/normalized_update/pallas_call | solution.py:402
  106.3 1.1 %last_hop.1 = bf16[1024,256]{1,0:T(8,128)(2,1)} custom-call(s32[1]{0:T(128)} %bitcast.place_ref, f32[1024,1024]{1,0:T(8,128)S(1)} %get-tuple-element.62.partial_ref, s16[1040,256]{1,0:T(8,128)(2,1)S(1)} %collective-permute-done.19.right_ref, s16[1040,256]{1,0:T(8,128)(2,1)S(1)} %collective-permute-done.20.left_ref), custom_call_target="tpu_custom_call" | custom-call | flops 1 | bytes 1 | tf_op jit(solution)/shard_map/last_hop/pallas_call | solution.py:208
  (51 shorter events, 2.6 us)
Async XLA Ops:
  2.4 11.8 %copy-start.4 = (bf16[2064,128]{1,0:T(8,128)(2,1)}, bf16[2064,128]{1,0:T(8,128)(2,1)S(1)}, u32[]{:S(2)}) copy-start(bf16[2064,128]{1,0:T(8,128)(2,1)S(1)} %fusion.1.refs_0_) | copy-start | bytes 1585156
  2.4 19.1 %collective-permute-start.4 = (bf16[2064,128]{1,0:T(8,128)(2,1)S(1)}, bf16[2064,128]{1,0:T(8,128)(2,1)S(1)}, u32[]{:S(2)}, u32[]{:S(2)}) collective-permute-start(bf16[2064,128]{1,0:T(8,128)(2,1)S(1)} %fusion.1.refs_0_), channel_id=1, source_target_pairs={{0,16},{4,20},{8,24},{12,28},{16,0},{20,4},{24,8},{28,12},{1,17},{... | collective-permute-start | bytes 1585160 | tf_op jit(solution)/shard_map/ppermute | solution.py:461
  5.4 16.1 %collective-permute-start.3 = (bf16[2064,128]{1,0:T(8,128)(2,1)S(1)}, bf16[2064,128]{1,0:T(8,128)(2,1)S(1)}, u32[]{:S(2)}, u32[]{:S(2)}) collective-permute-start(bf16[2064,128]{1,0:T(8,128)(2,1)S(1)} %fusion.1.refs_0_), channel_id=1, source_target_pairs={{0,8},{4,12},{8,0},{12,4},{16,24},{20,28},{24,16},{28,20},{1,9},{5... | collective-permute-start | bytes 1585160 | tf_op jit(solution)/shard_map/ppermute | solution.py:461
  6.9 14.6 %collective-permute-start.2 = (bf16[2064,128]{1,0:T(8,128)(2,1)S(1)}, bf16[2064,128]{1,0:T(8,128)(2,1)}, u32[]{:S(2)}, u32[]{:S(2)}) collective-permute-start(bf16[2064,128]{1,0:T(8,128)(2,1)S(1)} %fusion.1.refs_0_), channel_id=1, source_target_pairs={{0,4},{4,0},{8,12},{12,8},{16,20},{20,16},{24,28},{28,24},{1,5},{5... | collective-permute-start | bytes 1585160 | tf_op jit(solution)/shard_map/ppermute | solution.py:461
  6.9 14.5 %collective-permute-start = (bf16[1024,256]{1,0:T(8,128)(2,1)}, bf16[1024,256]{1,0:T(8,128)(2,1)S(1)}, u32[]{:S(2)}, u32[]{:S(2)}) collective-permute-start(bf16[1024,256]{1,0:T(8,128)(2,1)} %own.1), channel_id=1, source_target_pairs={{0,1},{1,0},{2,3},{3,2},{4,5},{5,4},{6,7},{7,6},{8,9},{9,8},{10,11... | collective-permute-start | bytes 1572872 | tf_op jit(solution)/shard_map/ppermute | solution.py:464
  8.5 13.0 %collective-permute-start.1 = (bf16[1024,256]{1,0:T(8,128)(2,1)}, bf16[1024,256]{1,0:T(8,128)(2,1)S(1)}, u32[]{:S(2)}, u32[]{:S(2)}) collective-permute-start(bf16[1024,256]{1,0:T(8,128)(2,1)} %own.1), channel_id=1, source_target_pairs={{1,2},{2,1},{5,6},{6,5},{9,10},{10,9},{13,14},{14,13},{17,18},{18,... | collective-permute-start | bytes 1572872 | tf_op jit(solution)/shard_map/ppermute | solution.py:467
  9.2 2.2 %copy-start.3 = (bf16[1024,2048]{1,0:T(8,128)(2,1)S(1)}, bf16[1024,2048]{1,0:T(8,128)(2,1)}, u32[]{:S(2)}) copy-start(bf16[1024,2048]{1,0:T(8,128)(2,1)} %normed_ref.1) | copy-start | bytes 12582916
  11.4 1.0 copy-start.13
  14.2 2.0 %copy-start = (bf16[1024,2048]{1,0:T(8,128)(2,1)}, bf16[1024,2048]{1,0:T(8,128)(2,1)S(1)}, u32[]{:S(2)}) copy-start(bf16[1024,2048]{1,0:T(8,128)(2,1)S(1)} %get-tuple-element.45.normed_ref) | copy-start | bytes 12582916
  16.2 1.4 %copy-start.8 = (f32[256,2048]{1,0:T(8,128)}, f32[256,2048]{1,0:T(8,128)S(1)}, u32[]{:S(2)}) copy-start(f32[256,2048]{1,0:T(8,128)S(1)} %get-tuple-element.70.g1) | copy-start | bytes 6291460
  21.5 5.1 %copy-start.10 = (bf16[1024,256]{1,0:T(8,128)(2,1)}, bf16[1024,256]{1,0:T(8,128)(2,1)S(1)}, u32[]{:S(2)}) copy-start(bf16[1024,256]{1,0:T(8,128)(2,1)S(1)} %collective-permute-done.refs_0_.a_ref.a1) | copy-start | bytes 1572868
  21.5 5.1 %copy-start.6 = (bf16[1024,256]{1,0:T(8,128)(2,1)}, bf16[1024,256]{1,0:T(8,128)(2,1)S(1)}, u32[]{:S(2)}) copy-start(bf16[1024,256]{1,0:T(8,128)(2,1)S(1)} %collective-permute-done.1.b_ref.refs_0_.b1) | copy-start | bytes 1572868
  21.6 9.5 %collective-permute-start.7 = (bf16[2064,128]{1,0:T(8,128)(2,1)S(1)}, bf16[2064,128]{1,0:T(8,128)(2,1)}, u32[]{:S(2)}, u32[]{:S(2)}) collective-permute-start(bf16[2064,128]{1,0:T(8,128)(2,1)S(1)} %broadcast_select_fusion), channel_id=1, source_target_pairs={{0,8},{4,20},{8,0},{12,28},{16,24},{20,4},{24,16},{28,12},{1,9},{5... | collective-permute-start | bytes 1585160 | tf_op jit(solution)/shard_map/ppermute | solution.py:490
  23.3 16.5 %collective-permute-start.10 = (bf16[1072,256]{1,0:T(8,128)(2,1)}, bf16[1072,256]{1,0:T(8,128)(2,1)}, u32[]{:S(2)}, u32[]{:S(2)}) collective-permute-start(bf16[1072,256]{1,0:T(8,128)(2,1)} %get-tuple-element.55), channel_id=1, source_target_pairs={{1,2},{2,1},{5,6},{6,5},{9,10},{10,9},{13,14},{14,13},{17,18},{18,... | collective-permute-start | bytes 1646600 | tf_op jit(solution)/shard_map/ppermute | solution.py:467
  24.7 19.8 %collective-permute-start.11 = (bf16[1072,256]{1,0:T(8,128)(2,1)}, bf16[1072,256]{1,0:T(8,128)(2,1)}, u32[]{:S(2)}, u32[]{:S(2)}) collective-permute-start(bf16[1072,256]{1,0:T(8,128)(2,1)} %get-tuple-element.56), channel_id=1, source_target_pairs={{1,0},{2,3},{5,4},{6,7},{9,8},{10,11},{13,12},{14,15},{17,16},{18,... | collective-permute-start | bytes 1646600 | tf_op jit(solution)/shard_map/ppermute | solution.py:470
  26.0 5.3 %collective-permute-start.5 = (bf16[2064,128]{1,0:T(8,128)(2,1)S(1)}, bf16[2064,128]{1,0:T(8,128)(2,1)}, u32[]{:S(2)}, u32[]{:S(2)}) collective-permute-start(bf16[2064,128]{1,0:T(8,128)(2,1)S(1)} %collective-permute-done.3.refs_2_), channel_id=1, source_target_pairs={{0,4},{4,0},{8,12},{12,8},{16,20},{20,16},{24,28},{28,24},{1,5},{5... | collective-permute-start | bytes 1585160 | tf_op jit(solution)/shard_map/ppermute | solution.py:461
  26.1 5.2 %collective-permute-start.6 = (bf16[2064,128]{1,0:T(8,128)(2,1)S(1)}, bf16[2064,128]{1,0:T(8,128)(2,1)}, u32[]{:S(2)}, u32[]{:S(2)}) collective-permute-start(bf16[2064,128]{1,0:T(8,128)(2,1)S(1)} %collective-permute-done.4.refs_4_), channel_id=1, source_target_pairs={{0,4},{4,0},{8,12},{12,8},{16,20},{20,16},{24,28},{28,24},{1,5},{5... | collective-permute-start | bytes 1585160 | tf_op jit(solution)/shard_map/ppermute | solution.py:461
  26.6 2.2 %copy-start.1 = (bf16[1024,2048]{1,0:T(8,128)(2,1)S(1)}, bf16[1024,2048]{1,0:T(8,128)(2,1)}, u32[]{:S(2)}) copy-start(bf16[1024,2048]{1,0:T(8,128)(2,1)} %copy-done) | copy-start | bytes 12582916
  28.8 1.0 copy-start.11
  31.1 2.3 %collective-permute-start.8 = (bf16[2064,128]{1,0:T(8,128)(2,1)}, bf16[2064,128]{1,0:T(8,128)(2,1)}, u32[]{:S(2)}, u32[]{:S(2)}) collective-permute-start(bf16[2064,128]{1,0:T(8,128)(2,1)} %collective-permute-done.7.refs_6_), channel_id=1, source_target_pairs={{0,4},{4,0},{8,12},{12,8},{16,20},{20,16},{24,28},{28,24},{1,5},{5... | collective-permute-start | bytes 1585160 | tf_op jit(solution)/shard_map/ppermute | solution.py:461
  31.3 7.1 %copy-start.2 = (bf16[1024,2048]{1,0:T(8,128)(2,1)S(1)}, bf16[1024,2048]{1,0:T(8,128)(2,1)}, u32[]{:S(2)}) copy-start(bf16[1024,2048]{1,0:T(8,128)(2,1)} %copy-done) | copy-start | bytes 12582916
  33.4 1.0 copy-start.5
  44.5 11.1 %copy-start.7 = (bf16[1024,256]{1,0:T(8,128)(2,1)S(1)}, bf16[1024,256]{1,0:T(8,128)(2,1)}, u32[]{:S(2)}) copy-start(bf16[1024,256]{1,0:T(8,128)(2,1)} %copy-done.6) | copy-start | bytes 1572868
  44.5 17.8 %collective-permute-start.12 = (bf16[1072,256]{1,0:T(8,128)(2,1)}, bf16[1072,256]{1,0:T(8,128)(2,1)S(1)}, u32[]{:S(2)}, u32[]{:S(2)}) collective-permute-start(bf16[1072,256]{1,0:T(8,128)(2,1)} %collective-permute-done.10.m2), channel_id=1, source_target_pairs={{1,0},{2,3},{5,4},{6,7},{9,8},{10,11},{13,12},{14,15},{17,16},{18,... | collective-permute-start | bytes 1646600 | tf_op jit(solution)/shard_map/ppermute | solution.py:470
  45.9 16.4 %collective-permute-start.9 = (s16[1040,256]{1,0:T(8,128)(2,1)S(1)}, s16[1040,256]{1,0:T(8,128)(2,1)S(1)}, u32[]{:S(2)}, u32[]{:S(2)}) collective-permute-start(s16[1040,256]{1,0:T(8,128)(2,1)S(1)} %first_values.1), channel_id=1, source_target_pairs={{0,1},{3,2},{4,5},{7,6},{8,9},{11,10},{12,13},{15,14},{16,17},{19,... | collective-permute-start | bytes 1597448 | tf_op jit(solution)/shard_map/ppermute | solution.py:473
  62.3 1.6 %copy-start.9 = (f32[256,2048]{1,0:T(8,128)S(1)}, f32[256,2048]{1,0:T(8,128)}, u32[]{:S(2)}) copy-start(f32[256,2048]{1,0:T(8,128)} %copy-done.8) | copy-start | bytes 6291460
  69.2 2.0 %collective-permute-start.16 = (s16[2096,128]{1,0:T(8,128)(2,1)S(1)}, s16[2096,128]{1,0:T(8,128)(2,1)S(1)}, u32[]{:S(2)}, u32[]{:S(2)}) collective-permute-start(s16[2096,128]{1,0:T(8,128)(2,1)S(1)} %get-tuple-element.76), channel_id=1, source_target_pairs={{0,4},{4,0},{8,12},{12,8},{16,20},{20,16},{24,28},{28,24},{1,5},{5... | collective-permute-start | bytes 1609736 | tf_op jit(solution)/shard_map/ppermute | solution.py:461
  69.2 8.0 %collective-permute-start.17 = (s16[2096,128]{1,0:T(8,128)(2,1)S(1)}, s16[2096,128]{1,0:T(8,128)(2,1)S(1)}, u32[]{:S(2)}, u32[]{:S(2)}) collective-permute-start(s16[2096,128]{1,0:T(8,128)(2,1)S(1)} %get-tuple-element.78), channel_id=1, source_target_pairs={{0,4},{4,0},{8,12},{12,8},{16,20},{20,16},{24,28},{28,24},{1,5},{5... | collective-permute-start | bytes 1609736 | tf_op jit(solution)/shard_map/ppermute | solution.py:461
  69.7 9.5 %collective-permute-start.18 = (s16[2096,128]{1,0:T(8,128)(2,1)S(1)}, s16[2096,128]{1,0:T(8,128)(2,1)S(1)}, u32[]{:S(2)}, u32[]{:S(2)}) collective-permute-start(s16[2096,128]{1,0:T(8,128)(2,1)S(1)} %get-tuple-element.80), channel_id=1, source_target_pairs={{0,4},{4,0},{8,12},{12,8},{16,20},{20,16},{24,28},{28,24},{1,5},{5... | collective-permute-start | bytes 1609736 | tf_op jit(solution)/shard_map/ppermute | solution.py:461
  69.8 10.3 %collective-permute-start.15 = (s16[2096,128]{1,0:T(8,128)(2,1)S(1)}, s16[2096,128]{1,0:T(8,128)(2,1)S(1)}, u32[]{:S(2)}, u32[]{:S(2)}) collective-permute-start(s16[2096,128]{1,0:T(8,128)(2,1)S(1)} %get-tuple-element.74), channel_id=1, source_target_pairs={{0,4},{4,0},{8,12},{12,8},{16,20},{20,16},{24,28},{28,24},{1,5},{5... | collective-permute-start | bytes 1609736 | tf_op jit(solution)/shard_map/ppermute | solution.py:461
  70.3 11.6 %collective-permute-start.13 = (s16[1040,256]{1,0:T(8,128)(2,1)S(1)}, s16[1040,256]{1,0:T(8,128)(2,1)S(1)}, u32[]{:S(2)}, u32[]{:S(2)}) collective-permute-start(s16[1040,256]{1,0:T(8,128)(2,1)S(1)} %hop.3), channel_id=1, source_target_pairs={{1,2},{2,1},{5,6},{6,5},{9,10},{10,9},{13,14},{14,13},{17,18},{18,... | collective-permute-start | bytes 1597448 | tf_op jit(solution)/shard_map/ppermute | solution.py:467
  71.2 17.0 %collective-permute-start.14 = (s16[1040,256]{1,0:T(8,128)(2,1)S(1)}, s16[1040,256]{1,0:T(8,128)(2,1)S(1)}, u32[]{:S(2)}, u32[]{:S(2)}) collective-permute-start(s16[1040,256]{1,0:T(8,128)(2,1)S(1)} %get-tuple-element.67), channel_id=1, source_target_pairs={{0,1},{3,2},{4,5},{7,6},{8,9},{11,10},{12,13},{15,14},{16,17},{19,... | collective-permute-start | bytes 1597448 | tf_op jit(solution)/shard_map/ppermute | solution.py:473
  77.3 25.9 %collective-permute-start.23 = (s16[2096,128]{1,0:T(8,128)(2,1)S(1)}, s16[2096,128]{1,0:T(8,128)(2,1)S(1)}, u32[]{:S(2)}, u32[]{:S(2)}) collective-permute-start(s16[2096,128]{1,0:T(8,128)(2,1)S(1)} %combine.5), channel_id=1, source_target_pairs={{0,8},{4,12},{8,0},{12,4},{16,24},{20,28},{24,16},{28,20},{1,9},{5... | collective-permute-start | bytes 1609736 | tf_op jit(solution)/shard_map/ppermute | solution.py:461
  79.2 24.9 %collective-permute-start.22 = (s16[2096,128]{1,0:T(8,128)(2,1)S(1)}, s16[2096,128]{1,0:T(8,128)(2,1)S(1)}, u32[]{:S(2)}, u32[]{:S(2)}) collective-permute-start(s16[2096,128]{1,0:T(8,128)(2,1)S(1)} %combine.6), channel_id=1, source_target_pairs={{0,16},{4,20},{8,24},{12,28},{16,0},{20,4},{24,8},{28,12},{1,17},{... | collective-permute-start | bytes 1609736 | tf_op jit(solution)/shard_map/ppermute | solution.py:461
  80.2 23.9 %collective-permute-start.21 = (s16[2096,128]{1,0:T(8,128)(2,1)S(1)}, s16[2096,128]{1,0:T(8,128)(2,1)S(1)}, u32[]{:S(2)}, u32[]{:S(2)}) collective-permute-start(s16[2096,128]{1,0:T(8,128)(2,1)S(1)} %combine.7), channel_id=1, source_target_pairs={{0,24},{4,28},{8,16},{12,20},{16,8},{20,12},{24,0},{28,4},{1,25},{... | collective-permute-start | bytes 1609736 | tf_op jit(solution)/shard_map/ppermute | solution.py:461
  88.5 6.9 %copy-start.12 = (bf16[1024,256]{1,0:T(8,128)(2,1)S(1)}, bf16[1024,256]{1,0:T(8,128)(2,1)}, u32[]{:S(2)}) copy-start(bf16[1024,256]{1,0:T(8,128)(2,1)} %copy-done.10) | copy-start | bytes 1572868
  88.5 6.9 %copy-start.14 = (bf16[1024,256]{1,0:T(8,128)(2,1)S(1)}, bf16[1024,256]{1,0:T(8,128)(2,1)}, u32[]{:S(2)}) copy-start(bf16[1024,256]{1,0:T(8,128)(2,1)} %own.1) | copy-start | bytes 1572868
  88.5 17.5 %collective-permute-start.20 = (s16[1040,256]{1,0:T(8,128)(2,1)S(1)}, s16[1040,256]{1,0:T(8,128)(2,1)S(1)}, u32[]{:S(2)}, u32[]{:S(2)}) collective-permute-start(s16[1040,256]{1,0:T(8,128)(2,1)S(1)} %hop.5), channel_id=1, source_target_pairs={{1,2},{2,1},{5,6},{6,5},{9,10},{10,9},{13,14},{14,13},{17,18},{18,... | collective-permute-start | bytes 1597448 | tf_op jit(solution)/shard_map/ppermute | solution.py:467
  89.9 16.4 %collective-permute-start.19 = (s16[1040,256]{1,0:T(8,128)(2,1)S(1)}, s16[1040,256]{1,0:T(8,128)(2,1)S(1)}, u32[]{:S(2)}, u32[]{:S(2)}) collective-permute-start(s16[1040,256]{1,0:T(8,128)(2,1)S(1)} %hop.4), channel_id=1, source_target_pairs={{0,1},{1,0},{2,3},{3,2},{4,5},{5,4},{6,7},{7,6},{8,9},{9,8},{10,11... | collective-permute-start | bytes 1597448 | tf_op jit(solution)/shard_map/ppermute | solution.py:464

commit v10 on v9

--- a/solution.py
+++ b/solution.py
@@ -10,7 +10,6 @@
 MIB = 1024 * 1024
 GROUP = 128
 PAD = 16
-WIDE = 48
 
 
 def encode(block):
@@ -107,7 +106,7 @@
             pltpu.SemaphoreType.DMA,
         ],
         compiler_params=params(12),
-        cost_estimate=LITTLE,
+        cost_estimate=pl.CostEstimate(flops=0, bytes_accessed=8 * MIB, transcendentals=0),
         name="assembled",
     )(*messages)
 
@@ -225,24 +224,25 @@
     )
 
 
-def widen_kernel(a_ref, b_ref, wide_a_ref, wide_b_ref):
-    tokens = a_ref.shape[0]
-    for ref, wide_ref in ((a_ref, wide_a_ref), (b_ref, wide_b_ref)):
-        wide_ref[:tokens, :] = ref[...]
-        wide_ref[tokens:, :] = jnp.zeros((WIDE, ref.shape[1]), ref.dtype)
-
-
-def widen(a, b):
-    shape = (a.shape[0] + WIDE, a.shape[1])
+def widen_kernel(chunk_ref, *wide_refs):
+    tokens = chunk_ref.shape[0]
+    for wide_ref in wide_refs:
+        spare = wide_ref.shape[0] - tokens
+        wide_ref[:tokens, :] = chunk_ref[...]
+        wide_ref[tokens:, :] = jnp.zeros((spare, chunk_ref.shape[1]), chunk_ref.dtype)
+
+
+def widen(chunk, *spares):
+    tokens, width = chunk.shape
     return pl.pallas_call(
         widen_kernel,
-        in_specs=[VMEM, VMEM],
-        out_specs=[VMEM, VMEM],
-        out_shape=[jax.ShapeDtypeStruct(shape, a.dtype)] * 2,
+        in_specs=[VMEM],
+        out_specs=[VMEM] * len(spares),
+        out_shape=[jax.ShapeDtypeStruct((tokens + spare, width), chunk.dtype) for spare in spares],
         compiler_params=params(5),
         cost_estimate=LITTLE,
         name="widen",
-    )(a, b)
+    )(chunk)
 
 
 def product(turned, normed_ref, out_ref):
@@ -475,44 +475,33 @@
     positions = jnp.where(tile_columns >= 0, tile_rows * column_blocks + tile_columns + 1, 0)
     positions = jnp.pad(positions.astype(jnp.bfloat16), ((0, PAD - 1), (0, tile - capacity)))
     message = jnp.concatenate([tile_values.reshape(rows, tile), positions], axis=0)
-    direct = [1, 2] if chips == 4 else list(range(1, chips))
-    same_core = [message] + [swap(message, 2 * chip) for chip in direct]
+    wider, wide = widen(cotangent, 2 * PAD, PAD)
+    a1, b1 = pairs(wider), middle(wide)
+    normed, g1 = own_gradient(normed, cotangent)
+    same_core = [message] + [swap(message, 2 * chip) for chip in range(1, chips)]
     beside = swap(message, 1)
-    a1, b1 = pairs(cotangent), middle(cotangent)
-    normed, g1 = own_gradient(normed, cotangent)
-    a1, b1, g1, beside, *same_core = lax.optimization_barrier((a1, b1, g1, beside, *same_core))
-    wide_a, wide_b = widen(a1, b1)
-    m2, e2 = middle(wide_a), outward(wide_b)
+    a1, b1, g1, beside = lax.optimization_barrier((a1, b1, g1, beside))
+    m2, e2 = middle(a1), outward(b1)
     g2 = chunk_gradient(normed, a1)
-    across = [beside] + [swap(m, 1) for m in same_core[1:]]
-    if chips == 4:
-        even = lax.axis_index("fsdp") % 2 == 0
-        diagonal = lax.ppermute(
-            jnp.where(even, same_core[2], same_core[1]),
-            "fsdp",
-            [(i, i ^ 2 if i % 2 == 0 else i ^ 4) for i in range(devices)],
-        )
-        diagonal, g2 = lax.optimization_barrier((diagonal, g2))
-        same_core.append(diagonal)
-        across.append(swap(diagonal, 1))
-    gathered = []
-    for pair in zip(same_core, across):
-        gathered += pair
+    *same_core, g2 = lax.optimization_barrier((*same_core, g2))
+    gathered = [same_core[0], beside]
+    for m in same_core[1:]:
+        gathered += [m, swap(m, 1)]
+    m2, e2, *gathered = lax.optimization_barrier((m2, e2, *gathered))
+    d3 = outward(m2)
 
     weight, codes = assembled(gathered, normed.shape[1], column_blocks)
     first = first_values(place, normed, weight, parts)
     arrived = inward(first)
-    m2, e2, codes, _ = lax.optimization_barrier((m2, e2, codes, first))
-    d3 = outward(m2)
+    weight, codes, _ = lax.optimization_barrier((weight, codes, first))
+    partial, second = partial_values(place, normed, weight, first.shape)
     g3 = chunk_gradient(normed, b1, e2)
-    partial, second = partial_values(place, normed, weight, first.shape)
-    arrived, d3, g2, g3, partial = lax.optimization_barrier((arrived, d3, g2, g3, partial))
-    third = hop(lambda p: p ^ 2, place, partial, arrived)
-    third, second, codes = lax.optimization_barrier((third, second, codes))
+    g3, partial, second = lax.optimization_barrier((g3, partial, second))
     keep, send = slot_terms(codes, place, normed, (m2, d3), (g1, g2, g3), capacity, column_blocks)
+    arrived, keep, send = lax.optimization_barrier((arrived, keep, send))
 
     to_middle = inward(second)
-    crossing = middle(third)
+    crossing = middle(hop(lambda p: p ^ 2, place, partial, arrived))
     other = [swap(m, 1) for m in send]
     sums = [combine(keep[chip], other[chip], jnp.int16) for chip in range(1, chips)]
     own = combine(keep[0], other[0], jnp.float32)

time: 108 us -> 109 us (level)
  local copies, waits for them, and re-layouts: 12.1 us -> 19.4 us
  Pallas kernels: 34.6 us -> 31 us
  waiting for transfers between devices: 23 us -> 20.5 us
    ppermute x13 -> x14, waiting for transfers between devices: 3.34 us -> 12 us  [swap(): return lax.ppermute(x, 'fsdp', [(i, i ^ mask) for i in range(devices)])]
    unnamed x30 -> x52, local copies, waits for them, and re-layouts: 12.1 us -> 19.4 us
    ppermute x2, waiting for transfers between devices: 10.6 us -> 5.71 us  [inward(): return lax.ppermute(x, 'tensor', [(0, 1), (3, 2)])]
    ppermute x2, waiting for transfers between devices: 4.77 us -> 1.2 us  [outward(): return lax.ppermute(x, 'tensor', [(1, 0), (2, 3)])]
    ppermute x2, waiting for transfers between devices: 4.21 us -> 1.56 us  [pairs(): return lax.ppermute(x, 'tensor', [(0, 1), (1, 0), (2, 3), (3, 2)])]
    pallas_call x1, Pallas kernels: 3.88 us -> 2.21 us  [assembled(): pl.pallas_call(functools.partial(assembly_kernel, column_blocks, features...]
    ppermute x2, starting transfers between devices: 7.06 us -> 8.4 us  [pairs(): return lax.ppermute(x, 'tensor', [(0, 1), (1, 0), (2, 3), (3, 2)])]
    ppermute x13 -> x14, starting transfers between devices: 10 us -> 9.29 us  [swap(): return lax.ppermute(x, 'fsdp', [(i, i ^ mask) for i in range(devices)])]
  transfers between devices with their start and end apart: 24 -> 24, of which waited for: 8 -> 7; matrix products, arithmetic and copies ran while one was open for 0% -> 0% of each run, Pallas kernels for 26% -> 28%
where the time goes in v10:
time: 109 us; the launch traced here: 108 us
  starting transfers between devices  34.4 us (32%)
  Pallas kernels  31 us (28%)
  waiting for transfers between devices  20.5 us (19%)
  local copies, waits for them, and re-layouts  19.4 us (18%)
  other arithmetic  1.76 us (2%)
    unnamed x52, local copies, waits for them, and re-layouts  19.4 us
    ppermute x14, waiting for transfers between devices, swap(): return lax.ppermute(x, 'fsdp', [(i, i ^ mask) for i in range(devices)])  12 us
    ppermute x2, starting transfers between devices, inward(): return lax.ppermute(x, 'tensor', [(0, 1), (3, 2)])  10.2 us
    ppermute x14, starting transfers between devices, swap(): return lax.ppermute(x, 'fsdp', [(i, i ^ mask) for i in range(devices)])  9.29 us
    ppermute x2, starting transfers between devices, pairs(): return lax.ppermute(x, 'tensor', [(0, 1), (1, 0), (2, 3), (3, 2)])  8.4 us
    pallas_call x1, Pallas kernels, grad_inputs(): pl.pallas_call(grad_input_kernel, grid_spec=pltpu.PrefetchScalarGridSpec(...  7.69 us
    ppermute x2, waiting for transfers between devices, inward(): return lax.ppermute(x, 'tensor', [(0, 1), (3, 2)])  5.71 us
    pallas_call x1, Pallas kernels, slot_terms(): pl.pallas_call(functools.partial(slots_kernel, chips, column_blocks), in_...  5.43 us
  transfers between devices with their start and end apart: 24, of which 7 were waited for; matrix products, arithmetic and copies ran while one was open for 0% of the time, Pallas kernels for 28%

profile of v10, /device:TPU:0, one launch (start us, length us, event | category | flops | bytes accessed | tf_op | source)
XLA Modules:
  0.0 108.1 jit_solution(3862120930295388817)
XLA Ops:
  1.3 1.1 fusion.1.refs_0_
  2.9 1.0 copy-done.3
  4.0 2.7 %collective-permute-start = (bf16[1056,256]{1,0:T(8,128)(2,1)S(1)}, bf16[1056,256]{1,0:T(8,128)(2,1)S(1)}, u32[]{:S(2)}, u32[]{:S(2)}) collective-permute-start(bf16[1056,256]{1,0:T(8,128)(2,1)S(1)} %get-tuple-element.59), channel_id=1, source_target_pairs={{0,1},{1,0},{2,3},{3,2},{4,5},{5,4},{6,7},{7,6},{8,9},{9,8},{10,11... | collective-permute-start | bytes 1622024 | tf_op jit(solution)/shard_map/ppermute | solution.py:464
  7.4 2.5 %collective-permute-start.7 = (bf16[2064,128]{1,0:T(8,128)(2,1)S(1)}, bf16[2064,128]{1,0:T(8,128)(2,1)S(1)}, u32[]{:S(2)}, u32[]{:S(2)}) collective-permute-start(bf16[2064,128]{1,0:T(8,128)(2,1)S(1)} %fusion.1.refs_0_), channel_id=1, source_target_pairs={{0,24},{4,28},{8,16},{12,20},{16,8},{20,12},{24,0},{28,4},{1,25},{... | collective-permute-start | bytes 1585160 | tf_op jit(solution)/shard_map/ppermute | solution.py:461
  10.4 0.8 copy-done.12
  11.7 2.2 %copy-done.2 = bf16[1024,2048]{1,0:T(8,128)(2,1)S(1)} copy-done((bf16[1024,2048]{1,0:T(8,128)(2,1)S(1)}, bf16[1024,2048]{1,0:T(8,128)(2,1)}, u32[]{:S(2)}) %copy-start.2) | copy-done | bytes 4194328
  13.9 1.0 copy-done.4
  15.0 1.7 %own_gradient.1 = (bf16[1024,2048]{1,0:T(8,128)(2,1)S(1)}, f32[256,2048]{1,0:T(8,128)S(1)}) custom-call(bf16[1024,2048]{1,0:T(8,128)(2,1)S(1)} %copy-done.2, bf16[1024,256]{1,0:T(8,128)(2,1)S(1)} %copy-done.4), custom_call_target="tpu_custom_call" | custom-call | flops 1 | bytes 1 | tf_op jit(solution)/shard_map/own_gradient/pallas_call | solution.py:272
  16.7 1.3 %copy-done.6 = f32[256,2048]{1,0:T(8,128)} copy-done((f32[256,2048]{1,0:T(8,128)}, f32[256,2048]{1,0:T(8,128)S(1)}, u32[]{:S(2)}) %copy-start.6) | copy-done | bytes 2097176
  18.0 1.6 %collective-permute-done.refs_0_.a1 = bf16[1056,256]{1,0:T(8,128)(2,1)S(1)} collective-permute-done((bf16[1056,256]{1,0:T(8,128)(2,1)S(1)}, bf16[1056,256]{1,0:T(8,128)(2,1)S(1)}, u32[]{:S(2)}, u32[]{:S(2)}) %collective-permute-start) | collective-permute-done | bytes 540704 | tf_op jit(solution)/shard_map/ppermute | solution.py:464
  19.6 1.5 %collective-permute-start.3 = (bf16[1056,256]{1,0:T(8,128)(2,1)S(1)}, bf16[1056,256]{1,0:T(8,128)(2,1)}, u32[]{:S(2)}, u32[]{:S(2)}) collective-permute-start(bf16[1056,256]{1,0:T(8,128)(2,1)S(1)} %collective-permute-done.refs_0_.a1), channel_id=1, source_target_pairs={{1,2},{2,1},{5,6},{6,5},{9,10},{10,9},{13,14},{14,13},{17,18},{18,... | collective-permute-start | bytes 1622024 | tf_op jit(solution)/shard_map/ppermute | solution.py:467
  21.1 1.3 %collective-permute-start.4 = (bf16[1040,256]{1,0:T(8,128)(2,1)S(1)}, bf16[1040,256]{1,0:T(8,128)(2,1)S(1)}, u32[]{:S(2)}, u32[]{:S(2)}) collective-permute-start(bf16[1040,256]{1,0:T(8,128)(2,1)S(1)} %collective-permute-done.1.refs_0_.b1), channel_id=1, source_target_pairs={{1,0},{2,3},{5,4},{6,7},{9,8},{10,11},{13,12},{14,15},{17,16},{18,... | collective-permute-start | bytes 1597448 | tf_op jit(solution)/shard_map/ppermute | solution.py:470
  22.4 1.3 %chunk_gradient.2.g2 = f32[256,2048]{1,0:T(8,128)S(1)} custom-call(bf16[1024,2048]{1,0:T(8,128)(2,1)S(1)} %get-tuple-element.58.normed_ref, bf16[1056,256]{1,0:T(8,128)(2,1)S(1)} %collective-permute-done.refs_0_.a1), custom_call_target="tpu_custom_call" | custom-call | flops 1 | bytes 1 | tf_op jit(solution)/shard_map/chunk_gradient/pallas_call | solution.py:288
  23.7 10.1 %collective-permute-done.6.refs_4_ = bf16[2064,128]{1,0:T(8,128)(2,1)S(1)} collective-permute-done((bf16[2064,128]{1,0:T(8,128)(2,1)S(1)}, bf16[2064,128]{1,0:T(8,128)(2,1)S(1)}, u32[]{:S(2)}, u32[]{:S(2)}) %collective-permute-start.6) | collective-permute-done | bytes 528416 | tf_op jit(solution)/shard_map/ppermute | solution.py:461
  33.9 0.8 copy-done.18
  35.2 0.8 copy-done.16
  36.0 0.8 copy-done.14
  36.9 0.8 copy-done.20
  37.7 0.8 copy-done.22
  38.5 0.8 copy-done.24
  39.3 1.2 %collective-permute-done.4.refs_1_.e2 = bf16[1040,256]{1,0:T(8,128)(2,1)S(1)} collective-permute-done((bf16[1040,256]{1,0:T(8,128)(2,1)S(1)}, bf16[1040,256]{1,0:T(8,128)(2,1)S(1)}, u32[]{:S(2)}, u32[]{:S(2)}) %collective-permute-start.4) | collective-permute-done | bytes 532512 | tf_op jit(solution)/shard_map/ppermute | solution.py:470
  40.5 0.8 copy-done.10
  41.3 1.3 %collective-permute-start.12 = (bf16[1056,256]{1,0:T(8,128)(2,1)}, bf16[1056,256]{1,0:T(8,128)(2,1)}, u32[]{:S(2)}, u32[]{:S(2)}) collective-permute-start(bf16[1056,256]{1,0:T(8,128)(2,1)} %collective-permute-done.3.m2), channel_id=1, source_target_pairs={{1,0},{2,3},{5,4},{6,7},{9,8},{10,11},{13,12},{14,15},{17,16},{18,... | collective-permute-start | bytes 1622024 | tf_op jit(solution)/shard_map/ppermute | solution.py:470
  42.6 1.0 copy-done.13
  43.6 1.0 copy-done.15
  44.7 1.0 copy-done.17
  45.7 1.0 copy-done.19
  46.8 1.0 copy-done.21
  47.8 1.0 copy-done.23
  48.9 1.0 copy-done.25
  49.9 2.2 %assembled.1 = (bf16[2176,1024]{1,0:T(8,128)(2,1)S(1)}, s32[8,128]{1,0:T(8,128)S(1)}) custom-call(bf16[2064,128]{1,0:T(8,128)(2,1)S(1)} %fusion.1.refs_0_, bf16[2064,128]{1,0:T(8,128)(2,1)S(1)} %copy-done.13, bf16[2064,128]{1,0:T(8,128)(2,1)S(1)} %copy-done.19, bf16[2064,128]{1,0:T(8,128)(2,1)S(1)} %copy-done.21, bf16[2064,128]{1,0:T(8,128)(2,1)S(1)} %copy-done.17, ...), custom_call_target="tpu_custom_call" | custom-call | bytes 8388608 | tf_op jit(solution)/shard_map/assembled/pallas_call | solution.py:96
  52.2 1.3 %first_values.1 = s16[1040,256]{1,0:T(8,128)(2,1)S(1)} custom-call(s32[1]{0:T(128)} %bitcast.place_ref, bf16[1024,2048]{1,0:T(8,128)(2,1)S(1)} %copy-done.1, bf16[2176,1024]{1,0:T(8,128)(2,1)S(1)} %get-tuple-element.80.weight_ref), custom_call_target="tpu_custom_call" | custom-call | flops 1 | bytes 1 | tf_op jit(solution)/shard_map/first_values/pallas_call | solution.py:128
  53.5 5.8 %collective-permute-start.11 = (s16[1040,256]{1,0:T(8,128)(2,1)S(1)}, s16[1040,256]{1,0:T(8,128)(2,1)S(1)}, u32[]{:S(2)}, u32[]{:S(2)}) collective-permute-start(s16[1040,256]{1,0:T(8,128)(2,1)S(1)} %first_values.1), channel_id=1, source_target_pairs={{0,1},{3,2},{4,5},{7,6},{8,9},{11,10},{12,13},{15,14},{16,17},{19,... | collective-permute-start | bytes 1597448 | tf_op jit(solution)/shard_map/ppermute | solution.py:473
  59.3 1.3 %chunk_gradient.3.g3 = f32[256,2048]{1,0:T(8,128)S(1)} custom-call(bf16[1024,2048]{1,0:T(8,128)(2,1)S(1)} %copy-done.1, bf16[1040,256]{1,0:T(8,128)(2,1)S(1)} %copy-done.9, bf16[1040,256]{1,0:T(8,128)(2,1)S(1)} %copy-done.11), custom_call_target="tpu_custom_call" | custom-call | flops 1 | bytes 1 | tf_op jit(solution)/shard_map/chunk_gradient/pallas_call | solution.py:288
  60.7 4.7 %partial_values.1 = (f32[1024,1024]{1,0:T(8,128)S(1)}, s16[1040,256]{1,0:T(8,128)(2,1)S(1)}) custom-call(s32[1]{0:T(128)} %bitcast.place_ref, bf16[1024,2048]{1,0:T(8,128)(2,1)S(1)} %copy-done.1, bf16[2176,1024]{1,0:T(8,128)(2,1)S(1)} %get-tuple-element.80.weight_ref), custom_call_target="tpu_custom_call" | custom-call | flops 1 | bytes 1 | tf_op jit(solution)/shard_map/partial_values/pallas_call | solution.py:157
  65.4 5.4 %slot_terms.1 = (f32[2048,128]{1,0:T(8,128)S(1)}, f32[2048,128]{1,0:T(8,128)S(1)}, f32[2048,128]{1,0:T(8,128)S(1)}, f32[2048,128]{1,0:T(8,128)S(1)}, s16[2096,12...) custom-call(s32[8,128]{1,0:T(8,128)S(1)} %get-tuple-element.84.codes, ...), custom_call_target="tpu_custom_call" | custom-call | flops 1 | bytes 1 | tf_op jit(solution)/shard_map/slot_terms/pallas_call | solution.py:344
  72.1 4.4 %collective-permute-start.14 = (s16[1040,256]{1,0:T(8,128)(2,1)S(1)}, s16[1040,256]{1,0:T(8,128)(2,1)S(1)}, u32[]{:S(2)}, u32[]{:S(2)}) collective-permute-start(s16[1040,256]{1,0:T(8,128)(2,1)S(1)} %get-tuple-element.98), channel_id=1, source_target_pairs={{0,1},{3,2},{4,5},{7,6},{8,9},{11,10},{12,13},{15,14},{16,17},{19,... | collective-permute-start | bytes 1597448 | tf_op jit(solution)/shard_map/ppermute | solution.py:473
  76.9 0.7 collective-permute-start.13
  78.0 1.6 %collective-permute-start.23 = (s16[2096,128]{1,0:T(8,128)(2,1)S(1)}, s16[2096,128]{1,0:T(8,128)(2,1)S(1)}, u32[]{:S(2)}, u32[]{:S(2)}) collective-permute-start(s16[2096,128]{1,0:T(8,128)(2,1)S(1)} %combine.5), channel_id=1, source_target_pairs={{0,8},{4,12},{8,0},{12,4},{16,24},{20,28},{24,16},{28,20},{1,9},{5... | collective-permute-start | bytes 1609736 | tf_op jit(solution)/shard_map/ppermute | solution.py:461
  79.9 0.8 collective-permute-start.22
  81.1 1.3 %collective-permute-start.21 = (s16[2096,128]{1,0:T(8,128)(2,1)S(1)}, s16[2096,128]{1,0:T(8,128)(2,1)S(1)}, u32[]{:S(2)}, u32[]{:S(2)}) collective-permute-start(s16[2096,128]{1,0:T(8,128)(2,1)S(1)} %combine.7), channel_id=1, source_target_pairs={{0,24},{4,28},{8,16},{12,20},{16,8},{20,12},{24,0},{28,4},{1,25},{... | collective-permute-start | bytes 1609736 | tf_op jit(solution)/shard_map/ppermute | solution.py:461
  82.6 5.5 %collective-permute-done.14.arrived_ref = s16[1040,256]{1,0:T(8,128)(2,1)S(1)} collective-permute-done((s16[1040,256]{1,0:T(8,128)(2,1)S(1)}, s16[1040,256]{1,0:T(8,128)(2,1)S(1)}, u32[]{:S(2)}, u32[]{:S(2)}) %collective-permute-start.14) | collective-permute-done | bytes 532512 | tf_op jit(solution)/shard_map/ppermute | solution.py:473
  88.4 1.0 collective-permute-start.20
  89.8 5.8 %collective-permute-start.19 = (s16[1040,256]{1,0:T(8,128)(2,1)S(1)}, s16[1040,256]{1,0:T(8,128)(2,1)S(1)}, u32[]{:S(2)}, u32[]{:S(2)}) collective-permute-start(s16[1040,256]{1,0:T(8,128)(2,1)S(1)} %hop.4), channel_id=1, source_target_pairs={{0,1},{1,0},{2,3},{3,2},{4,5},{5,4},{6,7},{7,6},{8,9},{9,8},{10,11... | collective-permute-start | bytes 1597448 | tf_op jit(solution)/shard_map/ppermute | solution.py:464
  95.5 7.7 %grad_inputs.1 = bf16[1024,2048]{1,0:T(8,128)(2,1)} custom-call(s32[1]{0:T(128)} %bitcast.place_ref, bf16[2176,1024]{1,0:T(8,128)(2,1)S(1)} %get-tuple-element.80.weight_ref, bf16[1024,256]{1,0:T(8,128)(2,1)S(1)} %copy-done.5, bf16[1056,256]{1,0:T(8,128)(2,1)S(1)} %collective-permute-done.refs_0_.a1, bf16[1040,256]{1,0:T(8,128)(2,1)S(1)} %copy-done.9, ...), custom_call_target="tpu_custom_call" | custom-call | flops 4294967296 | bytes 12582912 | tf_op jit(solution)/shard_map/grad_inputs/pallas_call | solution.py:432
  103.2 1.8 %collective-permute-done.22.refs_2_ = s16[2096,128]{1,0:T(8,128)(2,1)S(1)} collective-permute-done((s16[2096,128]{1,0:T(8,128)(2,1)S(1)}, s16[2096,128]{1,0:T(8,128)(2,1)S(1)}, u32[]{:S(2)}, u32[]{:S(2)}) %collective-permute-start.22) | collective-permute-done | bytes 536608 | tf_op jit(solution)/shard_map/ppermute | solution.py:461
  105.0 1.9 %normalized_update.1 = bf16[16,128,128]{2,1,0:T(8,128)(2,1)} custom-call(f32[2048,128]{1,0:T(8,128)S(1)} %combine.4.refs_0_, s16[2096,128]{1,0:T(8,128)(2,1)S(1)} %collective-permute-done.21.refs_1_, s16[2096,128]{1,0:T(8,128)(2,1)S(1)} %collective-permute-done.22.refs_2_, s16[2096,128]{1,0:T(8,128)(2,1)S(1)} %collective-permute-done.23.refs_3_), custom_call_target="tpu_custom_call" | custom-call | flops 1 | bytes 1 | tf_op jit(solution)/shard_map/normalized_update/pallas_call | solution.py:402
  107.0 1.1 %last_hop.1 = bf16[1024,256]{1,0:T(8,128)(2,1)} custom-call(s32[1]{0:T(128)} %bitcast.place_ref, f32[1024,1024]{1,0:T(8,128)S(1)} %get-tuple-element.83.partial_ref, s16[1040,256]{1,0:T(8,128)(2,1)S(1)} %collective-permute-done.19.right_ref, s16[1040,256]{1,0:T(8,128)(2,1)S(1)} %collective-permute-done.20.left_ref), custom_call_target="tpu_custom_call" | custom-call | flops 1 | bytes 1 | tf_op jit(solution)/shard_map/last_hop/pallas_call | solution.py:207
  (72 shorter events, 7.2 us)
Async XLA Ops:
  2.4 8.0 %collective-permute-start.2 = (bf16[2064,128]{1,0:T(8,128)(2,1)S(1)}, bf16[2064,128]{1,0:T(8,128)(2,1)S(1)}, u32[]{:S(2)}, u32[]{:S(2)}) collective-permute-start(bf16[2064,128]{1,0:T(8,128)(2,1)S(1)} %fusion.1.refs_0_), channel_id=1, source_target_pairs={{0,4},{4,0},{8,12},{12,8},{16,20},{20,16},{24,28},{28,24},{1,5},{5... | collective-permute-start | bytes 1585160 | tf_op jit(solution)/shard_map/ppermute | solution.py:461
  2.9 1.0 copy-start.3
  4.0 15.6 %collective-permute-start = (bf16[1056,256]{1,0:T(8,128)(2,1)S(1)}, bf16[1056,256]{1,0:T(8,128)(2,1)S(1)}, u32[]{:S(2)}, u32[]{:S(2)}) collective-permute-start(bf16[1056,256]{1,0:T(8,128)(2,1)S(1)} %get-tuple-element.59), channel_id=1, source_target_pairs={{0,1},{1,0},{2,3},{3,2},{4,5},{5,4},{6,7},{7,6},{8,9},{9,8},{10,11... | collective-permute-start | bytes 1622024 | tf_op jit(solution)/shard_map/ppermute | solution.py:464
  6.7 11.4 %collective-permute-start.1 = (bf16[1040,256]{1,0:T(8,128)(2,1)S(1)}, bf16[1040,256]{1,0:T(8,128)(2,1)S(1)}, u32[]{:S(2)}, u32[]{:S(2)}) collective-permute-start(bf16[1040,256]{1,0:T(8,128)(2,1)S(1)} %get-tuple-element.60), channel_id=1, source_target_pairs={{1,2},{2,1},{5,6},{6,5},{9,10},{10,9},{13,14},{14,13},{17,18},{18,... | collective-permute-start | bytes 1597448 | tf_op jit(solution)/shard_map/ppermute | solution.py:467
  7.4 16.3 %collective-permute-start.7 = (bf16[2064,128]{1,0:T(8,128)(2,1)S(1)}, bf16[2064,128]{1,0:T(8,128)(2,1)S(1)}, u32[]{:S(2)}, u32[]{:S(2)}) collective-permute-start(bf16[2064,128]{1,0:T(8,128)(2,1)S(1)} %fusion.1.refs_0_), channel_id=1, source_target_pairs={{0,24},{4,28},{8,16},{12,20},{16,8},{20,12},{24,0},{28,4},{1,25},{... | collective-permute-start | bytes 1585160 | tf_op jit(solution)/shard_map/ppermute | solution.py:461
  9.9 23.9 %collective-permute-start.6 = (bf16[2064,128]{1,0:T(8,128)(2,1)S(1)}, bf16[2064,128]{1,0:T(8,128)(2,1)S(1)}, u32[]{:S(2)}, u32[]{:S(2)}) collective-permute-start(bf16[2064,128]{1,0:T(8,128)(2,1)S(1)} %fusion.1.refs_0_), channel_id=1, source_target_pairs={{0,16},{4,20},{8,24},{12,28},{16,0},{20,4},{24,8},{28,12},{1,17},{... | collective-permute-start | bytes 1585160 | tf_op jit(solution)/shard_map/ppermute | solution.py:461
  10.4 0.8 copy-start.12
  11.2 22.7 %collective-permute-start.5 = (bf16[2064,128]{1,0:T(8,128)(2,1)S(1)}, bf16[2064,128]{1,0:T(8,128)(2,1)S(1)}, u32[]{:S(2)}, u32[]{:S(2)}) collective-permute-start(bf16[2064,128]{1,0:T(8,128)(2,1)S(1)} %fusion.1.refs_0_), channel_id=1, source_target_pairs={{0,8},{4,12},{8,0},{12,4},{16,24},{20,28},{24,16},{28,20},{1,9},{5... | collective-permute-start | bytes 1585160 | tf_op jit(solution)/shard_map/ppermute | solution.py:461
  11.7 2.2 %copy-start.2 = (bf16[1024,2048]{1,0:T(8,128)(2,1)S(1)}, bf16[1024,2048]{1,0:T(8,128)(2,1)}, u32[]{:S(2)}) copy-start(bf16[1024,2048]{1,0:T(8,128)(2,1)} %normed_ref.1) | copy-start | bytes 12582916
  13.9 1.0 copy-start.4
  16.7 1.3 %copy-start.6 = (f32[256,2048]{1,0:T(8,128)}, f32[256,2048]{1,0:T(8,128)S(1)}, u32[]{:S(2)}) copy-start(f32[256,2048]{1,0:T(8,128)S(1)} %get-tuple-element.86.g1) | copy-start | bytes 6291460
  18.0 5.6 %copy-start = (bf16[1024,2048]{1,0:T(8,128)(2,1)}, bf16[1024,2048]{1,0:T(8,128)(2,1)S(1)}, u32[]{:S(2)}) copy-start(bf16[1024,2048]{1,0:T(8,128)(2,1)S(1)} %get-tuple-element.58.normed_ref) | copy-start | bytes 12582916
  18.0 5.6 %copy-start.8 = (bf16[1040,256]{1,0:T(8,128)(2,1)}, bf16[1040,256]{1,0:T(8,128)(2,1)S(1)}, u32[]{:S(2)}) copy-start(bf16[1040,256]{1,0:T(8,128)(2,1)S(1)} %collective-permute-done.1.refs_0_.b1) | copy-start | bytes 1597444
  19.6 21.7 %collective-permute-start.3 = (bf16[1056,256]{1,0:T(8,128)(2,1)S(1)}, bf16[1056,256]{1,0:T(8,128)(2,1)}, u32[]{:S(2)}, u32[]{:S(2)}) collective-permute-start(bf16[1056,256]{1,0:T(8,128)(2,1)S(1)} %collective-permute-done.refs_0_.a1), channel_id=1, source_target_pairs={{1,2},{2,1},{5,6},{6,5},{9,10},{10,9},{13,14},{14,13},{17,18},{18,... | collective-permute-start | bytes 1622024 | tf_op jit(solution)/shard_map/ppermute | solution.py:467
  21.1 19.4 %collective-permute-start.4 = (bf16[1040,256]{1,0:T(8,128)(2,1)S(1)}, bf16[1040,256]{1,0:T(8,128)(2,1)S(1)}, u32[]{:S(2)}, u32[]{:S(2)}) collective-permute-start(bf16[1040,256]{1,0:T(8,128)(2,1)S(1)} %collective-permute-done.1.refs_0_.b1), channel_id=1, source_target_pairs={{1,0},{2,3},{5,4},{6,7},{9,8},{10,11},{13,12},{14,15},{17,16},{18,... | collective-permute-start | bytes 1597448 | tf_op jit(solution)/shard_map/ppermute | solution.py:470
  33.9 3.0 %collective-permute-start.8 = (bf16[2064,128]{1,0:T(8,128)(2,1)S(1)}, bf16[2064,128]{1,0:T(8,128)(2,1)S(1)}, u32[]{:S(2)}, u32[]{:S(2)}) collective-permute-start(bf16[2064,128]{1,0:T(8,128)(2,1)S(1)} %collective-permute-done.5.refs_2_), channel_id=1, source_target_pairs={{0,4},{4,0},{8,12},{12,8},{16,20},{20,16},{24,28},{28,24},{1,5},{5... | collective-permute-start | bytes 1585160 | tf_op jit(solution)/shard_map/ppermute | solution.py:461
  34.7 3.0 %collective-permute-start.9 = (bf16[2064,128]{1,0:T(8,128)(2,1)S(1)}, bf16[2064,128]{1,0:T(8,128)(2,1)S(1)}, u32[]{:S(2)}, u32[]{:S(2)}) collective-permute-start(bf16[2064,128]{1,0:T(8,128)(2,1)S(1)} %collective-permute-done.6.refs_4_), channel_id=1, source_target_pairs={{0,4},{4,0},{8,12},{12,8},{16,20},{20,16},{24,28},{28,24},{1,5},{5... | collective-permute-start | bytes 1585160 | tf_op jit(solution)/shard_map/ppermute | solution.py:461
  35.2 0.8 copy-start.16
  36.0 2.5 %collective-permute-start.10 = (bf16[2064,128]{1,0:T(8,128)(2,1)S(1)}, bf16[2064,128]{1,0:T(8,128)(2,1)S(1)}, u32[]{:S(2)}, u32[]{:S(2)}) collective-permute-start(bf16[2064,128]{1,0:T(8,128)(2,1)S(1)} %collective-permute-done.7.refs_6_), channel_id=1, source_target_pairs={{0,4},{4,0},{8,12},{12,8},{16,20},{20,16},{24,28},{28,24},{1,5},{5... | collective-permute-start | bytes 1585160 | tf_op jit(solution)/shard_map/ppermute | solution.py:461
  36.0 0.8 copy-start.14
  36.9 0.8 copy-start.20
  38.5 0.8 copy-start.24
  40.5 0.8 copy-start.10
  41.3 24.1 %collective-permute-start.12 = (bf16[1056,256]{1,0:T(8,128)(2,1)}, bf16[1056,256]{1,0:T(8,128)(2,1)}, u32[]{:S(2)}, u32[]{:S(2)}) collective-permute-start(bf16[1056,256]{1,0:T(8,128)(2,1)} %collective-permute-done.3.m2), channel_id=1, source_target_pairs={{1,0},{2,3},{5,4},{6,7},{9,8},{10,11},{13,12},{14,15},{17,16},{18,... | collective-permute-start | bytes 1622024 | tf_op jit(solution)/shard_map/ppermute | solution.py:470
  42.6 1.0 copy-start.13
  43.6 1.0 copy-start.15
  44.7 1.0 copy-start.17
  45.7 1.0 copy-start.19
  46.8 1.0 copy-start.21
  47.8 1.0 copy-start.23
  48.9 1.0 copy-start.25
  49.9 2.2 %copy-start.1 = (bf16[1024,2048]{1,0:T(8,128)(2,1)S(1)}, bf16[1024,2048]{1,0:T(8,128)(2,1)}, u32[]{:S(2)}) copy-start(bf16[1024,2048]{1,0:T(8,128)(2,1)} %copy-done) | copy-start | bytes 12582916
  52.1 7.2 %copy-start.9 = (bf16[1040,256]{1,0:T(8,128)(2,1)S(1)}, bf16[1040,256]{1,0:T(8,128)(2,1)}, u32[]{:S(2)}) copy-start(bf16[1040,256]{1,0:T(8,128)(2,1)} %copy-done.8) | copy-start | bytes 1597444
  52.1 7.2 %copy-start.11 = (bf16[1040,256]{1,0:T(8,128)(2,1)S(1)}, bf16[1040,256]{1,0:T(8,128)(2,1)}, u32[]{:S(2)}) copy-start(bf16[1040,256]{1,0:T(8,128)(2,1)} %copy-done.10) | copy-start | bytes 1597444
  53.5 17.6 %collective-permute-start.11 = (s16[1040,256]{1,0:T(8,128)(2,1)S(1)}, s16[1040,256]{1,0:T(8,128)(2,1)S(1)}, u32[]{:S(2)}, u32[]{:S(2)}) collective-permute-start(s16[1040,256]{1,0:T(8,128)(2,1)S(1)} %first_values.1), channel_id=1, source_target_pairs={{0,1},{3,2},{4,5},{7,6},{8,9},{11,10},{12,13},{15,14},{16,17},{19,... | collective-permute-start | bytes 1597448 | tf_op jit(solution)/shard_map/ppermute | solution.py:473
  60.7 4.7 %copy-start.7 = (f32[256,2048]{1,0:T(8,128)S(1)}, f32[256,2048]{1,0:T(8,128)}, u32[]{:S(2)}) copy-start(f32[256,2048]{1,0:T(8,128)} %copy-done.6) | copy-start | bytes 6291460
  71.1 5.8 %collective-permute-start.16 = (s16[2096,128]{1,0:T(8,128)(2,1)S(1)}, s16[2096,128]{1,0:T(8,128)(2,1)S(1)}, u32[]{:S(2)}, u32[]{:S(2)}) collective-permute-start(s16[2096,128]{1,0:T(8,128)(2,1)S(1)} %get-tuple-element.102), channel_id=1, source_target_pairs={{0,4},{4,0},{8,12},{12,8},{16,20},{20,16},{24,28},{28,24},{1,5},{5... | collective-permute-start | bytes 1609736 | tf_op jit(solution)/shard_map/ppermute | solution.py:461
  71.1 6.8 %collective-permute-start.17 = (s16[2096,128]{1,0:T(8,128)(2,1)S(1)}, s16[2096,128]{1,0:T(8,128)(2,1)S(1)}, u32[]{:S(2)}, u32[]{:S(2)}) collective-permute-start(s16[2096,128]{1,0:T(8,128)(2,1)S(1)} %get-tuple-element.104), channel_id=1, source_target_pairs={{0,4},{4,0},{8,12},{12,8},{16,20},{20,16},{24,28},{28,24},{1,5},{5... | collective-permute-start | bytes 1609736 | tf_op jit(solution)/shard_map/ppermute | solution.py:461
  71.6 8.3 %collective-permute-start.18 = (s16[2096,128]{1,0:T(8,128)(2,1)S(1)}, s16[2096,128]{1,0:T(8,128)(2,1)S(1)}, u32[]{:S(2)}, u32[]{:S(2)}) collective-permute-start(s16[2096,128]{1,0:T(8,128)(2,1)S(1)} %get-tuple-element.106), channel_id=1, source_target_pairs={{0,4},{4,0},{8,12},{12,8},{16,20},{20,16},{24,28},{28,24},{1,5},{5... | collective-permute-start | bytes 1609736 | tf_op jit(solution)/shard_map/ppermute | solution.py:461
  71.6 9.4 %collective-permute-start.15 = (s16[2096,128]{1,0:T(8,128)(2,1)S(1)}, s16[2096,128]{1,0:T(8,128)(2,1)S(1)}, u32[]{:S(2)}, u32[]{:S(2)}) collective-permute-start(s16[2096,128]{1,0:T(8,128)(2,1)S(1)} %get-tuple-element.100), channel_id=1, source_target_pairs={{0,4},{4,0},{8,12},{12,8},{16,20},{20,16},{24,28},{28,24},{1,5},{5... | collective-permute-start | bytes 1609736 | tf_op jit(solution)/shard_map/ppermute | solution.py:461
  72.1 15.9 %collective-permute-start.14 = (s16[1040,256]{1,0:T(8,128)(2,1)S(1)}, s16[1040,256]{1,0:T(8,128)(2,1)S(1)}, u32[]{:S(2)}, u32[]{:S(2)}) collective-permute-start(s16[1040,256]{1,0:T(8,128)(2,1)S(1)} %get-tuple-element.98), channel_id=1, source_target_pairs={{0,1},{3,2},{4,5},{7,6},{8,9},{11,10},{12,13},{15,14},{16,17},{19,... | collective-permute-start | bytes 1597448 | tf_op jit(solution)/shard_map/ppermute | solution.py:473
  76.9 11.1 %collective-permute-start.13 = (s16[1040,256]{1,0:T(8,128)(2,1)S(1)}, s16[1040,256]{1,0:T(8,128)(2,1)S(1)}, u32[]{:S(2)}, u32[]{:S(2)}) collective-permute-start(s16[1040,256]{1,0:T(8,128)(2,1)S(1)} %hop.3), channel_id=1, source_target_pairs={{1,2},{2,1},{5,6},{6,5},{9,10},{10,9},{13,14},{14,13},{17,18},{18,... | collective-permute-start | bytes 1597448 | tf_op jit(solution)/shard_map/ppermute | solution.py:467
  78.0 25.2 %collective-permute-start.23 = (s16[2096,128]{1,0:T(8,128)(2,1)S(1)}, s16[2096,128]{1,0:T(8,128)(2,1)S(1)}, u32[]{:S(2)}, u32[]{:S(2)}) collective-permute-start(s16[2096,128]{1,0:T(8,128)(2,1)S(1)} %combine.5), channel_id=1, source_target_pairs={{0,8},{4,12},{8,0},{12,4},{16,24},{20,28},{24,16},{28,20},{1,9},{5... | collective-permute-start | bytes 1609736 | tf_op jit(solution)/shard_map/ppermute | solution.py:461
  79.9 25.1 %collective-permute-start.22 = (s16[2096,128]{1,0:T(8,128)(2,1)S(1)}, s16[2096,128]{1,0:T(8,128)(2,1)S(1)}, u32[]{:S(2)}, u32[]{:S(2)}) collective-permute-start(s16[2096,128]{1,0:T(8,128)(2,1)S(1)} %combine.6), channel_id=1, source_target_pairs={{0,16},{4,20},{8,24},{12,28},{16,0},{20,4},{24,8},{28,12},{1,17},{... | collective-permute-start | bytes 1609736 | tf_op jit(solution)/shard_map/ppermute | solution.py:461
  81.1 23.9 %collective-permute-start.21 = (s16[2096,128]{1,0:T(8,128)(2,1)S(1)}, s16[2096,128]{1,0:T(8,128)(2,1)S(1)}, u32[]{:S(2)}, u32[]{:S(2)}) collective-permute-start(s16[2096,128]{1,0:T(8,128)(2,1)S(1)} %combine.7), channel_id=1, source_target_pairs={{0,24},{4,28},{8,16},{12,20},{16,8},{20,12},{24,0},{28,4},{1,25},{... | collective-permute-start | bytes 1609736 | tf_op jit(solution)/shard_map/ppermute | solution.py:461
  88.4 7.2 %copy-start.5 = (bf16[1024,256]{1,0:T(8,128)(2,1)S(1)}, bf16[1024,256]{1,0:T(8,128)(2,1)}, u32[]{:S(2)}) copy-start(bf16[1024,256]{1,0:T(8,128)(2,1)} %own.1) | copy-start | bytes 1572868
  88.4 18.6 %collective-permute-start.20 = (s16[1040,256]{1,0:T(8,128)(2,1)S(1)}, s16[1040,256]{1,0:T(8,128)(2,1)S(1)}, u32[]{:S(2)}, u32[]{:S(2)}) collective-permute-start(s16[1040,256]{1,0:T(8,128)(2,1)S(1)} %hop.5), channel_id=1, source_target_pairs={{1,2},{2,1},{5,6},{6,5},{9,10},{10,9},{13,14},{14,13},{17,18},{18,... | collective-permute-start | bytes 1597448 | tf_op jit(solution)/shard_map/ppermute | solution.py:467
  89.8 17.2 %collective-permute-start.19 = (s16[1040,256]{1,0:T(8,128)(2,1)S(1)}, s16[1040,256]{1,0:T(8,128)(2,1)S(1)}, u32[]{:S(2)}, u32[]{:S(2)}) collective-permute-start(s16[1040,256]{1,0:T(8,128)(2,1)S(1)} %hop.4), channel_id=1, source_target_pairs={{0,1},{1,0},{2,3},{3,2},{4,5},{5,4},{6,7},{7,6},{8,9},{9,8},{10,11... | collective-permute-start | bytes 1597448 | tf_op jit(solution)/shard_map/ppermute | solution.py:464
  (2 other events, 1.6 us)

commit v11 on v7

--- a/solution.py
+++ b/solution.py
@@ -210,19 +210,22 @@
     )
 
 
-def widen_kernel(chunk_ref, wide_ref):
+def widen_kernel(chunk_ref, *wide_refs):
     tokens = chunk_ref.shape[0]
-    wide_ref[:tokens, :] = chunk_ref[...]
-    wide_ref[tokens:, :] = jnp.zeros((PAD, chunk_ref.shape[1]), chunk_ref.dtype)
-
-
-def widen(chunk):
+    for wide_ref in wide_refs:
+        spare = wide_ref.shape[0] - tokens
+        wide_ref[:tokens, :] = chunk_ref[...]
+        wide_ref[tokens:, :] = jnp.zeros((spare, chunk_ref.shape[1]), chunk_ref.dtype)
+
+
+def widen(chunk, *spares):
+    tokens, width = chunk.shape
     return pl.pallas_call(
         widen_kernel,
         in_specs=[VMEM],
-        out_specs=VMEM,
-        out_shape=jax.ShapeDtypeStruct((chunk.shape[0] + PAD, chunk.shape[1]), chunk.dtype),
-        compiler_params=params(4),
+        out_specs=[VMEM] * len(spares),
+        out_shape=[jax.ShapeDtypeStruct((tokens + spare, width), chunk.dtype) for spare in spares],
+        compiler_params=params(5),
         cost_estimate=LITTLE,
         name="widen",
     )(chunk)
@@ -243,30 +246,6 @@
     product(joined(normed_ref.shape[0], refs[:-1]).T, normed_ref, refs[-1])
 
 
-def own_kernel(normed_ref, chunk_ref, held_ref, out_ref, sem):
-    copy = pltpu.make_async_copy(normed_ref, held_ref, sem)
-    copy.start()
-    turned = chunk_ref[...].T
-    copy.wait()
-    product(turned, held_ref, out_ref)
-
-
-def own_gradient(normed, chunk):
-    return pl.pallas_call(
-        own_kernel,
-        in_specs=[pl.BlockSpec(memory_space=pl.ANY), VMEM],
-        out_specs=[VMEM, VMEM],
-        out_shape=[
-            jax.ShapeDtypeStruct(normed.shape, normed.dtype),
-            jax.ShapeDtypeStruct((chunk.shape[1], normed.shape[1]), jnp.float32),
-        ],
-        scratch_shapes=[pltpu.SemaphoreType.DMA],
-        compiler_params=params(16),
-        cost_estimate=LITTLE,
-        name="own_gradient",
-    )(normed, chunk)
-
-
 def chunk_gradient(normed, *chunks):
     return pl.pallas_call(
         chunk_kernel,
@@ -280,18 +259,26 @@
 
 
 def slots_kernel(
-    chips, column_blocks, codes_ref, place_ref, normed_ref, m2, d3, g1, g2, g3, *refs
+    chips, column_blocks, codes_ref, place_ref, normed_ref, b1, e2, m2, d3, g1, g2, *refs
 ):
     keep_refs = refs[:chips]
     send_refs = refs[chips : 2 * chips]
-    gradient, sems = refs[2 * chips :]
+    gradient, turned, sems = refs[2 * chips :]
     place = place_ref[0]
     copies = [
-        pltpu.make_async_copy(g, gradient.at[i], sems.at[i]) for i, g in enumerate((g1, g2, g3))
+        pltpu.make_async_copy(g, gradient.at[i], sems.at[i]) for i, g in enumerate((g1, g2))
     ]
     for copy in copies:
         copy.start()
-    product(joined(normed_ref.shape[0], (m2, d3)).T, normed_ref, gradient.at[3])
+    tokens, width = normed_ref.shape[0], gradient.shape[1]
+    turned[:width, :] = joined(tokens, (b1, e2)).T
+    turned[width:, :] = joined(tokens, (m2, d3)).T
+    step = 512
+    for n in range(normed_ref.shape[1] // step):
+        span = slice(n * step, (n + 1) * step)
+        both = jnp.dot(turned[...], normed_ref[:, span], preferred_element_type=jnp.float32)
+        gradient[2, :, span] = both[:width, :]
+        gradient[3, :, span] = both[width:, :]
     for copy in copies:
         copy.wait()
     order = chunk_order(place)
@@ -331,7 +318,8 @@
         + [pl.BlockSpec(memory_space=pl.ANY)] * len(early),
         out_specs=[VMEM] * len(shapes),
         scratch_shapes=[
-            pltpu.VMEM((len(early) + 1, width, features), jnp.float32),
+            pltpu.VMEM((len(early) + 2, width, features), jnp.float32),
+            pltpu.VMEM((2 * width, normed.shape[0]), jnp.bfloat16),
             pltpu.SemaphoreType.DMA((len(early),)),
         ],
         out_shape=[jax.ShapeDtypeStruct(shape, kind) for shape, kind in shapes],
@@ -458,9 +446,9 @@
     positions = jnp.where(tile_columns >= 0, tile_rows * column_blocks + tile_columns + 1, 0)
     positions = jnp.pad(positions.astype(jnp.bfloat16), ((0, PAD - 1), (0, tile - capacity)))
     message = jnp.concatenate([tile_values.reshape(rows, tile), positions], axis=0)
-    wide = widen(cotangent)
-    a1, b1 = pairs(wide), middle(wide)
-    normed, g1 = own_gradient(normed, cotangent)
+    wider, wide = widen(cotangent, 2 * PAD, PAD)
+    a1, b1 = pairs(wider), middle(wide)
+    g1 = chunk_gradient(normed, cotangent)
     same_core = [message] + [swap(message, 2 * chip) for chip in range(1, chips)]
     beside = swap(message, 1)
     a1, b1, g1, beside = lax.optimization_barrier((a1, b1, g1, beside))
@@ -476,9 +464,9 @@
     weight, first, codes = first_values(place, normed, gathered, parts, column_blocks)
     arrived = inward(first)
     partial, second = partial_values(place, normed, weight, first.shape)
-    g3 = chunk_gradient(normed, b1, e2)
-    g3, partial, second = lax.optimization_barrier((g3, partial, second))
-    keep, send = slot_terms(codes, place, normed, (m2, d3), (g1, g2, g3), capacity, column_blocks)
+    codes, partial, second = lax.optimization_barrier((codes, partial, second))
+    late = (b1, e2, m2, d3)
+    keep, send = slot_terms(codes, place, normed, late, (g1, g2), capacity, column_blocks)
     arrived, keep, send = lax.optimization_barrier((arrived, keep, send))
 
     to_middle = inward(second)

time: 104 us -> 111 us (1.067)
  local copies, waits for them, and re-layouts: 8.62 us -> 21.5 us
  Pallas kernels: 35.4 us -> 29.9 us
  starting transfers between devices: 34.7 us -> 33.5 us
    unnamed x20 -> x56, local copies, waits for them, and re-layouts: 8.62 us -> 21.5 us
    ppermute x2, starting transfers between devices: 7.72 us -> 10.1 us  [inward(): return lax.ppermute(x, 'tensor', [(0, 1), (3, 2)])]
    pallas_call x2, Pallas kernels: 4.82 us -> 2.53 us  [chunk_gradient(): pl.pallas_call(chunk_kernel, in_specs=[VMEM] + [VMEM] * len(chunks), out_...]
    ppermute x2, starting transfers between devices: 10.5 us -> 8.36 us  [pairs(): return lax.ppermute(x, 'tensor', [(0, 1), (1, 0), (2, 3), (3, 2)])]
    pallas_call x1, Pallas kernels: 5.54 us -> 3.54 us  [first_values(): pl.pallas_call(functools.partial(first_kernel, column_blocks), in_specs=[...]
    pallas_call x2 -> x1, Pallas kernels: 1.76 us -> 0.07 us  [widen(): pl.pallas_call(widen_kernel, in_specs=[VMEM], out_specs=[VMEM] * len(spar...]
    ppermute x14, waiting for transfers between devices: 13.3 us -> 11.6 us  [swap(): return lax.ppermute(x, 'fsdp', [(i, i ^ mask) for i in range(devices)])]
    ppermute x4, starting transfers between devices: 4.55 us -> 3.11 us  [middle(): return lax.ppermute(x, 'tensor', [(1, 2), (2, 1)])]
  transfers between devices with their start and end apart: 24 -> 24, of which waited for: 8 -> 7; matrix products, arithmetic and copies ran while one was open for 0% -> 0% of each run, Pallas kernels for 33% -> 26%
where the time goes in v11:
time: 111 us; the launch traced here: 110 us
  starting transfers between devices  33.5 us (30%)
  Pallas kernels  29.9 us (27%)
  waiting for transfers between devices  22.5 us (20%)
  local copies, waits for them, and re-layouts  21.5 us (19%)
  other arithmetic  1.76 us (2%)
    unnamed x56, local copies, waits for them, and re-layouts  21.5 us
    ppermute x14, waiting for transfers between devices, swap(): return lax.ppermute(x, 'fsdp', [(i, i ^ mask) for i in range(devices)])  11.6 us
    ppermute x2, starting transfers between devices, inward(): return lax.ppermute(x, 'tensor', [(0, 1), (3, 2)])  10.1 us
    ppermute x14, starting transfers between devices, swap(): return lax.ppermute(x, 'fsdp', [(i, i ^ mask) for i in range(devices)])  9.29 us
    ppermute x2, starting transfers between devices, pairs(): return lax.ppermute(x, 'tensor', [(0, 1), (1, 0), (2, 3), (3, 2)])  8.36 us
    pallas_call x1, Pallas kernels, grad_inputs(): pl.pallas_call(grad_input_kernel, grid_spec=pltpu.PrefetchScalarGridSpec(...  7.52 us
    ppermute x2, waiting for transfers between devices, inward(): return lax.ppermute(x, 'tensor', [(0, 1), (3, 2)])  6.26 us
    pallas_call x1, Pallas kernels, slot_terms(): pl.pallas_call(functools.partial(slots_kernel, chips, column_blocks), in_...  6.23 us
  transfers between devices with their start and end apart: 24, of which 7 were waited for; matrix products, arithmetic and copies ran while one was open for 0% of the time, Pallas kernels for 26%

profile of v11, /device:TPU:0, one launch (start us, length us, event | category | flops | bytes accessed | tf_op | source)
XLA Modules:
  0.0 110.1 jit_solution(6440013313710592739)
XLA Ops:
  1.3 1.1 fusion.1.refs_0_
  2.9 1.0 copy-done.5
  4.0 2.7 %collective-permute-start = (bf16[1056,256]{1,0:T(8,128)(2,1)S(1)}, bf16[1056,256]{1,0:T(8,128)(2,1)S(1)}, u32[]{:S(2)}, u32[]{:S(2)}) collective-permute-start(bf16[1056,256]{1,0:T(8,128)(2,1)S(1)} %get-tuple-element.55), channel_id=1, source_target_pairs={{0,1},{1,0},{2,3},{3,2},{4,5},{5,4},{6,7},{7,6},{8,9},{9,8},{10,11... | collective-permute-start | bytes 1622024 | tf_op jit(solution)/shard_map/ppermute | solution.py:435
  7.4 2.5 %collective-permute-start.7 = (bf16[2064,128]{1,0:T(8,128)(2,1)S(1)}, bf16[2064,128]{1,0:T(8,128)(2,1)S(1)}, u32[]{:S(2)}, u32[]{:S(2)}) collective-permute-start(bf16[2064,128]{1,0:T(8,128)(2,1)S(1)} %fusion.1.refs_0_), channel_id=1, source_target_pairs={{0,24},{4,28},{8,16},{12,20},{16,8},{20,12},{24,0},{28,4},{1,25},{... | collective-permute-start | bytes 1585160 | tf_op jit(solution)/shard_map/ppermute | solution.py:432
  10.4 0.8 copy-done.14
  11.7 2.2 %copy-done = bf16[1024,2048]{1,0:T(8,128)(2,1)S(1)} copy-done((bf16[1024,2048]{1,0:T(8,128)(2,1)S(1)}, bf16[1024,2048]{1,0:T(8,128)(2,1)}, u32[]{:S(2)}) %copy-start) | copy-done | bytes 4194328
  13.9 1.0 copy-done.6
  15.0 1.3 %chunk_gradient.2.g1 = f32[256,2048]{1,0:T(8,128)S(1)} custom-call(bf16[1024,2048]{1,0:T(8,128)(2,1)S(1)} %copy-done, bf16[1024,256]{1,0:T(8,128)(2,1)S(1)} %copy-done.6), custom_call_target="tpu_custom_call" | custom-call | flops 1 | bytes 1 | tf_op jit(solution)/shard_map/chunk_gradient/pallas_call | solution.py:250
  16.2 3.4 %collective-permute-done.refs_0_.a1 = bf16[1056,256]{1,0:T(8,128)(2,1)S(1)} collective-permute-done((bf16[1056,256]{1,0:T(8,128)(2,1)S(1)}, bf16[1056,256]{1,0:T(8,128)(2,1)S(1)}, u32[]{:S(2)}, u32[]{:S(2)}) %collective-permute-start) | collective-permute-done | bytes 540704 | tf_op jit(solution)/shard_map/ppermute | solution.py:435
  19.6 0.7 collective-permute-start.3
  20.3 1.3 %collective-permute-start.4 = (bf16[1040,256]{1,0:T(8,128)(2,1)S(1)}, bf16[1040,256]{1,0:T(8,128)(2,1)S(1)}, u32[]{:S(2)}, u32[]{:S(2)}) collective-permute-start(bf16[1040,256]{1,0:T(8,128)(2,1)S(1)} %collective-permute-done.1.b1), channel_id=1, source_target_pairs={{1,0},{2,3},{5,4},{6,7},{9,8},{10,11},{13,12},{14,15},{17,16},{18,... | collective-permute-start | bytes 1597448 | tf_op jit(solution)/shard_map/ppermute | solution.py:441
  21.6 1.3 %chunk_gradient.3.g2 = f32[256,2048]{1,0:T(8,128)S(1)} custom-call(bf16[1024,2048]{1,0:T(8,128)(2,1)S(1)} %copy-done, bf16[1056,256]{1,0:T(8,128)(2,1)S(1)} %collective-permute-done.refs_0_.a1), custom_call_target="tpu_custom_call" | custom-call | flops 1 | bytes 1 | tf_op jit(solution)/shard_map/chunk_gradient/pallas_call | solution.py:250
  22.9 1.3 %copy-done.3 = f32[256,2048]{1,0:T(8,128)} copy-done((f32[256,2048]{1,0:T(8,128)}, f32[256,2048]{1,0:T(8,128)S(1)}, u32[]{:S(2)}) %copy-start.3) | copy-done | bytes 2097176
  24.2 9.6 %collective-permute-done.6.refs_4_ = bf16[2064,128]{1,0:T(8,128)(2,1)S(1)} collective-permute-done((bf16[2064,128]{1,0:T(8,128)(2,1)S(1)}, bf16[2064,128]{1,0:T(8,128)(2,1)S(1)}, u32[]{:S(2)}, u32[]{:S(2)}) %collective-permute-start.6) | collective-permute-done | bytes 528416 | tf_op jit(solution)/shard_map/ppermute | solution.py:432
  33.9 0.8 copy-done.20
  35.2 0.8 copy-done.18
  36.0 0.8 copy-done.16
  36.8 0.8 copy-done.22
  37.6 0.8 copy-done.24
  38.4 0.8 copy-done.26
  39.2 1.3 %collective-permute-done.4.e2 = bf16[1040,256]{1,0:T(8,128)(2,1)S(1)} collective-permute-done((bf16[1040,256]{1,0:T(8,128)(2,1)S(1)}, bf16[1040,256]{1,0:T(8,128)(2,1)S(1)}, u32[]{:S(2)}, u32[]{:S(2)}) %collective-permute-start.4) | collective-permute-done | bytes 532512 | tf_op jit(solution)/shard_map/ppermute | solution.py:441
  40.5 0.8 copy-done.12
  41.3 1.3 %collective-permute-start.12 = (bf16[1056,256]{1,0:T(8,128)(2,1)S(1)}, bf16[1056,256]{1,0:T(8,128)(2,1)}, u32[]{:S(2)}, u32[]{:S(2)}) collective-permute-start(bf16[1056,256]{1,0:T(8,128)(2,1)S(1)} %collective-permute-done.3.m2), channel_id=1, source_target_pairs={{1,0},{2,3},{5,4},{6,7},{9,8},{10,11},{13,12},{14,15},{17,16},{18,... | collective-permute-start | bytes 1622024 | tf_op jit(solution)/shard_map/ppermute | solution.py:441
  42.6 2.2 %copy-done.1 = bf16[1024,2048]{1,0:T(8,128)(2,1)S(1)} copy-done((bf16[1024,2048]{1,0:T(8,128)(2,1)S(1)}, bf16[1024,2048]{1,0:T(8,128)(2,1)}, u32[]{:S(2)}) %copy-start.1) | copy-done | bytes 4194328
  44.8 1.0 copy-done.15
  45.8 1.0 copy-done.17
  46.9 1.0 copy-done.19
  47.9 1.0 copy-done.21
  49.0 1.0 copy-done.23
  50.0 1.0 copy-done.25
  51.1 1.0 copy-done.27
  52.1 3.5 %first_values.1 = (bf16[2176,1024]{1,0:T(8,128)(2,1)S(1)}, s16[1040,256]{1,0:T(8,128)(2,1)S(1)}, s32[8,128]{1,0:T(8,128)S(1)}) custom-call(s32[1]{0:T(128)} %bitcast.place_ref, bf16[1024,2048]{1,0:T(8,128)(2,1)S(1)} %copy-done.1, bf16[2064,128]{1,0:T(8,128)(2,1)S(1)} %fusion.1.refs_0_, bf16[2064,128]{1,0:T(8,128)(2,1)S(1)} %copy-done.15, ...), custom_call_target="tpu_custom_call" | custom-call | flops 1 | bytes 1 | tf_op jit(solution)/shard_map/first_values/pallas_call | solution.py:106
  55.7 5.7 %collective-permute-start.11 = (s16[1040,256]{1,0:T(8,128)(2,1)S(1)}, s16[1040,256]{1,0:T(8,128)(2,1)S(1)}, u32[]{:S(2)}, u32[]{:S(2)}) collective-permute-start(s16[1040,256]{1,0:T(8,128)(2,1)S(1)} %get-tuple-element.77), channel_id=1, source_target_pairs={{0,1},{3,2},{4,5},{7,6},{8,9},{11,10},{12,13},{15,14},{16,17},{19,... | collective-permute-start | bytes 1597448 | tf_op jit(solution)/shard_map/ppermute | solution.py:444
  61.4 4.7 %partial_values.1 = (f32[1024,1024]{1,0:T(8,128)S(1)}, s16[1040,256]{1,0:T(8,128)(2,1)S(1)}) custom-call(s32[1]{0:T(128)} %bitcast.place_ref, bf16[1024,2048]{1,0:T(8,128)(2,1)S(1)} %copy-done.2, bf16[2176,1024]{1,0:T(8,128)(2,1)S(1)} %get-tuple-element.73.weight_ref), custom_call_target="tpu_custom_call" | custom-call | flops 1 | bytes 1 | tf_op jit(solution)/shard_map/partial_values/pallas_call | solution.py:143
  66.2 6.2 %slot_terms.1 = (f32[2048,128]{1,0:T(8,128)S(1)}, f32[2048,128]{1,0:T(8,128)S(1)}, f32[2048,128]{1,0:T(8,128)S(1)}, f32[2048,128]{1,0:T(8,128)S(1)}, s16[2096,12...) custom-call(s32[8,128]{1,0:T(8,128)S(1)} %get-tuple-element.78.codes, ...), custom_call_target="tpu_custom_call" | custom-call | flops 1 | bytes 1 | tf_op jit(solution)/shard_map/slot_terms/pallas_call | solution.py:314
  72.4 0.8 collective-permute-done.11.arrived_ref
  74.2 4.4 %collective-permute-start.14 = (s16[1040,256]{1,0:T(8,128)(2,1)S(1)}, s16[1040,256]{1,0:T(8,128)(2,1)S(1)}, u32[]{:S(2)}, u32[]{:S(2)}) collective-permute-start(s16[1040,256]{1,0:T(8,128)(2,1)S(1)} %get-tuple-element.92), channel_id=1, source_target_pairs={{0,1},{3,2},{4,5},{7,6},{8,9},{11,10},{12,13},{15,14},{16,17},{19,... | collective-permute-start | bytes 1597448 | tf_op jit(solution)/shard_map/ppermute | solution.py:444
  79.0 0.7 collective-permute-start.13
  80.1 1.6 %collective-permute-start.23 = (s16[2096,128]{1,0:T(8,128)(2,1)S(1)}, s16[2096,128]{1,0:T(8,128)(2,1)S(1)}, u32[]{:S(2)}, u32[]{:S(2)}) collective-permute-start(s16[2096,128]{1,0:T(8,128)(2,1)S(1)} %combine.5), channel_id=1, source_target_pairs={{0,8},{4,12},{8,0},{12,4},{16,24},{20,28},{24,16},{28,20},{1,9},{5... | collective-permute-start | bytes 1609736 | tf_op jit(solution)/shard_map/ppermute | solution.py:432
  82.0 0.8 collective-permute-start.22
  83.2 1.3 %collective-permute-start.21 = (s16[2096,128]{1,0:T(8,128)(2,1)S(1)}, s16[2096,128]{1,0:T(8,128)(2,1)S(1)}, u32[]{:S(2)}, u32[]{:S(2)}) collective-permute-start(s16[2096,128]{1,0:T(8,128)(2,1)S(1)} %combine.7), channel_id=1, source_target_pairs={{0,24},{4,28},{8,16},{12,20},{16,8},{20,12},{24,0},{28,4},{1,25},{... | collective-permute-start | bytes 1609736 | tf_op jit(solution)/shard_map/ppermute | solution.py:432
  84.7 5.5 %collective-permute-done.14.arrived_ref = s16[1040,256]{1,0:T(8,128)(2,1)S(1)} collective-permute-done((s16[1040,256]{1,0:T(8,128)(2,1)S(1)}, s16[1040,256]{1,0:T(8,128)(2,1)S(1)}, u32[]{:S(2)}, u32[]{:S(2)}) %collective-permute-start.14) | collective-permute-done | bytes 532512 | tf_op jit(solution)/shard_map/ppermute | solution.py:444
  90.5 1.0 collective-permute-start.20
  91.9 5.7 %collective-permute-start.19 = (s16[1040,256]{1,0:T(8,128)(2,1)S(1)}, s16[1040,256]{1,0:T(8,128)(2,1)S(1)}, u32[]{:S(2)}, u32[]{:S(2)}) collective-permute-start(s16[1040,256]{1,0:T(8,128)(2,1)S(1)} %hop.4), channel_id=1, source_target_pairs={{0,1},{1,0},{2,3},{3,2},{4,5},{5,4},{6,7},{7,6},{8,9},{9,8},{10,11... | collective-permute-start | bytes 1597448 | tf_op jit(solution)/shard_map/ppermute | solution.py:435
  97.6 7.5 %grad_inputs.1 = bf16[1024,2048]{1,0:T(8,128)(2,1)} custom-call(s32[1]{0:T(128)} %bitcast.place_ref, bf16[2176,1024]{1,0:T(8,128)(2,1)S(1)} %get-tuple-element.73.weight_ref, bf16[1024,256]{1,0:T(8,128)(2,1)S(1)} %copy-done.7, bf16[1056,256]{1,0:T(8,128)(2,1)S(1)} %copy-done.9, bf16[1040,256]{1,0:T(8,128)(2,1)S(1)} %copy-done.11, ...), custom_call_target="tpu_custom_call" | custom-call | flops 4294967296 | bytes 12582912 | tf_op jit(solution)/shard_map/grad_inputs/pallas_call | solution.py:403
  105.1 2.0 %collective-permute-done.22.refs_2_ = s16[2096,128]{1,0:T(8,128)(2,1)S(1)} collective-permute-done((s16[2096,128]{1,0:T(8,128)(2,1)S(1)}, s16[2096,128]{1,0:T(8,128)(2,1)S(1)}, u32[]{:S(2)}, u32[]{:S(2)}) %collective-permute-start.22) | collective-permute-done | bytes 536608 | tf_op jit(solution)/shard_map/ppermute | solution.py:432
  107.1 1.9 %normalized_update.1 = bf16[16,128,128]{2,1,0:T(8,128)(2,1)} custom-call(f32[2048,128]{1,0:T(8,128)S(1)} %combine.4.refs_0_, s16[2096,128]{1,0:T(8,128)(2,1)S(1)} %collective-permute-done.21.refs_1_, s16[2096,128]{1,0:T(8,128)(2,1)S(1)} %collective-permute-done.22.refs_2_, s16[2096,128]{1,0:T(8,128)(2,1)S(1)} %collective-permute-done.23.refs_3_), custom_call_target="tpu_custom_call" | custom-call | flops 1 | bytes 1 | tf_op jit(solution)/shard_map/normalized_update/pallas_call | solution.py:373
  109.0 1.1 last_hop.1
  (74 shorter events, 7.0 us)
Async XLA Ops:
  2.4 8.0 %collective-permute-start.2 = (bf16[2064,128]{1,0:T(8,128)(2,1)S(1)}, bf16[2064,128]{1,0:T(8,128)(2,1)S(1)}, u32[]{:S(2)}, u32[]{:S(2)}) collective-permute-start(bf16[2064,128]{1,0:T(8,128)(2,1)S(1)} %fusion.1.refs_0_), channel_id=1, source_target_pairs={{0,4},{4,0},{8,12},{12,8},{16,20},{20,16},{24,28},{28,24},{1,5},{5... | collective-permute-start | bytes 1585160 | tf_op jit(solution)/shard_map/ppermute | solution.py:432
  2.9 1.0 copy-start.5
  4.0 15.6 %collective-permute-start = (bf16[1056,256]{1,0:T(8,128)(2,1)S(1)}, bf16[1056,256]{1,0:T(8,128)(2,1)S(1)}, u32[]{:S(2)}, u32[]{:S(2)}) collective-permute-start(bf16[1056,256]{1,0:T(8,128)(2,1)S(1)} %get-tuple-element.55), channel_id=1, source_target_pairs={{0,1},{1,0},{2,3},{3,2},{4,5},{5,4},{6,7},{7,6},{8,9},{9,8},{10,11... | collective-permute-start | bytes 1622024 | tf_op jit(solution)/shard_map/ppermute | solution.py:435
  6.7 9.5 %collective-permute-start.1 = (bf16[1040,256]{1,0:T(8,128)(2,1)S(1)}, bf16[1040,256]{1,0:T(8,128)(2,1)S(1)}, u32[]{:S(2)}, u32[]{:S(2)}) collective-permute-start(bf16[1040,256]{1,0:T(8,128)(2,1)S(1)} %get-tuple-element.56), channel_id=1, source_target_pairs={{1,2},{2,1},{5,6},{6,5},{9,10},{10,9},{13,14},{14,13},{17,18},{18,... | collective-permute-start | bytes 1597448 | tf_op jit(solution)/shard_map/ppermute | solution.py:438
  7.4 16.9 %collective-permute-start.7 = (bf16[2064,128]{1,0:T(8,128)(2,1)S(1)}, bf16[2064,128]{1,0:T(8,128)(2,1)S(1)}, u32[]{:S(2)}, u32[]{:S(2)}) collective-permute-start(bf16[2064,128]{1,0:T(8,128)(2,1)S(1)} %fusion.1.refs_0_), channel_id=1, source_target_pairs={{0,24},{4,28},{8,16},{12,20},{16,8},{20,12},{24,0},{28,4},{1,25},{... | collective-permute-start | bytes 1585160 | tf_op jit(solution)/shard_map/ppermute | solution.py:432
  9.9 23.9 %collective-permute-start.6 = (bf16[2064,128]{1,0:T(8,128)(2,1)S(1)}, bf16[2064,128]{1,0:T(8,128)(2,1)S(1)}, u32[]{:S(2)}, u32[]{:S(2)}) collective-permute-start(bf16[2064,128]{1,0:T(8,128)(2,1)S(1)} %fusion.1.refs_0_), channel_id=1, source_target_pairs={{0,16},{4,20},{8,24},{12,28},{16,0},{20,4},{24,8},{28,12},{1,17},{... | collective-permute-start | bytes 1585160 | tf_op jit(solution)/shard_map/ppermute | solution.py:432
  11.2 22.7 %collective-permute-start.5 = (bf16[2064,128]{1,0:T(8,128)(2,1)S(1)}, bf16[2064,128]{1,0:T(8,128)(2,1)S(1)}, u32[]{:S(2)}, u32[]{:S(2)}) collective-permute-start(bf16[2064,128]{1,0:T(8,128)(2,1)S(1)} %fusion.1.refs_0_), channel_id=1, source_target_pairs={{0,8},{4,12},{8,0},{12,4},{16,24},{20,28},{24,16},{28,20},{1,9},{5... | collective-permute-start | bytes 1585160 | tf_op jit(solution)/shard_map/ppermute | solution.py:432
  11.7 2.2 %copy-start = (bf16[1024,2048]{1,0:T(8,128)(2,1)S(1)}, bf16[1024,2048]{1,0:T(8,128)(2,1)}, u32[]{:S(2)}) copy-start(bf16[1024,2048]{1,0:T(8,128)(2,1)} %normed_ref.9) | copy-start | bytes 12582916
  13.9 1.0 copy-start.6
  16.2 6.7 %copy-start.10 = (bf16[1040,256]{1,0:T(8,128)(2,1)}, bf16[1040,256]{1,0:T(8,128)(2,1)S(1)}, u32[]{:S(2)}) copy-start(bf16[1040,256]{1,0:T(8,128)(2,1)S(1)} %collective-permute-done.1.b1) | copy-start | bytes 1597444
  19.6 3.3 %copy-start.8 = (bf16[1056,256]{1,0:T(8,128)(2,1)}, bf16[1056,256]{1,0:T(8,128)(2,1)S(1)}, u32[]{:S(2)}) copy-start(bf16[1056,256]{1,0:T(8,128)(2,1)S(1)} %collective-permute-done.refs_0_.a1) | copy-start | bytes 1622020
  19.6 21.7 %collective-permute-start.3 = (bf16[1056,256]{1,0:T(8,128)(2,1)S(1)}, bf16[1056,256]{1,0:T(8,128)(2,1)S(1)}, u32[]{:S(2)}, u32[]{:S(2)}) collective-permute-start(bf16[1056,256]{1,0:T(8,128)(2,1)S(1)} %collective-permute-done.refs_0_.a1), channel_id=1, source_target_pairs={{1,2},{2,1},{5,6},{6,5},{9,10},{10,9},{13,14},{14,13},{17,18},{18,... | collective-permute-start | bytes 1622024 | tf_op jit(solution)/shard_map/ppermute | solution.py:438
  20.3 20.2 %collective-permute-start.4 = (bf16[1040,256]{1,0:T(8,128)(2,1)S(1)}, bf16[1040,256]{1,0:T(8,128)(2,1)S(1)}, u32[]{:S(2)}, u32[]{:S(2)}) collective-permute-start(bf16[1040,256]{1,0:T(8,128)(2,1)S(1)} %collective-permute-done.1.b1), channel_id=1, source_target_pairs={{1,0},{2,3},{5,4},{6,7},{9,8},{10,11},{13,12},{14,15},{17,16},{18,... | collective-permute-start | bytes 1597448 | tf_op jit(solution)/shard_map/ppermute | solution.py:441
  22.9 1.3 %copy-start.3 = (f32[256,2048]{1,0:T(8,128)}, f32[256,2048]{1,0:T(8,128)S(1)}, u32[]{:S(2)}) copy-start(f32[256,2048]{1,0:T(8,128)S(1)} %chunk_gradient.3.g2) | copy-start | bytes 6291460
  33.9 2.9 %collective-permute-start.8 = (bf16[2064,128]{1,0:T(8,128)(2,1)S(1)}, bf16[2064,128]{1,0:T(8,128)(2,1)S(1)}, u32[]{:S(2)}, u32[]{:S(2)}) collective-permute-start(bf16[2064,128]{1,0:T(8,128)(2,1)S(1)} %collective-permute-done.5.refs_2_), channel_id=1, source_target_pairs={{0,4},{4,0},{8,12},{12,8},{16,20},{20,16},{24,28},{28,24},{1,5},{5... | collective-permute-start | bytes 1585160 | tf_op jit(solution)/shard_map/ppermute | solution.py:432
  33.9 0.8 copy-start.20
  34.7 2.9 %collective-permute-start.9 = (bf16[2064,128]{1,0:T(8,128)(2,1)S(1)}, bf16[2064,128]{1,0:T(8,128)(2,1)S(1)}, u32[]{:S(2)}, u32[]{:S(2)}) collective-permute-start(bf16[2064,128]{1,0:T(8,128)(2,1)S(1)} %collective-permute-done.6.refs_4_), channel_id=1, source_target_pairs={{0,4},{4,0},{8,12},{12,8},{16,20},{20,16},{24,28},{28,24},{1,5},{5... | collective-permute-start | bytes 1585160 | tf_op jit(solution)/shard_map/ppermute | solution.py:432
  35.2 0.8 copy-start.18
  36.0 2.4 %collective-permute-start.10 = (bf16[2064,128]{1,0:T(8,128)(2,1)S(1)}, bf16[2064,128]{1,0:T(8,128)(2,1)S(1)}, u32[]{:S(2)}, u32[]{:S(2)}) collective-permute-start(bf16[2064,128]{1,0:T(8,128)(2,1)S(1)} %collective-permute-done.7.refs_6_), channel_id=1, source_target_pairs={{0,4},{4,0},{8,12},{12,8},{16,20},{20,16},{24,28},{28,24},{1,5},{5... | collective-permute-start | bytes 1585160 | tf_op jit(solution)/shard_map/ppermute | solution.py:432
  37.6 0.8 copy-start.24
  38.4 0.8 copy-start.26
  41.3 24.8 %collective-permute-start.12 = (bf16[1056,256]{1,0:T(8,128)(2,1)S(1)}, bf16[1056,256]{1,0:T(8,128)(2,1)}, u32[]{:S(2)}, u32[]{:S(2)}) collective-permute-start(bf16[1056,256]{1,0:T(8,128)(2,1)S(1)} %collective-permute-done.3.m2), channel_id=1, source_target_pairs={{1,0},{2,3},{5,4},{6,7},{9,8},{10,11},{13,12},{14,15},{17,16},{18,... | collective-permute-start | bytes 1622024 | tf_op jit(solution)/shard_map/ppermute | solution.py:441
  42.6 2.2 %copy-start.1 = (bf16[1024,2048]{1,0:T(8,128)(2,1)S(1)}, bf16[1024,2048]{1,0:T(8,128)(2,1)}, u32[]{:S(2)}) copy-start(bf16[1024,2048]{1,0:T(8,128)(2,1)} %normed_ref.9) | copy-start | bytes 12582916
  44.8 1.0 copy-start.15
  45.8 1.0 copy-start.17
  46.9 1.0 copy-start.19
  47.9 1.0 copy-start.21
  49.0 1.0 copy-start.23
  50.0 1.0 copy-start.25
  51.1 1.0 copy-start.27
  52.1 9.3 %copy-start.2 = (bf16[1024,2048]{1,0:T(8,128)(2,1)S(1)}, bf16[1024,2048]{1,0:T(8,128)(2,1)}, u32[]{:S(2)}) copy-start(bf16[1024,2048]{1,0:T(8,128)(2,1)} %normed_ref.9) | copy-start | bytes 12582916
  55.7 17.6 %collective-permute-start.11 = (s16[1040,256]{1,0:T(8,128)(2,1)S(1)}, s16[1040,256]{1,0:T(8,128)(2,1)S(1)}, u32[]{:S(2)}, u32[]{:S(2)}) collective-permute-start(s16[1040,256]{1,0:T(8,128)(2,1)S(1)} %get-tuple-element.77), channel_id=1, source_target_pairs={{0,1},{3,2},{4,5},{7,6},{8,9},{11,10},{12,13},{15,14},{16,17},{19,... | collective-permute-start | bytes 1597448 | tf_op jit(solution)/shard_map/ppermute | solution.py:444
  61.4 4.7 %copy-start.4 = (f32[256,2048]{1,0:T(8,128)S(1)}, f32[256,2048]{1,0:T(8,128)}, u32[]{:S(2)}) copy-start(f32[256,2048]{1,0:T(8,128)} %copy-done.3) | copy-start | bytes 6291460
  61.4 4.7 %copy-start.11 = (bf16[1040,256]{1,0:T(8,128)(2,1)S(1)}, bf16[1040,256]{1,0:T(8,128)(2,1)}, u32[]{:S(2)}) copy-start(bf16[1040,256]{1,0:T(8,128)(2,1)} %copy-done.10) | copy-start | bytes 1597444
  61.4 4.7 %copy-start.13 = (bf16[1040,256]{1,0:T(8,128)(2,1)S(1)}, bf16[1040,256]{1,0:T(8,128)(2,1)}, u32[]{:S(2)}) copy-start(bf16[1040,256]{1,0:T(8,128)(2,1)} %copy-done.12) | copy-start | bytes 1597444
  73.2 5.8 %collective-permute-start.16 = (s16[2096,128]{1,0:T(8,128)(2,1)S(1)}, s16[2096,128]{1,0:T(8,128)(2,1)S(1)}, u32[]{:S(2)}, u32[]{:S(2)}) collective-permute-start(s16[2096,128]{1,0:T(8,128)(2,1)S(1)} %get-tuple-element.96), channel_id=1, source_target_pairs={{0,4},{4,0},{8,12},{12,8},{16,20},{20,16},{24,28},{28,24},{1,5},{5... | collective-permute-start | bytes 1609736 | tf_op jit(solution)/shard_map/ppermute | solution.py:432
  73.2 6.8 %collective-permute-start.17 = (s16[2096,128]{1,0:T(8,128)(2,1)S(1)}, s16[2096,128]{1,0:T(8,128)(2,1)S(1)}, u32[]{:S(2)}, u32[]{:S(2)}) collective-permute-start(s16[2096,128]{1,0:T(8,128)(2,1)S(1)} %get-tuple-element.98), channel_id=1, source_target_pairs={{0,4},{4,0},{8,12},{12,8},{16,20},{20,16},{24,28},{28,24},{1,5},{5... | collective-permute-start | bytes 1609736 | tf_op jit(solution)/shard_map/ppermute | solution.py:432
  73.7 8.3 %collective-permute-start.18 = (s16[2096,128]{1,0:T(8,128)(2,1)S(1)}, s16[2096,128]{1,0:T(8,128)(2,1)S(1)}, u32[]{:S(2)}, u32[]{:S(2)}) collective-permute-start(s16[2096,128]{1,0:T(8,128)(2,1)S(1)} %get-tuple-element.100), channel_id=1, source_target_pairs={{0,4},{4,0},{8,12},{12,8},{16,20},{20,16},{24,28},{28,24},{1,5},{5... | collective-permute-start | bytes 1609736 | tf_op jit(solution)/shard_map/ppermute | solution.py:432
  73.7 9.4 %collective-permute-start.15 = (s16[2096,128]{1,0:T(8,128)(2,1)S(1)}, s16[2096,128]{1,0:T(8,128)(2,1)S(1)}, u32[]{:S(2)}, u32[]{:S(2)}) collective-permute-start(s16[2096,128]{1,0:T(8,128)(2,1)S(1)} %get-tuple-element.94), channel_id=1, source_target_pairs={{0,4},{4,0},{8,12},{12,8},{16,20},{20,16},{24,28},{28,24},{1,5},{5... | collective-permute-start | bytes 1609736 | tf_op jit(solution)/shard_map/ppermute | solution.py:432
  74.2 15.9 %collective-permute-start.14 = (s16[1040,256]{1,0:T(8,128)(2,1)S(1)}, s16[1040,256]{1,0:T(8,128)(2,1)S(1)}, u32[]{:S(2)}, u32[]{:S(2)}) collective-permute-start(s16[1040,256]{1,0:T(8,128)(2,1)S(1)} %get-tuple-element.92), channel_id=1, source_target_pairs={{0,1},{3,2},{4,5},{7,6},{8,9},{11,10},{12,13},{15,14},{16,17},{19,... | collective-permute-start | bytes 1597448 | tf_op jit(solution)/shard_map/ppermute | solution.py:444
  79.0 11.1 %collective-permute-start.13 = (s16[1040,256]{1,0:T(8,128)(2,1)S(1)}, s16[1040,256]{1,0:T(8,128)(2,1)S(1)}, u32[]{:S(2)}, u32[]{:S(2)}) collective-permute-start(s16[1040,256]{1,0:T(8,128)(2,1)S(1)} %hop.3), channel_id=1, source_target_pairs={{1,2},{2,1},{5,6},{6,5},{9,10},{10,9},{13,14},{14,13},{17,18},{18,... | collective-permute-start | bytes 1597448 | tf_op jit(solution)/shard_map/ppermute | solution.py:438
  80.1 25.1 %collective-permute-start.23 = (s16[2096,128]{1,0:T(8,128)(2,1)S(1)}, s16[2096,128]{1,0:T(8,128)(2,1)S(1)}, u32[]{:S(2)}, u32[]{:S(2)}) collective-permute-start(s16[2096,128]{1,0:T(8,128)(2,1)S(1)} %combine.5), channel_id=1, source_target_pairs={{0,8},{4,12},{8,0},{12,4},{16,24},{20,28},{24,16},{28,20},{1,9},{5... | collective-permute-start | bytes 1609736 | tf_op jit(solution)/shard_map/ppermute | solution.py:432
  82.0 25.1 %collective-permute-start.22 = (s16[2096,128]{1,0:T(8,128)(2,1)S(1)}, s16[2096,128]{1,0:T(8,128)(2,1)S(1)}, u32[]{:S(2)}, u32[]{:S(2)}) collective-permute-start(s16[2096,128]{1,0:T(8,128)(2,1)S(1)} %combine.6), channel_id=1, source_target_pairs={{0,16},{4,20},{8,24},{12,28},{16,0},{20,4},{24,8},{28,12},{1,17},{... | collective-permute-start | bytes 1609736 | tf_op jit(solution)/shard_map/ppermute | solution.py:432
  83.2 23.9 %collective-permute-start.21 = (s16[2096,128]{1,0:T(8,128)(2,1)S(1)}, s16[2096,128]{1,0:T(8,128)(2,1)S(1)}, u32[]{:S(2)}, u32[]{:S(2)}) collective-permute-start(s16[2096,128]{1,0:T(8,128)(2,1)S(1)} %combine.7), channel_id=1, source_target_pairs={{0,24},{4,28},{8,16},{12,20},{16,8},{20,12},{24,0},{28,4},{1,25},{... | collective-permute-start | bytes 1609736 | tf_op jit(solution)/shard_map/ppermute | solution.py:432
  90.5 7.1 %copy-start.7 = (bf16[1024,256]{1,0:T(8,128)(2,1)S(1)}, bf16[1024,256]{1,0:T(8,128)(2,1)}, u32[]{:S(2)}) copy-start(bf16[1024,256]{1,0:T(8,128)(2,1)} %own.1) | copy-start | bytes 1572868
  90.5 7.1 %copy-start.9 = (bf16[1056,256]{1,0:T(8,128)(2,1)S(1)}, bf16[1056,256]{1,0:T(8,128)(2,1)}, u32[]{:S(2)}) copy-start(bf16[1056,256]{1,0:T(8,128)(2,1)} %copy-done.8) | copy-start | bytes 1622020
  90.5 18.5 %collective-permute-start.20 = (s16[1040,256]{1,0:T(8,128)(2,1)S(1)}, s16[1040,256]{1,0:T(8,128)(2,1)S(1)}, u32[]{:S(2)}, u32[]{:S(2)}) collective-permute-start(s16[1040,256]{1,0:T(8,128)(2,1)S(1)} %hop.5), channel_id=1, source_target_pairs={{1,2},{2,1},{5,6},{6,5},{9,10},{10,9},{13,14},{14,13},{17,18},{18,... | collective-permute-start | bytes 1597448 | tf_op jit(solution)/shard_map/ppermute | solution.py:438
  91.9 17.1 %collective-permute-start.19 = (s16[1040,256]{1,0:T(8,128)(2,1)S(1)}, s16[1040,256]{1,0:T(8,128)(2,1)S(1)}, u32[]{:S(2)}, u32[]{:S(2)}) collective-permute-start(s16[1040,256]{1,0:T(8,128)(2,1)S(1)} %hop.4), channel_id=1, source_target_pairs={{0,1},{1,0},{2,3},{3,2},{4,5},{5,4},{6,7},{7,6},{8,9},{9,8},{10,11... | collective-permute-start | bytes 1597448 | tf_op jit(solution)/shard_map/ppermute | solution.py:435
  (4 other events, 3.2 us)

commit v12 on v10

--- a/solution.py
+++ b/solution.py
@@ -106,7 +106,7 @@
             pltpu.SemaphoreType.DMA,
         ],
         compiler_params=params(12),
-        cost_estimate=pl.CostEstimate(flops=0, bytes_accessed=8 * MIB, transcendentals=0),
+        cost_estimate=LITTLE,
         name="assembled",
     )(*messages)
 
@@ -487,10 +487,10 @@
     gathered = [same_core[0], beside]
     for m in same_core[1:]:
         gathered += [m, swap(m, 1)]
-    m2, e2, *gathered = lax.optimization_barrier((m2, e2, *gathered))
+
+    weight, codes = assembled(gathered, normed.shape[1], column_blocks)
+    m2, e2, weight, codes = lax.optimization_barrier((m2, e2, weight, codes))
     d3 = outward(m2)
-
-    weight, codes = assembled(gathered, normed.shape[1], column_blocks)
     first = first_values(place, normed, weight, parts)
     arrived = inward(first)
     weight, codes, _ = lax.optimization_barrier((weight, codes, first))

time: 109 us -> 106 us (0.972)
  local copies, waits for them, and re-layouts: 19.4 us -> 13 us
  waiting for transfers between devices: 20.5 us -> 23.7 us
    unnamed x52 -> x34, local copies, waits for them, and re-layouts: 19.4 us -> 13 us
    ppermute x14, waiting for transfers between devices: 12 us -> 15.9 us  [swap(): return lax.ppermute(x, 'fsdp', [(i, i ^ mask) for i in range(devices)])]
    ppermute x2, starting transfers between devices: 10.2 us -> 11.5 us  [inward(): return lax.ppermute(x, 'tensor', [(0, 1), (3, 2)])]
    ppermute x2, waiting for transfers between devices: 1.2 us -> 0.01 us  [outward(): return lax.ppermute(x, 'tensor', [(1, 0), (2, 3)])]
  transfers between devices with their start and end apart: 24 -> 24, of which waited for: 7 -> 10; matrix products, arithmetic and copies ran while one was open for 0% -> 0% of each run, Pallas kernels for 28% -> 28%
where the time goes in v12:
time: 106 us; the launch traced here: 105 us
  starting transfers between devices  34.9 us (33%)
  Pallas kernels  30.7 us (29%)
  waiting for transfers between devices  23.7 us (22%)
  local copies, waits for them, and re-layouts  13 us (12%)
  other arithmetic  1.76 us (2%)
    ppermute x14, waiting for transfers between devices, swap(): return lax.ppermute(x, 'fsdp', [(i, i ^ mask) for i in range(devices)])  15.9 us
    unnamed x34, local copies, waits for them, and re-layouts  13 us
    ppermute x2, starting transfers between devices, inward(): return lax.ppermute(x, 'tensor', [(0, 1), (3, 2)])  11.5 us
    ppermute x14, starting transfers between devices, swap(): return lax.ppermute(x, 'fsdp', [(i, i ^ mask) for i in range(devices)])  9.3 us
    ppermute x2, starting transfers between devices, pairs(): return lax.ppermute(x, 'tensor', [(0, 1), (1, 0), (2, 3), (3, 2)])  8.37 us
    pallas_call x1, Pallas kernels, grad_inputs(): pl.pallas_call(grad_input_kernel, grid_spec=pltpu.PrefetchScalarGridSpec(...  7.56 us
    ppermute x2, waiting for transfers between devices, inward(): return lax.ppermute(x, 'tensor', [(0, 1), (3, 2)])  5.51 us
    pallas_call x1, Pallas kernels, slot_terms(): pl.pallas_call(functools.partial(slots_kernel, chips, column_blocks), in_...  5.27 us
  transfers between devices with their start and end apart: 24, of which 10 were waited for; matrix products, arithmetic and copies ran while one was open for 0% of the time, Pallas kernels for 28%

profile of v12, /device:TPU:0, one launch (start us, length us, event | category | flops | bytes accessed | tf_op | source)
XLA Modules:
  0.0 105.1 jit_solution(3119870728402463333)
XLA Ops:
  0.6 0.7 fusion.2
  1.3 1.1 %fusion.1.refs_0_ = bf16[2064,128]{1,0:T(8,128)(2,1)S(1)} fusion(bf16[1,16]{1,0:T(2,128)(2,1)S(1)} %fusion.2, bf16[2048,128]{1,0:T(8,128)(2,1)} %bitcast.6), kind=kLoop, calls=%fused_computation.2 | loop fusion | flops 1585152 | bytes 1052704 | tf_op jit(solution)/shard_map/concatenate | solution.py:477
  2.4 0.5 collective-permute-start.2
  2.9 1.0 copy-done.6
  4.0 2.7 %collective-permute-start = (bf16[1056,256]{1,0:T(8,128)(2,1)S(1)}, bf16[1056,256]{1,0:T(8,128)(2,1)S(1)}, u32[]{:S(2)}, u32[]{:S(2)}) collective-permute-start(bf16[1056,256]{1,0:T(8,128)(2,1)S(1)} %get-tuple-element.53), channel_id=1, source_target_pairs={{0,1},{1,0},{2,3},{3,2},{4,5},{5,4},{6,7},{7,6},{8,9},{9,8},{10,11... | collective-permute-start | bytes 1622024 | tf_op jit(solution)/shard_map/ppermute | solution.py:464
  6.7 0.7 collective-permute-start.1
  7.4 2.5 %collective-permute-start.7 = (bf16[2064,128]{1,0:T(8,128)(2,1)S(1)}, bf16[2064,128]{1,0:T(8,128)(2,1)S(1)}, u32[]{:S(2)}, u32[]{:S(2)}) collective-permute-start(bf16[2064,128]{1,0:T(8,128)(2,1)S(1)} %fusion.1.refs_0_), channel_id=1, source_target_pairs={{0,24},{4,28},{8,16},{12,20},{16,8},{20,12},{24,0},{28,4},{1,25},{... | collective-permute-start | bytes 1585160 | tf_op jit(solution)/shard_map/ppermute | solution.py:461
  9.9 0.5 collective-permute-start.6
  10.4 0.5 collective-permute-start.5
  10.9 2.2 %copy-done.5 = bf16[1024,2048]{1,0:T(8,128)(2,1)S(1)} copy-done((bf16[1024,2048]{1,0:T(8,128)(2,1)S(1)}, bf16[1024,2048]{1,0:T(8,128)(2,1)}, u32[]{:S(2)}) %copy-start.5) | copy-done | bytes 4194328
  13.1 1.0 copy-done.7
  14.2 1.7 %own_gradient.1 = (bf16[1024,2048]{1,0:T(8,128)(2,1)S(1)}, f32[256,2048]{1,0:T(8,128)S(1)}) custom-call(bf16[1024,2048]{1,0:T(8,128)(2,1)S(1)} %copy-done.5, bf16[1024,256]{1,0:T(8,128)(2,1)S(1)} %copy-done.7), custom_call_target="tpu_custom_call" | custom-call | flops 1 | bytes 1 | tf_op jit(solution)/shard_map/own_gradient/pallas_call | solution.py:272
  15.9 1.4 %copy-done.9 = f32[256,2048]{1,0:T(8,128)} copy-done((f32[256,2048]{1,0:T(8,128)}, f32[256,2048]{1,0:T(8,128)S(1)}, u32[]{:S(2)}) %copy-start.9) | copy-done | bytes 2097176
  17.3 2.3 %collective-permute-done.refs_0_.a1 = bf16[1056,256]{1,0:T(8,128)(2,1)S(1)} collective-permute-done((bf16[1056,256]{1,0:T(8,128)(2,1)S(1)}, bf16[1056,256]{1,0:T(8,128)(2,1)S(1)}, u32[]{:S(2)}, u32[]{:S(2)}) %collective-permute-start) | collective-permute-done | bytes 540704 | tf_op jit(solution)/shard_map/ppermute | solution.py:464
  19.6 0.7 collective-permute-start.3
  20.3 1.3 %collective-permute-start.4 = (bf16[1040,256]{1,0:T(8,128)(2,1)S(1)}, bf16[1040,256]{1,0:T(8,128)(2,1)S(1)}, u32[]{:S(2)}, u32[]{:S(2)}) collective-permute-start(bf16[1040,256]{1,0:T(8,128)(2,1)S(1)} %collective-permute-done.1.refs_0_.b1), channel_id=1, source_target_pairs={{1,0},{2,3},{5,4},{6,7},{9,8},{10,11},{13,12},{14,15},{17,16},{18,... | collective-permute-start | bytes 1597448 | tf_op jit(solution)/shard_map/ppermute | solution.py:470
  21.6 1.3 %chunk_gradient.2.g2 = f32[256,2048]{1,0:T(8,128)S(1)} custom-call(bf16[1024,2048]{1,0:T(8,128)(2,1)S(1)} %get-tuple-element.52.normed_ref, bf16[1056,256]{1,0:T(8,128)(2,1)S(1)} %collective-permute-done.refs_0_.a1), custom_call_target="tpu_custom_call" | custom-call | flops 1 | bytes 1 | tf_op jit(solution)/shard_map/chunk_gradient/pallas_call | solution.py:288
  23.2 10.6 %collective-permute-done.6.refs_4_ = bf16[2064,128]{1,0:T(8,128)(2,1)S(1)} collective-permute-done((bf16[2064,128]{1,0:T(8,128)(2,1)S(1)}, bf16[2064,128]{1,0:T(8,128)(2,1)S(1)}, u32[]{:S(2)}, u32[]{:S(2)}) %collective-permute-start.6) | collective-permute-done | bytes 528416 | tf_op jit(solution)/shard_map/ppermute | solution.py:461
  33.9 0.5 collective-permute-start.9
  34.4 1.4 %collective-permute-done.8.refs_3_ = bf16[2064,128]{1,0:T(8,128)(2,1)S(1)} collective-permute-done((bf16[2064,128]{1,0:T(8,128)(2,1)S(1)}, bf16[2064,128]{1,0:T(8,128)(2,1)S(1)}, u32[]{:S(2)}, u32[]{:S(2)}) %collective-permute-start.8) | collective-permute-done | bytes 528416 | tf_op jit(solution)/shard_map/ppermute | solution.py:461
  35.8 0.8 collective-permute-done.9.refs_5_
  36.6 0.8 collective-permute-done.10.refs_7_
  37.3 2.2 %assembled.1 = (bf16[2176,1024]{1,0:T(8,128)(2,1)S(1)}, s32[8,128]{1,0:T(8,128)S(1)}) custom-call(bf16[2064,128]{1,0:T(8,128)(2,1)S(1)} %fusion.1.refs_0_, bf16[2064,128]{1,0:T(8,128)(2,1)S(1)} %collective-permute-done.2.refs_1_, bf16[2064,128]{1,0:T(8,128)(2,1)S(1)} %collective-permute-done.5.refs_2_, bf16[2064,128]{1,0:T(8,128)(2,1)S(1)} %collective-permute-done.8.refs_3_, ...), custom_call_target="tpu_custom_call" | custom-call | flops 1 | bytes 1 | tf_op jit(solution)/shard_map/assembled/pallas_call | solution.py:96
  39.5 2.1 %copy-done.3 = bf16[2176,1024]{1,0:T(8,128)(2,1)} copy-done((bf16[2176,1024]{1,0:T(8,128)(2,1)}, bf16[2176,1024]{1,0:T(8,128)(2,1)S(1)}, u32[]{:S(2)}) %copy-start.3) | copy-done | bytes 4456472
  41.6 0.8 copy-done.13
  42.5 1.3 %collective-permute-start.12 = (bf16[1056,256]{1,0:T(8,128)(2,1)S(1)}, bf16[1056,256]{1,0:T(8,128)(2,1)}, u32[]{:S(2)}, u32[]{:S(2)}) collective-permute-start(bf16[1056,256]{1,0:T(8,128)(2,1)S(1)} %collective-permute-done.3.m2), channel_id=1, source_target_pairs={{1,0},{2,3},{5,4},{6,7},{9,8},{10,11},{13,12},{14,15},{17,16},{18,... | collective-permute-start | bytes 1622024 | tf_op jit(solution)/shard_map/ppermute | solution.py:470
  43.8 2.2 %copy-done.1 = bf16[1024,2048]{1,0:T(8,128)(2,1)S(1)} copy-done((bf16[1024,2048]{1,0:T(8,128)(2,1)S(1)}, bf16[1024,2048]{1,0:T(8,128)(2,1)}, u32[]{:S(2)}) %copy-start.1) | copy-done | bytes 4194328
  46.0 2.3 %copy-done.4 = bf16[2176,1024]{1,0:T(8,128)(2,1)S(1)} copy-done((bf16[2176,1024]{1,0:T(8,128)(2,1)S(1)}, bf16[2176,1024]{1,0:T(8,128)(2,1)}, u32[]{:S(2)}) %copy-start.4) | copy-done | bytes 4456472
  48.2 1.3 %first_values.1 = s16[1040,256]{1,0:T(8,128)(2,1)S(1)} custom-call(s32[1]{0:T(128)} %bitcast.place_ref, bf16[1024,2048]{1,0:T(8,128)(2,1)S(1)} %copy-done.1, bf16[2176,1024]{1,0:T(8,128)(2,1)S(1)} %copy-done.4), custom_call_target="tpu_custom_call" | custom-call | flops 1 | bytes 1 | tf_op jit(solution)/shard_map/first_values/pallas_call | solution.py:128
  49.6 7.1 %collective-permute-start.11 = (s16[1040,256]{1,0:T(8,128)(2,1)S(1)}, s16[1040,256]{1,0:T(8,128)(2,1)S(1)}, u32[]{:S(2)}, u32[]{:S(2)}) collective-permute-start(s16[1040,256]{1,0:T(8,128)(2,1)S(1)} %first_values.1), channel_id=1, source_target_pairs={{0,1},{3,2},{4,5},{7,6},{8,9},{11,10},{12,13},{15,14},{16,17},{19,... | collective-permute-start | bytes 1597448 | tf_op jit(solution)/shard_map/ppermute | solution.py:473
  56.7 1.3 %chunk_gradient.3.g3 = f32[256,2048]{1,0:T(8,128)S(1)} custom-call(bf16[1024,2048]{1,0:T(8,128)(2,1)S(1)} %copy-done.2, bf16[1040,256]{1,0:T(8,128)(2,1)S(1)} %copy-done.12, bf16[1040,256]{1,0:T(8,128)(2,1)S(1)} %copy-done.14), custom_call_target="tpu_custom_call" | custom-call | flops 1 | bytes 1 | tf_op jit(solution)/shard_map/chunk_gradient/pallas_call | solution.py:288
  58.0 4.7 %partial_values.1 = (f32[1024,1024]{1,0:T(8,128)S(1)}, s16[1040,256]{1,0:T(8,128)(2,1)S(1)}) custom-call(s32[1]{0:T(128)} %bitcast.place_ref, bf16[1024,2048]{1,0:T(8,128)(2,1)S(1)} %copy-done.2, bf16[2176,1024]{1,0:T(8,128)(2,1)S(1)} %copy-done.4), custom_call_target="tpu_custom_call" | custom-call | flops 1 | bytes 1 | tf_op jit(solution)/shard_map/partial_values/pallas_call | solution.py:157
  62.8 5.3 %slot_terms.1 = (f32[2048,128]{1,0:T(8,128)S(1)}, f32[2048,128]{1,0:T(8,128)S(1)}, f32[2048,128]{1,0:T(8,128)S(1)}, f32[2048,128]{1,0:T(8,128)S(1)}, s16[2096,12...) custom-call(s32[8,128]{1,0:T(8,128)S(1)} %get-tuple-element.72.codes, ...), custom_call_target="tpu_custom_call" | custom-call | flops 1 | bytes 1 | tf_op jit(solution)/shard_map/slot_terms/pallas_call | solution.py:344
  68.2 0.5 collective-permute-start.17
  68.7 0.4 collective-permute-start.15
  69.2 4.4 %collective-permute-start.14 = (s16[1040,256]{1,0:T(8,128)(2,1)S(1)}, s16[1040,256]{1,0:T(8,128)(2,1)S(1)}, u32[]{:S(2)}, u32[]{:S(2)}) collective-permute-start(s16[1040,256]{1,0:T(8,128)(2,1)S(1)} %get-tuple-element.86), channel_id=1, source_target_pairs={{0,1},{3,2},{4,5},{7,6},{8,9},{11,10},{12,13},{15,14},{16,17},{19,... | collective-permute-start | bytes 1597448 | tf_op jit(solution)/shard_map/ppermute | solution.py:473
  73.9 0.7 collective-permute-start.13
  74.6 0.4 combine.5
  75.0 1.6 %collective-permute-start.23 = (s16[2096,128]{1,0:T(8,128)(2,1)S(1)}, s16[2096,128]{1,0:T(8,128)(2,1)S(1)}, u32[]{:S(2)}, u32[]{:S(2)}) collective-permute-start(s16[2096,128]{1,0:T(8,128)(2,1)S(1)} %combine.5), channel_id=1, source_target_pairs={{0,8},{4,12},{8,0},{12,4},{16,24},{20,28},{24,16},{28,20},{1,9},{5... | collective-permute-start | bytes 1609736 | tf_op jit(solution)/shard_map/ppermute | solution.py:461
  76.9 0.8 collective-permute-start.22
  78.1 1.3 %collective-permute-start.21 = (s16[2096,128]{1,0:T(8,128)(2,1)S(1)}, s16[2096,128]{1,0:T(8,128)(2,1)S(1)}, u32[]{:S(2)}, u32[]{:S(2)}) collective-permute-start(s16[2096,128]{1,0:T(8,128)(2,1)S(1)} %combine.7), channel_id=1, source_target_pairs={{0,24},{4,28},{8,16},{12,20},{16,8},{20,12},{24,0},{28,4},{1,25},{... | collective-permute-start | bytes 1609736 | tf_op jit(solution)/shard_map/ppermute | solution.py:461
  79.6 5.5 %collective-permute-done.14.arrived_ref = s16[1040,256]{1,0:T(8,128)(2,1)S(1)} collective-permute-done((s16[1040,256]{1,0:T(8,128)(2,1)S(1)}, s16[1040,256]{1,0:T(8,128)(2,1)S(1)}, u32[]{:S(2)}, u32[]{:S(2)}) %collective-permute-start.14) | collective-permute-done | bytes 532512 | tf_op jit(solution)/shard_map/ppermute | solution.py:473
  85.4 1.0 collective-permute-start.20
  86.8 5.7 %collective-permute-start.19 = (s16[1040,256]{1,0:T(8,128)(2,1)S(1)}, s16[1040,256]{1,0:T(8,128)(2,1)S(1)}, u32[]{:S(2)}, u32[]{:S(2)}) collective-permute-start(s16[1040,256]{1,0:T(8,128)(2,1)S(1)} %hop.4), channel_id=1, source_target_pairs={{0,1},{1,0},{2,3},{3,2},{4,5},{5,4},{6,7},{7,6},{8,9},{9,8},{10,11... | collective-permute-start | bytes 1597448 | tf_op jit(solution)/shard_map/ppermute | solution.py:464
  92.5 7.6 %grad_inputs.1 = bf16[1024,2048]{1,0:T(8,128)(2,1)} custom-call(s32[1]{0:T(128)} %bitcast.place_ref, bf16[2176,1024]{1,0:T(8,128)(2,1)S(1)} %bitcast.4, bf16[1024,256]{1,0:T(8,128)(2,1)S(1)} %copy-done.8, bf16[1056,256]{1,0:T(8,128)(2,1)S(1)} %collective-permute-done.refs_0_.a1, bf16[1040,256]{1,0:T(8,128)(2,1)S(1)} %copy-done.12, ...), custom_call_target="tpu_custom_call" | custom-call | flops 4294967296 | bytes 12582912 | tf_op jit(solution)/shard_map/grad_inputs/pallas_call | solution.py:432
  100.1 1.9 %collective-permute-done.22.refs_2_ = s16[2096,128]{1,0:T(8,128)(2,1)S(1)} collective-permute-done((s16[2096,128]{1,0:T(8,128)(2,1)S(1)}, s16[2096,128]{1,0:T(8,128)(2,1)S(1)}, u32[]{:S(2)}, u32[]{:S(2)}) %collective-permute-start.22) | collective-permute-done | bytes 536608 | tf_op jit(solution)/shard_map/ppermute | solution.py:461
  102.0 1.9 %normalized_update.1 = bf16[16,128,128]{2,1,0:T(8,128)(2,1)} custom-call(f32[2048,128]{1,0:T(8,128)S(1)} %combine.4.refs_0_, s16[2096,128]{1,0:T(8,128)(2,1)S(1)} %collective-permute-done.21.refs_1_, s16[2096,128]{1,0:T(8,128)(2,1)S(1)} %collective-permute-done.22.refs_2_, s16[2096,128]{1,0:T(8,128)(2,1)S(1)} %collective-permute-done.23.refs_3_), custom_call_target="tpu_custom_call" | custom-call | flops 1 | bytes 1 | tf_op jit(solution)/shard_map/normalized_update/pallas_call | solution.py:402
  104.0 1.1 %last_hop.1 = bf16[1024,256]{1,0:T(8,128)(2,1)} custom-call(s32[1]{0:T(128)} %bitcast.place_ref, f32[1024,1024]{1,0:T(8,128)S(1)} %get-tuple-element.71.partial_ref, s16[1040,256]{1,0:T(8,128)(2,1)S(1)} %collective-permute-done.19.right_ref, s16[1040,256]{1,0:T(8,128)(2,1)S(1)} %collective-permute-done.20.left_ref), custom_call_target="tpu_custom_call" | custom-call | flops 1 | bytes 1 | tf_op jit(solution)/shard_map/last_hop/pallas_call | solution.py:207
  (55 shorter events, 2.6 us)
Async XLA Ops:
  2.4 8.0 %collective-permute-start.2 = (bf16[2064,128]{1,0:T(8,128)(2,1)S(1)}, bf16[2064,128]{1,0:T(8,128)(2,1)S(1)}, u32[]{:S(2)}, u32[]{:S(2)}) collective-permute-start(bf16[2064,128]{1,0:T(8,128)(2,1)S(1)} %fusion.1.refs_0_), channel_id=1, source_target_pairs={{0,4},{4,0},{8,12},{12,8},{16,20},{20,16},{24,28},{28,24},{1,5},{5... | collective-permute-start | bytes 1585160 | tf_op jit(solution)/shard_map/ppermute | solution.py:461
  2.9 1.0 copy-start.6
  4.0 15.6 %collective-permute-start = (bf16[1056,256]{1,0:T(8,128)(2,1)S(1)}, bf16[1056,256]{1,0:T(8,128)(2,1)S(1)}, u32[]{:S(2)}, u32[]{:S(2)}) collective-permute-start(bf16[1056,256]{1,0:T(8,128)(2,1)S(1)} %get-tuple-element.53), channel_id=1, source_target_pairs={{0,1},{1,0},{2,3},{3,2},{4,5},{5,4},{6,7},{7,6},{8,9},{9,8},{10,11... | collective-permute-start | bytes 1622024 | tf_op jit(solution)/shard_map/ppermute | solution.py:464
  6.7 10.6 %collective-permute-start.1 = (bf16[1040,256]{1,0:T(8,128)(2,1)S(1)}, bf16[1040,256]{1,0:T(8,128)(2,1)S(1)}, u32[]{:S(2)}, u32[]{:S(2)}) collective-permute-start(bf16[1040,256]{1,0:T(8,128)(2,1)S(1)} %get-tuple-element.54), channel_id=1, source_target_pairs={{1,2},{2,1},{5,6},{6,5},{9,10},{10,9},{13,14},{14,13},{17,18},{18,... | collective-permute-start | bytes 1597448 | tf_op jit(solution)/shard_map/ppermute | solution.py:467
  7.4 15.9 %collective-permute-start.7 = (bf16[2064,128]{1,0:T(8,128)(2,1)S(1)}, bf16[2064,128]{1,0:T(8,128)(2,1)S(1)}, u32[]{:S(2)}, u32[]{:S(2)}) collective-permute-start(bf16[2064,128]{1,0:T(8,128)(2,1)S(1)} %fusion.1.refs_0_), channel_id=1, source_target_pairs={{0,24},{4,28},{8,16},{12,20},{16,8},{20,12},{24,0},{28,4},{1,25},{... | collective-permute-start | bytes 1585160 | tf_op jit(solution)/shard_map/ppermute | solution.py:461
  9.9 23.9 %collective-permute-start.6 = (bf16[2064,128]{1,0:T(8,128)(2,1)S(1)}, bf16[2064,128]{1,0:T(8,128)(2,1)S(1)}, u32[]{:S(2)}, u32[]{:S(2)}) collective-permute-start(bf16[2064,128]{1,0:T(8,128)(2,1)S(1)} %fusion.1.refs_0_), channel_id=1, source_target_pairs={{0,16},{4,20},{8,24},{12,28},{16,0},{20,4},{24,8},{28,12},{1,17},{... | collective-permute-start | bytes 1585160 | tf_op jit(solution)/shard_map/ppermute | solution.py:461
  10.4 23.5 %collective-permute-start.5 = (bf16[2064,128]{1,0:T(8,128)(2,1)S(1)}, bf16[2064,128]{1,0:T(8,128)(2,1)S(1)}, u32[]{:S(2)}, u32[]{:S(2)}) collective-permute-start(bf16[2064,128]{1,0:T(8,128)(2,1)S(1)} %fusion.1.refs_0_), channel_id=1, source_target_pairs={{0,8},{4,12},{8,0},{12,4},{16,24},{20,28},{24,16},{28,20},{1,9},{5... | collective-permute-start | bytes 1585160 | tf_op jit(solution)/shard_map/ppermute | solution.py:461
  10.9 2.2 %copy-start.5 = (bf16[1024,2048]{1,0:T(8,128)(2,1)S(1)}, bf16[1024,2048]{1,0:T(8,128)(2,1)}, u32[]{:S(2)}) copy-start(bf16[1024,2048]{1,0:T(8,128)(2,1)} %normed_ref.1) | copy-start | bytes 12582916
  13.1 1.0 copy-start.7
  15.9 1.4 %copy-start.9 = (f32[256,2048]{1,0:T(8,128)}, f32[256,2048]{1,0:T(8,128)S(1)}, u32[]{:S(2)}) copy-start(f32[256,2048]{1,0:T(8,128)S(1)} %get-tuple-element.74.g1) | copy-start | bytes 6291460
  17.3 5.6 %copy-start = (bf16[1024,2048]{1,0:T(8,128)(2,1)}, bf16[1024,2048]{1,0:T(8,128)(2,1)S(1)}, u32[]{:S(2)}) copy-start(bf16[1024,2048]{1,0:T(8,128)(2,1)S(1)} %get-tuple-element.52.normed_ref) | copy-start | bytes 12582916
  17.3 5.6 %copy-start.11 = (bf16[1040,256]{1,0:T(8,128)(2,1)}, bf16[1040,256]{1,0:T(8,128)(2,1)S(1)}, u32[]{:S(2)}) copy-start(bf16[1040,256]{1,0:T(8,128)(2,1)S(1)} %collective-permute-done.1.refs_0_.b1) | copy-start | bytes 1597444
  19.6 22.9 %collective-permute-start.3 = (bf16[1056,256]{1,0:T(8,128)(2,1)S(1)}, bf16[1056,256]{1,0:T(8,128)(2,1)S(1)}, u32[]{:S(2)}, u32[]{:S(2)}) collective-permute-start(bf16[1056,256]{1,0:T(8,128)(2,1)S(1)} %collective-permute-done.refs_0_.a1), channel_id=1, source_target_pairs={{1,2},{2,1},{5,6},{6,5},{9,10},{10,9},{13,14},{14,13},{17,18},{18,... | collective-permute-start | bytes 1622024 | tf_op jit(solution)/shard_map/ppermute | solution.py:467
  20.3 21.3 %collective-permute-start.4 = (bf16[1040,256]{1,0:T(8,128)(2,1)S(1)}, bf16[1040,256]{1,0:T(8,128)(2,1)S(1)}, u32[]{:S(2)}, u32[]{:S(2)}) collective-permute-start(bf16[1040,256]{1,0:T(8,128)(2,1)S(1)} %collective-permute-done.1.refs_0_.b1), channel_id=1, source_target_pairs={{1,0},{2,3},{5,4},{6,7},{9,8},{10,11},{13,12},{14,15},{17,16},{18,... | collective-permute-start | bytes 1597448 | tf_op jit(solution)/shard_map/ppermute | solution.py:470
  33.9 1.9 %collective-permute-start.8 = (bf16[2064,128]{1,0:T(8,128)(2,1)S(1)}, bf16[2064,128]{1,0:T(8,128)(2,1)S(1)}, u32[]{:S(2)}, u32[]{:S(2)}) collective-permute-start(bf16[2064,128]{1,0:T(8,128)(2,1)S(1)} %collective-permute-done.5.refs_2_), channel_id=1, source_target_pairs={{0,4},{4,0},{8,12},{12,8},{16,20},{20,16},{24,28},{28,24},{1,5},{5... | collective-permute-start | bytes 1585160 | tf_op jit(solution)/shard_map/ppermute | solution.py:461
  33.9 2.7 %collective-permute-start.9 = (bf16[2064,128]{1,0:T(8,128)(2,1)S(1)}, bf16[2064,128]{1,0:T(8,128)(2,1)S(1)}, u32[]{:S(2)}, u32[]{:S(2)}) collective-permute-start(bf16[2064,128]{1,0:T(8,128)(2,1)S(1)} %collective-permute-done.6.refs_4_), channel_id=1, source_target_pairs={{0,4},{4,0},{8,12},{12,8},{16,20},{20,16},{24,28},{28,24},{1,5},{5... | collective-permute-start | bytes 1585160 | tf_op jit(solution)/shard_map/ppermute | solution.py:461
  34.4 2.9 %collective-permute-start.10 = (bf16[2064,128]{1,0:T(8,128)(2,1)S(1)}, bf16[2064,128]{1,0:T(8,128)(2,1)S(1)}, u32[]{:S(2)}, u32[]{:S(2)}) collective-permute-start(bf16[2064,128]{1,0:T(8,128)(2,1)S(1)} %collective-permute-done.7.refs_6_), channel_id=1, source_target_pairs={{0,4},{4,0},{8,12},{12,8},{16,20},{20,16},{24,28},{28,24},{1,5},{5... | collective-permute-start | bytes 1585160 | tf_op jit(solution)/shard_map/ppermute | solution.py:461
  39.5 2.1 %copy-start.3 = (bf16[2176,1024]{1,0:T(8,128)(2,1)}, bf16[2176,1024]{1,0:T(8,128)(2,1)S(1)}, u32[]{:S(2)}) copy-start(bf16[2176,1024]{1,0:T(8,128)(2,1)S(1)} %get-tuple-element.68.weight_ref) | copy-start | bytes 13369348
  41.6 0.9 copy-start.13
  42.5 20.3 %collective-permute-start.12 = (bf16[1056,256]{1,0:T(8,128)(2,1)S(1)}, bf16[1056,256]{1,0:T(8,128)(2,1)}, u32[]{:S(2)}, u32[]{:S(2)}) collective-permute-start(bf16[1056,256]{1,0:T(8,128)(2,1)S(1)} %collective-permute-done.3.m2), channel_id=1, source_target_pairs={{1,0},{2,3},{5,4},{6,7},{9,8},{10,11},{13,12},{14,15},{17,16},{18,... | collective-permute-start | bytes 1622024 | tf_op jit(solution)/shard_map/ppermute | solution.py:470
  43.8 2.2 %copy-start.1 = (bf16[1024,2048]{1,0:T(8,128)(2,1)S(1)}, bf16[1024,2048]{1,0:T(8,128)(2,1)}, u32[]{:S(2)}) copy-start(bf16[1024,2048]{1,0:T(8,128)(2,1)} %copy-done) | copy-start | bytes 12582916
  46.0 2.3 %copy-start.4 = (bf16[2176,1024]{1,0:T(8,128)(2,1)S(1)}, bf16[2176,1024]{1,0:T(8,128)(2,1)}, u32[]{:S(2)}) copy-start(bf16[2176,1024]{1,0:T(8,128)(2,1)} %copy-done.3) | copy-start | bytes 13369348
  48.2 8.5 %copy-start.2 = (bf16[1024,2048]{1,0:T(8,128)(2,1)S(1)}, bf16[1024,2048]{1,0:T(8,128)(2,1)}, u32[]{:S(2)}) copy-start(bf16[1024,2048]{1,0:T(8,128)(2,1)} %copy-done) | copy-start | bytes 12582916
  48.2 8.5 %copy-start.12 = (bf16[1040,256]{1,0:T(8,128)(2,1)S(1)}, bf16[1040,256]{1,0:T(8,128)(2,1)}, u32[]{:S(2)}) copy-start(bf16[1040,256]{1,0:T(8,128)(2,1)} %copy-done.11) | copy-start | bytes 1597444
  48.2 8.5 %copy-start.14 = (bf16[1040,256]{1,0:T(8,128)(2,1)S(1)}, bf16[1040,256]{1,0:T(8,128)(2,1)}, u32[]{:S(2)}) copy-start(bf16[1040,256]{1,0:T(8,128)(2,1)} %copy-done.13) | copy-start | bytes 1597444
  49.6 18.6 %collective-permute-start.11 = (s16[1040,256]{1,0:T(8,128)(2,1)S(1)}, s16[1040,256]{1,0:T(8,128)(2,1)S(1)}, u32[]{:S(2)}, u32[]{:S(2)}) collective-permute-start(s16[1040,256]{1,0:T(8,128)(2,1)S(1)} %first_values.1), channel_id=1, source_target_pairs={{0,1},{3,2},{4,5},{7,6},{8,9},{11,10},{12,13},{15,14},{16,17},{19,... | collective-permute-start | bytes 1597448 | tf_op jit(solution)/shard_map/ppermute | solution.py:473
  58.0 4.7 %copy-start.10 = (f32[256,2048]{1,0:T(8,128)S(1)}, f32[256,2048]{1,0:T(8,128)}, u32[]{:S(2)}) copy-start(f32[256,2048]{1,0:T(8,128)} %copy-done.9) | copy-start | bytes 6291460
  68.1 5.8 %collective-permute-start.16 = (s16[2096,128]{1,0:T(8,128)(2,1)S(1)}, s16[2096,128]{1,0:T(8,128)(2,1)S(1)}, u32[]{:S(2)}, u32[]{:S(2)}) collective-permute-start(s16[2096,128]{1,0:T(8,128)(2,1)S(1)} %get-tuple-element.90), channel_id=1, source_target_pairs={{0,4},{4,0},{8,12},{12,8},{16,20},{20,16},{24,28},{28,24},{1,5},{5... | collective-permute-start | bytes 1609736 | tf_op jit(solution)/shard_map/ppermute | solution.py:461
  68.2 6.8 %collective-permute-start.17 = (s16[2096,128]{1,0:T(8,128)(2,1)S(1)}, s16[2096,128]{1,0:T(8,128)(2,1)S(1)}, u32[]{:S(2)}, u32[]{:S(2)}) collective-permute-start(s16[2096,128]{1,0:T(8,128)(2,1)S(1)} %get-tuple-element.92), channel_id=1, source_target_pairs={{0,4},{4,0},{8,12},{12,8},{16,20},{20,16},{24,28},{28,24},{1,5},{5... | collective-permute-start | bytes 1609736 | tf_op jit(solution)/shard_map/ppermute | solution.py:461
  68.7 8.3 %collective-permute-start.18 = (s16[2096,128]{1,0:T(8,128)(2,1)S(1)}, s16[2096,128]{1,0:T(8,128)(2,1)S(1)}, u32[]{:S(2)}, u32[]{:S(2)}) collective-permute-start(s16[2096,128]{1,0:T(8,128)(2,1)S(1)} %get-tuple-element.94), channel_id=1, source_target_pairs={{0,4},{4,0},{8,12},{12,8},{16,20},{20,16},{24,28},{28,24},{1,5},{5... | collective-permute-start | bytes 1609736 | tf_op jit(solution)/shard_map/ppermute | solution.py:461
  68.7 9.3 %collective-permute-start.15 = (s16[2096,128]{1,0:T(8,128)(2,1)S(1)}, s16[2096,128]{1,0:T(8,128)(2,1)S(1)}, u32[]{:S(2)}, u32[]{:S(2)}) collective-permute-start(s16[2096,128]{1,0:T(8,128)(2,1)S(1)} %get-tuple-element.88), channel_id=1, source_target_pairs={{0,4},{4,0},{8,12},{12,8},{16,20},{20,16},{24,28},{28,24},{1,5},{5... | collective-permute-start | bytes 1609736 | tf_op jit(solution)/shard_map/ppermute | solution.py:461
  69.2 15.9 %collective-permute-start.14 = (s16[1040,256]{1,0:T(8,128)(2,1)S(1)}, s16[1040,256]{1,0:T(8,128)(2,1)S(1)}, u32[]{:S(2)}, u32[]{:S(2)}) collective-permute-start(s16[1040,256]{1,0:T(8,128)(2,1)S(1)} %get-tuple-element.86), channel_id=1, source_target_pairs={{0,1},{3,2},{4,5},{7,6},{8,9},{11,10},{12,13},{15,14},{16,17},{19,... | collective-permute-start | bytes 1597448 | tf_op jit(solution)/shard_map/ppermute | solution.py:473
  73.9 11.1 %collective-permute-start.13 = (s16[1040,256]{1,0:T(8,128)(2,1)S(1)}, s16[1040,256]{1,0:T(8,128)(2,1)S(1)}, u32[]{:S(2)}, u32[]{:S(2)}) collective-permute-start(s16[1040,256]{1,0:T(8,128)(2,1)S(1)} %hop.3), channel_id=1, source_target_pairs={{1,2},{2,1},{5,6},{6,5},{9,10},{10,9},{13,14},{14,13},{17,18},{18,... | collective-permute-start | bytes 1597448 | tf_op jit(solution)/shard_map/ppermute | solution.py:467
  75.0 25.1 %collective-permute-start.23 = (s16[2096,128]{1,0:T(8,128)(2,1)S(1)}, s16[2096,128]{1,0:T(8,128)(2,1)S(1)}, u32[]{:S(2)}, u32[]{:S(2)}) collective-permute-start(s16[2096,128]{1,0:T(8,128)(2,1)S(1)} %combine.5), channel_id=1, source_target_pairs={{0,8},{4,12},{8,0},{12,4},{16,24},{20,28},{24,16},{28,20},{1,9},{5... | collective-permute-start | bytes 1609736 | tf_op jit(solution)/shard_map/ppermute | solution.py:461
  76.9 25.1 %collective-permute-start.22 = (s16[2096,128]{1,0:T(8,128)(2,1)S(1)}, s16[2096,128]{1,0:T(8,128)(2,1)S(1)}, u32[]{:S(2)}, u32[]{:S(2)}) collective-permute-start(s16[2096,128]{1,0:T(8,128)(2,1)S(1)} %combine.6), channel_id=1, source_target_pairs={{0,16},{4,20},{8,24},{12,28},{16,0},{20,4},{24,8},{28,12},{1,17},{... | collective-permute-start | bytes 1609736 | tf_op jit(solution)/shard_map/ppermute | solution.py:461
  78.1 23.9 %collective-permute-start.21 = (s16[2096,128]{1,0:T(8,128)(2,1)S(1)}, s16[2096,128]{1,0:T(8,128)(2,1)S(1)}, u32[]{:S(2)}, u32[]{:S(2)}) collective-permute-start(s16[2096,128]{1,0:T(8,128)(2,1)S(1)} %combine.7), channel_id=1, source_target_pairs={{0,24},{4,28},{8,16},{12,20},{16,8},{20,12},{24,0},{28,4},{1,25},{... | collective-permute-start | bytes 1609736 | tf_op jit(solution)/shard_map/ppermute | solution.py:461
  79.4 13.1 %slice-start = ((s8[4456448]{0:T(1024)(128)(4,1)}), s8[4194304]{0:T(1024)(128)(4,1)S(1)}, s32[]{:S(2)}) async-start(s8[4456448]{0:T(1024)(128)(4,1)} %bitcast.3), calls=%async_computation | async-start | bytes 8388608
  79.6 12.9 %slice-start.1 = ((s8[4456448]{0:T(1024)(128)(4,1)}), s8[262144]{0:T(1024)(128)(4,1)S(1)}, s32[]{:S(2)}) async-start(s8[4456448]{0:T(1024)(128)(4,1)} %bitcast.3), calls=%async_computation.1 | async-start | bytes 524288
  85.4 7.1 %copy-start.8 = (bf16[1024,256]{1,0:T(8,128)(2,1)S(1)}, bf16[1024,256]{1,0:T(8,128)(2,1)}, u32[]{:S(2)}) copy-start(bf16[1024,256]{1,0:T(8,128)(2,1)} %own.1) | copy-start | bytes 1572868
  85.4 18.6 %collective-permute-start.20 = (s16[1040,256]{1,0:T(8,128)(2,1)S(1)}, s16[1040,256]{1,0:T(8,128)(2,1)S(1)}, u32[]{:S(2)}, u32[]{:S(2)}) collective-permute-start(s16[1040,256]{1,0:T(8,128)(2,1)S(1)} %hop.5), channel_id=1, source_target_pairs={{1,2},{2,1},{5,6},{6,5},{9,10},{10,9},{13,14},{14,13},{17,18},{18,... | collective-permute-start | bytes 1597448 | tf_op jit(solution)/shard_map/ppermute | solution.py:467
  86.8 17.2 %collective-permute-start.19 = (s16[1040,256]{1,0:T(8,128)(2,1)S(1)}, s16[1040,256]{1,0:T(8,128)(2,1)S(1)}, u32[]{:S(2)}, u32[]{:S(2)}) collective-permute-start(s16[1040,256]{1,0:T(8,128)(2,1)S(1)} %hop.4), channel_id=1, source_target_pairs={{0,1},{1,0},{2,3},{3,2},{4,5},{5,4},{6,7},{7,6},{8,9},{9,8},{10,11... | collective-permute-start | bytes 1597448 | tf_op jit(solution)/shard_map/ppermute | solution.py:464

commit v13 on v12

--- a/solution.py
+++ b/solution.py
@@ -480,39 +480,39 @@
     normed, g1 = own_gradient(normed, cotangent)
     same_core = [message] + [swap(message, 2 * chip) for chip in range(1, chips)]
     beside = swap(message, 1)
-    a1, b1, g1, beside = lax.optimization_barrier((a1, b1, g1, beside))
+    a1, b1, _, _ = lax.optimization_barrier((a1, b1, g1, beside))
     m2, e2 = middle(a1), outward(b1)
     g2 = chunk_gradient(normed, a1)
-    *same_core, g2 = lax.optimization_barrier((*same_core, g2))
+    *same_core, _ = lax.optimization_barrier((*same_core, g2))
     gathered = [same_core[0], beside]
     for m in same_core[1:]:
         gathered += [m, swap(m, 1)]
 
     weight, codes = assembled(gathered, normed.shape[1], column_blocks)
-    m2, e2, weight, codes = lax.optimization_barrier((m2, e2, weight, codes))
+    m2, e2, codes = lax.optimization_barrier((m2, e2, codes))
     d3 = outward(m2)
     first = first_values(place, normed, weight, parts)
     arrived = inward(first)
-    weight, codes, _ = lax.optimization_barrier((weight, codes, first))
+    codes, _ = lax.optimization_barrier((codes, first))
     partial, second = partial_values(place, normed, weight, first.shape)
     g3 = chunk_gradient(normed, b1, e2)
-    g3, partial, second = lax.optimization_barrier((g3, partial, second))
+    codes, _, _ = lax.optimization_barrier((codes, g3, second))
     keep, send = slot_terms(codes, place, normed, (m2, d3), (g1, g2, g3), capacity, column_blocks)
-    arrived, keep, send = lax.optimization_barrier((arrived, keep, send))
+    arrived, send = lax.optimization_barrier((arrived, send))
 
     to_middle = inward(second)
     crossing = middle(hop(lambda p: p ^ 2, place, partial, arrived))
     other = [swap(m, 1) for m in send]
     sums = [combine(keep[chip], other[chip], jnp.int16) for chip in range(1, chips)]
     own = combine(keep[0], other[0], jnp.float32)
-    crossing, to_middle, own, _ = lax.optimization_barrier((crossing, to_middle, own, sums))
+    crossing, to_middle, _, _ = lax.optimization_barrier((crossing, to_middle, own, sums))
     terms = [swap(m, 2 * chip) for chip, m in reversed(list(enumerate(sums, 1)))]
 
     by_pair = pairs(hop(lambda p: p ^ 1, place, partial, crossing))
     by_middle = middle(hop(lambda p: 3 - p, place, partial, to_middle))
     grad_input = grad_inputs(place, normed.shape[1], weight, cotangent, a1, b1, e2, m2, d3)
     update = normalized_update(own, terms, tile_values.shape[1:])
-    by_pair, by_middle, update = lax.optimization_barrier((by_pair, by_middle, update))
+    by_pair, by_middle, _ = lax.optimization_barrier((by_pair, by_middle, update))
     values = last_hop(place, partial, by_pair, by_middle)
     return values, grad_input, update[None]
 

time: 106 us -> 106 us (level)
  transfers between devices with their start and end apart: 24 -> 24, of which waited for: 10 -> 9; matrix products, arithmetic and copies ran while one was open for 0% -> 0% of each run, Pallas kernels for 28% -> 28%
where the time goes in v13:
time: 106 us; the launch traced here: 105 us
  starting transfers between devices  34.7 us (33%)
  Pallas kernels  30.7 us (29%)
  waiting for transfers between devices  23.7 us (22%)
  local copies, waits for them, and re-layouts  13.3 us (13%)
  other arithmetic  1.76 us (2%)
    ppermute x14, waiting for transfers between devices, swap(): return lax.ppermute(x, 'fsdp', [(i, i ^ mask) for i in range(devices)])  15.9 us
    unnamed x34, local copies, waits for them, and re-layouts  13.3 us
    ppermute x2, starting transfers between devices, inward(): return lax.ppermute(x, 'tensor', [(0, 1), (3, 2)])  11.3 us
    ppermute x14, starting transfers between devices, swap(): return lax.ppermute(x, 'fsdp', [(i, i ^ mask) for i in range(devices)])  9.35 us
    ppermute x2, starting transfers between devices, pairs(): return lax.ppermute(x, 'tensor', [(0, 1), (1, 0), (2, 3), (3, 2)])  8.38 us
    pallas_call x1, Pallas kernels, grad_inputs(): pl.pallas_call(grad_input_kernel, grid_spec=pltpu.PrefetchScalarGridSpec(...  7.55 us
    ppermute x2, waiting for transfers between devices, inward(): return lax.ppermute(x, 'tensor', [(0, 1), (3, 2)])  5.43 us
    pallas_call x1, Pallas kernels, slot_terms(): pl.pallas_call(functools.partial(slots_kernel, chips, column_blocks), in_...  5.27 us
  transfers between devices with their start and end apart: 24, of which 9 were waited for; matrix products, arithmetic and copies ran while one was open for 0% of the time, Pallas kernels for 28%

profile of v13, /device:TPU:0, one launch (start us, length us, event | category | flops | bytes accessed | tf_op | source)
XLA Modules:
  0.0 105.1 jit_solution(6506515204106509689)
XLA Ops:
  0.6 0.7 fusion.2
  1.3 1.1 %fusion.1.refs_0_ = bf16[2064,128]{1,0:T(8,128)(2,1)S(1)} fusion(bf16[1,16]{1,0:T(2,128)(2,1)S(1)} %fusion.2, bf16[2048,128]{1,0:T(8,128)(2,1)} %bitcast.6), kind=kLoop, calls=%fused_computation.2 | loop fusion | flops 1585152 | bytes 1052704 | tf_op jit(solution)/shard_map/concatenate | solution.py:477
  2.4 0.5 collective-permute-start.5
  2.9 1.0 copy-done.6
  4.0 2.7 %collective-permute-start.3 = (bf16[1056,256]{1,0:T(8,128)(2,1)S(1)}, bf16[1056,256]{1,0:T(8,128)(2,1)S(1)}, u32[]{:S(2)}, u32[]{:S(2)}) collective-permute-start(bf16[1056,256]{1,0:T(8,128)(2,1)S(1)} %get-tuple-element.40), channel_id=1, source_target_pairs={{0,1},{1,0},{2,3},{3,2},{4,5},{5,4},{6,7},{7,6},{8,9},{9,8},{10,11... | collective-permute-start | bytes 1622024 | tf_op jit(solution)/shard_map/ppermute | solution.py:464
  6.7 0.7 collective-permute-start.4
  7.4 2.5 %collective-permute-start.2 = (bf16[2064,128]{1,0:T(8,128)(2,1)S(1)}, bf16[2064,128]{1,0:T(8,128)(2,1)S(1)}, u32[]{:S(2)}, u32[]{:S(2)}) collective-permute-start(bf16[2064,128]{1,0:T(8,128)(2,1)S(1)} %fusion.1.refs_0_), channel_id=1, source_target_pairs={{0,24},{4,28},{8,16},{12,20},{16,8},{20,12},{24,0},{28,4},{1,25},{... | collective-permute-start | bytes 1585160 | tf_op jit(solution)/shard_map/ppermute | solution.py:461
  9.9 0.5 collective-permute-start.1
  10.4 0.5 collective-permute-start
  10.9 2.2 %copy-done.5 = bf16[1024,2048]{1,0:T(8,128)(2,1)S(1)} copy-done((bf16[1024,2048]{1,0:T(8,128)(2,1)S(1)}, bf16[1024,2048]{1,0:T(8,128)(2,1)}, u32[]{:S(2)}) %copy-start.5) | copy-done | bytes 4194328
  13.1 1.0 copy-done.7
  14.2 1.7 %own_gradient.1 = (bf16[1024,2048]{1,0:T(8,128)(2,1)S(1)}, f32[256,2048]{1,0:T(8,128)S(1)}) custom-call(bf16[1024,2048]{1,0:T(8,128)(2,1)S(1)} %copy-done.5, bf16[1024,256]{1,0:T(8,128)(2,1)S(1)} %copy-done.7), custom_call_target="tpu_custom_call" | custom-call | flops 1 | bytes 1 | tf_op jit(solution)/shard_map/own_gradient/pallas_call | solution.py:272
  15.9 1.4 %copy-done.9 = f32[256,2048]{1,0:T(8,128)} copy-done((f32[256,2048]{1,0:T(8,128)}, f32[256,2048]{1,0:T(8,128)S(1)}, u32[]{:S(2)}) %copy-start.9) | copy-done | bytes 2097176
  17.3 2.3 %collective-permute-done.3.refs_0_.a1 = bf16[1056,256]{1,0:T(8,128)(2,1)S(1)} collective-permute-done((bf16[1056,256]{1,0:T(8,128)(2,1)S(1)}, bf16[1056,256]{1,0:T(8,128)(2,1)S(1)}, u32[]{:S(2)}, u32[]{:S(2)}) %collective-permute-start.3) | collective-permute-done | bytes 540704 | tf_op jit(solution)/shard_map/ppermute | solution.py:464
  19.6 0.7 collective-permute-start.10
  20.3 1.3 %collective-permute-start.11 = (bf16[1040,256]{1,0:T(8,128)(2,1)S(1)}, bf16[1040,256]{1,0:T(8,128)(2,1)S(1)}, u32[]{:S(2)}, u32[]{:S(2)}) collective-permute-start(bf16[1040,256]{1,0:T(8,128)(2,1)S(1)} %collective-permute-done.4.refs_0_.b1), channel_id=1, source_target_pairs={{1,0},{2,3},{5,4},{6,7},{9,8},{10,11},{13,12},{14,15},{17,16},{18,... | collective-permute-start | bytes 1597448 | tf_op jit(solution)/shard_map/ppermute | solution.py:470
  21.6 1.3 %chunk_gradient.2.g2 = f32[256,2048]{1,0:T(8,128)S(1)} custom-call(bf16[1024,2048]{1,0:T(8,128)(2,1)S(1)} %get-tuple-element.39.normed_ref, bf16[1056,256]{1,0:T(8,128)(2,1)S(1)} %collective-permute-done.3.refs_0_.a1), custom_call_target="tpu_custom_call" | custom-call | flops 1 | bytes 1 | tf_op jit(solution)/shard_map/chunk_gradient/pallas_call | solution.py:288
  23.2 10.6 %collective-permute-done.1.refs_4_ = bf16[2064,128]{1,0:T(8,128)(2,1)S(1)} collective-permute-done((bf16[2064,128]{1,0:T(8,128)(2,1)S(1)}, bf16[2064,128]{1,0:T(8,128)(2,1)S(1)}, u32[]{:S(2)}, u32[]{:S(2)}) %collective-permute-start.1) | collective-permute-done | bytes 528416 | tf_op jit(solution)/shard_map/ppermute | solution.py:461
  33.9 0.5 collective-permute-start.7
  34.4 1.4 %collective-permute-done.6.refs_3_ = bf16[2064,128]{1,0:T(8,128)(2,1)S(1)} collective-permute-done((bf16[2064,128]{1,0:T(8,128)(2,1)S(1)}, bf16[2064,128]{1,0:T(8,128)(2,1)S(1)}, u32[]{:S(2)}, u32[]{:S(2)}) %collective-permute-start.6) | collective-permute-done | bytes 528416 | tf_op jit(solution)/shard_map/ppermute | solution.py:461
  35.8 0.8 collective-permute-done.7.refs_5_
  36.6 0.8 collective-permute-done.8.refs_7_
  37.3 2.2 %assembled.1 = (bf16[2176,1024]{1,0:T(8,128)(2,1)S(1)}, s32[8,128]{1,0:T(8,128)S(1)}) custom-call(bf16[2064,128]{1,0:T(8,128)(2,1)S(1)} %fusion.1.refs_0_, bf16[2064,128]{1,0:T(8,128)(2,1)S(1)} %collective-permute-done.5.refs_1_, bf16[2064,128]{1,0:T(8,128)(2,1)S(1)} %collective-permute-done.refs_2_, bf16[2064,128]{1,0:T(8,128)(2,1)S(1)} %collective-permute-done.6.refs_3_, ...), custom_call_target="tpu_custom_call" | custom-call | flops 1 | bytes 1 | tf_op jit(solution)/shard_map/assembled/pallas_call | solution.py:96
  39.5 2.1 %copy-done.3 = bf16[2176,1024]{1,0:T(8,128)(2,1)} copy-done((bf16[2176,1024]{1,0:T(8,128)(2,1)}, bf16[2176,1024]{1,0:T(8,128)(2,1)S(1)}, u32[]{:S(2)}) %copy-start.3) | copy-done | bytes 4456472
  41.6 0.8 copy-done.13
  42.5 1.3 %collective-permute-start.12 = (bf16[1056,256]{1,0:T(8,128)(2,1)S(1)}, bf16[1056,256]{1,0:T(8,128)(2,1)}, u32[]{:S(2)}, u32[]{:S(2)}) collective-permute-start(bf16[1056,256]{1,0:T(8,128)(2,1)S(1)} %collective-permute-done.10.m2), channel_id=1, source_target_pairs={{1,0},{2,3},{5,4},{6,7},{9,8},{10,11},{13,12},{14,15},{17,16},{18,... | collective-permute-start | bytes 1622024 | tf_op jit(solution)/shard_map/ppermute | solution.py:470
  43.8 2.2 %copy-done.1 = bf16[1024,2048]{1,0:T(8,128)(2,1)S(1)} copy-done((bf16[1024,2048]{1,0:T(8,128)(2,1)S(1)}, bf16[1024,2048]{1,0:T(8,128)(2,1)}, u32[]{:S(2)}) %copy-start.1) | copy-done | bytes 4194328
  46.0 2.3 %copy-done.4 = bf16[2176,1024]{1,0:T(8,128)(2,1)S(1)} copy-done((bf16[2176,1024]{1,0:T(8,128)(2,1)S(1)}, bf16[2176,1024]{1,0:T(8,128)(2,1)}, u32[]{:S(2)}) %copy-start.4) | copy-done | bytes 4456472
  48.2 1.3 %first_values.1 = s16[1040,256]{1,0:T(8,128)(2,1)S(1)} custom-call(s32[1]{0:T(128)} %bitcast.place_ref, bf16[1024,2048]{1,0:T(8,128)(2,1)S(1)} %copy-done.1, bf16[2176,1024]{1,0:T(8,128)(2,1)S(1)} %copy-done.4), custom_call_target="tpu_custom_call" | custom-call | flops 1 | bytes 1 | tf_op jit(solution)/shard_map/first_values/pallas_call | solution.py:128
  49.6 7.1 %collective-permute-start.9 = (s16[1040,256]{1,0:T(8,128)(2,1)S(1)}, s16[1040,256]{1,0:T(8,128)(2,1)S(1)}, u32[]{:S(2)}, u32[]{:S(2)}) collective-permute-start(s16[1040,256]{1,0:T(8,128)(2,1)S(1)} %first_values.1), channel_id=1, source_target_pairs={{0,1},{3,2},{4,5},{7,6},{8,9},{11,10},{12,13},{15,14},{16,17},{19,... | collective-permute-start | bytes 1597448 | tf_op jit(solution)/shard_map/ppermute | solution.py:473
  56.7 4.7 %partial_values.1 = (f32[1024,1024]{1,0:T(8,128)S(1)}, s16[1040,256]{1,0:T(8,128)(2,1)S(1)}) custom-call(s32[1]{0:T(128)} %bitcast.place_ref, bf16[1024,2048]{1,0:T(8,128)(2,1)S(1)} %copy-done.2, bf16[2176,1024]{1,0:T(8,128)(2,1)S(1)} %copy-done.4), custom_call_target="tpu_custom_call" | custom-call | flops 1 | bytes 1 | tf_op jit(solution)/shard_map/partial_values/pallas_call | solution.py:157
  61.5 1.3 %chunk_gradient.3.g3 = f32[256,2048]{1,0:T(8,128)S(1)} custom-call(bf16[1024,2048]{1,0:T(8,128)(2,1)S(1)} %copy-done.2, bf16[1040,256]{1,0:T(8,128)(2,1)S(1)} %copy-done.12, bf16[1040,256]{1,0:T(8,128)(2,1)S(1)} %copy-done.14), custom_call_target="tpu_custom_call" | custom-call | flops 1 | bytes 1 | tf_op jit(solution)/shard_map/chunk_gradient/pallas_call | solution.py:288
  63.1 5.3 %slot_terms.1 = (f32[2048,128]{1,0:T(8,128)S(1)}, f32[2048,128]{1,0:T(8,128)S(1)}, f32[2048,128]{1,0:T(8,128)S(1)}, f32[2048,128]{1,0:T(8,128)S(1)}, s16[2096,12...) custom-call(s32[8,128]{1,0:T(8,128)S(1)} %get-tuple-element.56.codes, ...), custom_call_target="tpu_custom_call" | custom-call | flops 1 | bytes 1 | tf_op jit(solution)/shard_map/slot_terms/pallas_call | solution.py:344
  68.4 0.5 collective-permute-start.17
  69.0 0.4 collective-permute-start.15
  69.4 4.1 %collective-permute-start.14 = (s16[1040,256]{1,0:T(8,128)(2,1)S(1)}, s16[1040,256]{1,0:T(8,128)(2,1)S(1)}, u32[]{:S(2)}, u32[]{:S(2)}) collective-permute-start(s16[1040,256]{1,0:T(8,128)(2,1)S(1)} %get-tuple-element.55), channel_id=1, source_target_pairs={{0,1},{3,2},{4,5},{7,6},{8,9},{11,10},{12,13},{15,14},{16,17},{19,... | collective-permute-start | bytes 1597448 | tf_op jit(solution)/shard_map/ppermute | solution.py:473
  73.9 0.7 collective-permute-start.13
  75.0 1.6 %collective-permute-start.23 = (s16[2096,128]{1,0:T(8,128)(2,1)S(1)}, s16[2096,128]{1,0:T(8,128)(2,1)S(1)}, u32[]{:S(2)}, u32[]{:S(2)}) collective-permute-start(s16[2096,128]{1,0:T(8,128)(2,1)S(1)} %combine.5), channel_id=1, source_target_pairs={{0,8},{4,12},{8,0},{12,4},{16,24},{20,28},{24,16},{28,20},{1,9},{5... | collective-permute-start | bytes 1609736 | tf_op jit(solution)/shard_map/ppermute | solution.py:461
  76.6 0.4 combine.6
  77.0 0.8 collective-permute-start.22
  78.1 1.3 %collective-permute-start.21 = (s16[2096,128]{1,0:T(8,128)(2,1)S(1)}, s16[2096,128]{1,0:T(8,128)(2,1)S(1)}, u32[]{:S(2)}, u32[]{:S(2)}) collective-permute-start(s16[2096,128]{1,0:T(8,128)(2,1)S(1)} %combine.7), channel_id=1, source_target_pairs={{0,24},{4,28},{8,16},{12,20},{16,8},{20,12},{24,0},{28,4},{1,25},{... | collective-permute-start | bytes 1609736 | tf_op jit(solution)/shard_map/ppermute | solution.py:461
  79.6 5.4 %collective-permute-done.14.arrived_ref = s16[1040,256]{1,0:T(8,128)(2,1)S(1)} collective-permute-done((s16[1040,256]{1,0:T(8,128)(2,1)S(1)}, s16[1040,256]{1,0:T(8,128)(2,1)S(1)}, u32[]{:S(2)}, u32[]{:S(2)}) %collective-permute-start.14) | collective-permute-done | bytes 532512 | tf_op jit(solution)/shard_map/ppermute | solution.py:473
  85.4 1.0 collective-permute-start.20
  86.8 5.7 %collective-permute-start.19 = (s16[1040,256]{1,0:T(8,128)(2,1)S(1)}, s16[1040,256]{1,0:T(8,128)(2,1)S(1)}, u32[]{:S(2)}, u32[]{:S(2)}) collective-permute-start(s16[1040,256]{1,0:T(8,128)(2,1)S(1)} %hop.4), channel_id=1, source_target_pairs={{0,1},{1,0},{2,3},{3,2},{4,5},{5,4},{6,7},{7,6},{8,9},{9,8},{10,11... | collective-permute-start | bytes 1597448 | tf_op jit(solution)/shard_map/ppermute | solution.py:464
  92.5 7.6 %grad_inputs.1 = bf16[1024,2048]{1,0:T(8,128)(2,1)} custom-call(s32[1]{0:T(128)} %bitcast.place_ref, bf16[2176,1024]{1,0:T(8,128)(2,1)S(1)} %bitcast.4, bf16[1024,256]{1,0:T(8,128)(2,1)S(1)} %copy-done.8, bf16[1056,256]{1,0:T(8,128)(2,1)S(1)} %collective-permute-done.3.refs_0_.a1, bf16[1040,256]{1,0:T(8,128)(2,1)S(1)} %copy-done.12, ...), custom_call_target="tpu_custom_call" | custom-call | flops 4294967296 | bytes 12582912 | tf_op jit(solution)/shard_map/grad_inputs/pallas_call | solution.py:432
  100.1 2.0 %collective-permute-done.22.refs_2_ = s16[2096,128]{1,0:T(8,128)(2,1)S(1)} collective-permute-done((s16[2096,128]{1,0:T(8,128)(2,1)S(1)}, s16[2096,128]{1,0:T(8,128)(2,1)S(1)}, u32[]{:S(2)}, u32[]{:S(2)}) %collective-permute-start.22) | collective-permute-done | bytes 536608 | tf_op jit(solution)/shard_map/ppermute | solution.py:461
  102.1 1.9 %normalized_update.1 = bf16[16,128,128]{2,1,0:T(8,128)(2,1)} custom-call(f32[2048,128]{1,0:T(8,128)S(1)} %combine.4.refs_0_, s16[2096,128]{1,0:T(8,128)(2,1)S(1)} %collective-permute-done.21.refs_1_, s16[2096,128]{1,0:T(8,128)(2,1)S(1)} %collective-permute-done.22.refs_2_, s16[2096,128]{1,0:T(8,128)(2,1)S(1)} %collective-permute-done.23.refs_3_), custom_call_target="tpu_custom_call" | custom-call | flops 1 | bytes 1 | tf_op jit(solution)/shard_map/normalized_update/pallas_call | solution.py:402
  104.0 1.1 %last_hop.1 = bf16[1024,256]{1,0:T(8,128)(2,1)} custom-call(s32[1]{0:T(128)} %bitcast.place_ref, f32[1024,1024]{1,0:T(8,128)S(1)} %get-tuple-element.49.partial_ref, s16[1040,256]{1,0:T(8,128)(2,1)S(1)} %collective-permute-done.19.right_ref, s16[1040,256]{1,0:T(8,128)(2,1)S(1)} %collective-permute-done.20.left_ref), custom_call_target="tpu_custom_call" | custom-call | flops 1 | bytes 1 | tf_op jit(solution)/shard_map/last_hop/pallas_call | solution.py:207
  (55 shorter events, 2.9 us)
Async XLA Ops:
  2.4 8.0 %collective-permute-start.5 = (bf16[2064,128]{1,0:T(8,128)(2,1)S(1)}, bf16[2064,128]{1,0:T(8,128)(2,1)S(1)}, u32[]{:S(2)}, u32[]{:S(2)}) collective-permute-start(bf16[2064,128]{1,0:T(8,128)(2,1)S(1)} %fusion.1.refs_0_), channel_id=1, source_target_pairs={{0,4},{4,0},{8,12},{12,8},{16,20},{20,16},{24,28},{28,24},{1,5},{5... | collective-permute-start | bytes 1585160 | tf_op jit(solution)/shard_map/ppermute | solution.py:461
  2.9 1.0 copy-start.6
  4.0 15.6 %collective-permute-start.3 = (bf16[1056,256]{1,0:T(8,128)(2,1)S(1)}, bf16[1056,256]{1,0:T(8,128)(2,1)S(1)}, u32[]{:S(2)}, u32[]{:S(2)}) collective-permute-start(bf16[1056,256]{1,0:T(8,128)(2,1)S(1)} %get-tuple-element.40), channel_id=1, source_target_pairs={{0,1},{1,0},{2,3},{3,2},{4,5},{5,4},{6,7},{7,6},{8,9},{9,8},{10,11... | collective-permute-start | bytes 1622024 | tf_op jit(solution)/shard_map/ppermute | solution.py:464
  6.7 10.6 %collective-permute-start.4 = (bf16[1040,256]{1,0:T(8,128)(2,1)S(1)}, bf16[1040,256]{1,0:T(8,128)(2,1)S(1)}, u32[]{:S(2)}, u32[]{:S(2)}) collective-permute-start(bf16[1040,256]{1,0:T(8,128)(2,1)S(1)} %get-tuple-element.41), channel_id=1, source_target_pairs={{1,2},{2,1},{5,6},{6,5},{9,10},{10,9},{13,14},{14,13},{17,18},{18,... | collective-permute-start | bytes 1597448 | tf_op jit(solution)/shard_map/ppermute | solution.py:467
  7.4 15.9 %collective-permute-start.2 = (bf16[2064,128]{1,0:T(8,128)(2,1)S(1)}, bf16[2064,128]{1,0:T(8,128)(2,1)S(1)}, u32[]{:S(2)}, u32[]{:S(2)}) collective-permute-start(bf16[2064,128]{1,0:T(8,128)(2,1)S(1)} %fusion.1.refs_0_), channel_id=1, source_target_pairs={{0,24},{4,28},{8,16},{12,20},{16,8},{20,12},{24,0},{28,4},{1,25},{... | collective-permute-start | bytes 1585160 | tf_op jit(solution)/shard_map/ppermute | solution.py:461
  9.9 23.9 %collective-permute-start.1 = (bf16[2064,128]{1,0:T(8,128)(2,1)S(1)}, bf16[2064,128]{1,0:T(8,128)(2,1)S(1)}, u32[]{:S(2)}, u32[]{:S(2)}) collective-permute-start(bf16[2064,128]{1,0:T(8,128)(2,1)S(1)} %fusion.1.refs_0_), channel_id=1, source_target_pairs={{0,16},{4,20},{8,24},{12,28},{16,0},{20,4},{24,8},{28,12},{1,17},{... | collective-permute-start | bytes 1585160 | tf_op jit(solution)/shard_map/ppermute | solution.py:461
  10.4 23.5 %collective-permute-start = (bf16[2064,128]{1,0:T(8,128)(2,1)S(1)}, bf16[2064,128]{1,0:T(8,128)(2,1)S(1)}, u32[]{:S(2)}, u32[]{:S(2)}) collective-permute-start(bf16[2064,128]{1,0:T(8,128)(2,1)S(1)} %fusion.1.refs_0_), channel_id=1, source_target_pairs={{0,8},{4,12},{8,0},{12,4},{16,24},{20,28},{24,16},{28,20},{1,9},{5... | collective-permute-start | bytes 1585160 | tf_op jit(solution)/shard_map/ppermute | solution.py:461
  10.9 2.2 %copy-start.5 = (bf16[1024,2048]{1,0:T(8,128)(2,1)S(1)}, bf16[1024,2048]{1,0:T(8,128)(2,1)}, u32[]{:S(2)}) copy-start(bf16[1024,2048]{1,0:T(8,128)(2,1)} %normed_ref.1) | copy-start | bytes 12582916
  13.1 1.0 copy-start.7
  15.9 1.4 %copy-start.9 = (f32[256,2048]{1,0:T(8,128)}, f32[256,2048]{1,0:T(8,128)S(1)}, u32[]{:S(2)}) copy-start(f32[256,2048]{1,0:T(8,128)S(1)} %get-tuple-element.42.g1) | copy-start | bytes 6291460
  17.3 5.6 %copy-start = (bf16[1024,2048]{1,0:T(8,128)(2,1)}, bf16[1024,2048]{1,0:T(8,128)(2,1)S(1)}, u32[]{:S(2)}) copy-start(bf16[1024,2048]{1,0:T(8,128)(2,1)S(1)} %get-tuple-element.39.normed_ref) | copy-start | bytes 12582916
  17.3 5.6 %copy-start.11 = (bf16[1040,256]{1,0:T(8,128)(2,1)}, bf16[1040,256]{1,0:T(8,128)(2,1)S(1)}, u32[]{:S(2)}) copy-start(bf16[1040,256]{1,0:T(8,128)(2,1)S(1)} %collective-permute-done.4.refs_0_.b1) | copy-start | bytes 1597444
  19.6 22.9 %collective-permute-start.10 = (bf16[1056,256]{1,0:T(8,128)(2,1)S(1)}, bf16[1056,256]{1,0:T(8,128)(2,1)S(1)}, u32[]{:S(2)}, u32[]{:S(2)}) collective-permute-start(bf16[1056,256]{1,0:T(8,128)(2,1)S(1)} %collective-permute-done.3.refs_0_.a1), channel_id=1, source_target_pairs={{1,2},{2,1},{5,6},{6,5},{9,10},{10,9},{13,14},{14,13},{17,18},{18,... | collective-permute-start | bytes 1622024 | tf_op jit(solution)/shard_map/ppermute | solution.py:467
  20.3 21.3 %collective-permute-start.11 = (bf16[1040,256]{1,0:T(8,128)(2,1)S(1)}, bf16[1040,256]{1,0:T(8,128)(2,1)S(1)}, u32[]{:S(2)}, u32[]{:S(2)}) collective-permute-start(bf16[1040,256]{1,0:T(8,128)(2,1)S(1)} %collective-permute-done.4.refs_0_.b1), channel_id=1, source_target_pairs={{1,0},{2,3},{5,4},{6,7},{9,8},{10,11},{13,12},{14,15},{17,16},{18,... | collective-permute-start | bytes 1597448 | tf_op jit(solution)/shard_map/ppermute | solution.py:470
  33.9 1.9 %collective-permute-start.6 = (bf16[2064,128]{1,0:T(8,128)(2,1)S(1)}, bf16[2064,128]{1,0:T(8,128)(2,1)S(1)}, u32[]{:S(2)}, u32[]{:S(2)}) collective-permute-start(bf16[2064,128]{1,0:T(8,128)(2,1)S(1)} %collective-permute-done.refs_2_), channel_id=1, source_target_pairs={{0,4},{4,0},{8,12},{12,8},{16,20},{20,16},{24,28},{28,24},{1,5},{5... | collective-permute-start | bytes 1585160 | tf_op jit(solution)/shard_map/ppermute | solution.py:461
  33.9 2.7 %collective-permute-start.7 = (bf16[2064,128]{1,0:T(8,128)(2,1)S(1)}, bf16[2064,128]{1,0:T(8,128)(2,1)S(1)}, u32[]{:S(2)}, u32[]{:S(2)}) collective-permute-start(bf16[2064,128]{1,0:T(8,128)(2,1)S(1)} %collective-permute-done.1.refs_4_), channel_id=1, source_target_pairs={{0,4},{4,0},{8,12},{12,8},{16,20},{20,16},{24,28},{28,24},{1,5},{5... | collective-permute-start | bytes 1585160 | tf_op jit(solution)/shard_map/ppermute | solution.py:461
  34.4 2.9 %collective-permute-start.8 = (bf16[2064,128]{1,0:T(8,128)(2,1)S(1)}, bf16[2064,128]{1,0:T(8,128)(2,1)S(1)}, u32[]{:S(2)}, u32[]{:S(2)}) collective-permute-start(bf16[2064,128]{1,0:T(8,128)(2,1)S(1)} %collective-permute-done.2.refs_6_), channel_id=1, source_target_pairs={{0,4},{4,0},{8,12},{12,8},{16,20},{20,16},{24,28},{28,24},{1,5},{5... | collective-permute-start | bytes 1585160 | tf_op jit(solution)/shard_map/ppermute | solution.py:461
  39.5 2.1 %copy-start.3 = (bf16[2176,1024]{1,0:T(8,128)(2,1)}, bf16[2176,1024]{1,0:T(8,128)(2,1)S(1)}, u32[]{:S(2)}) copy-start(bf16[2176,1024]{1,0:T(8,128)(2,1)S(1)} %get-tuple-element.48.weight_ref) | copy-start | bytes 13369348
  41.6 0.9 copy-start.13
  42.5 20.3 %collective-permute-start.12 = (bf16[1056,256]{1,0:T(8,128)(2,1)S(1)}, bf16[1056,256]{1,0:T(8,128)(2,1)}, u32[]{:S(2)}, u32[]{:S(2)}) collective-permute-start(bf16[1056,256]{1,0:T(8,128)(2,1)S(1)} %collective-permute-done.10.m2), channel_id=1, source_target_pairs={{1,0},{2,3},{5,4},{6,7},{9,8},{10,11},{13,12},{14,15},{17,16},{18,... | collective-permute-start | bytes 1622024 | tf_op jit(solution)/shard_map/ppermute | solution.py:470
  43.8 2.2 %copy-start.1 = (bf16[1024,2048]{1,0:T(8,128)(2,1)S(1)}, bf16[1024,2048]{1,0:T(8,128)(2,1)}, u32[]{:S(2)}) copy-start(bf16[1024,2048]{1,0:T(8,128)(2,1)} %copy-done) | copy-start | bytes 12582916
  46.0 2.3 %copy-start.4 = (bf16[2176,1024]{1,0:T(8,128)(2,1)S(1)}, bf16[2176,1024]{1,0:T(8,128)(2,1)}, u32[]{:S(2)}) copy-start(bf16[2176,1024]{1,0:T(8,128)(2,1)} %copy-done.3) | copy-start | bytes 13369348
  48.2 8.5 %copy-start.2 = (bf16[1024,2048]{1,0:T(8,128)(2,1)S(1)}, bf16[1024,2048]{1,0:T(8,128)(2,1)}, u32[]{:S(2)}) copy-start(bf16[1024,2048]{1,0:T(8,128)(2,1)} %copy-done) | copy-start | bytes 12582916
  49.6 11.9 %copy-start.12 = (bf16[1040,256]{1,0:T(8,128)(2,1)S(1)}, bf16[1040,256]{1,0:T(8,128)(2,1)}, u32[]{:S(2)}) copy-start(bf16[1040,256]{1,0:T(8,128)(2,1)} %copy-done.11) | copy-start | bytes 1597444
  49.6 11.9 %copy-start.14 = (bf16[1040,256]{1,0:T(8,128)(2,1)S(1)}, bf16[1040,256]{1,0:T(8,128)(2,1)}, u32[]{:S(2)}) copy-start(bf16[1040,256]{1,0:T(8,128)(2,1)} %copy-done.13) | copy-start | bytes 1597444
  49.6 18.8 %collective-permute-start.9 = (s16[1040,256]{1,0:T(8,128)(2,1)S(1)}, s16[1040,256]{1,0:T(8,128)(2,1)S(1)}, u32[]{:S(2)}, u32[]{:S(2)}) collective-permute-start(s16[1040,256]{1,0:T(8,128)(2,1)S(1)} %first_values.1), channel_id=1, source_target_pairs={{0,1},{3,2},{4,5},{7,6},{8,9},{11,10},{12,13},{15,14},{16,17},{19,... | collective-permute-start | bytes 1597448 | tf_op jit(solution)/shard_map/ppermute | solution.py:473
  61.5 1.6 %copy-start.10 = (f32[256,2048]{1,0:T(8,128)S(1)}, f32[256,2048]{1,0:T(8,128)}, u32[]{:S(2)}) copy-start(f32[256,2048]{1,0:T(8,128)} %copy-done.9) | copy-start | bytes 6291460
  68.4 5.6 %collective-permute-start.16 = (s16[2096,128]{1,0:T(8,128)(2,1)S(1)}, s16[2096,128]{1,0:T(8,128)(2,1)S(1)}, u32[]{:S(2)}, u32[]{:S(2)}) collective-permute-start(s16[2096,128]{1,0:T(8,128)(2,1)S(1)} %get-tuple-element.66), channel_id=1, source_target_pairs={{0,4},{4,0},{8,12},{12,8},{16,20},{20,16},{24,28},{28,24},{1,5},{5... | collective-permute-start | bytes 1609736 | tf_op jit(solution)/shard_map/ppermute | solution.py:461
  68.4 6.6 %collective-permute-start.17 = (s16[2096,128]{1,0:T(8,128)(2,1)S(1)}, s16[2096,128]{1,0:T(8,128)(2,1)S(1)}, u32[]{:S(2)}, u32[]{:S(2)}) collective-permute-start(s16[2096,128]{1,0:T(8,128)(2,1)S(1)} %get-tuple-element.68), channel_id=1, source_target_pairs={{0,4},{4,0},{8,12},{12,8},{16,20},{20,16},{24,28},{28,24},{1,5},{5... | collective-permute-start | bytes 1609736 | tf_op jit(solution)/shard_map/ppermute | solution.py:461
  68.9 8.0 %collective-permute-start.18 = (s16[2096,128]{1,0:T(8,128)(2,1)S(1)}, s16[2096,128]{1,0:T(8,128)(2,1)S(1)}, u32[]{:S(2)}, u32[]{:S(2)}) collective-permute-start(s16[2096,128]{1,0:T(8,128)(2,1)S(1)} %get-tuple-element.70), channel_id=1, source_target_pairs={{0,4},{4,0},{8,12},{12,8},{16,20},{20,16},{24,28},{28,24},{1,5},{5... | collective-permute-start | bytes 1609736 | tf_op jit(solution)/shard_map/ppermute | solution.py:461
  69.0 9.1 %collective-permute-start.15 = (s16[2096,128]{1,0:T(8,128)(2,1)S(1)}, s16[2096,128]{1,0:T(8,128)(2,1)S(1)}, u32[]{:S(2)}, u32[]{:S(2)}) collective-permute-start(s16[2096,128]{1,0:T(8,128)(2,1)S(1)} %get-tuple-element.64), channel_id=1, source_target_pairs={{0,4},{4,0},{8,12},{12,8},{16,20},{20,16},{24,28},{28,24},{1,5},{5... | collective-permute-start | bytes 1609736 | tf_op jit(solution)/shard_map/ppermute | solution.py:461
  69.4 15.6 %collective-permute-start.14 = (s16[1040,256]{1,0:T(8,128)(2,1)S(1)}, s16[1040,256]{1,0:T(8,128)(2,1)S(1)}, u32[]{:S(2)}, u32[]{:S(2)}) collective-permute-start(s16[1040,256]{1,0:T(8,128)(2,1)S(1)} %get-tuple-element.55), channel_id=1, source_target_pairs={{0,1},{3,2},{4,5},{7,6},{8,9},{11,10},{12,13},{15,14},{16,17},{19,... | collective-permute-start | bytes 1597448 | tf_op jit(solution)/shard_map/ppermute | solution.py:473
  73.9 11.1 %collective-permute-start.13 = (s16[1040,256]{1,0:T(8,128)(2,1)S(1)}, s16[1040,256]{1,0:T(8,128)(2,1)S(1)}, u32[]{:S(2)}, u32[]{:S(2)}) collective-permute-start(s16[1040,256]{1,0:T(8,128)(2,1)S(1)} %hop.3), channel_id=1, source_target_pairs={{1,2},{2,1},{5,6},{6,5},{9,10},{10,9},{13,14},{14,13},{17,18},{18,... | collective-permute-start | bytes 1597448 | tf_op jit(solution)/shard_map/ppermute | solution.py:467
  75.0 25.1 %collective-permute-start.23 = (s16[2096,128]{1,0:T(8,128)(2,1)S(1)}, s16[2096,128]{1,0:T(8,128)(2,1)S(1)}, u32[]{:S(2)}, u32[]{:S(2)}) collective-permute-start(s16[2096,128]{1,0:T(8,128)(2,1)S(1)} %combine.5), channel_id=1, source_target_pairs={{0,8},{4,12},{8,0},{12,4},{16,24},{20,28},{24,16},{28,20},{1,9},{5... | collective-permute-start | bytes 1609736 | tf_op jit(solution)/shard_map/ppermute | solution.py:461
  77.0 25.1 %collective-permute-start.22 = (s16[2096,128]{1,0:T(8,128)(2,1)S(1)}, s16[2096,128]{1,0:T(8,128)(2,1)S(1)}, u32[]{:S(2)}, u32[]{:S(2)}) collective-permute-start(s16[2096,128]{1,0:T(8,128)(2,1)S(1)} %combine.6), channel_id=1, source_target_pairs={{0,16},{4,20},{8,24},{12,28},{16,0},{20,4},{24,8},{28,12},{1,17},{... | collective-permute-start | bytes 1609736 | tf_op jit(solution)/shard_map/ppermute | solution.py:461
  78.1 23.9 %collective-permute-start.21 = (s16[2096,128]{1,0:T(8,128)(2,1)S(1)}, s16[2096,128]{1,0:T(8,128)(2,1)S(1)}, u32[]{:S(2)}, u32[]{:S(2)}) collective-permute-start(s16[2096,128]{1,0:T(8,128)(2,1)S(1)} %combine.7), channel_id=1, source_target_pairs={{0,24},{4,28},{8,16},{12,20},{16,8},{20,12},{24,0},{28,4},{1,25},{... | collective-permute-start | bytes 1609736 | tf_op jit(solution)/shard_map/ppermute | solution.py:461
  79.5 13.1 %slice-start = ((s8[4456448]{0:T(1024)(128)(4,1)}), s8[4194304]{0:T(1024)(128)(4,1)S(1)}, s32[]{:S(2)}) async-start(s8[4456448]{0:T(1024)(128)(4,1)} %bitcast.3), calls=%async_computation | async-start | bytes 8388608
  79.6 12.9 %slice-start.1 = ((s8[4456448]{0:T(1024)(128)(4,1)}), s8[262144]{0:T(1024)(128)(4,1)S(1)}, s32[]{:S(2)}) async-start(s8[4456448]{0:T(1024)(128)(4,1)} %bitcast.3), calls=%async_computation.1 | async-start | bytes 524288
  85.4 7.1 %copy-start.8 = (bf16[1024,256]{1,0:T(8,128)(2,1)S(1)}, bf16[1024,256]{1,0:T(8,128)(2,1)}, u32[]{:S(2)}) copy-start(bf16[1024,256]{1,0:T(8,128)(2,1)} %own.1) | copy-start | bytes 1572868
  85.4 18.6 %collective-permute-start.20 = (s16[1040,256]{1,0:T(8,128)(2,1)S(1)}, s16[1040,256]{1,0:T(8,128)(2,1)S(1)}, u32[]{:S(2)}, u32[]{:S(2)}) collective-permute-start(s16[1040,256]{1,0:T(8,128)(2,1)S(1)} %hop.5), channel_id=1, source_target_pairs={{1,2},{2,1},{5,6},{6,5},{9,10},{10,9},{13,14},{14,13},{17,18},{18,... | collective-permute-start | bytes 1597448 | tf_op jit(solution)/shard_map/ppermute | solution.py:467
  86.8 17.2 %collective-permute-start.19 = (s16[1040,256]{1,0:T(8,128)(2,1)S(1)}, s16[1040,256]{1,0:T(8,128)(2,1)S(1)}, u32[]{:S(2)}, u32[]{:S(2)}) collective-permute-start(s16[1040,256]{1,0:T(8,128)(2,1)S(1)} %hop.4), channel_id=1, source_target_pairs={{0,1},{1,0},{2,3},{3,2},{4,5},{5,4},{6,7},{7,6},{8,9},{9,8},{10,11... | collective-permute-start | bytes 1597448 | tf_op jit(solution)/shard_map/ppermute | solution.py:464
